TPU v7x, 32 devices: a whole 2x2x4 slice. The times are simulated.
32 devices in a mesh: groups: 2 (over x), tensor: 8 (over z, y), batch: 2 (over core).
Axes of the slice: x: 2, y: 2, z: 4, core: 2. Of those that a mesh axis runs over, the one named last changes fastest.
Arguments:
- token_ids: int32 [4, 256], P(None, ('groups', 'batch')), parts along dimension 1, may hold values from 0 to 511
- embed: bfloat16 [512, 8192], P(None, 'tensor')
- norm_gain: bfloat16 [8192], P('tensor'), may hold values from 0.099609375 to 1.8984375
- w_in: bfloat16 [8192, 24576], P(None, 'tensor'), may hold values from -0.0625 to 0.0625
- filters: bfloat16 [8192, 128], P('tensor'), may hold values from -0.59765625 to 0.59765625
- w_out: bfloat16 [8192, 8192], P('tensor'), may hold values from -0.09375 to 0.09375
- cache_rows: bfloat16 [256, 127, 8192], P(('groups', 'tensor', 'batch')), parts along dimension 0, may hold values from -6 to 6
- owner: int32 [256], P('groups'), parts along dimension 0, may hold values from 0 to 127, as said below
- lengths: int32 [256], P(('groups', 'batch')), parts along dimension 0, may hold values from 8 to 255
Outputs:
- block_out: bfloat16 [4, 256, 8192], P(None, ('groups', 'batch'), 'tensor'), parts along dimension 1
There are 2 independent parts, one for each index of `groups`. A program takes and returns all parts, laid end to end along the dimension named above; an argument that names none is the same for every part. Nothing has to cross between parts.
Inputs may be any that keep to these rules, and one draw needn't show every extreme that they name: owner names every sequence exactly once; the prefill rows come in aligned blocks of 8 rows, and block k holds only sequences k % 2 * 64 to k % 2 * 64 + 63.
All inputs are finite; a program needn't handle non-finite values.
Results may differ from a plain program's by a relative error of at most 0.0046.
Values may be sent and summed in bfloat16 or wider, within the bound.
No kernel may reach another device: no remote copies, remote signals or barrier semaphores. Data moves between devices by JAX's collectives and lax.ppermute only.
A program may use at most 256 MiB of HBM per device.

v0:
```python
import jax
import jax.numpy as jnp
from jax import lax
from jax.sharding import PartitionSpec as P

D = 8192


EPSILON = 1e-05


def shifted_taps(filters, count):
    width = filters.shape[1]
    padded = jnp.concatenate(
        [filters.astype(jnp.float32), jnp.zeros((filters.shape[0], count), jnp.float32)], axis=1
    )
    return jnp.stack([padded[:, offset + 1 : offset + width].T for offset in range(count)])


def prefill_terms(cached, tap_table, row_lengths):
    lag_index = jnp.arange(cached.shape[1], dtype=jnp.int32)
    in_range = lag_index[None, :] < row_lengths[:, None]
    masked = jnp.where(in_range[:, :, None], cached, jnp.zeros((), jnp.bfloat16))
    return jnp.einsum(
        "smc,tmc->stc", masked.astype(jnp.float32), tap_table, precision=lax.Precision.HIGHEST
    )


def project_in(stream, norm_gain, w_in):
    squares = lax.psum(jnp.sum(stream * stream, axis=1), "tensor")
    inv_rms = lax.rsqrt(squares / D + EPSILON)
    normed = (stream * inv_rms[:, None] * norm_gain.astype(jnp.float32)).astype(jnp.bfloat16)
    return jnp.dot(
        lax.all_gather(normed, "tensor", axis=1, tiled=True),
        w_in,
        preferred_element_type=jnp.float32,
    )


def project_out(gated_rows, w_out):
    return lax.psum_scatter(
        lax.dot_general(
            w_out, gated_rows, (((0,), (1,)), ((), ())), preferred_element_type=jnp.float32
        ),
        "tensor",
        scatter_dimension=0,
        tiled=True,
    ).T


def per_device(token_ids, embed, norm_gain, w_in, filters, w_out, cache_rows, owner, lengths):
    seq_count = token_ids.shape[1]
    channels = embed.shape[1]
    vocab_count = embed.shape[0]
    row_count = cache_rows.shape[0]
    step_count = token_ids.shape[0]
    tensor_count = lax.axis_size("tensor")
    batch_count = lax.axis_size("batch")
    half_index = lax.axis_index("batch")
    owner_grid = owner.reshape(tensor_count, batch_count, row_count)
    arrived = (
        lax.dynamic_index_in_dim(owner_grid, half_index, 1, keepdims=False).reshape(seq_count)
        - half_index * seq_count
    )
    placed = (
        jnp.zeros((seq_count,), jnp.int32).at[arrived].set(jnp.arange(seq_count, dtype=jnp.int32))
    )
    relayed = lax.all_to_all(cache_rows, "tensor", split_axis=2, concat_axis=0, tiled=True)
    history = prefill_terms(relayed[placed], shifted_taps(filters, step_count), lengths)
    tap_values = filters.astype(jnp.float32)
    labels = jnp.arange(vocab_count, dtype=jnp.int32)
    streams = []
    for position in range(step_count):
        onehot = (token_ids[position][:, None] == labels[None, :]).astype(jnp.bfloat16)
        streams.append(jnp.dot(onehot, embed, preferred_element_type=jnp.float32))
    projections = [project_in(streams[position], norm_gain, w_in) for position in range(step_count)]
    recent = []
    gated_list = []
    for position in range(step_count):
        projected = projections[position]
        queries = projected[:, :channels]
        keys_part = projected[:, channels : 2 * channels]
        values_part = projected[:, 2 * channels :]
        recent.append((keys_part * values_part).astype(jnp.bfloat16))
        filtered = history[:, position]
        for lag_back in range(position + 1):
            filtered = filtered + tap_values[:, lag_back] * recent[position - lag_back].astype(
                jnp.float32
            )
        gated_list.append((queries * filtered).astype(jnp.bfloat16))
    summed_list = [project_out(gated_list[position], w_out) for position in range(step_count)]
    outputs = [
        (streams[position] + summed_list[position]).astype(jnp.bfloat16)
        for position in range(step_count)
    ]
    return jnp.stack(outputs)


def solution(mesh):
    in_specs = (
        P(None, ("groups", "batch")),
        P(None, "tensor"),
        P("tensor"),
        P(None, "tensor"),
        P("tensor", None),
        P("tensor", None),
        P(("groups", "tensor", "batch"), None, None),
        P("groups"),
        P(("groups", "batch")),
    )
    out_specs = P(None, ("groups", "batch"), "tensor")
    return jax.shard_map(
        per_device, mesh=mesh, in_specs=in_specs, out_specs=out_specs, check_vma=False
    )
```

profile of v0, /device:TPU:18, one launch (start us, length us, event | category | flops | bytes accessed | tf_op | source)
XLA Modules:
  0.0 872.4 jit_solution(15064470661394109697)
XLA Ops:
  6.5 24.0 %copy.30 = bf16[8,127,8192]{1,0,2:T(8,128)(2,1)} copy(bf16[8,127,8192]{2,0,1:T(8,128)(2,1)} %param.15) | data formatting | bytes 33292288 | tf_op args[6]
  30.6 0.0 copy-start.19
  30.6 6.3 all-to-all-start
  36.9 0.0 copy-done.16
  37.0 0.4 multiply_reduce_fusion.1
  37.4 0.4 multiply_reduce_fusion.2
  37.8 0.4 multiply_reduce_fusion.3
  38.3 0.4 multiply_reduce_fusion
  38.7 369.0 %all-reduce.1 = (f32[64]{0:T(128)S(1)}, f32[64]{0:T(128)S(1)}, f32[64]{0:T(128)S(1)}, f32[64]{0:T(128)S(1)}) all-reduce(f32[64]{0:T(128)S(1)} %get-tuple-element.24, f32[64]{0:T(128)S(1)} %get-tuple-element.26, f32[64]{0:T(128)S(1)} %get-tuple-element.28, ...), channel_id=1, replica_groups=mesh['groups'=2,'tensor'=8,'batch'=2] {'tensor'}, use_global_device_ids=true, to_apply=%region_8.9 | all-reduce | flops 256 | bytes 2048 | tf_op jit(solution)/shard_map/psum | solution.py:30
  407.7 0.9 multiply_convert_fusion
  408.6 0.0 all-gather.5.cloned.1.call-update
  408.7 0.0 all-gather.7.cloned.1.call-start
  408.7 0.7 all-gather.7.cloned.1.call-update
  409.4 0.0 all-gather.9.cloned.1.call-start
  409.5 0.7 all-gather.9.cloned.1.call-update
  410.2 0.0 all-gather.11.cloned.1.call-start
  410.2 0.5 all-gather.11.cloned.1.call-update
  410.7 0.0 reduce-scatter.5.cloned.1.call-start
  410.8 0.9 slice.121
  411.8 0.1 reshape.60
  411.9 0.1 sub.18
  412.0 1.0 scatter_custom_fusion
  413.0 1.3 slice_reduce_fusion.3
  414.3 1.6 pad_slice_fusion.2
  415.9 0.1 iota_compare_fusion.8
  416.0 30.4 %all-gather.5.cloned.1.call-done = bf16[64,8192]{1,0:T(8,128)(2,1)} async-done(((bf16[64,1024]{1,0:T(8,128)(2,1)}), bf16[64,8192]{1,0:T(8,128)(2,1)}) %all-gather.5.cloned.1.call-update) | async-done | bytes 1048592 | tf_op jit(solution)/shard_map/all_gather | solution.py:34
  446.4 20.2 %fusion.64 = f32[64,3072]{1,0:T(8,128)S(1)} fusion(bf16[64,8192]{1,0:T(8,128)(2,1)} %all-gather.5.cloned.1.call-done, bf16[8192,3072]{1,0:T(8,128)(2,1)} %param.12), kind=kOutput, calls=%fused_computation.121 | convolution fusion | flops 3221225472 | bytes 52166656 | tf_op jit(solution)/shard_map/dot_general | solution.py:33
  466.7 0.0 all-to-all-done
  466.7 25.9 %copy.31 = bf16[8,127,8,1024]{3,1,0,2:T(8,128)(2,1)} copy(bf16[8,127,8,1024]{1,0,3,2:T(8,128)(2,1)} %bitcast.12) | data formatting | bytes 33292288 | tf_op jit(solution)/shard_map/all_to_all | solution.py:68
  492.6 13.5 %gather_fusion = bf16[64,127,1024]{2,1,0:T(8,128)(2,1)} fusion(bf16[64,127,1024]{2,1,0:T(8,128)(2,1)} %bitcast.112, s32[1024]{0:T(1024)S(1)} %pad_clamp_fusion), kind=kCustom, calls=%fused_computation | custom fusion | bytes 33292544 | tf_op jit(solution)/shard_map/gather | solution.py:69
  506.1 14.1 %broadcast_select_fusion = bf16[64,127,1024]{2,1,0:T(8,128)(2,1)} fusion(bf16[64,127,1024]{2,1,0:T(8,128)(2,1)} %gather_fusion, pred[64,127]{1,0:T(8,128)(4,1)S(1)} %iota_compare_fusion.8), kind=kLoop, calls=%fused_computation.2 | loop fusion | flops 8323072 | bytes 33300416 | tf_op jit(solution)/shard_map/jit(_where)/select_n | solution.py:23
  520.2 23.3 %copy.32 = bf16[64,127,1024]{1,0,2:T(8,128)(2,1)} copy(bf16[64,127,1024]{2,1,0:T(8,128)(2,1)} %broadcast_select_fusion) | data formatting | bytes 33292288 | tf_op jit(solution)/shard_map/jit(_where)/select_n | solution.py:23
  543.5 0.0 copy-done.14
  543.5 28.7 %fusion = f32[1024,4,64]{2,1,0:T(4,128)S(1)} fusion(bf16[64,127,1024]{1,0,2:T(8,128)(2,1)} %copy.32, f32[1,127,1024]{1,0,2:T(1,128)} %bitcast.120, f32[1,127,1024]{1,0,2:T(1,128)} %bitcast.119, f32[1,127,1024]{1,0,2:T(1,128)S(1)} %bitcast.118, f32[1,127,1024]{1,0,2:T(1,128)S(1)} %bitcast.117), kind=kOutput, calls=%fused_computation.7 | convolution fusion | flops 401068032 | bytes 19775488 | tf_op jit(solution)/shard_map/smc,tmc->stc/dot_general | solution.py:24
  572.2 1.0 copy.33
  573.3 10.6 %convolution_bitcast_fusion.3 = f32[8192,64]{0,1:T(8,128)} fusion(bf16[1024,8192]{1,0:T(8,128)(2,1)} %param.14, bf16[64,1024]{1,0:T(8,128)(2,1)S(1)} %fusion.29, f32[64,4,1024]{2,0,1:T(8,128)S(1)} %bitcast.113, f32[64,3072]{1,0:T(8,128)} %copy-done.3, f32[1024]{0:T(1024)S(1)} %get-tuple-element.5), kind=kOutput, calls=%fused_computation.6 | convolution fusion | flops 1074069504 | bytes 19533824 | tf_op jit(solution)/shard_map/dot_general | solution.py:42
  583.9 0.0 reduce-scatter.5.cloned.1.call-update
  583.9 0.0 reduce-scatter.7.cloned.1.call-start
  583.9 0.0 all-gather.7.cloned.1.call-done
  584.0 20.3 %fusion.65 = f32[64,3072]{1,0:T(8,128)S(1)} fusion(bf16[64,8192]{1,0:T(8,128)(2,1)} %all-gather.7.cloned.1.call-done, bf16[8192,3072]{1,0:T(8,128)(2,1)} %param.12), kind=kOutput, calls=%fused_computation.122 | convolution fusion | flops 3221225472 | bytes 52166656 | tf_op jit(solution)/shard_map/dot_general | solution.py:33
  604.3 10.3 %convolution_bitcast_fusion.2 = f32[8192,64]{0,1:T(8,128)} fusion(bf16[1024,8192]{1,0:T(8,128)(2,1)} %param.14, bf16[64,1024]{1,0:T(8,128)(2,1)S(1)} %fusion.28, bf16[64,1024]{1,0:T(8,128)(2,1)S(1)} %fusion.29, f32[64,4,1024]{2,0,1:T(8,128)S(1)} %bitcast.114, f32[64,3072]{1,0:T(8,128)S(1)} %fusion.65, f32[1024]{0:T(1024)S(1)} %get-tuple-element.8, ...), kind=kOutput, calls=%fused_computation.5 | convolution fusion | flops 1074266112 | bytes 19668992 | tf_op jit(solution)/shard_map/dot_general | solution.py:42
  614.7 0.0 reduce-scatter.7.cloned.1.call-update
  614.7 0.0 reduce-scatter.9.cloned.1.call-start
  614.7 0.0 all-gather.9.cloned.1.call-done
  614.8 20.7 %fusion.66 = f32[64,3072]{1,0:T(8,128)S(1)} fusion(bf16[64,8192]{1,0:T(8,128)(2,1)} %all-gather.9.cloned.1.call-done, bf16[8192,3072]{1,0:T(8,128)(2,1)} %param.12), kind=kOutput, calls=%fused_computation.123 | convolution fusion | flops 3221225472 | bytes 52166656 | tf_op jit(solution)/shard_map/dot_general | solution.py:33
  635.5 10.3 %convolution_bitcast_fusion.1 = f32[8192,64]{0,1:T(8,128)} fusion(bf16[1024,8192]{1,0:T(8,128)(2,1)} %param.14, bf16[64,1024]{1,0:T(8,128)(2,1)S(1)} %fusion.27, bf16[64,1024]{1,0:T(8,128)(2,1)S(1)} %fusion.28, bf16[64,1024]{1,0:T(8,128)(2,1)S(1)} %fusion.29, f32[64,4,1024]{2,0,1:T(8,128)S(1)} %bitcast.115, f32[64,3072]{1,0:T(8,128)S(1)} %fusion.66, ...), kind=kOutput, calls=%fused_computation.4 | convolution fusion | flops 1074462720 | bytes 19804160 | tf_op jit(solution)/shard_map/dot_general | solution.py:42
  645.8 0.0 reduce-scatter.9.cloned.1.call-update
  645.8 0.0 copy-start.15
  645.8 0.0 reduce-scatter.11.cloned.1.call-start
  645.8 0.0 all-gather.11.cloned.1.call-done
  645.9 0.0 copy-start.1
  645.9 20.3 %fusion.67 = f32[64,3072]{1,0:T(8,128)S(1)} fusion(bf16[64,8192]{1,0:T(8,128)(2,1)} %all-gather.11.cloned.1.call-done, bf16[8192,3072]{1,0:T(8,128)(2,1)} %param.12), kind=kOutput, calls=%fused_computation.124 | convolution fusion | flops 3221225472 | bytes 52166656 | tf_op jit(solution)/shard_map/dot_general | solution.py:33
  666.2 10.4 %convolution_bitcast_fusion = f32[8192,64]{0,1:T(8,128)} fusion(bf16[1024,8192]{1,0:T(8,128)(2,1)} %param.14, bf16[64,1024]{1,0:T(8,128)(2,1)S(1)} %fusion.27, bf16[64,1024]{1,0:T(8,128)(2,1)S(1)} %fusion.28, bf16[64,1024]{1,0:T(8,128)(2,1)S(1)} %fusion.29, f32[64,4,1024]{2,0,1:T(8,128)} %bitcast.116, f32[64,3072]{1,0:T(8,128)S(1)} %fusion.67, ...), kind=kOutput, calls=%fused_computation.3 | convolution fusion | flops 1074790400 | bytes 20332544 | tf_op jit(solution)/shard_map/dot_general | solution.py:42
  676.7 0.0 reduce-scatter.11.cloned.1.call-update
  676.7 0.0 reduce-scatter.5.cloned.1.call-done
  676.7 1.0 fusion.34
  677.7 44.7 %reduce-scatter.7.cloned.1.call-done = f32[1024,64]{0,1:T(8,128)} async-done(((f32[8192,64]{0,1:T(8,128)}), f32[1024,64]{0,1:T(8,128)}) %reduce-scatter.7.cloned.1.call-update) | async-done | bytes 262160 | tf_op jit(solution)/shard_map/reduce_scatter | solution.py:41
  722.4 1.0 fusion.35
  723.4 69.8 %reduce-scatter.9.cloned.1.call-done = f32[1024,64]{0,1:T(8,128)} async-done(((f32[8192,64]{0,1:T(8,128)}), f32[1024,64]{0,1:T(8,128)}) %reduce-scatter.9.cloned.1.call-update) | async-done | bytes 262160 | tf_op jit(solution)/shard_map/reduce_scatter | solution.py:41
  793.1 0.0 copy-done.6
  793.1 1.0 fusion.36
  794.1 69.6 %reduce-scatter.11.cloned.1.call-done = f32[1024,64]{0,1:T(8,128)} async-done(((f32[8192,64]{0,1:T(8,128)}), f32[1024,64]{0,1:T(8,128)}) %reduce-scatter.11.cloned.1.call-update) | async-done | bytes 262160 | tf_op jit(solution)/shard_map/reduce_scatter | solution.py:41
  863.7 1.0 fusion.37
  864.7 0.9 pad_maximum_fusion
  (48 shorter events, 0.3 us)
Async XLA Ops:
  6.5 30.4 %copy-start = (bf16[512,1024]{1,0:T(8,128)(2,1)S(1)}, bf16[512,1024]{1,0:T(8,128)(2,1)}, u32[]{:S(2)}) copy-start(bf16[512,1024]{1,0:T(8,128)(2,1)} %param.10) | copy-start | bytes 3145732
  30.6 6.3 copy-start.16
  30.6 6.4 copy-start.17
  30.6 380.2 %copy-start.4 = (bf16[1024,128]{1,0:T(8,128)(2,1)S(1)}, bf16[1024,128]{1,0:T(8,128)(2,1)}, u32[]{:S(2)}) copy-start(bf16[1024,128]{1,0:T(8,128)(2,1)} %param.13) | copy-start | bytes 786436
  30.6 381.2 %copy-start.18 = (s32[128]{0:T(128)S(1)}, s32[128]{0:T(128)}, u32[]{:S(2)}) copy-start(s32[128]{0:T(128)} %param.16) | copy-start | bytes 1540
  30.6 385.3 %copy-start.19 = (s32[64]{0:T(128)S(1)}, s32[64]{0:T(128)}, u32[]{:S(2)}) copy-start(s32[64]{0:T(128)} %param.17) | copy-start | bytes 772
  30.6 436.1 %all-to-all-start = ((bf16[8,127,8192]{1,0,2:T(8,128)(2,1)}), bf16[8,127,8192]{1,0,2:T(8,128)(2,1)}, u32[]{:S(2)}, u32[]{:S(2)}) async-start(bf16[8,127,8192]{1,0,2:T(8,128)(2,1)} %copy.30), calls=%async_computation | async-start | bytes 33554432 | tf_op jit(solution)/shard_map/all_to_all | solution.py:68
  36.9 409.5 %all-gather.5.cloned.1.call-start = ((), (), s32[]{:S(2)}) async-start(), calls=%async_computation.5 | async-start | bytes 1179648 | tf_op jit(solution)/shard_map/all_gather | solution.py:34
  37.4 429.2 %copy-start.5 = (f32[64,1024]{1,0:T(8,128)}, f32[64,1024]{1,0:T(8,128)S(1)}, u32[]{:S(2)}) copy-start(f32[64,1024]{1,0:T(8,128)S(1)} %get-tuple-element.25) | copy-start | bytes 786436
  37.8 428.8 %copy-start.9 = (f32[64,1024]{1,0:T(8,128)}, f32[64,1024]{1,0:T(8,128)S(1)}, u32[]{:S(2)}) copy-start(f32[64,1024]{1,0:T(8,128)S(1)} %get-tuple-element.27) | copy-start | bytes 786436
  38.3 428.3 %copy-start.11 = (f32[64,1024]{1,0:T(8,128)}, f32[64,1024]{1,0:T(8,128)S(1)}, u32[]{:S(2)}) copy-start(f32[64,1024]{1,0:T(8,128)S(1)} %get-tuple-element.29) | copy-start | bytes 786436
  38.7 427.9 %copy-start.7 = (f32[64,1024]{1,0:T(8,128)}, f32[64,1024]{1,0:T(8,128)S(1)}, u32[]{:S(2)}) copy-start(f32[64,1024]{1,0:T(8,128)S(1)} %get-tuple-element.31) | copy-start | bytes 786436
  408.7 175.3 %all-gather.7.cloned.1.call-start = ((), (), s32[]{:S(2)}) async-start(), calls=%async_computation.7 | async-start | bytes 1179648 | tf_op jit(solution)/shard_map/all_gather | solution.py:34
  409.4 205.3 %all-gather.9.cloned.1.call-start = ((), (), s32[]{:S(2)}) async-start(), calls=%async_computation.9 | async-start | bytes 1179648 | tf_op jit(solution)/shard_map/all_gather | solution.py:34
  410.2 235.7 %all-gather.11.cloned.1.call-start = ((), (), s32[]{:S(2)}) async-start(), calls=%async_computation.11 | async-start | bytes 1179648 | tf_op jit(solution)/shard_map/all_gather | solution.py:34
  410.7 266.0 %reduce-scatter.5.cloned.1.call-start = ((), (), s32[]{:S(2)}) async-start(), calls=%async_computation.6 | async-start | bytes 2359296 | tf_op jit(solution)/shard_map/reduce_scatter | solution.py:41
  466.6 26.0 %copy-start.3 = (f32[64,3072]{1,0:T(8,128)}, f32[64,3072]{1,0:T(8,128)S(1)}, u32[]{:S(2)}) copy-start(f32[64,3072]{1,0:T(8,128)S(1)} %fusion.64) | copy-start | bytes 2359300
  520.2 23.3 %copy-start.13 = (f32[1024,127]{1,0:T(8,128)S(1)}, f32[1024,127]{1,0:T(8,128)}, u32[]{:S(2)}) copy-start(f32[1024,127]{1,0:T(8,128)} %slice.121) | copy-start | bytes 1560580
  520.2 23.3 %copy-start.14 = (f32[1024,127]{1,0:T(8,128)S(1)}, f32[1024,127]{1,0:T(8,128)}, u32[]{:S(2)}) copy-start(f32[1024,127]{1,0:T(8,128)} %get-tuple-element.13) | copy-start | bytes 1560580
  573.2 62.2 %copy-start.2 = (f32[1024,4,64]{0,2,1:T(8,128)}, f32[1024,4,64]{0,2,1:T(8,128)S(1)}, u32[]{:S(2)}) copy-start(f32[1024,4,64]{0,2,1:T(8,128)S(1)} %copy.33) | copy-start | bytes 3145732
  583.9 138.5 %reduce-scatter.7.cloned.1.call-start = ((), (), s32[]{:S(2)}) async-start(), calls=%async_computation.8 | async-start | bytes 2359296 | tf_op jit(solution)/shard_map/reduce_scatter | solution.py:41
  614.7 178.4 %reduce-scatter.9.cloned.1.call-start = ((), (), s32[]{:S(2)}) async-start(), calls=%async_computation.10 | async-start | bytes 2359296 | tf_op jit(solution)/shard_map/reduce_scatter | solution.py:41
  645.8 20.4 %copy-start.15 = (f32[1024]{0:T(1024)S(1)}, f32[1024]{0:T(1024)}, u32[]{:S(2)}) copy-start(f32[1024]{0:T(1024)} %get-tuple-element.6) | copy-start | bytes 12292
  645.8 217.9 %reduce-scatter.11.cloned.1.call-start = ((), (), s32[]{:S(2)}) async-start(), calls=%async_computation.12 | async-start | bytes 2359296 | tf_op jit(solution)/shard_map/reduce_scatter | solution.py:41
  645.9 219.7 %copy-start.1 = (bf16[512,1024]{1,0:T(8,128)(2,1)S(1)}, bf16[512,1024]{1,0:T(8,128)(2,1)}, u32[]{:S(2)}) copy-start(bf16[512,1024]{1,0:T(8,128)(2,1)} %param.10) | copy-start | bytes 3145732
  666.2 10.6 %copy-start.12 = (f32[64,1024]{1,0:T(8,128)S(1)}, f32[64,1024]{1,0:T(8,128)}, u32[]{:S(2)}) copy-start(f32[64,1024]{1,0:T(8,128)} %copy-done.11) | copy-start | bytes 786436
  666.2 56.2 %copy-start.10 = (f32[64,1024]{1,0:T(8,128)S(1)}, f32[64,1024]{1,0:T(8,128)}, u32[]{:S(2)}) copy-start(f32[64,1024]{1,0:T(8,128)} %copy-done.9) | copy-start | bytes 786436
  666.2 126.9 %copy-start.6 = (f32[64,1024]{1,0:T(8,128)S(1)}, f32[64,1024]{1,0:T(8,128)}, u32[]{:S(2)}) copy-start(f32[64,1024]{1,0:T(8,128)} %copy-done.5) | copy-start | bytes 786436
  666.2 197.5 %copy-start.8 = (f32[64,1024]{1,0:T(8,128)S(1)}, f32[64,1024]{1,0:T(8,128)}, u32[]{:S(2)}) copy-start(f32[64,1024]{1,0:T(8,128)} %copy-done.7) | copy-start | bytes 786436
Sparse Core Ops, SparseCore 0:
  408.8 37.5 all-gather.4
  448.6 38.8 all-gather.6
  489.7 38.9 all-gather.8
  530.7 38.9 all-gather.10
  584.0 67.8 reduce-scatter.4
  655.3 67.0 reduce-scatter.6
  725.9 67.1 reduce-scatter.8
  796.6 66.9 reduce-scatter.10
where the time goes:
time: 877 us; the launch traced here: 872 us
  blocking collectives  369 us (42%)
  waiting for transfers between devices  216 us (25%)
  matrix products  154 us (18%)
  local copies, waits for them, and re-layouts  92.9 us (11%)
  other arithmetic  20 us (2%)
  between operations  13.9 us (2%)
    psum x1, blocking collectives, project_in(): squares = lax.psum(jnp.sum(stream * stream, axis=1), 'tensor')  369 us
    reduce_scatter x4, waiting for transfers between devices, project_out(): lax.psum_scatter(lax.dot_general(w_out, gated_rows, (((0,), (1,)), ((), (...  184 us
    dot_general x4, matrix products, project_in(): jnp.dot(lax.all_gather(normed, 'tensor', axis=1, tiled=True), w_in, prefe...  81.4 us
    dot_general x4, matrix products, project_out(): lax.dot_general(w_out, gated_rows, (((0,), (1,)), ((), ())), preferred_el...  41.7 us
    all_gather x4, waiting for transfers between devices, project_in(): lax.all_gather(normed, 'tensor', axis=1, tiled=True)  30.4 us
    dot_general x1, matrix products, prefill_terms(): jnp.einsum('smc,tmc->stc', masked.astype(jnp.float32), tap_table, precisi...  28.7 us
    all_to_all x1, local copies, waits for them, and re-layouts, per_device(): lax.all_to_all(cache_rows, 'tensor', split_axis=2, concat_axis=0, tiled=T...  25.9 us
    unnamed x41, local copies, waits for them, and re-layouts  24.1 us
  transfers between devices with their start and end apart: 9, of which 4 were waited for; matrix products, arithmetic and copies ran while one was open for 28% of the time, Pallas kernels for 0%

commit v1 on v0

v1 whole, which is shorter than its diff:
```python
import functools

import jax
import jax.numpy as jnp
from jax import lax
from jax.experimental import pallas as pl
from jax.experimental.pallas import tpu as pltpu
from jax.sharding import PartitionSpec as P

D = 8192
EPSILON = 1e-05
LANES = 128
SUBLANES = 8
PACKED = 16
VMEM_LIMIT = 56 * 1024 * 1024


def history_kernel(steps, lags, row_lengths, taps_ref, cache_ref, out_ref, taps_scr):
    rows, _, channels = cache_ref.shape
    width = taps_scr.shape[0] - PACKED
    taps_scr[pl.ds(0, width), :] = taps_ref[0, pl.ds(0, width), :].astype(jnp.float32)
    taps_scr[pl.ds(width, PACKED), :] = jnp.zeros((PACKED, channels), jnp.float32)
    lag_index = lax.broadcasted_iota(jnp.int32, (PACKED, LANES), 0)

    def one_chunk(chunk, carry):
        at = pl.ds(pl.multiple_of(chunk * LANES, LANES), LANES)
        sums = [[jnp.zeros((SUBLANES, LANES), jnp.float32) for _ in range(rows)] for _ in range(steps)]
        for first in range(0, lags, PACKED):
            taps = [taps_scr[pl.ds(first + 1 + step, PACKED), at] for step in range(steps)]
            count = min(PACKED, lags - first)
            for row in range(rows):
                values = cache_ref[row, pl.ds(first, count), at].astype(jnp.float32)
                if count < PACKED:
                    values = jnp.concatenate(
                        [values, jnp.zeros((PACKED - count, LANES), jnp.float32)], axis=0
                    )
                values = jnp.where(lag_index < row_lengths[row] - first, values, 0.0)
                for step in range(steps):
                    terms = values * taps[step]
                    sums[step][row] += terms[:SUBLANES] + terms[SUBLANES:]
        for step in range(steps):
            totals = [jnp.sum(sums[step][row], axis=0, keepdims=True) for row in range(rows)]
            out_ref[0, step, :, at] = jnp.concatenate(totals, axis=0).astype(out_ref.dtype)
        return carry

    lax.fori_loop(0, channels // LANES, one_chunk, 0)


def history_terms(cache_rows, taps_all, row_lengths, steps):
    rows, lags, width = cache_rows.shape
    owners, tap_rows, channels = taps_all.shape
    return pl.pallas_call(
        functools.partial(history_kernel, steps, lags),
        grid_spec=pltpu.PrefetchScalarGridSpec(
            num_scalar_prefetch=1,
            grid=(owners,),
            in_specs=[
                pl.BlockSpec((1, tap_rows, channels), lambda block, _: (block, 0, 0)),
                pl.BlockSpec((rows, lags, channels), lambda block, _: (0, 0, block)),
            ],
            out_specs=pl.BlockSpec((1, steps, rows, channels), lambda block, _: (block, 0, 0, 0)),
            scratch_shapes=[pltpu.VMEM((lags + 1 + PACKED, channels), jnp.float32)],
        ),
        out_shape=jax.ShapeDtypeStruct((owners, steps, rows, channels), jnp.bfloat16),
        compiler_params=pltpu.CompilerParams(vmem_limit_bytes=VMEM_LIMIT),
        cost_estimate=pl.CostEstimate(
            flops=2 * steps * rows * lags * width,
            bytes_accessed=2 * rows * lags * width,
            transcendentals=0,
        ),
        name="history_terms",
    )(row_lengths, taps_all, cache_rows)


def gate_kernel(steps, shards, x_ref, wq_ref, wk_ref, wv_ref, taps_ref, hist_ref, out_ref, acc):
    part = pl.program_id(1)
    channels = x_ref.shape[2]

    @pl.when(part == 0)
    def _():
        acc[...] = jnp.zeros_like(acc)

    for index, w_ref in enumerate((wq_ref, wk_ref, wv_ref)):
        total = acc[index]
        for shard in range(shards):
            total += jnp.dot(
                x_ref[part * shards + shard],
                w_ref[pl.ds(shard * channels, channels), :],
                preferred_element_type=jnp.float32,
            )
        acc[index] = total

    @pl.when(part == pl.num_programs(1) - 1)
    def _():
        seqs = out_ref.shape[0] // steps
        recent = (acc[1] * acc[2]).astype(jnp.bfloat16)
        for step in range(steps):
            at = pl.ds(step * seqs, seqs)
            filtered = hist_ref[at, :]
            for back in range(step + 1):
                older = recent[(step - back) * seqs : (step - back + 1) * seqs]
                filtered += taps_ref[pl.ds(back, 1), :].astype(jnp.float32) * older.astype(jnp.float32)
            out_ref[at, :] = (acc[0, at, :] * filtered).astype(jnp.bfloat16)


def gated_rows(normed, w_in, taps, history, steps):
    owners, rows, channels = normed.shape
    block = min(256, channels)
    blocks = channels // block
    shards = max(1, min(owners, 2048 // channels))
    weights = [
        pl.BlockSpec((shards * channels, block), functools.partial(lambda first, c, k: (k, first + c), index * blocks))
        for index in range(3)
    ]
    return pl.pallas_call(
        functools.partial(gate_kernel, steps, shards),
        grid=(blocks, owners // shards),
        in_specs=[
            pl.BlockSpec((owners, rows, channels), lambda c, k: (0, 0, 0)),
            *weights,
            pl.BlockSpec((PACKED, block), lambda c, k: (0, c)),
            pl.BlockSpec((rows, block), lambda c, k: (0, c)),
        ],
        out_specs=pl.BlockSpec((rows, block), lambda c, k: (0, c)),
        out_shape=jax.ShapeDtypeStruct((rows, channels), jnp.bfloat16),
        scratch_shapes=[pltpu.VMEM((3, rows, block), jnp.float32)],
        compiler_params=pltpu.CompilerParams(vmem_limit_bytes=VMEM_LIMIT),
        cost_estimate=pl.CostEstimate(
            flops=2 * rows * w_in.shape[0] * w_in.shape[1],
            bytes_accessed=2 * w_in.shape[0] * w_in.shape[1],
            transcendentals=0,
        ),
        name="gated_rows",
    )(normed, w_in, w_in, w_in, taps, history)


def share_kernel(x_ref, w_ref, out_ref):
    out_ref[0] = jnp.dot(x_ref[...], w_ref[...], preferred_element_type=jnp.float32).astype(
        out_ref.dtype
    )


def output_shares(gated, w_out, owners):
    rows, channels = gated.shape
    block = w_out.shape[1] // owners
    return pl.pallas_call(
        share_kernel,
        grid=(owners,),
        in_specs=[
            pl.BlockSpec((rows, channels), lambda n: (0, 0)),
            pl.BlockSpec((channels, block), lambda n: (0, n)),
        ],
        out_specs=pl.BlockSpec((1, rows, block), lambda n: (n, 0, 0)),
        out_shape=jax.ShapeDtypeStruct((owners, rows, block), jnp.bfloat16),
        compiler_params=pltpu.CompilerParams(vmem_limit_bytes=VMEM_LIMIT),
        cost_estimate=pl.CostEstimate(
            flops=2 * rows * channels * w_out.shape[1],
            bytes_accessed=2 * channels * w_out.shape[1],
            transcendentals=0,
        ),
        name="output_shares",
    )(gated, w_out)


def per_device(token_ids, embed, norm_gain, w_in, filters, w_out, cache_rows, owner, lengths):
    steps, seqs = token_ids.shape
    vocab, channels = embed.shape
    rows = cache_rows.shape[0]
    taps = filters.shape[1]
    owners = lax.axis_size("tensor")
    halves = lax.axis_size("batch")
    mine = lax.axis_index("tensor")
    half = lax.axis_index("batch")

    small = jnp.concatenate(
        [filters.T, norm_gain[None, :], jnp.zeros((PACKED - 1, channels), jnp.bfloat16)], axis=0
    )
    small_all = lax.all_gather(small, "tensor")

    onehot = token_ids.reshape(-1)[:, None] == jnp.arange(vocab, dtype=jnp.int32)[None, :]
    stream = jnp.dot(onehot.astype(jnp.bfloat16), embed, preferred_element_type=jnp.float32)
    stream_all = lax.all_gather(stream.astype(jnp.bfloat16), "tensor")

    owner_grid = owner.reshape(owners, halves, rows)
    arrived = lax.dynamic_index_in_dim(owner_grid, half, 1, keepdims=False) - half * seqs
    own = lax.dynamic_index_in_dim(arrived, mine, 0, keepdims=False)
    seq_index = jnp.arange(seqs, dtype=jnp.int32)
    row_lengths = jnp.sum(jnp.where(own[:, None] == seq_index[None, :], lengths[None, :], 0), axis=1)

    history = history_terms(cache_rows, small_all, row_lengths, steps)
    history = lax.all_to_all(history, "tensor", 0, 0, tiled=True)
    step_index = jnp.arange(steps, dtype=jnp.int32)
    place = (
        (step_index[:, None, None, None, None] == step_index[None, None, None, :, None])
        & (seq_index[None, :, None, None, None] == arrived[None, None, :, None, :])
    ).reshape(steps * seqs, owners * steps * rows)
    history = jnp.dot(
        place.astype(jnp.bfloat16),
        history.reshape(owners * steps * rows, channels),
        preferred_element_type=jnp.float32,
    )

    wide = stream_all.astype(jnp.float32)
    inv_rms = lax.rsqrt(jnp.sum(wide * wide, axis=(0, 2)) / D + EPSILON)
    gain = small_all[:, taps, :].astype(jnp.float32)
    normed = (wide * inv_rms[None, :, None] * gain[:, None, :]).astype(jnp.bfloat16)

    gated = gated_rows(normed, w_in, small, history, steps)
    shares = lax.all_to_all(output_shares(gated, w_out, owners), "tensor", 0, 0, tiled=True)
    summed = jnp.sum(shares.astype(jnp.float32), axis=0)
    return (stream + summed).astype(jnp.bfloat16).reshape(steps, seqs, channels)


def solution(mesh):
    in_specs = (
        P(None, ("groups", "batch")),
        P(None, "tensor"),
        P("tensor"),
        P(None, "tensor"),
        P("tensor", None),
        P("tensor", None),
        P(("groups", "tensor", "batch"), None, None),
        P("groups"),
        P(("groups", "batch")),
    )
    out_specs = P(None, ("groups", "batch"), "tensor")
    return jax.shard_map(
        per_device, mesh=mesh, in_specs=in_specs, out_specs=out_specs, check_vma=False
    )
```

time: 877 us -> 299 us (0.34)
  blocking collectives: 369 us -> 95.7 us
  matrix products: 154 us -> 2.61 us
  waiting for transfers between devices: 216 us -> 82.3 us
  local copies, waits for them, and re-layouts: 92.9 us -> 22.4 us
  Pallas kernels: 0 us -> 60.3 us
    psum x1 -> x0, blocking collectives: 369 us -> none  [project_in(): squares = lax.psum(jnp.sum(stream * stream, axis=1), 'tensor')]
    reduce_scatter x4 -> x0, waiting for transfers between devices: 184 us -> none  [project_out(): lax.psum_scatter(lax.dot_general(w_out, gated_rows, (((0,), (1,)), ((), (...]
    dot_general x13 -> x2, matrix products: 154 us -> 2.61 us  [the longest x1 1.32 us: per_device(): jnp.dot(place.astype(jnp.bfloat16), history.reshape(owners * steps * rows...]
    all_to_all x0 -> x1, blocking collectives: none -> 95.7 us  [per_device(): lax.all_to_all(output_shares(gated, w_out, owners), 'tensor', 0, 0, tiled...]
    pallas_call x0 -> x3, Pallas kernels: none -> 60.3 us  [the longest x1 28.1 us: gated_rows(): pl.pallas_call(functools.partial(gate_kernel, steps, shards), grid=(block...]
    all_gather x4 -> x2, waiting for transfers between devices: 30.4 us -> 69.2 us  [the longest x1 38.7 us: per_device(): stream_all = lax.all_gather(stream.astype(jnp.bfloat16), 'tensor')]
    all_to_all x1 -> x0, local copies, waits for them, and re-layouts: 25.9 us -> none  [per_device(): lax.all_to_all(cache_rows, 'tensor', split_axis=2, concat_axis=0, tiled=T...]
    select_n x1 -> x0, local copies, waits for them, and re-layouts: 23.3 us -> none  [prefill_terms(): jnp.where(in_range[:, :, None], cached, jnp.zeros((), jnp.bfloat16))]
  transfers between devices with their start and end apart: 9 -> 3, of which waited for: 4 -> 3; matrix products, arithmetic and copies ran while one was open for 28% -> 8% of each run, Pallas kernels for 0% -> 7%
where the time goes in v1:
time: 299 us; the launch traced here: 295 us
  blocking collectives  95.7 us (32%)
  waiting for transfers between devices  82.3 us (28%)
  Pallas kernels  60.3 us (20%)
  local copies, waits for them, and re-layouts  22.4 us (7%)
  between operations  13.5 us (5%)
  other arithmetic  13.3 us (4%)
  starting transfers between devices  4.52 us (2%)
    all_to_all x1, blocking collectives, per_device(): lax.all_to_all(output_shares(gated, w_out, owners), 'tensor', 0, 0, tiled...  95.7 us
    all_gather x1, waiting for transfers between devices, per_device(): stream_all = lax.all_gather(stream.astype(jnp.bfloat16), 'tensor')  38.7 us
    all_gather x1, waiting for transfers between devices, per_device(): small_all = lax.all_gather(small, 'tensor')  30.5 us
    pallas_call x1, Pallas kernels, gated_rows(): pl.pallas_call(functools.partial(gate_kernel, steps, shards), grid=(block...  28.1 us
    pallas_call x1, Pallas kernels, history_terms(): pl.pallas_call(functools.partial(history_kernel, steps, lags), grid_spec=...  20.1 us
    unnamed x9, local copies, waits for them, and re-layouts  19.9 us
    all_to_all x1, waiting for transfers between devices, per_device(): history = lax.all_to_all(history, 'tensor', 0, 0, tiled=True)  13.1 us
    pallas_call x1, Pallas kernels, output_shares(): pl.pallas_call(share_kernel, grid=(owners,), in_specs=[pl.BlockSpec((rows...  12.1 us
  transfers between devices with their start and end apart: 3, of which 3 were waited for; matrix products, arithmetic and copies ran while one was open for 8% of the time, Pallas kernels for 7%

profile of v1, /device:TPU:18, one launch (start us, length us, event | category | flops | bytes accessed | tf_op | source)
XLA Modules:
  0.0 294.6 jit_solution(3765216575795925449)
XLA Ops:
  6.5 0.0 copy-start
  6.5 0.0 all-gather.7.cloned.1.call-start
  6.5 1.2 copy.14
  7.7 0.7 broadcast_in_dim.16
  8.4 0.1 pad.2.clone
  8.5 0.8 maximum_maximum_fusion.taps_ref
  9.3 0.0 all-gather.7.cloned.1.call-update
  9.4 0.0 all-gather.5.cloned.1.call-start
  9.4 0.8 eq.66
  10.2 0.0 copy-done
  10.2 1.3 fusion.5
  11.5 0.0 all-gather.5.cloned.1.call-update
  11.5 0.7 reshape.62
  12.2 0.0 copy-start.2
  12.3 18.7 %copy.15.cache_ref = bf16[8,127,8192]{2,1,0:T(8,128)(2,1)} copy(bf16[8,127,8192]{2,0,1:T(8,128)(2,1)} %param.15) | data formatting | bytes 33292288 | tf_op args[6]
  30.9 0.0 copy-done.2
  31.0 0.7 select_reduce_fusion.row_lengths
  31.7 30.5 %all-gather.7.cloned.1.call-done = bf16[1152,1024]{1,0:T(8,128)(2,1)} async-done(((bf16[144,1024]{1,0:T(8,128)(2,1)}), bf16[1152,1024]{1,0:T(8,128)(2,1)}) %all-gather.7.cloned.1.call-update) | async-done | bytes 2359312 | tf_op jit(solution)/shard_map/all_gather | solution.py:178
  62.2 20.1 %history_terms.1 = bf16[8,4,8,1024]{3,2,1,0:T(8,128)(2,1)} custom-call(s32[8]{0:T(128)} %select_reduce_fusion.row_lengths, bf16[8,144,1024]{2,1,0:T(8,128)(2,1)} %bitcast.19, bf16[8,127,8192]{2,1,0:T(8,128)(2,1)} %copy.15.cache_ref), custom_call_target="tpu_custom_call" | custom-call | flops 66584576 | bytes 16646144 | tf_op jit(solution)/shard_map/history_terms/pallas_call | solution.py:52
  82.2 4.5 %all-to-all-start = ((bf16[8,4,8,1024]{3,2,1,0:T(8,128)(2,1)}), bf16[8,4,8,1024]{3,2,1,0:T(8,128)(2,1)S(1)}, u32[]{:S(2)}, u32[]{:S(2)}) async-start(bf16[8,4,8,1024]{3,2,1,0:T(8,128)(2,1)} %history_terms.1), calls=%async_computation | async-start | bytes 1048576 | tf_op jit(solution)/shard_map/all_to_all | solution.py:191
  86.7 0.1 iota_compare_fusion.2
  86.8 0.2 broadcast_and_fusion
  87.0 0.3 and.28
  87.2 0.9 slice_convert_fusion
  88.2 13.1 %all-to-all-done = bf16[8,4,8,1024]{3,2,1,0:T(8,128)(2,1)S(1)} async-done(((bf16[8,4,8,1024]{3,2,1,0:T(8,128)(2,1)}), bf16[8,4,8,1024]{3,2,1,0:T(8,128)(2,1)S(1)}, u32[]{:S(2)}, u32[]{:S(2)}) %all-to-all-start) | async-done | bytes 524320 | tf_op jit(solution)/shard_map/all_to_all | solution.py:191
  101.3 1.3 fusion.6.hist_ref
  102.6 38.7 %all-gather.5.cloned.1.call-done = bf16[2048,1024]{1,0:T(8,128)(2,1)} async-done(((bf16[256,1024]{1,0:T(8,128)(2,1)}), bf16[2048,1024]{1,0:T(8,128)(2,1)}) %all-gather.5.cloned.1.call-update) | async-done | bytes 4194320 | tf_op jit(solution)/shard_map/all_gather | solution.py:182
  141.3 3.1 %fusion = f32[256]{0:T(256)S(1)} fusion(bf16[8,256,1024]{2,1,0:T(8,128)(2,1)} %bitcast.18), kind=kLoop, calls=%fused_computation.2 | loop fusion | flops 6291200 | bytes 4195328 | tf_op jit(solution)/shard_map/reduce_sum | solution.py:204
  144.4 5.7 %fusion.2.x_ref = bf16[8,256,1024]{2,1,0:T(8,128)(2,1)} fusion(f32[8,1024]{1,0:T(8,128)S(1)} %bitcast.23, f32[256]{0:T(256)S(1)} %add_rsqrt_fusion, bf16[2048,1024]{1,0:T(8,128)(2,1)} %all-gather.5.cloned.1.call-done), kind=kLoop, calls=%fused_computation.4 | loop fusion | flops 8388608 | bytes 8422400 | tf_op jit(solution)/shard_map/convert_element_type | solution.py:206
  150.1 28.1 %gated_rows.1.x_ref = bf16[256,1024]{1,0:T(8,128)(2,1)} custom-call(bf16[8,256,1024]{2,1,0:T(8,128)(2,1)} %fusion.2.x_ref, bf16[8192,3072]{1,0:T(8,128)(2,1)} %wv_ref.1, bf16[8192,3072]{1,0:T(8,128)(2,1)} %wv_ref.1, bf16[8192,3072]{1,0:T(8,128)(2,1)} %wv_ref.1, bf16[144,1024]{1,0:T(8,128)(2,1)} %maximum_maximum_fusion.taps_ref, f32[256,1024]{1,0:T(8,128)} %fusion.6.hist_ref), custom_call_target="tpu_custom_call" | custom-call | flops 12884901888 | bytes 50331648 | tf_op jit(solution)/shard_map/gated_rows/pallas_call | solution.py:115
  178.2 0.0 copy-start.1
  178.2 12.1 %output_shares.1 = bf16[8,256,1024]{2,1,0:T(8,128)(2,1)} custom-call(bf16[256,1024]{1,0:T(8,128)(2,1)} %gated_rows.1.x_ref, bf16[1024,8192]{1,0:T(8,128)(2,1)} %w_ref.1), custom_call_target="tpu_custom_call" | custom-call | flops 4294967296 | bytes 16777216 | tf_op jit(solution)/shard_map/output_shares/pallas_call | solution.py:146
  190.3 95.7 %all_to_all.10 = bf16[8,256,1024]{2,1,0:T(8,128)(2,1)S(1)} all-to-all(bf16[8,256,1024]{2,1,0:T(8,128)(2,1)} %output_shares.1), channel_id=1, replica_groups=mesh['groups'=2,'tensor'=8,'batch'=2] {'tensor'}, dimensions={0} | all-to-all | bytes 8388608 | tf_op jit(solution)/shard_map/all_to_all | solution.py:209
  286.0 0.8 convert_reduce_fusion
  286.8 0.9 add_convert_fusion
  287.7 0.0 copy-done.1
  (6 shorter events, 0.0 us)
Async XLA Ops:
  6.5 3.6 %copy-start = (bf16[512,1024]{1,0:T(8,128)(2,1)S(1)}, bf16[512,1024]{1,0:T(8,128)(2,1)}, u32[]{:S(2)}) copy-start(bf16[512,1024]{1,0:T(8,128)(2,1)} %param.10) | copy-start | bytes 3145732
  6.5 55.6 %all-gather.7.cloned.1.call-start = ((), (), s32[]{:S(2)}) async-start(), calls=%async_computation.3 | async-start | bytes 2654208 | tf_op jit(solution)/shard_map/all_gather | solution.py:178
  9.4 131.9 %all-gather.5.cloned.1.call-start = ((), (), s32[]{:S(2)}) async-start(), calls=%async_computation.2 | async-start | bytes 4718592 | tf_op jit(solution)/shard_map/all_gather | solution.py:182
  12.2 18.7 %copy-start.2 = (s32[64]{0:T(128)S(1)}, s32[64]{0:T(128)}, u32[]{:S(2)}) copy-start(s32[64]{0:T(128)} %param.17) | copy-start | bytes 772
  82.2 19.0 %all-to-all-start = ((bf16[8,4,8,1024]{3,2,1,0:T(8,128)(2,1)}), bf16[8,4,8,1024]{3,2,1,0:T(8,128)(2,1)S(1)}, u32[]{:S(2)}, u32[]{:S(2)}) async-start(bf16[8,4,8,1024]{3,2,1,0:T(8,128)(2,1)} %history_terms.1), calls=%async_computation | async-start | bytes 1048576 | tf_op jit(solution)/shard_map/all_to_all | solution.py:191
  178.2 109.5 %copy-start.1 = (bf16[512,1024]{1,0:T(8,128)(2,1)S(1)}, bf16[512,1024]{1,0:T(8,128)(2,1)}, u32[]{:S(2)}) copy-start(bf16[512,1024]{1,0:T(8,128)(2,1)} %param.10) | copy-start | bytes 3145732
Sparse Core Ops, SparseCore 0:
  9.5 52.5 all-gather.6
  64.3 76.9 all-gather.4

commit v2 on v1

v2 whole, which is shorter than its diff:
```python
import functools

import jax
import jax.numpy as jnp
from jax import lax
from jax.experimental import pallas as pl
from jax.experimental.pallas import tpu as pltpu
from jax.sharding import PartitionSpec as P

D = 8192
EPSILON = 1e-05
LANES = 128
PACKED = 16
INNER = 2
RING_MOST = 8
VMEM_LIMIT = 28 * 1024 * 1024


def place_of(mine, owners):
    return mine // INNER, mine % INNER, owners // INNER


def moved(array, outer_by, flip):
    owners = lax.axis_size("tensor")
    outer_size = owners // INNER
    pairs = []
    for source in range(owners):
        outer, inner = source // INNER, source % INNER
        pairs.append((source, (outer + outer_by) % outer_size * INNER + (inner ^ flip)))
    return lax.ppermute(array, "tensor", pairs)


def spread(block):
    outer_size = lax.axis_size("tensor") // INNER
    blocks = []
    held = block
    for step in range(outer_size):
        if step:
            held = moved(held, 1, 0)
        blocks.append((held, moved(held, 0, 1)))
    return blocks


def history_kernel(steps, spot, lengths_ref, near_ref, far_ref, cache_ref, near_out, far_out, taps_scr):
    lags, rows, channels = cache_ref.shape
    part = pl.program_id(0)
    parts = pl.num_programs(0) // 2
    width = min(4 * LANES, channels)
    at_part = pl.ds(pl.multiple_of(part % parts * channels, channels), channels)

    @pl.when(part < parts)
    def _():
        taps_scr[...] = near_ref[pl.ds(0, lags + 1), at_part].astype(jnp.float32)

    @pl.when(part >= parts)
    def _():
        taps_scr[...] = far_ref[pl.ds(0, lags + 1), at_part].astype(jnp.float32)

    lengths = jnp.concatenate([lengths_ref[...]] * (width // LANES), axis=1)

    def one_chunk(chunk, carry):
        at = pl.ds(pl.multiple_of(chunk * width, width), width)
        taps = [
            jnp.broadcast_to(taps_scr[pl.ds(1 + step, 1), at], (rows, width)) for step in range(steps)
        ]
        sums = [jnp.zeros((rows, width), jnp.float32) for _ in range(steps)]
        for lag in range(lags):
            values = jnp.where(lengths > lag, cache_ref[lag, :, at].astype(jnp.float32), 0.0)
            for step in range(min(steps, lags - lag)):
                sums[step] += values * taps[step]
            taps = taps[1:]
            if lag + 1 + steps <= lags:
                taps.append(
                    jnp.broadcast_to(taps_scr[pl.ds(lag + 1 + steps, 1), at], (rows, width))
                )

        @pl.when(part < parts)
        def _():
            for step in range(steps):
                near_out[step, :, at] = sums[step].astype(near_out.dtype)

        @pl.when(part >= parts)
        def _():
            for step in range(steps):
                far_out[step, :, at] = sums[step].astype(far_out.dtype)

        return carry

    lax.fori_loop(0, channels // width, one_chunk, 0)


def history_terms(cache, near, far, lengths, spot, steps):
    lags, rows, _ = cache.shape
    tap_rows, channels = near.shape
    parts = 2 if channels >= 8 * LANES else 1
    block = channels // parts

    def cache_at(part, spot):
        inner = (spot[1] + part // parts) % INNER
        return 0, 0, (spot[0] * INNER + inner) * parts + part % parts

    return pl.pallas_call(
        functools.partial(history_kernel, steps),
        grid_spec=pltpu.PrefetchScalarGridSpec(
            num_scalar_prefetch=1,
            grid=(2 * parts,),
            in_specs=[
                pl.BlockSpec((rows, LANES), lambda part, _: (0, 0)),
                pl.BlockSpec((tap_rows, channels), lambda part, _: (0, 0)),
                pl.BlockSpec((tap_rows, channels), lambda part, _: (0, 0)),
                pl.BlockSpec((lags, rows, block), cache_at),
            ],
            out_specs=[
                pl.BlockSpec((steps, rows, block), lambda part, _: (0, 0, jnp.minimum(part, parts - 1))),
                pl.BlockSpec((steps, rows, block), lambda part, _: (0, 0, jnp.maximum(part - parts, 0))),
            ],
            scratch_shapes=[pltpu.VMEM((lags + 1, block), jnp.float32)],
        ),
        out_shape=[jax.ShapeDtypeStruct((steps, rows, channels), jnp.bfloat16)] * 2,
        compiler_params=pltpu.CompilerParams(vmem_limit_bytes=VMEM_LIMIT),
        cost_estimate=pl.CostEstimate(
            flops=4 * steps * rows * lags * channels,
            bytes_accessed=4 * rows * lags * channels,
            transcendentals=0,
        ),
        name="history_terms",
    )(spot, lengths, near, far, cache)


def project_kernel(steps, first, last, *refs):
    refs = list(refs)
    spot, near, far, near_gain, far_gain, inv_ref, wq_ref, wk_ref, wv_ref = refs[:9]
    del refs[:9]
    earlier = None if first else refs.pop(0)
    taps_ref, hist_ref = (refs.pop(0), refs.pop(0)) if last else (None, None)
    out_ref, normed = refs
    rows, channels = near.shape

    @pl.when(pl.program_id(0) == 0)
    def _():
        inv_rms = inv_ref[:, :1]
        for flip, x_ref, gain_ref in ((0, near, near_gain), (1, far, far_gain)):
            gain = gain_ref[pl.ds(0, 1), :].astype(jnp.float32)
            scaled = x_ref[...].astype(jnp.float32) * inv_rms * gain
            normed[(spot[1] + flip) % INNER] = scaled.astype(jnp.bfloat16)

    totals = []
    for index, w_ref in enumerate((wq_ref, wk_ref, wv_ref)):
        total = None if first else earlier[index]
        for inner in range(INNER):
            term = jnp.dot(
                normed[inner],
                w_ref[pl.ds(inner * channels, channels), :],
                preferred_element_type=jnp.float32,
            )
            total = term if total is None else total + term
        totals.append(total)
    if not last:
        for index in range(3):
            out_ref[index] = totals[index]
        return
    seqs = rows // steps
    queries = totals[0]
    recent = (totals[1] * totals[2]).astype(jnp.bfloat16).astype(jnp.float32)
    for step in range(steps):
        filtered = hist_ref[pl.ds(step * seqs, seqs), :]
        for back in range(step + 1):
            older = recent[(step - back) * seqs : (step - back + 1) * seqs]
            filtered += taps_ref[pl.ds(back, 1), :].astype(jnp.float32) * older
        out_ref[pl.ds(step * seqs, seqs), :] = (
            queries[step * seqs : (step + 1) * seqs] * filtered
        ).astype(jnp.bfloat16)


def projected(spot, pair, gains, inv_rms, w_in, earlier, taps=None, history=None, steps=1):
    near, far = pair
    rows, channels = near.shape
    block = min(256, channels)
    blocks = channels // block
    first, last = earlier is None, history is not None
    tap_rows = gains[0].shape[0]
    in_specs = [
        pl.BlockSpec((rows, channels), lambda c, _: (0, 0)),
        pl.BlockSpec((rows, channels), lambda c, _: (0, 0)),
        pl.BlockSpec((PACKED, channels), lambda c, _: (tap_rows // PACKED - 1, 0)),
        pl.BlockSpec((PACKED, channels), lambda c, _: (tap_rows // PACKED - 1, 0)),
        pl.BlockSpec((rows, LANES), lambda c, _: (0, 0)),
    ]
    for index in range(3):
        in_specs.append(
            pl.BlockSpec(
                (INNER * channels, block),
                functools.partial(lambda start, c, spot: (spot[0], start + c), index * blocks),
            )
        )
    args = [near, far, *gains, inv_rms, w_in, w_in, w_in]
    total_spec = pl.BlockSpec((3, rows, block), lambda c, _: (0, 0, c))
    if not first:
        in_specs.append(total_spec)
        args.append(earlier)
    if last:
        in_specs += [
            pl.BlockSpec((PACKED, block), lambda c, _: (0, c)),
            pl.BlockSpec((rows, block), lambda c, _: (0, c)),
        ]
        args += [taps, history]
        out_spec = pl.BlockSpec((rows, block), lambda c, _: (0, c))
        out_shape = jax.ShapeDtypeStruct((rows, channels), jnp.bfloat16)
    else:
        out_spec = total_spec
        out_shape = jax.ShapeDtypeStruct((3, rows, channels), jnp.float32)
    return pl.pallas_call(
        functools.partial(project_kernel, steps, first, last),
        grid_spec=pltpu.PrefetchScalarGridSpec(
            num_scalar_prefetch=1,
            grid=(blocks,),
            in_specs=in_specs,
            out_specs=out_spec,
            scratch_shapes=[pltpu.VMEM((INNER, rows, channels), jnp.bfloat16)],
        ),
        out_shape=out_shape,
        compiler_params=pltpu.CompilerParams(vmem_limit_bytes=VMEM_LIMIT),
        cost_estimate=pl.CostEstimate(
            flops=2 * rows * INNER * channels * 3 * channels,
            bytes_accessed=2 * INNER * channels * 3 * channels,
            transcendentals=0,
        ),
        name="gated_rows" if last else "projected_part",
    )(spot, *args)


def share_kernel(spot, x_ref, w_ref, *refs):
    share = jnp.dot(x_ref[...], w_ref[...], preferred_element_type=jnp.float32)
    if len(refs) > 1:
        share += refs[0][...].astype(jnp.float32)
    refs[-1][...] = share.astype(refs[-1].dtype)


def output_share(spot, gated, w_out, owners, arrived=None):
    rows, channels = gated.shape
    wide = w_out.shape[1] // owners
    block = min(512, wide)
    blocks = wide // block
    specs = [
        pl.BlockSpec((rows, channels), lambda c, _: (0, 0)),
        pl.BlockSpec((channels, block), lambda c, spot: (0, spot[0] * blocks + c)),
    ]
    args = [gated, w_out]
    if arrived is not None:
        specs.append(pl.BlockSpec((rows, block), lambda c, _: (0, c)))
        args.append(arrived)
    return pl.pallas_call(
        share_kernel,
        grid_spec=pltpu.PrefetchScalarGridSpec(
            num_scalar_prefetch=1,
            grid=(blocks,),
            in_specs=specs,
            out_specs=pl.BlockSpec((rows, block), lambda c, _: (0, c)),
        ),
        out_shape=jax.ShapeDtypeStruct((rows, wide), jnp.bfloat16),
        compiler_params=pltpu.CompilerParams(vmem_limit_bytes=VMEM_LIMIT),
        cost_estimate=pl.CostEstimate(
            flops=2 * rows * channels * wide,
            bytes_accessed=2 * channels * wide,
            transcendentals=0,
        ),
        name="output_share",
    )(spot, *args)


def split_sums(values, channels):
    parts = []
    rest = values
    for _ in range(3):
        part = lax.reduce_precision(rest, 8, 7)
        parts.append(part.astype(jnp.bfloat16))
        rest = rest - part
    flat = jnp.concatenate(parts)
    count = -(-flat.shape[0] // channels)
    return jnp.pad(flat, (0, count * channels - flat.shape[0])).reshape(count, channels)


def per_device(token_ids, embed, norm_gain, w_in, filters, w_out, cache_rows, owner, lengths):
    steps, seqs = token_ids.shape
    vocab, channels = embed.shape
    rows = cache_rows.shape[0]
    taps = filters.shape[1]
    tokens = steps * seqs
    owners = lax.axis_size("tensor")
    halves = lax.axis_size("batch")
    mine = lax.axis_index("tensor")
    half = lax.axis_index("batch")
    outer, inner, outer_size = place_of(mine, owners)

    onehot = token_ids.reshape(-1)[:, None] == jnp.arange(vocab, dtype=jnp.int32)[None, :]
    stream = jnp.dot(onehot.astype(jnp.bfloat16), embed, preferred_element_type=jnp.float32)
    squares = split_sums(jnp.sum(stream * stream, axis=1), channels)
    filler = -(taps + 1 + squares.shape[0]) % PACKED
    small = jnp.concatenate(
        [filters.T, norm_gain[None, :], squares, jnp.zeros((filler, channels), jnp.bfloat16)], axis=0
    )
    smalls = spread(small)
    streams = spread(stream.astype(jnp.bfloat16))

    def spot_at(back):
        return jnp.stack([(outer + back) % outer_size, inner]).astype(jnp.int32)

    owner_grid = owner.reshape(owners, halves, rows)
    arrived = lax.dynamic_index_in_dim(owner_grid, half, 1, keepdims=False) - half * seqs
    seq_index = jnp.arange(seqs, dtype=jnp.int32)
    own = lax.dynamic_index_in_dim(arrived, mine, 0, keepdims=False)
    row_lengths = jnp.sum(jnp.where(own[:, None] == seq_index[None, :], lengths[None, :], 0), axis=1)
    row_lengths = jnp.broadcast_to(row_lengths[:, None], (rows, LANES))
    cache = cache_rows.transpose(1, 0, 2)

    pieces = []
    piece_owner = []
    for back, (near, far) in enumerate(smalls):
        terms = history_terms(cache, near, far, row_lengths, spot_at(-back), steps)
        for flip, piece in enumerate(terms):
            pieces.append(moved(piece, -back, flip) if back or flip else piece)
            piece_owner.append((outer + back) % outer_size * INNER + (inner + flip) % INNER)
    from_whom = jnp.stack(piece_owner)
    sent_rows = jnp.sum(
        jnp.where(
            (from_whom[:, None] == jnp.arange(owners)[None, :])[:, :, None], arrived[None], 0
        ),
        axis=1,
    )
    step_index = jnp.arange(steps, dtype=jnp.int32)
    place = (
        (step_index[:, None, None, None, None] == step_index[None, None, None, :, None])
        & (seq_index[None, :, None, None, None] == sent_rows[None, None, :, None, :])
    ).reshape(tokens, owners * steps * rows)
    history = jnp.dot(
        place.astype(jnp.bfloat16),
        jnp.concatenate(pieces, axis=0).reshape(owners * steps * rows, channels),
        preferred_element_type=jnp.float32,
    )

    total = 0.0
    for near, far in smalls:
        for block in (near, far):
            flat = block[taps + 1 : taps + 1 + squares.shape[0]].reshape(-1)[: 3 * tokens]
            total = total + jnp.sum(flat.astype(jnp.float32).reshape(3, tokens), axis=0)
    inv_rms = lax.rsqrt(total / D + EPSILON)
    inv_rms = jnp.broadcast_to(inv_rms[:, None], (tokens, LANES))

    sums = None
    for back in range(outer_size):
        ends = dict(taps=small, history=history, steps=steps) if back == outer_size - 1 else {}
        sums = projected(spot_at(-back), streams[back], smalls[back], inv_rms, w_in, sums, **ends)
    gated = sums

    def spot_to(ahead, flip):
        return ((outer + ahead) % outer_size * INNER + (inner + flip) % INNER)[None].astype(jnp.int32)

    order = sorted(range(outer_size), key=lambda ahead: (ahead == 0, -min(ahead, outer_size - ahead)))
    across = {
        ahead: moved(output_share(spot_to(ahead, 1), gated, w_out, owners), 0, 1) for ahead in order
    }
    out = stream
    for ahead in order:
        share = output_share(spot_to(ahead, 0), gated, w_out, owners, across[ahead])
        out = out + (moved(share, ahead, 0) if ahead else share).astype(jnp.float32)
    return out.astype(jnp.bfloat16).reshape(steps, seqs, channels)


def solution(mesh):
    in_specs = (
        P(None, ("groups", "batch")),
        P(None, "tensor"),
        P("tensor"),
        P(None, "tensor"),
        P("tensor", None),
        P("tensor", None),
        P(("groups", "tensor", "batch"), None, None),
        P("groups"),
        P(("groups", "batch")),
    )
    out_specs = P(None, ("groups", "batch"), "tensor")
    return jax.shard_map(
        per_device, mesh=mesh, in_specs=in_specs, out_specs=out_specs, check_vma=False
    )
```

time: 299 us -> 192 us (0.64)
  blocking collectives: 95.7 us -> 0 us
  starting transfers between devices: 4.52 us -> 37.3 us
  waiting for transfers between devices: 82.3 us -> 53.2 us
  between operations: 13.5 us -> 0.58 us
  other arithmetic: 13.3 us -> 3.25 us
  local copies, waits for them, and re-layouts: 22.4 us -> 30.7 us
    all_to_all x1 -> x0, blocking collectives: 95.7 us -> none  [per_device(): lax.all_to_all(output_shares(gated, w_out, owners), 'tensor', 0, 0, tiled...]
    all_gather x2 -> x0, waiting for transfers between devices: 69.2 us -> none  [the longest x1 38.7 us: per_device(): stream_all = lax.all_gather(stream.astype(jnp.bfloat16), 'tensor')]
    ppermute x0 -> x28, waiting for transfers between devices: none -> 53.2 us  [moved(): return lax.ppermute(array, 'tensor', pairs)]
    ppermute x0 -> x28, starting transfers between devices: none -> 37.3 us  [moved(): return lax.ppermute(array, 'tensor', pairs)]
    all_to_all x1 -> x0, waiting for transfers between devices: 13.1 us -> none  [per_device(): history = lax.all_to_all(history, 'tensor', 0, 0, tiled=True)]
    unnamed x9 -> x46, local copies, waits for them, and re-layouts: 19.9 us -> 27.8 us
    convert_element_type x2 -> x10, other arithmetic: 6.6 us -> 1.37 us  [the longest x1 1.24 us: per_device(): return out.astype(jnp.bfloat16).reshape(steps, seqs, channels)]
    all_to_all x1 -> x0, starting transfers between devices: 4.48 us -> none  [per_device(): history = lax.all_to_all(history, 'tensor', 0, 0, tiled=True)]
  transfers between devices with their start and end apart: 3 -> 28, of which waited for: 3 -> 13; matrix products, arithmetic and copies ran while one was open for 8% -> 3% of each run, Pallas kernels for 7% -> 28%
where the time goes in v2:
time: 192 us; the launch traced here: 190 us
  Pallas kernels  63 us (33%)
  waiting for transfers between devices  53.2 us (28%)
  starting transfers between devices  37.3 us (19%)
  local copies, waits for them, and re-layouts  30.7 us (16%)
  other arithmetic  3.25 us (2%)
    ppermute x28, waiting for transfers between devices, moved(): return lax.ppermute(array, 'tensor', pairs)  53.2 us
    ppermute x28, starting transfers between devices, moved(): return lax.ppermute(array, 'tensor', pairs)  37.3 us
    pallas_call x4, Pallas kernels, projected(): pl.pallas_call(functools.partial(project_kernel, steps, first, last), gri...  35.5 us
    unnamed x46, local copies, waits for them, and re-layouts  27.8 us
    pallas_call x4, Pallas kernels, history_terms(): pl.pallas_call(functools.partial(history_kernel, steps), grid_spec=pltpu....  16.1 us
    pallas_call x8, Pallas kernels, output_share(): pl.pallas_call(share_kernel, grid_spec=pltpu.PrefetchScalarGridSpec(num_s...  11.4 us
  transfers between devices with their start and end apart: 28, of which 13 were waited for; matrix products, arithmetic and copies ran while one was open for 3% of the time, Pallas kernels for 28%

profile of v2, /device:TPU:18, one launch (start us, length us, event | category | flops | bytes accessed | tf_op | source)
XLA Modules:
  0.0 189.9 jit_solution(14633835741210113006)
XLA Ops:
  0.0 0.8 eq.125
  1.2 1.5 multiply_reduce_fusion
  2.7 1.1 copy.12
  3.8 0.7 broadcast_in_dim.43
  4.7 1.6 collective-permute-start.8
  6.3 1.6 collective-permute-start.4
  8.6 0.7 reshape.156
  10.5 0.8 select_reduce_fusion.1
  11.4 3.3 %collective-permute-done.8.refs_4_.far_ref = bf16[144,1024]{1,0:T(8,128)(2,1)S(1)} collective-permute-done((bf16[144,1024]{1,0:T(8,128)(2,1)S(1)}, bf16[144,1024]{1,0:T(8,128)(2,1)S(1)}, u32[]{:S(2)}, u32[]{:S(2)}) %collective-permute-start.8) | collective-permute-done | bytes 294944 | tf_op jit(solution)/shard_map/ppermute | solution.py:30
  14.8 5.7 %copy-done.2 = bf16[8,127,8192]{2,0,1:T(8,128)(2,1)S(1)} copy-done((bf16[8,127,8192]{2,0,1:T(8,128)(2,1)S(1)}, bf16[8,127,8192]{2,0,1:T(8,128)(2,1)}, u32[]{:S(2)}) %copy-start.2) | copy-done | bytes 16646168
  20.5 4.0 %history_terms.4 = (bf16[4,8,1024]{2,1,0:T(8,128)(2,1)S(1)}, bf16[4,8,1024]{2,1,0:T(8,128)(2,1)S(1)}) custom-call(s32[2]{0:T(128)S(1)} %pad_add_fusion.3.refs_0_.spot, s32[8,128]{1,0:T(8,128)S(1)} %broadcast_in_dim.51.lengths_ref, bf16[144,1024]{1,0:T(8,128)(2,1)S(1)} %maximum_maximum_fusion.refs_3_.near_ref.refs_10_, ...), custom_call_target="tpu_custom_call" | custom-call | flops 16646144 | bytes 4161536 | tf_op jit(solution)/shard_map/history_terms/pallas_call | solution.py:102
  24.5 1.6 collective-permute-start.14
  26.7 1.6 collective-permute-start.5
  28.4 1.2 collective-permute-done.14
  29.6 1.6 collective-permute-start.12
  31.2 5.0 %collective-permute-done.9.refs_4_.far_ref = bf16[144,1024]{1,0:T(8,128)(2,1)S(1)} collective-permute-done((bf16[144,1024]{1,0:T(8,128)(2,1)S(1)}, bf16[144,1024]{1,0:T(8,128)(2,1)S(1)}, u32[]{:S(2)}, u32[]{:S(2)}) %collective-permute-start.9) | collective-permute-done | bytes 294944 | tf_op jit(solution)/shard_map/ppermute | solution.py:30
  36.2 5.7 %copy-done.3 = bf16[8,127,8192]{2,0,1:T(8,128)(2,1)S(1)} copy-done((bf16[8,127,8192]{2,0,1:T(8,128)(2,1)S(1)}, bf16[8,127,8192]{2,0,1:T(8,128)(2,1)}, u32[]{:S(2)}) %copy-start.3) | copy-done | bytes 16646168
  41.9 4.0 %history_terms.5 = (bf16[4,8,1024]{2,1,0:T(8,128)(2,1)S(1)}, bf16[4,8,1024]{2,1,0:T(8,128)(2,1)S(1)}) custom-call(s32[2]{0:T(128)S(1)} %pad_add_fusion.2.refs_0_.spot, s32[8,128]{1,0:T(8,128)S(1)} %broadcast_in_dim.51.lengths_ref, bf16[144,1024]{1,0:T(8,128)(2,1)S(1)} %collective-permute-done.4.refs_3_.near_ref, ...), custom_call_target="tpu_custom_call" | custom-call | flops 16646144 | bytes 4161536 | tf_op jit(solution)/shard_map/history_terms/pallas_call | solution.py:102
  46.5 1.3 collective-permute-start.10
  47.8 1.6 collective-permute-start.6
  49.5 1.5 collective-permute-done.15
  51.0 1.8 collective-permute-start.16
  52.8 9.4 %collective-permute-done.16 = bf16[4,8,1024]{2,1,0:T(8,128)(2,1)S(1)} collective-permute-done((bf16[4,8,1024]{2,1,0:T(8,128)(2,1)S(1)}, bf16[4,8,1024]{2,1,0:T(8,128)(2,1)S(1)}, u32[]{:S(2)}, u32[]{:S(2)}) %collective-permute-start.16) | collective-permute-done | bytes 65568 | tf_op jit(solution)/shard_map/ppermute | solution.py:30
  62.5 5.9 %copy-done.4 = bf16[8,127,8192]{2,0,1:T(8,128)(2,1)S(1)} copy-done((bf16[8,127,8192]{2,0,1:T(8,128)(2,1)S(1)}, bf16[8,127,8192]{2,0,1:T(8,128)(2,1)}, u32[]{:S(2)}) %copy-start.4) | copy-done | bytes 16646168
  68.4 4.0 %history_terms.6 = (bf16[4,8,1024]{2,1,0:T(8,128)(2,1)S(1)}, bf16[4,8,1024]{2,1,0:T(8,128)(2,1)S(1)}) custom-call(s32[2]{0:T(128)S(1)} %pad_add_fusion.1.refs_0_.spot, s32[8,128]{1,0:T(8,128)S(1)} %broadcast_in_dim.51.lengths_ref, bf16[144,1024]{1,0:T(8,128)(2,1)S(1)} %collective-permute-done.5.refs_3_.near_ref, ...), custom_call_target="tpu_custom_call" | custom-call | flops 16646144 | bytes 4161536 | tf_op jit(solution)/shard_map/history_terms/pallas_call | solution.py:102
  72.5 2.6 %collective-permute-start.17 = (bf16[4,8,1024]{2,1,0:T(8,128)(2,1)S(1)}, bf16[4,8,1024]{2,1,0:T(8,128)(2,1)S(1)}, u32[]{:S(2)}, u32[]{:S(2)}) collective-permute-start(bf16[4,8,1024]{2,1,0:T(8,128)(2,1)S(1)} %get-tuple-element.17), channel_id=1, source_target_pairs={{0,8},{2,10},{4,12},{6,14},{8,0},{10,2},{12,4},{14,6},{1,9},{3,11}... | collective-permute-start | bytes 196616 | tf_op jit(solution)/shard_map/ppermute | solution.py:30
  75.1 1.4 collective-permute-start.7
  76.6 1.1 collective-permute-done.17
  77.7 4.0 %collective-permute-start.18 = (bf16[4,8,1024]{2,1,0:T(8,128)(2,1)S(1)}, bf16[4,8,1024]{2,1,0:T(8,128)(2,1)S(1)}, u32[]{:S(2)}, u32[]{:S(2)}) collective-permute-start(bf16[4,8,1024]{2,1,0:T(8,128)(2,1)S(1)} %get-tuple-element.18), channel_id=1, source_target_pairs={{0,10},{2,8},{4,14},{6,12},{8,2},{10,0},{12,6},{14,4},{1,11},{3,9}... | collective-permute-start | bytes 196616 | tf_op jit(solution)/shard_map/ppermute | solution.py:30
  82.4 4.6 %collective-permute-done.18 = bf16[4,8,1024]{2,1,0:T(8,128)(2,1)S(1)} collective-permute-done((bf16[4,8,1024]{2,1,0:T(8,128)(2,1)S(1)}, bf16[4,8,1024]{2,1,0:T(8,128)(2,1)S(1)}, u32[]{:S(2)}, u32[]{:S(2)}) %collective-permute-start.18) | collective-permute-done | bytes 65568 | tf_op jit(solution)/shard_map/ppermute | solution.py:30
  87.0 0.6 constant_dynamic-update-slice_fusion.2
  87.6 1.3 collective-permute-start.11
  89.0 1.0 collective-permute-start.2
  89.9 5.7 %copy-done.5 = bf16[8,127,8192]{2,0,1:T(8,128)(2,1)S(1)} copy-done((bf16[8,127,8192]{2,0,1:T(8,128)(2,1)S(1)}, bf16[8,127,8192]{2,0,1:T(8,128)(2,1)}, u32[]{:S(2)}) %copy-start.5) | copy-done | bytes 16646168
  95.7 4.0 %history_terms.7 = (bf16[4,8,1024]{2,1,0:T(8,128)(2,1)S(1)}, bf16[4,8,1024]{2,1,0:T(8,128)(2,1)S(1)}) custom-call(s32[2]{0:T(128)S(1)} %pad_add_fusion.spot.refs_0_, s32[8,128]{1,0:T(8,128)S(1)} %broadcast_in_dim.51.lengths_ref, bf16[144,1024]{1,0:T(8,128)(2,1)S(1)} %collective-permute-done.6.near_ref.refs_3_, ...), custom_call_target="tpu_custom_call" | custom-call | flops 16646144 | bytes 4161536 | tf_op jit(solution)/shard_map/history_terms/pallas_call | solution.py:102
  99.7 4.0 %collective-permute-start.19 = (bf16[4,8,1024]{2,1,0:T(8,128)(2,1)S(1)}, bf16[4,8,1024]{2,1,0:T(8,128)(2,1)S(1)}, u32[]{:S(2)}, u32[]{:S(2)}) collective-permute-start(bf16[4,8,1024]{2,1,0:T(8,128)(2,1)S(1)} %get-tuple-element.19), channel_id=1, source_target_pairs={{0,4},{2,6},{4,8},{6,10},{8,12},{10,14},{12,0},{14,2},{1,5},{3,7},... | collective-permute-start | bytes 196616 | tf_op jit(solution)/shard_map/ppermute | solution.py:30
  103.8 1.0 collective-permute-start.20
  104.9 8.5 %projected_part.3.refs_9_ = f32[3,256,1024]{2,1,0:T(8,128)S(1)} custom-call(s32[2]{0:T(128)S(1)} %pad_add_fusion.3.refs_0_.spot, bf16[256,1024]{1,0:T(8,128)(2,1)S(1)} %get-tuple-element.22.refs_1_, bf16[256,1024]{1,0:T(8,128)(2,1)} %collective-permute-done.13.refs_2_, bf16[144,1024]{1,0:T(8,128)(2,1)S(1)} %maximum_maximum_fusion.refs_3_.near_ref.refs_10_, ...), custom_call_target="tpu_custom_call" | custom-call | flops 3221225472 | bytes 12582912 | tf_op jit(solution)/shard_map/projected_part/pallas_call | solution.py:212
  113.4 8.5 %projected_part.4.refs_9_ = f32[3,256,1024]{2,1,0:T(8,128)S(1)} custom-call(s32[2]{0:T(128)S(1)} %pad_add_fusion.2.refs_0_.spot, bf16[256,1024]{1,0:T(8,128)(2,1)} %collective-permute-done.refs_1_, bf16[256,1024]{1,0:T(8,128)(2,1)} %collective-permute-done.12.refs_2_, bf16[144,1024]{1,0:T(8,128)(2,1)S(1)} %collective-permute-done.4.refs_3_.near_ref, ...), custom_call_target="tpu_custom_call" | custom-call | flops 3221225472 | bytes 12582912 | tf_op jit(solution)/shard_map/projected_part/pallas_call | solution.py:212
  122.0 0.7 collective-permute-start.3
  123.1 9.9 %projected_part.5.refs_9_ = f32[3,256,1024]{2,1,0:T(8,128)S(1)} custom-call(s32[2]{0:T(128)S(1)} %pad_add_fusion.1.refs_0_.spot, bf16[256,1024]{1,0:T(8,128)(2,1)} %collective-permute-done.1.refs_1_, bf16[256,1024]{1,0:T(8,128)(2,1)} %collective-permute-done.11.refs_2_, bf16[144,1024]{1,0:T(8,128)(2,1)S(1)} %collective-permute-done.5.refs_3_.near_ref, ...), custom_call_target="tpu_custom_call" | custom-call | flops 3221225472 | bytes 12582912 | tf_op jit(solution)/shard_map/projected_part/pallas_call | solution.py:212
  133.1 8.6 %gated_rows.1.x_ref = bf16[256,1024]{1,0:T(8,128)(2,1)S(1)} custom-call(s32[2]{0:T(128)S(1)} %pad_add_fusion.spot.refs_0_, bf16[256,1024]{1,0:T(8,128)(2,1)} %collective-permute-done.2.refs_1_, bf16[256,1024]{1,0:T(8,128)(2,1)S(1)} %collective-permute-done.3.refs_2_, bf16[144,1024]{1,0:T(8,128)(2,1)S(1)} %collective-permute-done.6.near_ref.refs_3_, ...), custom_call_target="tpu_custom_call" | custom-call | flops 3221225472 | bytes 12582912 | tf_op jit(solution)/shard_map/gated_rows/pallas_call | solution.py:212
  141.7 1.1 output_share.8
  142.9 1.4 collective-permute-start.21
  144.3 1.1 output_share.10
  145.4 0.7 collective-permute-start.23
  146.1 1.1 output_share.12
  147.3 1.4 collective-permute-start.25
  148.7 1.1 output_share.14
  149.8 0.7 collective-permute-start.27
  150.6 7.2 %collective-permute-done.21.refs_0_ = bf16[256,1024]{1,0:T(8,128)(2,1)S(1)} collective-permute-done((bf16[256,1024]{1,0:T(8,128)(2,1)S(1)}, bf16[256,1024]{1,0:T(8,128)(2,1)S(1)}, u32[]{:S(2)}, u32[]{:S(2)}) %collective-permute-start.21) | collective-permute-done | bytes 524320 | tf_op jit(solution)/shard_map/ppermute | solution.py:30
  157.8 0.8 copy-done.6
  158.6 1.0 copy-done.7
  159.6 1.8 output_share.9
  161.5 3.8 %collective-permute-done.23.refs_0_ = bf16[256,1024]{1,0:T(8,128)(2,1)} collective-permute-done((bf16[256,1024]{1,0:T(8,128)(2,1)S(1)}, bf16[256,1024]{1,0:T(8,128)(2,1)}, u32[]{:S(2)}, u32[]{:S(2)}) %collective-permute-start.23) | collective-permute-done | bytes 524320 | tf_op jit(solution)/shard_map/ppermute | solution.py:30
  165.3 2.1 %output_share.11 = bf16[256,1024]{1,0:T(8,128)(2,1)S(1)} custom-call(s32[1]{0:T(128)} %bitcast.9.spot, bf16[256,1024]{1,0:T(8,128)(2,1)S(1)} %gated_rows.1.x_ref, bf16[1024,8192]{1,0:T(8,128)(2,1)S(1)} %bitcast.29, bf16[256,1024]{1,0:T(8,128)(2,1)} %collective-permute-done.23.refs_0_), custom_call_target="tpu_custom_call" | custom-call | flops 536870912 | bytes 2097152 | tf_op jit(solution)/shard_map/output_share/pallas_call | solution.py:252
  167.4 3.4 %collective-permute-done.25.refs_0_ = bf16[256,1024]{1,0:T(8,128)(2,1)} collective-permute-done((bf16[256,1024]{1,0:T(8,128)(2,1)S(1)}, bf16[256,1024]{1,0:T(8,128)(2,1)}, u32[]{:S(2)}, u32[]{:S(2)}) %collective-permute-start.25) | collective-permute-done | bytes 524320 | tf_op jit(solution)/shard_map/ppermute | solution.py:30
  170.9 2.0 %output_share.13 = bf16[256,1024]{1,0:T(8,128)(2,1)S(1)} custom-call(s32[1]{0:T(128)} %bitcast.12.spot, bf16[256,1024]{1,0:T(8,128)(2,1)S(1)} %gated_rows.1.x_ref, bf16[1024,8192]{1,0:T(8,128)(2,1)S(1)} %bitcast.29, bf16[256,1024]{1,0:T(8,128)(2,1)} %collective-permute-done.25.refs_0_), custom_call_target="tpu_custom_call" | custom-call | flops 536870912 | bytes 2097152 | tf_op jit(solution)/shard_map/output_share/pallas_call | solution.py:252
  172.9 2.1 %collective-permute-start.26 = (bf16[256,1024]{1,0:T(8,128)(2,1)S(1)}, bf16[256,1024]{1,0:T(8,128)(2,1)S(1)}, u32[]{:S(2)}, u32[]{:S(2)}) collective-permute-start(bf16[256,1024]{1,0:T(8,128)(2,1)S(1)} %output_share.13), channel_id=1, source_target_pairs={{0,12},{2,14},{4,0},{6,2},{8,4},{10,6},{12,8},{14,10},{1,13},{3,15... | collective-permute-start | bytes 1572872 | tf_op jit(solution)/shard_map/ppermute | solution.py:30
  174.9 1.5 collective-permute-done.27.refs_0_
  176.4 1.2 output_share.15
  177.6 3.1 %collective-permute-done.22 = bf16[256,1024]{1,0:T(8,128)(2,1)S(1)} collective-permute-done((bf16[256,1024]{1,0:T(8,128)(2,1)}, bf16[256,1024]{1,0:T(8,128)(2,1)S(1)}, u32[]{:S(2)}, u32[]{:S(2)}) %collective-permute-start.22) | collective-permute-done | bytes 524320 | tf_op jit(solution)/shard_map/ppermute | solution.py:30
  180.7 8.0 %collective-permute-done.24 = bf16[256,1024]{1,0:T(8,128)(2,1)S(1)} collective-permute-done((bf16[256,1024]{1,0:T(8,128)(2,1)S(1)}, bf16[256,1024]{1,0:T(8,128)(2,1)S(1)}, u32[]{:S(2)}, u32[]{:S(2)}) %collective-permute-start.24) | collective-permute-done | bytes 524320 | tf_op jit(solution)/shard_map/ppermute | solution.py:30
  188.7 1.2 add_convert_fusion
  (110 shorter events, 5.5 us)
Async XLA Ops:
  0.0 1.2 copy-start
  4.7 10.0 %collective-permute-start.8 = (bf16[144,1024]{1,0:T(8,128)(2,1)S(1)}, bf16[144,1024]{1,0:T(8,128)(2,1)S(1)}, u32[]{:S(2)}, u32[]{:S(2)}) collective-permute-start(bf16[144,1024]{1,0:T(8,128)(2,1)S(1)} %maximum_maximum_fusion.refs_3_.near_ref.refs_10_), channel_id=1, source_target_pairs={{0,2},{2,0},{4,6},{6,4},{8,10},{10,8},{12,14},{14,12},{1,3},{3,1},... | collective-permute-start | bytes 884744 | tf_op jit(solution)/shard_map/ppermute | solution.py:30
  6.3 19.8 %collective-permute-start.4 = (bf16[144,1024]{1,0:T(8,128)(2,1)S(1)}, bf16[144,1024]{1,0:T(8,128)(2,1)S(1)}, u32[]{:S(2)}, u32[]{:S(2)}) collective-permute-start(bf16[144,1024]{1,0:T(8,128)(2,1)S(1)} %maximum_maximum_fusion.refs_3_.near_ref.refs_10_), channel_id=1, source_target_pairs={{0,4},{2,6},{4,8},{6,10},{8,12},{10,14},{12,0},{14,2},{1,5},{3,7},... | collective-permute-start | bytes 884744 | tf_op jit(solution)/shard_map/ppermute | solution.py:30
  7.9 95.9 %collective-permute-start.13 = (bf16[256,1024]{1,0:T(8,128)(2,1)S(1)}, bf16[256,1024]{1,0:T(8,128)(2,1)}, u32[]{:S(2)}, u32[]{:S(2)}) collective-permute-start(bf16[256,1024]{1,0:T(8,128)(2,1)S(1)} %get-tuple-element.22.refs_1_), channel_id=1, source_target_pairs={{0,2},{2,0},{4,6},{6,4},{8,10},{10,8},{12,14},{14,12},{1,3},{3,1},... | collective-permute-start | bytes 1572872 | tf_op jit(solution)/shard_map/ppermute | solution.py:30
  8.4 21.2 %collective-permute-start = (bf16[256,1024]{1,0:T(8,128)(2,1)S(1)}, bf16[256,1024]{1,0:T(8,128)(2,1)}, u32[]{:S(2)}, u32[]{:S(2)}) collective-permute-start(bf16[256,1024]{1,0:T(8,128)(2,1)S(1)} %get-tuple-element.22.refs_1_), channel_id=1, source_target_pairs={{0,4},{2,6},{4,8},{6,10},{8,12},{10,14},{12,0},{14,2},{1,5},{3,7},... | collective-permute-start | bytes 1572872 | tf_op jit(solution)/shard_map/ppermute | solution.py:30
  14.8 5.7 %copy-start.2 = (bf16[8,127,8192]{2,0,1:T(8,128)(2,1)S(1)}, bf16[8,127,8192]{2,0,1:T(8,128)(2,1)}, u32[]{:S(2)}) copy-start(bf16[8,127,8192]{2,0,1:T(8,128)(2,1)} %param.15) | copy-start | bytes 49938436
  24.5 5.1 %collective-permute-start.14 = (bf16[4,8,1024]{2,1,0:T(8,128)(2,1)S(1)}, bf16[4,8,1024]{2,1,0:T(8,128)(2,1)S(1)}, u32[]{:S(2)}, u32[]{:S(2)}) collective-permute-start(bf16[4,8,1024]{2,1,0:T(8,128)(2,1)S(1)} %get-tuple-element.14), channel_id=1, source_target_pairs={{0,2},{2,0},{4,6},{6,4},{8,10},{10,8},{12,14},{14,12},{1,3},{3,1},... | collective-permute-start | bytes 196616 | tf_op jit(solution)/shard_map/ppermute | solution.py:30
  26.2 10.0 %collective-permute-start.9 = (bf16[144,1024]{1,0:T(8,128)(2,1)S(1)}, bf16[144,1024]{1,0:T(8,128)(2,1)S(1)}, u32[]{:S(2)}, u32[]{:S(2)}) collective-permute-start(bf16[144,1024]{1,0:T(8,128)(2,1)S(1)} %collective-permute-done.4.refs_3_.near_ref), channel_id=1, source_target_pairs={{0,2},{2,0},{4,6},{6,4},{8,10},{10,8},{12,14},{14,12},{1,3},{3,1},... | collective-permute-start | bytes 884744 | tf_op jit(solution)/shard_map/ppermute | solution.py:30
  26.7 19.7 %collective-permute-start.5 = (bf16[144,1024]{1,0:T(8,128)(2,1)S(1)}, bf16[144,1024]{1,0:T(8,128)(2,1)S(1)}, u32[]{:S(2)}, u32[]{:S(2)}) collective-permute-start(bf16[144,1024]{1,0:T(8,128)(2,1)S(1)} %collective-permute-done.4.refs_3_.near_ref), channel_id=1, source_target_pairs={{0,4},{2,6},{4,8},{6,10},{8,12},{10,14},{12,0},{14,2},{1,5},{3,7},... | collective-permute-start | bytes 884744 | tf_op jit(solution)/shard_map/ppermute | solution.py:30
  29.6 83.8 %collective-permute-start.12 = (bf16[256,1024]{1,0:T(8,128)(2,1)}, bf16[256,1024]{1,0:T(8,128)(2,1)}, u32[]{:S(2)}, u32[]{:S(2)}) collective-permute-start(bf16[256,1024]{1,0:T(8,128)(2,1)} %collective-permute-done.refs_1_), channel_id=1, source_target_pairs={{0,2},{2,0},{4,6},{6,4},{8,10},{10,8},{12,14},{14,12},{1,3},{3,1},... | collective-permute-start | bytes 1572872 | tf_op jit(solution)/shard_map/ppermute | solution.py:30
  36.2 5.7 %copy-start.3 = (bf16[8,127,8192]{2,0,1:T(8,128)(2,1)S(1)}, bf16[8,127,8192]{2,0,1:T(8,128)(2,1)}, u32[]{:S(2)}) copy-start(bf16[8,127,8192]{2,0,1:T(8,128)(2,1)} %param.15) | copy-start | bytes 49938436
  45.9 5.1 %collective-permute-start.15 = (bf16[4,8,1024]{2,1,0:T(8,128)(2,1)S(1)}, bf16[4,8,1024]{2,1,0:T(8,128)(2,1)S(1)}, u32[]{:S(2)}, u32[]{:S(2)}) collective-permute-start(bf16[4,8,1024]{2,1,0:T(8,128)(2,1)S(1)} %get-tuple-element.15), channel_id=1, source_target_pairs={{0,12},{2,14},{4,0},{6,2},{8,4},{10,6},{12,8},{14,10},{1,13},{3,15... | collective-permute-start | bytes 196616 | tf_op jit(solution)/shard_map/ppermute | solution.py:30
  46.5 16.0 %collective-permute-start.10 = (bf16[144,1024]{1,0:T(8,128)(2,1)S(1)}, bf16[144,1024]{1,0:T(8,128)(2,1)S(1)}, u32[]{:S(2)}, u32[]{:S(2)}) collective-permute-start(bf16[144,1024]{1,0:T(8,128)(2,1)S(1)} %collective-permute-done.5.refs_3_.near_ref), channel_id=1, source_target_pairs={{0,2},{2,0},{4,6},{6,4},{8,10},{10,8},{12,14},{14,12},{1,3},{3,1},... | collective-permute-start | bytes 884744 | tf_op jit(solution)/shard_map/ppermute | solution.py:30
  47.8 27.2 %collective-permute-start.6 = (bf16[144,1024]{1,0:T(8,128)(2,1)S(1)}, bf16[144,1024]{1,0:T(8,128)(2,1)S(1)}, u32[]{:S(2)}, u32[]{:S(2)}) collective-permute-start(bf16[144,1024]{1,0:T(8,128)(2,1)S(1)} %collective-permute-done.5.refs_3_.near_ref), channel_id=1, source_target_pairs={{0,4},{2,6},{4,8},{6,10},{8,12},{10,14},{12,0},{14,2},{1,5},{3,7},... | collective-permute-start | bytes 884744 | tf_op jit(solution)/shard_map/ppermute | solution.py:30
  51.0 11.2 %collective-permute-start.16 = (bf16[4,8,1024]{2,1,0:T(8,128)(2,1)S(1)}, bf16[4,8,1024]{2,1,0:T(8,128)(2,1)S(1)}, u32[]{:S(2)}, u32[]{:S(2)}) collective-permute-start(bf16[4,8,1024]{2,1,0:T(8,128)(2,1)S(1)} %get-tuple-element.16), channel_id=1, source_target_pairs={{0,14},{2,12},{4,2},{6,0},{8,6},{10,4},{12,10},{14,8},{1,15},{3,13... | collective-permute-start | bytes 196616 | tf_op jit(solution)/shard_map/ppermute | solution.py:30
  62.2 25.4 %collective-permute-start.1 = (bf16[256,1024]{1,0:T(8,128)(2,1)}, bf16[256,1024]{1,0:T(8,128)(2,1)}, u32[]{:S(2)}, u32[]{:S(2)}) collective-permute-start(bf16[256,1024]{1,0:T(8,128)(2,1)} %collective-permute-done.refs_1_), channel_id=1, source_target_pairs={{0,4},{2,6},{4,8},{6,10},{8,12},{10,14},{12,0},{14,2},{1,5},{3,7},... | collective-permute-start | bytes 1572872 | tf_op jit(solution)/shard_map/ppermute | solution.py:30
  62.5 12.6 %copy-start.9 = (bf16[32,8,1024]{2,1,0:T(8,128)(2,1)}, bf16[32,8,1024]{2,1,0:T(8,128)(2,1)S(1)}, u32[]{:S(2)}) copy-start(bf16[32,8,1024]{2,1,0:T(8,128)(2,1)S(1)} %constant_dynamic-update-slice_fusion.4) | copy-start | bytes 1572868
  62.5 5.9 %copy-start.4 = (bf16[8,127,8192]{2,0,1:T(8,128)(2,1)S(1)}, bf16[8,127,8192]{2,0,1:T(8,128)(2,1)}, u32[]{:S(2)}) copy-start(bf16[8,127,8192]{2,0,1:T(8,128)(2,1)} %param.15) | copy-start | bytes 49938436
  72.5 5.2 %collective-permute-start.17 = (bf16[4,8,1024]{2,1,0:T(8,128)(2,1)S(1)}, bf16[4,8,1024]{2,1,0:T(8,128)(2,1)S(1)}, u32[]{:S(2)}, u32[]{:S(2)}) collective-permute-start(bf16[4,8,1024]{2,1,0:T(8,128)(2,1)S(1)} %get-tuple-element.17), channel_id=1, source_target_pairs={{0,8},{2,10},{4,12},{6,14},{8,0},{10,2},{12,4},{14,6},{1,9},{3,11}... | collective-permute-start | bytes 196616 | tf_op jit(solution)/shard_map/ppermute | solution.py:30
  75.1 14.8 %collective-permute-start.7 = (bf16[144,1024]{1,0:T(8,128)(2,1)S(1)}, bf16[144,1024]{1,0:T(8,128)(2,1)S(1)}, u32[]{:S(2)}, u32[]{:S(2)}) collective-permute-start(bf16[144,1024]{1,0:T(8,128)(2,1)S(1)} %collective-permute-done.6.near_ref.refs_3_), channel_id=1, source_target_pairs={{0,2},{2,0},{4,6},{6,4},{8,10},{10,8},{12,14},{14,12},{1,3},{3,1},... | collective-permute-start | bytes 884744 | tf_op jit(solution)/shard_map/ppermute | solution.py:30
  77.7 9.3 %collective-permute-start.18 = (bf16[4,8,1024]{2,1,0:T(8,128)(2,1)S(1)}, bf16[4,8,1024]{2,1,0:T(8,128)(2,1)S(1)}, u32[]{:S(2)}, u32[]{:S(2)}) collective-permute-start(bf16[4,8,1024]{2,1,0:T(8,128)(2,1)S(1)} %get-tuple-element.18), channel_id=1, source_target_pairs={{0,10},{2,8},{4,14},{6,12},{8,2},{10,0},{12,6},{14,4},{1,11},{3,9}... | collective-permute-start | bytes 196616 | tf_op jit(solution)/shard_map/ppermute | solution.py:30
  87.6 35.5 %collective-permute-start.11 = (bf16[256,1024]{1,0:T(8,128)(2,1)}, bf16[256,1024]{1,0:T(8,128)(2,1)}, u32[]{:S(2)}, u32[]{:S(2)}) collective-permute-start(bf16[256,1024]{1,0:T(8,128)(2,1)} %collective-permute-done.1.refs_1_), channel_id=1, source_target_pairs={{0,2},{2,0},{4,6},{6,4},{8,10},{10,8},{12,14},{14,12},{1,3},{3,1},... | collective-permute-start | bytes 1572872 | tf_op jit(solution)/shard_map/ppermute | solution.py:30
  89.0 33.0 %collective-permute-start.2 = (bf16[256,1024]{1,0:T(8,128)(2,1)}, bf16[256,1024]{1,0:T(8,128)(2,1)}, u32[]{:S(2)}, u32[]{:S(2)}) collective-permute-start(bf16[256,1024]{1,0:T(8,128)(2,1)} %collective-permute-done.1.refs_1_), channel_id=1, source_target_pairs={{0,4},{2,6},{4,8},{6,10},{8,12},{10,14},{12,0},{14,2},{1,5},{3,7},... | collective-permute-start | bytes 1572872 | tf_op jit(solution)/shard_map/ppermute | solution.py:30
  89.9 5.7 %copy-start.5 = (bf16[8,127,8192]{2,0,1:T(8,128)(2,1)S(1)}, bf16[8,127,8192]{2,0,1:T(8,128)(2,1)}, u32[]{:S(2)}) copy-start(bf16[8,127,8192]{2,0,1:T(8,128)(2,1)} %param.15) | copy-start | bytes 49938436
  99.7 22.2 %collective-permute-start.19 = (bf16[4,8,1024]{2,1,0:T(8,128)(2,1)S(1)}, bf16[4,8,1024]{2,1,0:T(8,128)(2,1)S(1)}, u32[]{:S(2)}, u32[]{:S(2)}) collective-permute-start(bf16[4,8,1024]{2,1,0:T(8,128)(2,1)S(1)} %get-tuple-element.19), channel_id=1, source_target_pairs={{0,4},{2,6},{4,8},{6,10},{8,12},{10,14},{12,0},{14,2},{1,5},{3,7},... | collective-permute-start | bytes 196616 | tf_op jit(solution)/shard_map/ppermute | solution.py:30
  103.8 18.2 %collective-permute-start.20 = (bf16[4,8,1024]{2,1,0:T(8,128)(2,1)S(1)}, bf16[4,8,1024]{2,1,0:T(8,128)(2,1)S(1)}, u32[]{:S(2)}, u32[]{:S(2)}) collective-permute-start(bf16[4,8,1024]{2,1,0:T(8,128)(2,1)S(1)} %get-tuple-element.20), channel_id=1, source_target_pairs={{0,6},{2,4},{4,10},{6,8},{8,14},{10,12},{12,2},{14,0},{1,7},{3,5},... | collective-permute-start | bytes 196616 | tf_op jit(solution)/shard_map/ppermute | solution.py:30
  113.4 8.5 %copy-start.10 = (bf16[32,8,1024]{2,1,0:T(8,128)(2,1)S(1)}, bf16[32,8,1024]{2,1,0:T(8,128)(2,1)}, u32[]{:S(2)}) copy-start(bf16[32,8,1024]{2,1,0:T(8,128)(2,1)} %constant_dynamic-update-slice_fusion.2) | copy-start | bytes 1572868
  122.0 11.1 %collective-permute-start.3 = (bf16[256,1024]{1,0:T(8,128)(2,1)}, bf16[256,1024]{1,0:T(8,128)(2,1)S(1)}, u32[]{:S(2)}, u32[]{:S(2)}) collective-permute-start(bf16[256,1024]{1,0:T(8,128)(2,1)} %collective-permute-done.2.refs_1_), channel_id=1, source_target_pairs={{0,2},{2,0},{4,6},{6,4},{8,10},{10,8},{12,14},{14,12},{1,3},{3,1},... | collective-permute-start | bytes 1572872 | tf_op jit(solution)/shard_map/ppermute | solution.py:30
  123.1 18.6 %slice-start = ((s8[16777216]{0:T(1024)(128)(4,1)}), s8[4194304]{0:T(1024)(128)(4,1)S(1)}, s32[]{:S(2)}) async-start(s8[16777216]{0:T(1024)(128)(4,1)} %bitcast.26), calls=%async_computation | async-start | bytes 8388608
  123.1 18.6 %slice-start.1 = ((s8[16777216]{0:T(1024)(128)(4,1)}), s8[4194304]{0:T(1024)(128)(4,1)S(1)}, s32[]{:S(2)}) async-start(s8[16777216]{0:T(1024)(128)(4,1)} %bitcast.26), calls=%async_computation.1 | async-start | bytes 8388608
  123.1 18.6 %slice-start.2 = ((s8[16777216]{0:T(1024)(128)(4,1)}), s8[4194304]{0:T(1024)(128)(4,1)S(1)}, s32[]{:S(2)}) async-start(s8[16777216]{0:T(1024)(128)(4,1)} %bitcast.26), calls=%async_computation.2 | async-start | bytes 8388608
  133.1 8.6 %slice-start.3 = ((s8[16777216]{0:T(1024)(128)(4,1)}), s8[4194304]{0:T(1024)(128)(4,1)S(1)}, s32[]{:S(2)}) async-start(s8[16777216]{0:T(1024)(128)(4,1)} %bitcast.26), calls=%async_computation.3 | async-start | bytes 8388608
  142.9 14.9 %collective-permute-start.21 = (bf16[256,1024]{1,0:T(8,128)(2,1)S(1)}, bf16[256,1024]{1,0:T(8,128)(2,1)S(1)}, u32[]{:S(2)}, u32[]{:S(2)}) collective-permute-start(bf16[256,1024]{1,0:T(8,128)(2,1)S(1)} %output_share.8), channel_id=1, source_target_pairs={{0,2},{2,0},{4,6},{6,4},{8,10},{10,8},{12,14},{14,12},{1,3},{3,1},... | collective-permute-start | bytes 1572872 | tf_op jit(solution)/shard_map/ppermute | solution.py:30
  145.4 19.9 %collective-permute-start.23 = (bf16[256,1024]{1,0:T(8,128)(2,1)S(1)}, bf16[256,1024]{1,0:T(8,128)(2,1)}, u32[]{:S(2)}, u32[]{:S(2)}) collective-permute-start(bf16[256,1024]{1,0:T(8,128)(2,1)S(1)} %output_share.10), channel_id=1, source_target_pairs={{0,2},{2,0},{4,6},{6,4},{8,10},{10,8},{12,14},{14,12},{1,3},{3,1},... | collective-permute-start | bytes 1572872 | tf_op jit(solution)/shard_map/ppermute | solution.py:30
  147.2 18.0 %slice-start.4 = ((s8[16777216]{0:T(1024)(128)(4,1)}), s8[4194304]{0:T(1024)(128)(4,1)S(1)}, s32[]{:S(2)}) async-start(s8[16777216]{0:T(1024)(128)(4,1)} %bitcast.28), calls=%async_computation.4 | async-start | bytes 8388608
  147.3 18.0 %slice-start.5 = ((s8[16777216]{0:T(1024)(128)(4,1)}), s8[4194304]{0:T(1024)(128)(4,1)S(1)}, s32[]{:S(2)}) async-start(s8[16777216]{0:T(1024)(128)(4,1)} %bitcast.28), calls=%async_computation.5 | async-start | bytes 8388608
  147.3 23.6 %collective-permute-start.25 = (bf16[256,1024]{1,0:T(8,128)(2,1)S(1)}, bf16[256,1024]{1,0:T(8,128)(2,1)}, u32[]{:S(2)}, u32[]{:S(2)}) collective-permute-start(bf16[256,1024]{1,0:T(8,128)(2,1)S(1)} %output_share.12), channel_id=1, source_target_pairs={{0,2},{2,0},{4,6},{6,4},{8,10},{10,8},{12,14},{14,12},{1,3},{3,1},... | collective-permute-start | bytes 1572872 | tf_op jit(solution)/shard_map/ppermute | solution.py:30
  149.8 15.5 %slice-start.6 = ((s8[16777216]{0:T(1024)(128)(4,1)}), s8[4194304]{0:T(1024)(128)(4,1)S(1)}, s32[]{:S(2)}) async-start(s8[16777216]{0:T(1024)(128)(4,1)} %bitcast.28), calls=%async_computation.6 | async-start | bytes 8388608
  149.8 15.5 %slice-start.7 = ((s8[16777216]{0:T(1024)(128)(4,1)}), s8[4194304]{0:T(1024)(128)(4,1)S(1)}, s32[]{:S(2)}) async-start(s8[16777216]{0:T(1024)(128)(4,1)} %bitcast.28), calls=%async_computation.7 | async-start | bytes 8388608
  149.8 26.6 %collective-permute-start.27 = (bf16[256,1024]{1,0:T(8,128)(2,1)S(1)}, bf16[256,1024]{1,0:T(8,128)(2,1)S(1)}, u32[]{:S(2)}, u32[]{:S(2)}) collective-permute-start(bf16[256,1024]{1,0:T(8,128)(2,1)S(1)} %output_share.14), channel_id=1, source_target_pairs={{0,2},{2,0},{4,6},{6,4},{8,10},{10,8},{12,14},{14,12},{1,3},{3,1},... | collective-permute-start | bytes 1572872 | tf_op jit(solution)/shard_map/ppermute | solution.py:30
  157.8 0.8 copy-start.6
  158.6 1.0 copy-start.7
  161.4 19.2 %collective-permute-start.22 = (bf16[256,1024]{1,0:T(8,128)(2,1)}, bf16[256,1024]{1,0:T(8,128)(2,1)S(1)}, u32[]{:S(2)}, u32[]{:S(2)}) collective-permute-start(bf16[256,1024]{1,0:T(8,128)(2,1)} %output_share.9), channel_id=1, source_target_pairs={{0,8},{2,10},{4,12},{6,14},{8,0},{10,2},{12,4},{14,6},{1,9},{3,11}... | collective-permute-start | bytes 1572872 | tf_op jit(solution)/shard_map/ppermute | solution.py:30
  165.3 24.6 %copy-start.1 = (bf16[512,1024]{1,0:T(8,128)(2,1)S(1)}, bf16[512,1024]{1,0:T(8,128)(2,1)}, u32[]{:S(2)}) copy-start(bf16[512,1024]{1,0:T(8,128)(2,1)} %param.10) | copy-start | bytes 3145732
  167.4 21.3 %copy-start.8 = (f32[256,1024]{1,0:T(8,128)S(1)}, f32[256,1024]{1,0:T(8,128)}, u32[]{:S(2)}) copy-start(f32[256,1024]{1,0:T(8,128)} %get-tuple-element.28) | copy-start | bytes 3145732
  167.4 21.3 %collective-permute-start.24 = (bf16[256,1024]{1,0:T(8,128)(2,1)S(1)}, bf16[256,1024]{1,0:T(8,128)(2,1)S(1)}, u32[]{:S(2)}, u32[]{:S(2)}) collective-permute-start(bf16[256,1024]{1,0:T(8,128)(2,1)S(1)} %output_share.11), channel_id=1, source_target_pairs={{0,4},{2,6},{4,8},{6,10},{8,12},{10,14},{12,0},{14,2},{1,5},{3,7},... | collective-permute-start | bytes 1572872 | tf_op jit(solution)/shard_map/ppermute | solution.py:30
  172.9 15.8 %collective-permute-start.26 = (bf16[256,1024]{1,0:T(8,128)(2,1)S(1)}, bf16[256,1024]{1,0:T(8,128)(2,1)S(1)}, u32[]{:S(2)}, u32[]{:S(2)}) collective-permute-start(bf16[256,1024]{1,0:T(8,128)(2,1)S(1)} %output_share.13), channel_id=1, source_target_pairs={{0,12},{2,14},{4,0},{6,2},{8,4},{10,6},{12,8},{14,10},{1,13},{3,15... | collective-permute-start | bytes 1572872 | tf_op jit(solution)/shard_map/ppermute | solution.py:30

commit v3 on v2

v3 whole, which is shorter than its diff:
```python
import functools

import jax
import jax.numpy as jnp
from jax import lax
from jax.experimental import pallas as pl
from jax.experimental.pallas import tpu as pltpu
from jax.sharding import PartitionSpec as P

D = 8192
EPSILON = 1e-05
LANES = 128
PACKED = 16
INNER = 2
VMEM_LIMIT = 28 * 1024 * 1024
LARGE_LIMIT = 46 * 1024 * 1024


def place_of(mine, owners):
    return mine // INNER, mine % INNER, owners // INNER


def moved(array, outer_by, flip):
    owners = lax.axis_size("tensor")
    outer_size = owners // INNER
    pairs = []
    for source in range(owners):
        outer, inner = source // INNER, source % INNER
        pairs.append((source, (outer + outer_by) % outer_size * INNER + (inner ^ flip)))
    return lax.ppermute(array, "tensor", pairs)


def spread(block):
    outer_size = lax.axis_size("tensor") // INNER
    blocks = []
    held = block
    for step in range(outer_size):
        if step:
            held = moved(held, 1, 0)
        blocks.append((held, moved(held, 0, 1)))
    return blocks


def history_kernel(steps, spot, lengths_ref, *refs):
    *tap_refs, cache_ref, out_ref, taps_scr = refs
    lags, rows, channels = cache_ref.shape
    width = min(4 * LANES, channels)
    for index, tap_ref in enumerate(tap_refs):

        @pl.when(pl.program_id(1) == index)
        def _():
            taps_scr[...] = tap_ref[0].astype(jnp.float32)

    lengths = jnp.concatenate([lengths_ref[...]] * (width // LANES), axis=1)

    def one_chunk(chunk, carry):
        at = pl.ds(pl.multiple_of(chunk * width, width), width)
        taps = [
            jnp.broadcast_to(taps_scr[pl.ds(1 + step, 1), at], (rows, width)) for step in range(steps)
        ]
        sums = [jnp.zeros((rows, width), jnp.float32) for _ in range(steps)]
        for lag in range(lags):
            values = jnp.where(lengths > lag, cache_ref[lag, :, at].astype(jnp.float32), 0.0)
            for step in range(min(steps, lags - lag)):
                sums[step] += values * taps[step]
            taps = taps[1:]
            if lag + 1 + steps <= lags:
                taps.append(
                    jnp.broadcast_to(taps_scr[pl.ds(lag + 1 + steps, 1), at], (rows, width))
                )
        for step in range(steps):
            out_ref[0, step, :, at] = sums[step].astype(out_ref.dtype)
        return carry

    lax.fori_loop(0, channels // width, one_chunk, 0)


def history_terms(cache, tap_parts, spot, lengths, steps):
    lags, rows, width = cache.shape
    owners, tap_rows, channels = tap_parts[0].shape
    count = len(tap_parts)
    per_owner = width // owners // channels
    tap_spec = pl.BlockSpec((1, tap_rows, channels), lambda n, part, _: (n, 0, 0))
    return pl.pallas_call(
        functools.partial(history_kernel, steps),
        grid_spec=pltpu.PrefetchScalarGridSpec(
            num_scalar_prefetch=1,
            grid=(owners, count),
            in_specs=[
                pl.BlockSpec((rows, LANES), lambda n, part, _: (0, 0)),
                *[tap_spec] * count,
                pl.BlockSpec(
                    (lags, rows, channels),
                    lambda n, part, spot: (0, 0, n * per_owner + spot[0] + (spot[1] + part) % count),
                ),
            ],
            out_specs=pl.BlockSpec(
                (1, steps, rows, channels), lambda n, part, spot: (n, 0, 0, (spot[1] + part) % count)
            ),
            scratch_shapes=[pltpu.VMEM((tap_rows, channels), jnp.float32)],
        ),
        out_shape=jax.ShapeDtypeStruct((owners, steps, rows, count * channels), jnp.bfloat16),
        compiler_params=pltpu.CompilerParams(vmem_limit_bytes=LARGE_LIMIT),
        cost_estimate=pl.CostEstimate(
            flops=2 * steps * rows * lags * owners * count * channels,
            bytes_accessed=2 * rows * lags * owners * count * channels,
            transcendentals=0,
        ),
        name="history_terms",
    )(spot, lengths, *tap_parts, cache)


def project_kernel(steps, first, last, spot, near, far, gain_ref, inv_ref, w_ref, *refs):
    refs = list(refs)
    if not first:
        refs.pop(0)
    taps_ref, hist_ref = (refs.pop(0), refs.pop(0)) if last else (None, None)
    total_ref = refs.pop(0)
    gated_ref = refs.pop(0) if last else None
    (normed,) = refs
    rows, channels = near.shape
    depth, width = w_ref.shape
    block = min(512, channels)
    part = pl.program_id(0)
    parts = channels // depth
    inner = part // parts
    at = pl.ds(pl.multiple_of(part % parts * depth, depth), depth)
    scale = inv_ref[:, :1]
    gain = gain_ref[pl.ds(spot[0] * INNER + inner, 1), at]

    @pl.when(inner == spot[1])
    def _():
        normed[...] = (near[:, at].astype(jnp.float32) * scale * gain).astype(jnp.bfloat16)

    @pl.when(inner != spot[1])
    def _():
        normed[...] = (far[:, at].astype(jnp.float32) * scale * gain).astype(jnp.bfloat16)

    if first:

        @pl.when(part == 0)
        def _():
            total_ref[...] = jnp.zeros_like(total_ref)

    for start in range(0, width, block):
        columns = pl.ds(start, block)
        total_ref[:, columns] += jnp.dot(
            normed[...], w_ref[:, columns], preferred_element_type=jnp.float32
        )
    if not last:
        return

    @pl.when(part == pl.num_programs(0) - 1)
    def _():
        seqs = rows // steps
        for start in range(0, channels, LANES):
            columns = pl.ds(start, LANES)
            keys = total_ref[:, pl.ds(channels + start, LANES)]
            values = total_ref[:, pl.ds(2 * channels + start, LANES)]
            recent = (keys * values).astype(jnp.bfloat16).astype(jnp.float32)
            for step in range(steps):
                at_step = pl.ds(step * seqs, seqs)
                filtered = hist_ref[at_step, columns]
                for back in range(step + 1):
                    older = recent[(step - back) * seqs : (step - back + 1) * seqs]
                    filtered += taps_ref[pl.ds(back, 1), columns] * older
                gated_ref[at_step, columns] = (total_ref[at_step, columns] * filtered).astype(
                    jnp.bfloat16
                )


def projected(spot, pair, gains, inv_rms, w_in, earlier, taps=None, history=None, steps=1):
    near, far = pair
    rows, channels = near.shape
    first, last = earlier is None, history is not None
    depth = min(512, channels)
    parts = INNER * channels // depth

    def whole(shape):
        return pl.BlockSpec(shape, lambda part, _: (0,) * len(shape))

    in_place = pl.BlockSpec(memory_space=pltpu.VMEM)
    in_specs = [
        whole((rows, channels)),
        whole((rows, channels)),
        whole(gains.shape),
        whole((rows, LANES)),
        pl.BlockSpec((depth, w_in.shape[1]), lambda part, spot: (spot[0] * parts + part, 0)),
    ]
    args = [near, far, gains, inv_rms, w_in]
    aliases = {}
    if not first:
        in_specs.append(in_place)
        aliases = {len(args) + 1: 0}
        args.append(earlier)
    out_specs = [in_place]
    out_shape = [jax.ShapeDtypeStruct((rows, 3 * channels), jnp.float32)]
    if last:
        in_specs += [whole(taps.shape), whole((rows, channels))]
        args += [taps, history]
        out_specs.append(whole((rows, channels)))
        out_shape.append(jax.ShapeDtypeStruct((rows, channels), jnp.bfloat16))
    return pl.pallas_call(
        functools.partial(project_kernel, steps, first, last),
        grid_spec=pltpu.PrefetchScalarGridSpec(
            num_scalar_prefetch=1,
            grid=(parts,),
            in_specs=in_specs,
            out_specs=out_specs,
            scratch_shapes=[pltpu.VMEM((rows, depth), jnp.bfloat16)],
        ),
        out_shape=out_shape,
        input_output_aliases=aliases,
        compiler_params=pltpu.CompilerParams(vmem_limit_bytes=VMEM_LIMIT),
        cost_estimate=pl.CostEstimate(
            flops=2 * rows * INNER * channels * 3 * channels,
            bytes_accessed=2 * INNER * channels * 3 * channels,
            transcendentals=0,
        ),
        name="gated_rows" if last else "projected_part",
    )(spot, *args)[-1]


def share_kernel(spot, x_ref, w_ref, *refs):
    share = jnp.dot(x_ref[...], w_ref[...], preferred_element_type=jnp.float32)
    if len(refs) > 1:
        share += refs[0][...].astype(jnp.float32)
    refs[-1][...] = share.astype(refs[-1].dtype)


def output_share(spot, gated, w_out, owners, arrived=None):
    rows, channels = gated.shape
    wide = w_out.shape[1] // owners
    block = min(512, wide)
    blocks = wide // block
    specs = [
        pl.BlockSpec((rows, channels), lambda c, _: (0, 0)),
        pl.BlockSpec((channels, block), lambda c, spot: (0, spot[0] * blocks + c)),
    ]
    args = [gated, w_out]
    if arrived is not None:
        specs.append(pl.BlockSpec((rows, block), lambda c, _: (0, c)))
        args.append(arrived)
    return pl.pallas_call(
        share_kernel,
        grid_spec=pltpu.PrefetchScalarGridSpec(
            num_scalar_prefetch=1,
            grid=(blocks,),
            in_specs=specs,
            out_specs=pl.BlockSpec((rows, block), lambda c, _: (0, c)),
        ),
        out_shape=jax.ShapeDtypeStruct((rows, wide), jnp.bfloat16),
        compiler_params=pltpu.CompilerParams(vmem_limit_bytes=VMEM_LIMIT),
        cost_estimate=pl.CostEstimate(
            flops=2 * rows * channels * wide,
            bytes_accessed=2 * channels * wide,
            transcendentals=0,
        ),
        name="output_share",
    )(spot, *args)


def gathered_taps(filters):
    owners = lax.axis_size("tensor")
    channels = filters.shape[0]
    groups, halves = lax.axis_size("groups"), lax.axis_size("batch")
    group, half = lax.axis_index("groups"), lax.axis_index("batch")
    if groups != 2 or halves != 2 or channels % (4 * LANES):
        return [(0, 0, [lax.all_gather(filters.T, "tensor")])]
    quarter = channels // 4
    own = lax.dynamic_slice_in_dim(filters, (group * 2 + half) * quarter, quarter, 0).T
    own = jnp.broadcast_to(own[None], (owners, *own.shape))
    own = lax.all_to_all(own, "tensor", 0, 0, tiled=True)
    swap = [(0, 1), (1, 0)]
    across = lax.ppermute(own, "groups", swap)
    return [
        (group * 2, half, [own, lax.ppermute(own, "batch", swap)]),
        ((1 - group) * 2, half, [across, lax.ppermute(across, "batch", swap)]),
    ]


def per_device(token_ids, embed, norm_gain, w_in, filters, w_out, cache_rows, owner, lengths):
    steps, seqs = token_ids.shape
    vocab, channels = embed.shape
    rows = cache_rows.shape[0]
    tokens = steps * seqs
    owners = lax.axis_size("tensor")
    halves = lax.axis_size("batch")
    mine = lax.axis_index("tensor")
    half = lax.axis_index("batch")
    outer, inner, outer_size = place_of(mine, owners)

    onehot = token_ids.reshape(-1)[:, None] == jnp.arange(vocab, dtype=jnp.int32)[None, :]
    stream = jnp.dot(onehot.astype(jnp.bfloat16), embed, preferred_element_type=jnp.float32)
    streams = spread(stream.astype(jnp.bfloat16))

    tiny = jnp.concatenate([norm_gain.astype(jnp.float32), jnp.sum(stream * stream, axis=1)])
    tiny = tiny.reshape(-1, LANES)
    tiny = lax.all_to_all(
        jnp.broadcast_to(tiny[None], (owners, *tiny.shape)), "tensor", 0, 0, tiled=True
    )
    gain_rows = channels // LANES
    gains = tiny[:, :gain_rows].reshape(owners, channels)
    inv_rms = lax.rsqrt(jnp.sum(tiny[:, gain_rows:], axis=0).reshape(tokens) / D + EPSILON)
    inv_rms = jnp.broadcast_to(inv_rms[:, None], (tokens, LANES))

    owner_grid = owner.reshape(owners, halves, rows)
    arrived = lax.dynamic_index_in_dim(owner_grid, half, 1, keepdims=False) - half * seqs
    seq_index = jnp.arange(seqs, dtype=jnp.int32)
    own = lax.dynamic_index_in_dim(arrived, mine, 0, keepdims=False)
    row_lengths = jnp.sum(jnp.where(own[:, None] == seq_index[None, :], lengths[None, :], 0), axis=1)
    row_lengths = jnp.broadcast_to(row_lengths[:, None], (rows, LANES))
    step_index = jnp.arange(steps, dtype=jnp.int32)
    place = (
        (step_index[:, None, None, None, None] == step_index[None, None, None, :, None])
        & (seq_index[None, :, None, None, None] == arrived[None, None, :, None, :])
    ).reshape(tokens, owners * steps * rows)
    place = place.astype(jnp.bfloat16)

    cache = cache_rows.transpose(1, 0, 2)
    histories = []
    for first, listed, tap_parts in gathered_taps(filters):
        spot = jnp.stack([jnp.int32(first), jnp.int32(listed)])
        terms = history_terms(cache, tap_parts, spot, row_lengths, steps)
        terms = lax.all_to_all(terms, "tensor", 0, 0, tiled=True)
        histories.append(
            jnp.dot(
                place,
                terms.reshape(owners * steps * rows, terms.shape[3]),
                preferred_element_type=jnp.float32,
            )
        )
    history = jnp.concatenate(histories, axis=1)
    if len(histories) == 2:
        swapped = jnp.concatenate(histories[::-1], axis=1)
        history = jnp.where(lax.axis_index("groups") == 0, history, swapped)

    def spot_at(back):
        return jnp.stack([(outer + back) % outer_size, inner]).astype(jnp.int32)

    sums = None
    near_taps = filters[:, : 2 * steps].T.astype(jnp.float32)
    for back in range(outer_size):
        ends = dict(taps=near_taps, history=history, steps=steps) if back == outer_size - 1 else {}
        sums = projected(spot_at(-back), streams[back], gains, inv_rms, w_in, sums, **ends)
    gated = sums

    def spot_to(ahead, flip):
        return ((outer + ahead) % outer_size * INNER + (inner + flip) % INNER)[None].astype(jnp.int32)

    order = sorted(range(outer_size), key=lambda ahead: (ahead == 0, -min(ahead, outer_size - ahead)))
    across = {
        ahead: moved(output_share(spot_to(ahead, 1), gated, w_out, owners), 0, 1) for ahead in order
    }
    out = stream
    for ahead in order:
        share = output_share(spot_to(ahead, 0), gated, w_out, owners, across[ahead])
        out = out + (moved(share, ahead, 0) if ahead else share).astype(jnp.float32)
    return out.astype(jnp.bfloat16).reshape(steps, seqs, channels)


def solution(mesh):
    in_specs = (
        P(None, ("groups", "batch")),
        P(None, "tensor"),
        P("tensor"),
        P(None, "tensor"),
        P("tensor", None),
        P("tensor", None),
        P(("groups", "tensor", "batch"), None, None),
        P("groups"),
        P(("groups", "batch")),
    )
    out_specs = P(None, ("groups", "batch"), "tensor")
    return jax.shard_map(
        per_device, mesh=mesh, in_specs=in_specs, out_specs=out_specs, check_vma=False
    )
```

time: 192 us -> 224 us (1.17)
  Pallas kernels: 63 us -> 75.6 us
  local copies, waits for them, and re-layouts: 30.7 us -> 39.7 us
  waiting for transfers between devices: 53.2 us -> 58.3 us
  starting transfers between devices: 37.3 us -> 40 us
  matrix products: 1.8 us -> 4.06 us
    all_to_all x0 -> x4, starting transfers between devices: none -> 22.6 us  [the longest x2 12.2 us: per_device(): terms = lax.all_to_all(terms, 'tensor', 0, 0, tiled=True)]
    ppermute x28 -> x14, starting transfers between devices: 37.3 us -> 16.8 us  [moved(): return lax.ppermute(array, 'tensor', pairs)]
    all_to_all x0 -> x4, waiting for transfers between devices: none -> 17.6 us  [the longest x1 14.8 us: gathered_taps(): own = lax.all_to_all(own, 'tensor', 0, 0, tiled=True)]
    pallas_call x4 -> x2, Pallas kernels: 16.1 us -> 28.6 us  [history_terms(): pl.pallas_call(functools.partial(history_kernel, steps), grid_spec=pltpu....]
    ppermute x28 -> x14, waiting for transfers between devices: 53.2 us -> 40.7 us  [moved(): return lax.ppermute(array, 'tensor', pairs)]
    unnamed x46 -> x47, local copies, waits for them, and re-layouts: 27.8 us -> 36 us
    dot_general x1 -> x2, matrix products: 0.35 us -> 2.59 us  [per_device(): jnp.dot(place, terms.reshape(owners * steps * rows, terms.shape[3]), pref...]
  transfers between devices with their start and end apart: 28 -> 21, of which waited for: 13 -> 6; matrix products, arithmetic and copies ran while one was open for 3% -> 3% of each run, Pallas kernels for 28% -> 29%
where the time goes in v3:
time: 224 us; the launch traced here: 222 us
  Pallas kernels  75.6 us (34%)
  waiting for transfers between devices  58.3 us (26%)
  starting transfers between devices  40 us (18%)
  local copies, waits for them, and re-layouts  39.7 us (18%)
  matrix products  4.06 us (2%)
  other arithmetic  3.58 us (2%)
    ppermute x14, waiting for transfers between devices, moved(): return lax.ppermute(array, 'tensor', pairs)  40.7 us
    unnamed x47, local copies, waits for them, and re-layouts  36 us
    pallas_call x4, Pallas kernels, projected(): pl.pallas_call(functools.partial(project_kernel, steps, first, last), gri...  34.1 us
    pallas_call x2, Pallas kernels, history_terms(): pl.pallas_call(functools.partial(history_kernel, steps), grid_spec=pltpu....  28.6 us
    ppermute x14, starting transfers between devices, moved(): return lax.ppermute(array, 'tensor', pairs)  16.8 us
    all_to_all x1, waiting for transfers between devices, gathered_taps(): own = lax.all_to_all(own, 'tensor', 0, 0, tiled=True)  14.8 us
    pallas_call x8, Pallas kernels, output_share(): pl.pallas_call(share_kernel, grid_spec=pltpu.PrefetchScalarGridSpec(num_s...  13 us
    all_to_all x2, starting transfers between devices, per_device(): terms = lax.all_to_all(terms, 'tensor', 0, 0, tiled=True)  12.2 us
  transfers between devices with their start and end apart: 21, of which 6 were waited for; matrix products, arithmetic and copies ran while one was open for 3% of the time, Pallas kernels for 29%

profile of v3, /device:TPU:18, one launch (start us, length us, event | category | flops | bytes accessed | tf_op | source)
XLA Modules:
  0.0 221.7 jit_solution(15637573704445181888)
XLA Ops:
  0.0 0.9 eq.91
  0.9 0.4 copy-done
  1.3 1.5 multiply_reduce_fusion
  2.7 1.5 collective-permute-start.6
  4.3 1.6 collective-permute-start
  5.8 0.8 dynamic-slice_bitcast_fusion
  6.7 0.1 copy.20
  6.8 0.8 broadcast_in_dim.76
  7.6 4.2 %all-to-all-start.1 = ((bf16[8,128,256]{2,1,0:T(8,128)(2,1)}), bf16[8,128,256]{2,1,0:T(8,128)(2,1)S(1)}, u32[]{:S(2)}, u32[]{:S(2)}) async-start(bf16[8,128,256]{2,1,0:T(8,128)(2,1)} %broadcast_in_dim.76), calls=%async_computation.1 | async-start | bytes 1048576 | tf_op jit(solution)/shard_map/all_to_all | solution.py:273
  12.1 0.2 broadcast_and_fusion
  12.4 0.3 and.98
  12.7 0.1 copy.21
  13.1 0.2 select_reduce_fusion
  13.3 14.8 %all-to-all-done.1.refs_0_ = bf16[8,128,256]{2,1,0:T(8,128)(2,1)S(1)} async-done(((bf16[8,128,256]{2,1,0:T(8,128)(2,1)}), bf16[8,128,256]{2,1,0:T(8,128)(2,1)S(1)}, u32[]{:S(2)}, u32[]{:S(2)}) %all-to-all-start.1) | async-done | bytes 524320 | tf_op jit(solution)/shard_map/all_to_all | solution.py:273
  28.1 0.6 broadcast_in_dim.71
  28.7 6.2 %all-to-all-start = ((f32[8,10,128]{2,1,0:T(8,128)}), f32[8,10,128]{2,1,0:T(8,128)S(1)}, u32[]{:S(2)}, u32[]{:S(2)}) async-start(f32[8,10,128]{2,1,0:T(8,128)} %broadcast_in_dim.71), calls=%async_computation | async-start | bytes 131072 | tf_op jit(solution)/shard_map/all_to_all | solution.py:299
  35.1 1.5 collective-permute-start.1
  36.5 0.5 collective-permute-start.8
  37.1 2.7 %all-to-all-done = f32[8,10,128]{2,1,0:T(8,128)S(1)} async-done(((f32[8,10,128]{2,1,0:T(8,128)}), f32[8,10,128]{2,1,0:T(8,128)S(1)}, u32[]{:S(2)}, u32[]{:S(2)}) %all-to-all-start) | async-done | bytes 40992 | tf_op jit(solution)/shard_map/all_to_all | solution.py:299
  39.8 0.3 collective-permute-start.5
  40.1 8.9 %collective-permute-done.1.near = bf16[256,1024]{1,0:T(8,128)(2,1)} collective-permute-done((bf16[256,1024]{1,0:T(8,128)(2,1)}, bf16[256,1024]{1,0:T(8,128)(2,1)}, u32[]{:S(2)}, u32[]{:S(2)}) %collective-permute-start.1) | collective-permute-done | bytes 524320 | tf_op jit(solution)/shard_map/ppermute | solution.py:30
  49.0 1.8 collective-permute-start.4
  50.8 1.3 collective-permute-start.2
  52.2 14.2 %history_terms.2 = bf16[8,4,8,512]{3,2,1,0:T(8,128)(2,1)} custom-call(s32[2]{0:T(128)S(1)} %pad_add_fusion.4.spot, s32[8,128]{1,0:T(8,128)S(1)} %broadcast_in_dim.75.lengths_ref, bf16[8,128,256]{2,1,0:T(8,128)(2,1)S(1)} %all-to-all-done.1.refs_0_, bf16[8,128,256]{2,1,0:T(8,128)(2,1)S(1)} %collective-permute-done.7.refs_1_, bf16[127,8,8192]{2,1,0:T(8,128)(2,1)} %bitcast.50), custom_call_target="tpu_custom_call" | custom-call | flops 33292288 | bytes 8323072 | tf_op jit(solution)/shard_map/history_terms/pallas_call | solution.py:84
  66.4 7.1 %all-to-all-start.2 = ((bf16[8,4,8,512]{3,2,1,0:T(8,128)(2,1)}), bf16[8,4,8,512]{3,2,1,0:T(8,128)(2,1)}, u32[]{:S(2)}, u32[]{:S(2)}) async-start(bf16[8,4,8,512]{3,2,1,0:T(8,128)(2,1)} %history_terms.2), calls=%async_computation.2 | async-start | bytes 524288 | tf_op jit(solution)/shard_map/all_to_all | solution.py:325
  73.5 0.8 copy-done.11
  74.4 1.0 copy-done.10
  75.4 1.0 copy-done.12
  76.5 8.1 %projected_part.3.refs_0_ = f32[256,3072]{1,0:T(8,128)S(1)} custom-call(s32[2]{0:T(128)S(1)} %pad_add_fusion.3.spot, bf16[256,1024]{1,0:T(8,128)(2,1)S(1)} %copy-done.10, bf16[256,1024]{1,0:T(8,128)(2,1)S(1)} %copy-done.12, f32[8,1024]{1,0:T(8,128)S(1)} %bitcast.46, f32[256,128]{1,0:T(8,128)S(1)} %broadcast_in_dim.72.inv_ref, bf16[8192,3072]{1,0:T(8,128)(2,1)} %w_ref.15), custom_call_target="tpu_custom_call" | custom-call | flops 3221225472 | bytes 12582912 | tf_op jit(solution)/shard_map/projected_part/pallas_call | solution.py:203
  84.6 8.2 %projected_part.4.refs_0_ = f32[256,3072]{1,0:T(8,128)S(1)} custom-call(s32[2]{0:T(128)S(1)} %pad_add_fusion.2.spot, bf16[256,1024]{1,0:T(8,128)(2,1)} %collective-permute-done.near, bf16[256,1024]{1,0:T(8,128)(2,1)} %collective-permute-done.5.far, f32[8,1024]{1,0:T(8,128)S(1)} %bitcast.47, ...), custom_call_target="tpu_custom_call", output_to_operand_aliasing={{}: (6, {})} | custom-call | flops 3221225472 | bytes 12582912 | tf_op jit(solution)/shard_map/projected_part/pallas_call | solution.py:203
  92.9 1.5 collective-permute-start.3
  94.4 14.4 %history_terms.3 = bf16[8,4,8,512]{3,2,1,0:T(8,128)(2,1)} custom-call(s32[2]{0:T(128)S(1)} %pad_add_fusion.5.spot, s32[8,128]{1,0:T(8,128)S(1)} %broadcast_in_dim.75.lengths_ref, bf16[8,128,256]{2,1,0:T(8,128)(2,1)} %collective-permute-done.8.refs_0_, bf16[8,128,256]{2,1,0:T(8,128)(2,1)S(1)} %collective-permute-done.9.refs_1_, bf16[127,8,8192]{2,1,0:T(8,128)(2,1)} %bitcast.51), custom_call_target="tpu_custom_call" | custom-call | flops 33292288 | bytes 8323072 | tf_op jit(solution)/shard_map/history_terms/pallas_call | solution.py:84
  108.8 5.1 %all-to-all-start.3 = ((bf16[8,4,8,512]{3,2,1,0:T(8,128)(2,1)}), bf16[8,4,8,512]{3,2,1,0:T(8,128)(2,1)}, u32[]{:S(2)}, u32[]{:S(2)}) async-start(bf16[8,4,8,512]{3,2,1,0:T(8,128)(2,1)} %history_terms.3), calls=%async_computation.3 | async-start | bytes 524288 | tf_op jit(solution)/shard_map/all_to_all | solution.py:325
  113.9 8.2 %projected_part.5.refs_0_ = f32[256,3072]{1,0:T(8,128)S(1)} custom-call(s32[2]{0:T(128)S(1)} %pad_add_fusion.1.spot, bf16[256,1024]{1,0:T(8,128)(2,1)} %collective-permute-done.1.near, bf16[256,1024]{1,0:T(8,128)(2,1)} %collective-permute-done.4.far, f32[8,1024]{1,0:T(8,128)S(1)} %bitcast.48, ...), custom_call_target="tpu_custom_call", output_to_operand_aliasing={{}: (6, {})} | custom-call | flops 3221225472 | bytes 12582912 | tf_op jit(solution)/shard_map/projected_part/pallas_call | solution.py:203
  122.2 1.6 copy-done.7
  123.8 1.2 fusion.3
  125.0 1.4 fusion.4
  126.4 0.2 maximum_select_fusion.refs_2_
  126.7 2.0 copy-done.8
  128.7 9.5 %gated_rows.1 = (f32[256,3072]{1,0:T(8,128)S(1)}, bf16[256,1024]{1,0:T(8,128)(2,1)S(1)}) custom-call(s32[2]{0:T(128)S(1)} %pad_add_fusion.spot, bf16[256,1024]{1,0:T(8,128)(2,1)} %collective-permute-done.2.near, bf16[256,1024]{1,0:T(8,128)(2,1)} %collective-permute-done.3.far, f32[8,1024]{1,0:T(8,128)S(1)} %bitcast.49, ...), custom_call_target="tpu_custom_call", output_to_operand_aliasing={{0}: (6, {})} | custom-call | flops 3221225472 | bytes 12582912 | tf_op jit(solution)/shard_map/gated_rows/pallas_call | solution.py:203
  138.2 1.1 output_share.8
  139.4 1.5 collective-permute-start.10
  140.9 5.8 %copy-done.2 = bf16[1024,8192]{1,0:T(8,128)(2,1)S(1)} copy-done((bf16[1024,8192]{1,0:T(8,128)(2,1)S(1)}, bf16[1024,8192]{1,0:T(8,128)(2,1)}, u32[]{:S(2)}) %copy-start.2) | copy-done | bytes 16777240
  146.7 1.1 output_share.10
  147.8 0.6 collective-permute-start.12
  148.4 5.8 %copy-done.3 = bf16[1024,8192]{1,0:T(8,128)(2,1)S(1)} copy-done((bf16[1024,8192]{1,0:T(8,128)(2,1)S(1)}, bf16[1024,8192]{1,0:T(8,128)(2,1)}, u32[]{:S(2)}) %copy-start.3) | copy-done | bytes 16777240
  154.2 1.1 output_share.12
  155.3 1.5 collective-permute-start.14
  156.8 5.8 %copy-done.4 = bf16[1024,8192]{1,0:T(8,128)(2,1)S(1)} copy-done((bf16[1024,8192]{1,0:T(8,128)(2,1)S(1)}, bf16[1024,8192]{1,0:T(8,128)(2,1)}, u32[]{:S(2)}) %copy-start.4) | copy-done | bytes 16777240
  162.6 1.1 output_share.14
  163.7 0.6 collective-permute-start.16
  164.3 5.8 %copy-done.5 = bf16[1024,8192]{1,0:T(8,128)(2,1)S(1)} copy-done((bf16[1024,8192]{1,0:T(8,128)(2,1)S(1)}, bf16[1024,8192]{1,0:T(8,128)(2,1)}, u32[]{:S(2)}) %copy-start.5) | copy-done | bytes 16777240
  170.1 2.0 output_share.9
  172.1 0.1 collective-permute-start.11
  172.2 2.7 %output_share.11 = bf16[256,1024]{1,0:T(8,128)(2,1)} custom-call(s32[1]{0:T(128)} %bitcast.19.spot, bf16[256,1024]{1,0:T(8,128)(2,1)S(1)} %get-tuple-element.6.x_ref, bf16[1024,8192]{1,0:T(8,128)(2,1)S(1)} %copy-done.5, bf16[256,1024]{1,0:T(8,128)(2,1)} %collective-permute-done.12.refs_0_), custom_call_target="tpu_custom_call" | custom-call | flops 536870912 | bytes 2097152 | tf_op jit(solution)/shard_map/output_share/pallas_call | solution.py:244
  174.8 2.0 collective-permute-start.13
  176.8 1.8 output_share.13
  178.6 0.9 collective-permute-start.15
  179.6 7.2 %collective-permute-done.16.refs_0_ = bf16[256,1024]{1,0:T(8,128)(2,1)} collective-permute-done((bf16[256,1024]{1,0:T(8,128)(2,1)S(1)}, bf16[256,1024]{1,0:T(8,128)(2,1)}, u32[]{:S(2)}, u32[]{:S(2)}) %collective-permute-start.16) | collective-permute-done | bytes 524320 | tf_op jit(solution)/shard_map/ppermute | solution.py:30
  186.7 5.8 %copy-done.6 = bf16[1024,8192]{1,0:T(8,128)(2,1)S(1)} copy-done((bf16[1024,8192]{1,0:T(8,128)(2,1)S(1)}, bf16[1024,8192]{1,0:T(8,128)(2,1)}, u32[]{:S(2)}) %copy-start.6) | copy-done | bytes 16777240
  192.5 2.1 output_share.15
  194.6 11.5 %collective-permute-done.11 = bf16[256,1024]{1,0:T(8,128)(2,1)} collective-permute-done((bf16[256,1024]{1,0:T(8,128)(2,1)S(1)}, bf16[256,1024]{1,0:T(8,128)(2,1)}, u32[]{:S(2)}, u32[]{:S(2)}) %collective-permute-start.11) | collective-permute-done | bytes 524320 | tf_op jit(solution)/shard_map/ppermute | solution.py:30
  206.1 13.1 %collective-permute-done.13 = bf16[256,1024]{1,0:T(8,128)(2,1)} collective-permute-done((bf16[256,1024]{1,0:T(8,128)(2,1)}, bf16[256,1024]{1,0:T(8,128)(2,1)}, u32[]{:S(2)}, u32[]{:S(2)}) %collective-permute-start.13) | collective-permute-done | bytes 524320 | tf_op jit(solution)/shard_map/ppermute | solution.py:30
  219.3 2.4 %add_convert_fusion = bf16[256,1024]{1,0:T(8,128)(2,1)} fusion(bf16[256,1024]{1,0:T(8,128)(2,1)S(1)} %output_share.15, bf16[256,1024]{1,0:T(8,128)(2,1)S(1)} %collective-permute-done.15, bf16[256,1024]{1,0:T(8,128)(2,1)} %collective-permute-done.13, f32[256,1024]{1,0:T(8,128)S(1)} %copy-done.13, bf16[256,1024]{1,0:T(8,128)(2,1)} %collective-permute-done.11), kind=kLoop, calls=%fused_computation.1 | loop fusion | flops 2359296 | bytes 3670016 | tf_op jit(solution)/shard_map/convert_element_type | solution.py:359
  (71 shorter events, 1.0 us)
Async XLA Ops:
  0.0 1.3 copy-start
  0.0 12.7 %copy-start.14 = (bf16[1024,128]{1,0:T(8,128)(2,1)S(1)}, bf16[1024,128]{1,0:T(8,128)(2,1)}, u32[]{:S(2)}) copy-start(bf16[1024,128]{1,0:T(8,128)(2,1)} %param.13) | copy-start | bytes 786436
  0.0 11.8 %copy-start.16 = (s32[128]{0:T(128)S(1)}, s32[128]{0:T(128)}, u32[]{:S(2)}) copy-start(s32[128]{0:T(128)} %param.16) | copy-start | bytes 1540
  0.0 12.4 %copy-start.15 = (bf16[1024]{0:T(1024)(128)(2,1)S(1)}, bf16[1024]{0:T(1024)(128)(2,1)}, u32[]{:S(2)}) copy-start(bf16[1024]{0:T(1024)(128)(2,1)} %param.11) | copy-start | bytes 6148
  0.0 13.1 %copy-start.17 = (s32[64]{0:T(128)S(1)}, s32[64]{0:T(128)}, u32[]{:S(2)}) copy-start(s32[64]{0:T(128)} %param.17) | copy-start | bytes 772
  2.7 63.6 %copy-start.9 = (bf16[256,1024]{1,0:T(8,128)(2,1)}, bf16[256,1024]{1,0:T(8,128)(2,1)S(1)}, u32[]{:S(2)}) copy-start(bf16[256,1024]{1,0:T(8,128)(2,1)S(1)} %get-tuple-element.8.near) | copy-start | bytes 1572868
  2.7 70.7 %collective-permute-start.6 = (bf16[256,1024]{1,0:T(8,128)(2,1)S(1)}, bf16[256,1024]{1,0:T(8,128)(2,1)S(1)}, u32[]{:S(2)}, u32[]{:S(2)}) collective-permute-start(bf16[256,1024]{1,0:T(8,128)(2,1)S(1)} %get-tuple-element.8.near), channel_id=1, source_target_pairs={{0,2},{2,0},{4,6},{6,4},{8,10},{10,8},{12,14},{14,12},{1,3},{3,1},... | collective-permute-start | bytes 1572872 | tf_op jit(solution)/shard_map/ppermute | solution.py:30
  4.3 30.8 %collective-permute-start = (bf16[256,1024]{1,0:T(8,128)(2,1)S(1)}, bf16[256,1024]{1,0:T(8,128)(2,1)}, u32[]{:S(2)}, u32[]{:S(2)}) collective-permute-start(bf16[256,1024]{1,0:T(8,128)(2,1)S(1)} %get-tuple-element.8.near), channel_id=1, source_target_pairs={{0,4},{2,6},{4,8},{6,10},{8,12},{10,14},{12,0},{14,2},{1,5},{3,7},... | collective-permute-start | bytes 1572872 | tf_op jit(solution)/shard_map/ppermute | solution.py:30
  7.6 20.5 %all-to-all-start.1 = ((bf16[8,128,256]{2,1,0:T(8,128)(2,1)}), bf16[8,128,256]{2,1,0:T(8,128)(2,1)S(1)}, u32[]{:S(2)}, u32[]{:S(2)}) async-start(bf16[8,128,256]{2,1,0:T(8,128)(2,1)} %broadcast_in_dim.76), calls=%async_computation.1 | async-start | bytes 1048576 | tf_op jit(solution)/shard_map/all_to_all | solution.py:273
  28.7 11.0 %all-to-all-start = ((f32[8,10,128]{2,1,0:T(8,128)}), f32[8,10,128]{2,1,0:T(8,128)S(1)}, u32[]{:S(2)}, u32[]{:S(2)}) async-start(f32[8,10,128]{2,1,0:T(8,128)} %broadcast_in_dim.71), calls=%async_computation | async-start | bytes 131072 | tf_op jit(solution)/shard_map/all_to_all | solution.py:299
  35.1 13.9 %collective-permute-start.1 = (bf16[256,1024]{1,0:T(8,128)(2,1)}, bf16[256,1024]{1,0:T(8,128)(2,1)}, u32[]{:S(2)}, u32[]{:S(2)}) collective-permute-start(bf16[256,1024]{1,0:T(8,128)(2,1)} %collective-permute-done.near), channel_id=1, source_target_pairs={{0,4},{2,6},{4,8},{6,10},{8,12},{10,14},{12,0},{14,2},{1,5},{3,7},... | collective-permute-start | bytes 1572872 | tf_op jit(solution)/shard_map/ppermute | solution.py:30
  36.5 36.9 %collective-permute-start.8 = (bf16[8,128,256]{2,1,0:T(8,128)(2,1)S(1)}, bf16[8,128,256]{2,1,0:T(8,128)(2,1)}, u32[]{:S(2)}, u32[]{:S(2)}) collective-permute-start(bf16[8,128,256]{2,1,0:T(8,128)(2,1)S(1)} %all-to-all-done.1.refs_0_), channel_id=1, source_target_pairs={{0,16},{16,0},{1,17},{17,1},{2,18},{18,2},{3,19},{19,3},{4,20},{20... | collective-permute-start | bytes 1572872 | tf_op jit(solution)/shard_map/ppermute | solution.py:275
  37.1 13.7 %collective-permute-start.7 = (bf16[8,128,256]{2,1,0:T(8,128)(2,1)S(1)}, bf16[8,128,256]{2,1,0:T(8,128)(2,1)S(1)}, u32[]{:S(2)}, u32[]{:S(2)}) collective-permute-start(bf16[8,128,256]{2,1,0:T(8,128)(2,1)S(1)} %all-to-all-done.1.refs_0_), channel_id=1, source_target_pairs={{0,1},{1,0},{2,3},{3,2},{4,5},{5,4},{6,7},{7,6},{8,9},{9,8},{10,11... | collective-permute-start | bytes 1572872 | tf_op jit(solution)/shard_map/ppermute | solution.py:277
  39.8 44.8 %collective-permute-start.5 = (bf16[256,1024]{1,0:T(8,128)(2,1)}, bf16[256,1024]{1,0:T(8,128)(2,1)}, u32[]{:S(2)}, u32[]{:S(2)}) collective-permute-start(bf16[256,1024]{1,0:T(8,128)(2,1)} %collective-permute-done.near), channel_id=1, source_target_pairs={{0,2},{2,0},{4,6},{6,4},{8,10},{10,8},{12,14},{14,12},{1,3},{3,1},... | collective-permute-start | bytes 1572872 | tf_op jit(solution)/shard_map/ppermute | solution.py:30
  49.0 65.0 %collective-permute-start.4 = (bf16[256,1024]{1,0:T(8,128)(2,1)}, bf16[256,1024]{1,0:T(8,128)(2,1)}, u32[]{:S(2)}, u32[]{:S(2)}) collective-permute-start(bf16[256,1024]{1,0:T(8,128)(2,1)} %collective-permute-done.1.near), channel_id=1, source_target_pairs={{0,2},{2,0},{4,6},{6,4},{8,10},{10,8},{12,14},{14,12},{1,3},{3,1},... | collective-permute-start | bytes 1572872 | tf_op jit(solution)/shard_map/ppermute | solution.py:30
  50.8 42.1 %collective-permute-start.2 = (bf16[256,1024]{1,0:T(8,128)(2,1)}, bf16[256,1024]{1,0:T(8,128)(2,1)}, u32[]{:S(2)}, u32[]{:S(2)}) collective-permute-start(bf16[256,1024]{1,0:T(8,128)(2,1)} %collective-permute-done.1.near), channel_id=1, source_target_pairs={{0,4},{2,6},{4,8},{6,10},{8,12},{10,14},{12,0},{14,2},{1,5},{3,7},... | collective-permute-start | bytes 1572872 | tf_op jit(solution)/shard_map/ppermute | solution.py:30
  66.4 42.5 %all-to-all-start.2 = ((bf16[8,4,8,512]{3,2,1,0:T(8,128)(2,1)}), bf16[8,4,8,512]{3,2,1,0:T(8,128)(2,1)}, u32[]{:S(2)}, u32[]{:S(2)}) async-start(bf16[8,4,8,512]{3,2,1,0:T(8,128)(2,1)} %history_terms.2), calls=%async_computation.2 | async-start | bytes 524288 | tf_op jit(solution)/shard_map/all_to_all | solution.py:325
  73.5 20.9 %collective-permute-start.9 = (bf16[8,128,256]{2,1,0:T(8,128)(2,1)}, bf16[8,128,256]{2,1,0:T(8,128)(2,1)S(1)}, u32[]{:S(2)}, u32[]{:S(2)}) collective-permute-start(bf16[8,128,256]{2,1,0:T(8,128)(2,1)} %collective-permute-done.8.refs_0_), channel_id=1, source_target_pairs={{0,1},{1,0},{2,3},{3,2},{4,5},{5,4},{6,7},{7,6},{8,9},{9,8},{10,11... | collective-permute-start | bytes 1572872 | tf_op jit(solution)/shard_map/ppermute | solution.py:278
  73.5 0.8 copy-start.11
  74.4 1.0 copy-start.10
  75.4 1.0 copy-start.12
  92.9 33.8 %collective-permute-start.3 = (bf16[256,1024]{1,0:T(8,128)(2,1)}, bf16[256,1024]{1,0:T(8,128)(2,1)}, u32[]{:S(2)}, u32[]{:S(2)}) collective-permute-start(bf16[256,1024]{1,0:T(8,128)(2,1)} %collective-permute-done.2.near), channel_id=1, source_target_pairs={{0,2},{2,0},{4,6},{6,4},{8,10},{10,8},{12,14},{14,12},{1,3},{3,1},... | collective-permute-start | bytes 1572872 | tf_op jit(solution)/shard_map/ppermute | solution.py:30
  108.8 16.2 %all-to-all-start.3 = ((bf16[8,4,8,512]{3,2,1,0:T(8,128)(2,1)}), bf16[8,4,8,512]{3,2,1,0:T(8,128)(2,1)}, u32[]{:S(2)}, u32[]{:S(2)}) async-start(bf16[8,4,8,512]{3,2,1,0:T(8,128)(2,1)} %history_terms.3), calls=%async_computation.3 | async-start | bytes 524288 | tf_op jit(solution)/shard_map/all_to_all | solution.py:325
  122.1 1.6 copy-start.7
  125.0 13.2 %slice-start = ((s8[16777216]{0:T(1024)(128)(4,1)}), s8[4194304]{0:T(1024)(128)(4,1)S(1)}, s32[]{:S(2)}) async-start(s8[16777216]{0:T(1024)(128)(4,1)} %bitcast.44), calls=%async_computation.4 | async-start | bytes 8388608
  126.6 11.6 %slice-start.1 = ((s8[16777216]{0:T(1024)(128)(4,1)}), s8[4194304]{0:T(1024)(128)(4,1)S(1)}, s32[]{:S(2)}) async-start(s8[16777216]{0:T(1024)(128)(4,1)} %bitcast.44), calls=%async_computation.5 | async-start | bytes 8388608
  126.6 11.6 %slice-start.2 = ((s8[16777216]{0:T(1024)(128)(4,1)}), s8[4194304]{0:T(1024)(128)(4,1)S(1)}, s32[]{:S(2)}) async-start(s8[16777216]{0:T(1024)(128)(4,1)} %bitcast.44), calls=%async_computation.6 | async-start | bytes 8388608
  126.6 11.6 %slice-start.3 = ((s8[16777216]{0:T(1024)(128)(4,1)}), s8[4194304]{0:T(1024)(128)(4,1)S(1)}, s32[]{:S(2)}) async-start(s8[16777216]{0:T(1024)(128)(4,1)} %bitcast.44), calls=%async_computation.7 | async-start | bytes 8388608
  126.6 2.0 copy-start.8
  139.4 25.0 %collective-permute-start.10 = (bf16[256,1024]{1,0:T(8,128)(2,1)S(1)}, bf16[256,1024]{1,0:T(8,128)(2,1)}, u32[]{:S(2)}, u32[]{:S(2)}) collective-permute-start(bf16[256,1024]{1,0:T(8,128)(2,1)S(1)} %output_share.8), channel_id=1, source_target_pairs={{0,2},{2,0},{4,6},{6,4},{8,10},{10,8},{12,14},{14,12},{1,3},{3,1},... | collective-permute-start | bytes 1572872 | tf_op jit(solution)/shard_map/ppermute | solution.py:30
  140.9 5.8 %copy-start.2 = (bf16[1024,8192]{1,0:T(8,128)(2,1)S(1)}, bf16[1024,8192]{1,0:T(8,128)(2,1)}, u32[]{:S(2)}) copy-start(bf16[1024,8192]{1,0:T(8,128)(2,1)} %w_ref.23) | copy-start | bytes 50331652
  147.8 24.4 %collective-permute-start.12 = (bf16[256,1024]{1,0:T(8,128)(2,1)S(1)}, bf16[256,1024]{1,0:T(8,128)(2,1)}, u32[]{:S(2)}, u32[]{:S(2)}) collective-permute-start(bf16[256,1024]{1,0:T(8,128)(2,1)S(1)} %output_share.10), channel_id=1, source_target_pairs={{0,2},{2,0},{4,6},{6,4},{8,10},{10,8},{12,14},{14,12},{1,3},{3,1},... | collective-permute-start | bytes 1572872 | tf_op jit(solution)/shard_map/ppermute | solution.py:30
  148.4 5.8 %copy-start.3 = (bf16[1024,8192]{1,0:T(8,128)(2,1)S(1)}, bf16[1024,8192]{1,0:T(8,128)(2,1)}, u32[]{:S(2)}) copy-start(bf16[1024,8192]{1,0:T(8,128)(2,1)} %w_ref.23) | copy-start | bytes 50331652
  155.3 21.5 %collective-permute-start.14 = (bf16[256,1024]{1,0:T(8,128)(2,1)S(1)}, bf16[256,1024]{1,0:T(8,128)(2,1)S(1)}, u32[]{:S(2)}, u32[]{:S(2)}) collective-permute-start(bf16[256,1024]{1,0:T(8,128)(2,1)S(1)} %output_share.12), channel_id=1, source_target_pairs={{0,2},{2,0},{4,6},{6,4},{8,10},{10,8},{12,14},{14,12},{1,3},{3,1},... | collective-permute-start | bytes 1572872 | tf_op jit(solution)/shard_map/ppermute | solution.py:30
  156.8 5.8 %copy-start.4 = (bf16[1024,8192]{1,0:T(8,128)(2,1)S(1)}, bf16[1024,8192]{1,0:T(8,128)(2,1)}, u32[]{:S(2)}) copy-start(bf16[1024,8192]{1,0:T(8,128)(2,1)} %w_ref.23) | copy-start | bytes 50331652
  163.7 23.0 %collective-permute-start.16 = (bf16[256,1024]{1,0:T(8,128)(2,1)S(1)}, bf16[256,1024]{1,0:T(8,128)(2,1)}, u32[]{:S(2)}, u32[]{:S(2)}) collective-permute-start(bf16[256,1024]{1,0:T(8,128)(2,1)S(1)} %output_share.14), channel_id=1, source_target_pairs={{0,2},{2,0},{4,6},{6,4},{8,10},{10,8},{12,14},{14,12},{1,3},{3,1},... | collective-permute-start | bytes 1572872 | tf_op jit(solution)/shard_map/ppermute | solution.py:30
  164.3 5.8 %copy-start.5 = (bf16[1024,8192]{1,0:T(8,128)(2,1)S(1)}, bf16[1024,8192]{1,0:T(8,128)(2,1)}, u32[]{:S(2)}) copy-start(bf16[1024,8192]{1,0:T(8,128)(2,1)} %w_ref.23) | copy-start | bytes 50331652
  172.1 34.1 %collective-permute-start.11 = (bf16[256,1024]{1,0:T(8,128)(2,1)S(1)}, bf16[256,1024]{1,0:T(8,128)(2,1)}, u32[]{:S(2)}, u32[]{:S(2)}) collective-permute-start(bf16[256,1024]{1,0:T(8,128)(2,1)S(1)} %output_share.9), channel_id=1, source_target_pairs={{0,8},{2,10},{4,12},{6,14},{8,0},{10,2},{12,4},{14,6},{1,9},{3,11}... | collective-permute-start | bytes 1572872 | tf_op jit(solution)/shard_map/ppermute | solution.py:30
  174.8 44.4 %collective-permute-start.13 = (bf16[256,1024]{1,0:T(8,128)(2,1)}, bf16[256,1024]{1,0:T(8,128)(2,1)}, u32[]{:S(2)}, u32[]{:S(2)}) collective-permute-start(bf16[256,1024]{1,0:T(8,128)(2,1)} %output_share.11), channel_id=1, source_target_pairs={{0,4},{2,6},{4,8},{6,10},{8,12},{10,14},{12,0},{14,2},{1,5},{3,7},... | collective-permute-start | bytes 1572872 | tf_op jit(solution)/shard_map/ppermute | solution.py:30
  178.6 40.6 %collective-permute-start.15 = (bf16[256,1024]{1,0:T(8,128)(2,1)}, bf16[256,1024]{1,0:T(8,128)(2,1)S(1)}, u32[]{:S(2)}, u32[]{:S(2)}) collective-permute-start(bf16[256,1024]{1,0:T(8,128)(2,1)} %output_share.13), channel_id=1, source_target_pairs={{0,12},{2,14},{4,0},{6,2},{8,4},{10,6},{12,8},{14,10},{1,13},{3,15... | collective-permute-start | bytes 1572872 | tf_op jit(solution)/shard_map/ppermute | solution.py:30
  186.7 5.8 %copy-start.6 = (bf16[1024,8192]{1,0:T(8,128)(2,1)S(1)}, bf16[1024,8192]{1,0:T(8,128)(2,1)}, u32[]{:S(2)}) copy-start(bf16[1024,8192]{1,0:T(8,128)(2,1)} %w_ref.23) | copy-start | bytes 50331652
  192.5 26.8 %copy-start.13 = (f32[256,1024]{1,0:T(8,128)S(1)}, f32[256,1024]{1,0:T(8,128)}, u32[]{:S(2)}) copy-start(f32[256,1024]{1,0:T(8,128)} %get-tuple-element.9) | copy-start | bytes 3145732
  192.5 29.2 %copy-start.1 = (bf16[512,1024]{1,0:T(8,128)(2,1)S(1)}, bf16[512,1024]{1,0:T(8,128)(2,1)}, u32[]{:S(2)}) copy-start(bf16[512,1024]{1,0:T(8,128)(2,1)} %param.10) | copy-start | bytes 3145732

commit v4 on v3

--- a/solution.py
+++ b/solution.py
@@ -49,7 +49,7 @@
 
         @pl.when(pl.program_id(1) == index)
         def _():
-            taps_scr[...] = tap_ref[0].astype(jnp.float32)
+            taps_scr[...] = tap_ref[0].astype(jnp.float32).T
 
     lengths = jnp.concatenate([lengths_ref[...]] * (width // LANES), axis=1)
 
@@ -77,10 +77,9 @@
 
 def history_terms(cache, tap_parts, spot, lengths, steps):
     lags, rows, width = cache.shape
-    owners, tap_rows, channels = tap_parts[0].shape
+    owners, channels, tap_rows = tap_parts[0].shape
     count = len(tap_parts)
-    per_owner = width // owners // channels
-    tap_spec = pl.BlockSpec((1, tap_rows, channels), lambda n, part, _: (n, 0, 0))
+    tap_spec = pl.BlockSpec((1, channels, tap_rows), lambda n, part, _: (n, 0, 0))
     return pl.pallas_call(
         functools.partial(history_kernel, steps),
         grid_spec=pltpu.PrefetchScalarGridSpec(
@@ -91,11 +90,11 @@
                 *[tap_spec] * count,
                 pl.BlockSpec(
                     (lags, rows, channels),
-                    lambda n, part, spot: (0, 0, n * per_owner + spot[0] + (spot[1] + part) % count),
+                    lambda n, part, spot: (0, 0, n * count + (spot[0] + part) % count),
                 ),
             ],
             out_specs=pl.BlockSpec(
-                (1, steps, rows, channels), lambda n, part, spot: (n, 0, 0, (spot[1] + part) % count)
+                (1, steps, rows, channels), lambda n, part, spot: (n, 0, 0, (spot[0] + part) % count)
             ),
             scratch_shapes=[pltpu.VMEM((tap_rows, channels), jnp.float32)],
         ),
@@ -112,105 +111,95 @@
 
 def project_kernel(steps, first, last, spot, near, far, gain_ref, inv_ref, w_ref, *refs):
     refs = list(refs)
+    earlier = None if first else refs.pop(0)
+    taps_ref, place_ref, terms_ref = (refs.pop(0) for _ in range(3)) if last else (None,) * 3
+    out_ref, normed = refs[:2]
+    rows, channels = near.shape
+    step_at = pl.program_id(0)
+
+    @pl.when(step_at == 0)
+    def _():
+        scale = inv_ref[:, :1]
+        for flip, x_ref in ((0, near), (1, far)):
+            inner = (spot[1] + flip) % INNER
+            gain = gain_ref[pl.ds(spot[0] * INNER + inner, 1), :]
+            normed[:, pl.ds(pl.multiple_of(inner * channels, channels), channels)] = (
+                x_ref[...].astype(jnp.float32) * scale * gain
+            ).astype(jnp.bfloat16)
+
+    total = jnp.dot(normed[...], w_ref[...], preferred_element_type=jnp.float32)
     if not first:
-        refs.pop(0)
-    taps_ref, hist_ref = (refs.pop(0), refs.pop(0)) if last else (None, None)
-    total_ref = refs.pop(0)
-    gated_ref = refs.pop(0) if last else None
-    (normed,) = refs
-    rows, channels = near.shape
-    depth, width = w_ref.shape
-    block = min(512, channels)
-    part = pl.program_id(0)
-    parts = channels // depth
-    inner = part // parts
-    at = pl.ds(pl.multiple_of(part % parts * depth, depth), depth)
-    scale = inv_ref[:, :1]
-    gain = gain_ref[pl.ds(spot[0] * INNER + inner, 1), at]
-
-    @pl.when(inner == spot[1])
-    def _():
-        normed[...] = (near[:, at].astype(jnp.float32) * scale * gain).astype(jnp.bfloat16)
-
-    @pl.when(inner != spot[1])
-    def _():
-        normed[...] = (far[:, at].astype(jnp.float32) * scale * gain).astype(jnp.bfloat16)
-
-    if first:
-
-        @pl.when(part == 0)
-        def _():
-            total_ref[...] = jnp.zeros_like(total_ref)
-
-    for start in range(0, width, block):
-        columns = pl.ds(start, block)
-        total_ref[:, columns] += jnp.dot(
-            normed[...], w_ref[:, columns], preferred_element_type=jnp.float32
-        )
+        total += earlier[...]
     if not last:
+        out_ref[...] = total
         return
-
-    @pl.when(part == pl.num_programs(0) - 1)
+    parts = refs[2]
+    which = step_at % 3
+    parts[which] = total
+
+    @pl.when(which == 2)
     def _():
         seqs = rows // steps
-        for start in range(0, channels, LANES):
-            columns = pl.ds(start, LANES)
-            keys = total_ref[:, pl.ds(channels + start, LANES)]
-            values = total_ref[:, pl.ds(2 * channels + start, LANES)]
-            recent = (keys * values).astype(jnp.bfloat16).astype(jnp.float32)
-            for step in range(steps):
-                at_step = pl.ds(step * seqs, seqs)
-                filtered = hist_ref[at_step, columns]
-                for back in range(step + 1):
-                    older = recent[(step - back) * seqs : (step - back + 1) * seqs]
-                    filtered += taps_ref[pl.ds(back, 1), columns] * older
-                gated_ref[at_step, columns] = (total_ref[at_step, columns] * filtered).astype(
-                    jnp.bfloat16
-                )
-
-
-def projected(spot, pair, gains, inv_rms, w_in, earlier, taps=None, history=None, steps=1):
+        history = jnp.dot(place_ref[...], terms_ref[...], preferred_element_type=jnp.float32)
+        recent = (parts[1] * parts[2]).astype(jnp.bfloat16).astype(jnp.float32)
+        for step in range(steps):
+            at = slice(step * seqs, (step + 1) * seqs)
+            filtered = history[at]
+            for back in range(step + 1):
+                older = recent[(step - back) * seqs : (step - back + 1) * seqs]
+                filtered += taps_ref[pl.ds(back, 1), :] * older
+            out_ref[at, :] = (parts[0, at, :] * filtered).astype(jnp.bfloat16)
+
+
+def projected(spot, pair, gains, inv_rms, w_in, earlier, taps=None, place=None, terms=None, steps=1):
     near, far = pair
     rows, channels = near.shape
-    first, last = earlier is None, history is not None
-    depth = min(512, channels)
-    parts = INNER * channels // depth
+    block = min(256, channels)
+    blocks = channels // block
+    first, last = earlier is None, terms is not None
 
     def whole(shape):
-        return pl.BlockSpec(shape, lambda part, _: (0,) * len(shape))
-
-    in_place = pl.BlockSpec(memory_space=pltpu.VMEM)
+        return pl.BlockSpec(shape, lambda i, _: (0,) * len(shape))
+
+    def column(i):
+        return i % 3 * blocks + i // 3
+
     in_specs = [
         whole((rows, channels)),
         whole((rows, channels)),
         whole(gains.shape),
         whole((rows, LANES)),
-        pl.BlockSpec((depth, w_in.shape[1]), lambda part, spot: (spot[0] * parts + part, 0)),
+        pl.BlockSpec((INNER * channels, block), lambda i, spot: (spot[0], column(i))),
     ]
     args = [near, far, gains, inv_rms, w_in]
-    aliases = {}
+    total_spec = pl.BlockSpec((rows, block), lambda i, _: (0, column(i)))
     if not first:
-        in_specs.append(in_place)
-        aliases = {len(args) + 1: 0}
+        in_specs.append(total_spec)
         args.append(earlier)
-    out_specs = [in_place]
-    out_shape = [jax.ShapeDtypeStruct((rows, 3 * channels), jnp.float32)]
+    scratch = [pltpu.VMEM((rows, INNER * channels), jnp.bfloat16)]
     if last:
-        in_specs += [whole(taps.shape), whole((rows, channels))]
-        args += [taps, history]
-        out_specs.append(whole((rows, channels)))
-        out_shape.append(jax.ShapeDtypeStruct((rows, channels), jnp.bfloat16))
+        in_specs += [
+            pl.BlockSpec((taps.shape[0], block), lambda i, _: (0, i // 3)),
+            whole(place.shape),
+            pl.BlockSpec((terms.shape[0], block), lambda i, _: (0, i // 3)),
+        ]
+        args += [taps, place, terms]
+        scratch.append(pltpu.VMEM((3, rows, block), jnp.float32))
+        out_spec = pl.BlockSpec((rows, block), lambda i, _: (0, i // 3))
+        out_shape = jax.ShapeDtypeStruct((rows, channels), jnp.bfloat16)
+    else:
+        out_spec = total_spec
+        out_shape = jax.ShapeDtypeStruct((rows, 3 * channels), jnp.float32)
     return pl.pallas_call(
         functools.partial(project_kernel, steps, first, last),
         grid_spec=pltpu.PrefetchScalarGridSpec(
             num_scalar_prefetch=1,
-            grid=(parts,),
+            grid=(3 * blocks,),
             in_specs=in_specs,
-            out_specs=out_specs,
-            scratch_shapes=[pltpu.VMEM((rows, depth), jnp.bfloat16)],
+            out_specs=out_spec,
+            scratch_shapes=scratch,
         ),
         out_shape=out_shape,
-        input_output_aliases=aliases,
         compiler_params=pltpu.CompilerParams(vmem_limit_bytes=VMEM_LIMIT),
         cost_estimate=pl.CostEstimate(
             flops=2 * rows * INNER * channels * 3 * channels,
@@ -218,7 +207,7 @@
             transcendentals=0,
         ),
         name="gated_rows" if last else "projected_part",
-    )(spot, *args)[-1]
+    )(spot, *args)
 
 
 def share_kernel(spot, x_ref, w_ref, *refs):
@@ -250,7 +239,7 @@
             out_specs=pl.BlockSpec((rows, block), lambda c, _: (0, c)),
         ),
         out_shape=jax.ShapeDtypeStruct((rows, wide), jnp.bfloat16),
-        compiler_params=pltpu.CompilerParams(vmem_limit_bytes=VMEM_LIMIT),
+        compiler_params=pltpu.CompilerParams(vmem_limit_bytes=LARGE_LIMIT),
         cost_estimate=pl.CostEstimate(
             flops=2 * rows * channels * wide,
             bytes_accessed=2 * channels * wide,
@@ -261,22 +250,20 @@
 
 
 def gathered_taps(filters):
-    owners = lax.axis_size("tensor")
     channels = filters.shape[0]
-    groups, halves = lax.axis_size("groups"), lax.axis_size("batch")
-    group, half = lax.axis_index("groups"), lax.axis_index("batch")
-    if groups != 2 or halves != 2 or channels % (4 * LANES):
-        return [(0, 0, [lax.all_gather(filters.T, "tensor")])]
-    quarter = channels // 4
-    own = lax.dynamic_slice_in_dim(filters, (group * 2 + half) * quarter, quarter, 0).T
-    own = jnp.broadcast_to(own[None], (owners, *own.shape))
-    own = lax.all_to_all(own, "tensor", 0, 0, tiled=True)
-    swap = [(0, 1), (1, 0)]
-    across = lax.ppermute(own, "groups", swap)
-    return [
-        (group * 2, half, [own, lax.ppermute(own, "batch", swap)]),
-        ((1 - group) * 2, half, [across, lax.ppermute(across, "batch", swap)]),
-    ]
+    if not halved(channels):
+        return lax.all_gather(filters, "tensor")
+    wide = channels // 2
+    own = lax.dynamic_slice_in_dim(filters, lax.axis_index("batch") * wide, wide, 0)
+    return lax.all_gather(own, "tensor")
+
+
+def halved(channels):
+    return lax.axis_size("batch") == 2 and channels % (2 * LANES) == 0
+
+
+def after(array, earlier):
+    return lax.optimization_barrier((array, earlier))[0]
 
 
 def per_device(token_ids, embed, norm_gain, w_in, filters, w_out, cache_rows, owner, lengths):
@@ -318,32 +305,36 @@
     place = place.astype(jnp.bfloat16)
 
     cache = cache_rows.transpose(1, 0, 2)
-    histories = []
-    for first, listed, tap_parts in gathered_taps(filters):
-        spot = jnp.stack([jnp.int32(first), jnp.int32(listed)])
-        terms = history_terms(cache, tap_parts, spot, row_lengths, steps)
-        terms = lax.all_to_all(terms, "tensor", 0, 0, tiled=True)
-        histories.append(
-            jnp.dot(
-                place,
-                terms.reshape(owners * steps * rows, terms.shape[3]),
-                preferred_element_type=jnp.float32,
-            )
-        )
-    history = jnp.concatenate(histories, axis=1)
-    if len(histories) == 2:
-        swapped = jnp.concatenate(histories[::-1], axis=1)
-        history = jnp.where(lax.axis_index("groups") == 0, history, swapped)
+    own_taps = gathered_taps(filters)
 
     def spot_at(back):
         return jnp.stack([(outer + back) % outer_size, inner]).astype(jnp.int32)
 
+    near_taps = filters[:, : 2 * steps].T.astype(jnp.float32)
     sums = None
-    near_taps = filters[:, : 2 * steps].T.astype(jnp.float32)
-    for back in range(outer_size):
-        ends = dict(taps=near_taps, history=history, steps=steps) if back == outer_size - 1 else {}
-        sums = projected(spot_at(-back), streams[back], gains, inv_rms, w_in, sums, **ends)
-    gated = sums
+    for back in range(outer_size - 1):
+        sums = projected(spot_at(-back), streams[back], gains, inv_rms, w_in, sums)
+        if back == outer_size // 2 - 1:
+            own_taps = after(own_taps, sums)
+    tap_parts = [own_taps]
+    listed = jnp.int32(0)
+    if halved(channels):
+        tap_parts.append(lax.ppermute(own_taps, "batch", [(0, 1), (1, 0)]))
+        listed = half
+    terms = history_terms(cache, tap_parts, listed[None], row_lengths, steps)
+    terms = lax.all_to_all(terms, "tensor", 0, 0, tiled=True)
+    gated = projected(
+        spot_at(1 - outer_size),
+        streams[outer_size - 1],
+        gains,
+        inv_rms,
+        w_in,
+        sums,
+        taps=near_taps,
+        place=place,
+        terms=terms.reshape(owners * steps * rows, channels),
+        steps=steps,
+    )
 
     def spot_to(ahead, flip):
         return ((outer + ahead) % outer_size * INNER + (inner + flip) % INNER)[None].astype(jnp.int32)

time: 224 us -> 216 us (0.964)
  local copies, waits for them, and re-layouts: 39.7 us -> 15.6 us
  between operations: 0.44 us -> 13.7 us
  Pallas kernels: 75.6 us -> 87.6 us
  starting transfers between devices: 40 us -> 29.2 us
  matrix products: 4.06 us -> 1.44 us
  waiting for transfers between devices: 58.3 us -> 60.6 us
    unnamed x47 -> x29, local copies, waits for them, and re-layouts: 36 us -> 9.5 us
    pallas_call x4, Pallas kernels: 34.1 us -> 49.5 us  [projected(): pl.pallas_call(functools.partial(project_kernel, steps, first, last), gri...]
    all_to_all x1 -> x0, waiting for transfers between devices: 14.8 us -> none  [gathered_taps(): own = lax.all_to_all(own, 'tensor', 0, 0, tiled=True)]
    ppermute x14, waiting for transfers between devices: 40.7 us -> 50.1 us  [moved(): return lax.ppermute(array, 'tensor', pairs)]
    pallas_call x2 -> x1, Pallas kernels: 28.6 us -> 19.3 us  [history_terms(): pl.pallas_call(functools.partial(history_kernel, steps), grid_spec=pltpu....]
    all_to_all x1, waiting for transfers between devices: 2.72 us -> 10.5 us  [per_device(): lax.all_to_all(jnp.broadcast_to(tiny[None], (owners, *tiny.shape)), 'tens...]
    pallas_call x8, Pallas kernels: 13 us -> 18.9 us  [output_share(): pl.pallas_call(share_kernel, grid_spec=pltpu.PrefetchScalarGridSpec(num_s...]
    all_to_all x1 -> x0, starting transfers between devices: 4.2 us -> none  [gathered_taps(): own = lax.all_to_all(own, 'tensor', 0, 0, tiled=True)]
  transfers between devices with their start and end apart: 21 -> 18, of which waited for: 6 -> 7; matrix products, arithmetic and copies ran while one was open for 3% -> 4% of each run, Pallas kernels for 29% -> 34%
where the time goes in v4:
time: 216 us; the launch traced here: 213 us
  Pallas kernels  87.6 us (41%)
  waiting for transfers between devices  60.6 us (28%)
  starting transfers between devices  29.2 us (14%)
  local copies, waits for them, and re-layouts  15.6 us (7%)
  between operations  13.7 us (6%)
  other arithmetic  4.62 us (2%)
    ppermute x14, waiting for transfers between devices, moved(): return lax.ppermute(array, 'tensor', pairs)  50.1 us
    pallas_call x4, Pallas kernels, projected(): pl.pallas_call(functools.partial(project_kernel, steps, first, last), gri...  49.5 us
    pallas_call x1, Pallas kernels, history_terms(): pl.pallas_call(functools.partial(history_kernel, steps), grid_spec=pltpu....  19.3 us
    pallas_call x8, Pallas kernels, output_share(): pl.pallas_call(share_kernel, grid_spec=pltpu.PrefetchScalarGridSpec(num_s...  18.9 us
    ppermute x14, starting transfers between devices, moved(): return lax.ppermute(array, 'tensor', pairs)  16.3 us
    all_to_all x1, waiting for transfers between devices, per_device(): lax.all_to_all(jnp.broadcast_to(tiny[None], (owners, *tiny.shape)), 'tens...  10.5 us
    unnamed x29, local copies, waits for them, and re-layouts  9.5 us
    all_to_all x1, starting transfers between devices, per_device(): terms = lax.all_to_all(terms, 'tensor', 0, 0, tiled=True)  8.64 us
  transfers between devices with their start and end apart: 18, of which 7 were waited for; matrix products, arithmetic and copies ran while one was open for 4% of the time, Pallas kernels for 34%

profile of v4, /device:TPU:18, one launch (start us, length us, event | category | flops | bytes accessed | tf_op | source)
XLA Modules:
  0.0 212.8 jit_solution(381982278856015391)
XLA Ops:
  6.5 1.6 constant_dynamic-slice_fusion
  8.2 0.8 eq.88
  9.0 1.4 multiply_reduce_fusion
  10.4 1.5 collective-permute-start.6
  11.9 1.6 collective-permute-start
  13.5 0.7 convert_element_type.33
  14.2 0.6 broadcast_in_dim.68
  14.8 4.2 %all-to-all-start = ((f32[8,10,128]{2,1,0:T(8,128)}), f32[8,10,128]{2,1,0:T(8,128)S(1)}, u32[]{:S(2)}, u32[]{:S(2)}) async-start(f32[8,10,128]{2,1,0:T(8,128)} %broadcast_in_dim.68), calls=%async_computation | async-start | bytes 131072 | tf_op jit(solution)/shard_map/all_to_all | solution.py:286
  19.0 0.1 pad_add_fusion.3.spot
  19.1 0.1 pad_add_fusion.2.spot
  19.2 10.5 %all-to-all-done = f32[8,10,128]{2,1,0:T(8,128)S(1)} async-done(((f32[8,10,128]{2,1,0:T(8,128)}), f32[8,10,128]{2,1,0:T(8,128)S(1)}, u32[]{:S(2)}, u32[]{:S(2)}) %all-to-all-start) | async-done | bytes 40992 | tf_op jit(solution)/shard_map/all_to_all | solution.py:286
  29.7 1.3 collective-permute-start.5
  31.1 0.1 broadcast_in_dim.69.inv_ref
  31.2 12.1 %projected_part.3.refs_0_ = f32[256,3072]{1,0:T(8,128)S(1)} custom-call(s32[2]{0:T(128)S(1)} %pad_add_fusion.3.spot, bf16[256,1024]{1,0:T(8,128)(2,1)S(1)} %get-tuple-element.8.near, bf16[256,1024]{1,0:T(8,128)(2,1)S(1)} %collective-permute-done.6.far, f32[8,1024]{1,0:T(8,128)S(1)} %bitcast.38, f32[256,128]{1,0:T(8,128)S(1)} %broadcast_in_dim.69.inv_ref, ...), custom_call_target="tpu_custom_call" | custom-call | flops 3221225472 | bytes 12582912 | tf_op jit(solution)/shard_map/projected_part/pallas_call | solution.py:193
  43.3 1.0 copy-done.7
  44.3 12.1 %projected_part.4.refs_0_ = f32[256,3072]{1,0:T(8,128)S(1)} custom-call(s32[2]{0:T(128)S(1)} %pad_add_fusion.2.spot, bf16[256,1024]{1,0:T(8,128)(2,1)S(1)} %copy-done.7, bf16[256,1024]{1,0:T(8,128)(2,1)S(1)} %collective-permute-done.5.far, f32[8,1024]{1,0:T(8,128)S(1)} %bitcast.39, f32[256,128]{1,0:T(8,128)S(1)} %broadcast_in_dim.69.inv_ref, ...), custom_call_target="tpu_custom_call" | custom-call | flops 3221225472 | bytes 12582912 | tf_op jit(solution)/shard_map/projected_part/pallas_call | solution.py:193
  56.5 0.0 all-gather.3.cloned.1.call-done
  56.5 0.1 collective-permute-start.7
  56.6 0.1 reshape.69
  56.7 1.6 collective-permute-start.1
  58.3 0.2 select_reduce_fusion
  58.5 0.1 iota_compare_fusion.2
  58.5 13.2 %collective-permute-done.1.near = bf16[256,1024]{1,0:T(8,128)(2,1)} collective-permute-done((bf16[256,1024]{1,0:T(8,128)(2,1)}, bf16[256,1024]{1,0:T(8,128)(2,1)}, u32[]{:S(2)}, u32[]{:S(2)}) %collective-permute-start.1) | collective-permute-done | bytes 524320 | tf_op jit(solution)/shard_map/ppermute | solution.py:30
  71.8 1.1 collective-permute-start.2
  72.9 0.7 collective-permute-start.4
  73.6 0.1 broadcast_in_dim.73.lengths_ref
  73.7 1.2 copy-done.5
  74.9 19.3 %history_terms.1 = bf16[8,4,8,1024]{3,2,1,0:T(8,128)(2,1)S(1)} custom-call(s32[1]{0:T(128)} %bitcast.10.spot, s32[8,128]{1,0:T(8,128)S(1)} %broadcast_in_dim.73.lengths_ref, bf16[8,512,128]{2,1,0:T(8,128)(2,1)S(1)} %bitcast.37, bf16[8,512,128]{2,1,0:T(8,128)(2,1)} %collective-permute-done.7.refs_1_, bf16[127,8,8192]{2,1,0:T(8,128)(2,1)} %bitcast.42), custom_call_target="tpu_custom_call" | custom-call | flops 66584576 | bytes 16646144 | tf_op jit(solution)/shard_map/history_terms/pallas_call | solution.py:83
  94.3 0.8 copy-done.4
  95.0 8.6 %all-to-all-start.1 = ((bf16[8,4,8,1024]{3,2,1,0:T(8,128)(2,1)}), bf16[8,4,8,1024]{3,2,1,0:T(8,128)(2,1)}, u32[]{:S(2)}, u32[]{:S(2)}) async-start(bf16[8,4,8,1024]{3,2,1,0:T(8,128)(2,1)} %copy-done.4), calls=%async_computation.1 | async-start | bytes 1048576 | tf_op jit(solution)/shard_map/all_to_all | solution.py:325
  103.7 0.9 and_convert_fusion
  104.6 1.8 reshape.72
  106.4 1.0 copy.16.refs_2_
  107.4 1.0 copy.17
  108.5 0.1 pad_add_fusion.1.spot
  108.6 0.1 pad_add_fusion.spot
  108.7 1.5 collective-permute-start.3
  110.1 12.4 %projected_part.5.refs_0_ = f32[256,3072]{1,0:T(8,128)S(1)} custom-call(s32[2]{0:T(128)S(1)} %pad_add_fusion.1.spot, bf16[256,1024]{1,0:T(8,128)(2,1)} %collective-permute-done.1.near, bf16[256,1024]{1,0:T(8,128)(2,1)} %collective-permute-done.4.far, f32[8,1024]{1,0:T(8,128)S(1)} %bitcast.40, f32[256,128]{1,0:T(8,128)S(1)} %broadcast_in_dim.69.inv_ref, ...), custom_call_target="tpu_custom_call" | custom-call | flops 3221225472 | bytes 12582912 | tf_op jit(solution)/shard_map/projected_part/pallas_call | solution.py:193
  122.6 1.6 copy-done.2
  124.2 0.8 copy-done.8
  125.0 1.9 copy-done.3
  126.9 1.0 copy-done.9
  128.0 12.8 %gated_rows.1.x_ref = bf16[256,1024]{1,0:T(8,128)(2,1)S(1)} custom-call(s32[2]{0:T(128)S(1)} %pad_add_fusion.spot, bf16[256,1024]{1,0:T(8,128)(2,1)} %collective-permute-done.2.near, bf16[256,1024]{1,0:T(8,128)(2,1)S(1)} %copy-done.9, f32[8,1024]{1,0:T(8,128)S(1)} %bitcast.41, f32[256,128]{1,0:T(8,128)S(1)} %broadcast_in_dim.69.inv_ref, ...), custom_call_target="tpu_custom_call" | custom-call | flops 3221225472 | bytes 12582912 | tf_op jit(solution)/shard_map/gated_rows/pallas_call | solution.py:193
  140.8 2.2 %output_share.8 = bf16[256,1024]{1,0:T(8,128)(2,1)S(1)} custom-call(s32[1]{0:T(128)} %bitcast.15.spot, bf16[256,1024]{1,0:T(8,128)(2,1)S(1)} %gated_rows.1.x_ref, bf16[1024,8192]{1,0:T(8,128)(2,1)} %w_ref.23), custom_call_target="tpu_custom_call" | custom-call | flops 536870912 | bytes 2097152 | tf_op jit(solution)/shard_map/output_share/pallas_call | solution.py:233
  142.9 0.6 collective-permute-start.8
  143.6 2.1 %output_share.10 = bf16[256,1024]{1,0:T(8,128)(2,1)S(1)} custom-call(s32[1]{0:T(128)} %bitcast.17.spot, bf16[256,1024]{1,0:T(8,128)(2,1)S(1)} %gated_rows.1.x_ref, bf16[1024,8192]{1,0:T(8,128)(2,1)} %w_ref.23), custom_call_target="tpu_custom_call" | custom-call | flops 536870912 | bytes 2097152 | tf_op jit(solution)/shard_map/output_share/pallas_call | solution.py:233
  145.7 1.5 collective-permute-start.10
  147.3 2.1 %output_share.12 = bf16[256,1024]{1,0:T(8,128)(2,1)S(1)} custom-call(s32[1]{0:T(128)} %bitcast.19.spot, bf16[256,1024]{1,0:T(8,128)(2,1)S(1)} %gated_rows.1.x_ref, bf16[1024,8192]{1,0:T(8,128)(2,1)} %w_ref.23), custom_call_target="tpu_custom_call" | custom-call | flops 536870912 | bytes 2097152 | tf_op jit(solution)/shard_map/output_share/pallas_call | solution.py:233
  149.4 0.6 collective-permute-start.12
  150.0 2.1 %output_share.14 = bf16[256,1024]{1,0:T(8,128)(2,1)S(1)} custom-call(s32[1]{0:T(128)} %bitcast.21.spot, bf16[256,1024]{1,0:T(8,128)(2,1)S(1)} %gated_rows.1.x_ref, bf16[1024,8192]{1,0:T(8,128)(2,1)} %w_ref.23), custom_call_target="tpu_custom_call" | custom-call | flops 536870912 | bytes 2097152 | tf_op jit(solution)/shard_map/output_share/pallas_call | solution.py:233
  152.2 1.5 collective-permute-start.14
  153.7 4.3 %collective-permute-done.8.refs_0_ = bf16[256,1024]{1,0:T(8,128)(2,1)} collective-permute-done((bf16[256,1024]{1,0:T(8,128)(2,1)S(1)}, bf16[256,1024]{1,0:T(8,128)(2,1)}, u32[]{:S(2)}, u32[]{:S(2)}) %collective-permute-start.8) | collective-permute-done | bytes 524320 | tf_op jit(solution)/shard_map/ppermute | solution.py:30
  158.0 2.2 %output_share.9 = bf16[256,1024]{1,0:T(8,128)(2,1)S(1)} custom-call(s32[1]{0:T(128)} %bitcast.spot, bf16[256,1024]{1,0:T(8,128)(2,1)S(1)} %gated_rows.1.x_ref, bf16[1024,8192]{1,0:T(8,128)(2,1)} %w_ref.23, bf16[256,1024]{1,0:T(8,128)(2,1)} %collective-permute-done.8.refs_0_), custom_call_target="tpu_custom_call" | custom-call | flops 536870912 | bytes 2097152 | tf_op jit(solution)/shard_map/output_share/pallas_call | solution.py:233
  160.2 0.6 collective-permute-start.9
  160.8 8.4 %collective-permute-done.10.refs_0_ = bf16[256,1024]{1,0:T(8,128)(2,1)} collective-permute-done((bf16[256,1024]{1,0:T(8,128)(2,1)S(1)}, bf16[256,1024]{1,0:T(8,128)(2,1)}, u32[]{:S(2)}, u32[]{:S(2)}) %collective-permute-start.10) | collective-permute-done | bytes 524320 | tf_op jit(solution)/shard_map/ppermute | solution.py:30
  169.2 2.9 %output_share.11 = bf16[256,1024]{1,0:T(8,128)(2,1)} custom-call(s32[1]{0:T(128)} %bitcast.16.spot, bf16[256,1024]{1,0:T(8,128)(2,1)S(1)} %gated_rows.1.x_ref, bf16[1024,8192]{1,0:T(8,128)(2,1)} %w_ref.23, bf16[256,1024]{1,0:T(8,128)(2,1)} %collective-permute-done.10.refs_0_), custom_call_target="tpu_custom_call" | custom-call | flops 536870912 | bytes 2097152 | tf_op jit(solution)/shard_map/output_share/pallas_call | solution.py:233
  172.1 1.5 collective-permute-start.11
  173.6 6.8 %collective-permute-done.12.refs_0_ = bf16[256,1024]{1,0:T(8,128)(2,1)S(1)} collective-permute-done((bf16[256,1024]{1,0:T(8,128)(2,1)S(1)}, bf16[256,1024]{1,0:T(8,128)(2,1)S(1)}, u32[]{:S(2)}, u32[]{:S(2)}) %collective-permute-start.12) | collective-permute-done | bytes 524320 | tf_op jit(solution)/shard_map/ppermute | solution.py:30
  180.3 2.9 %output_share.13 = bf16[256,1024]{1,0:T(8,128)(2,1)} custom-call(s32[1]{0:T(128)} %bitcast.18.spot, bf16[256,1024]{1,0:T(8,128)(2,1)S(1)} %gated_rows.1.x_ref, bf16[1024,8192]{1,0:T(8,128)(2,1)} %w_ref.23, bf16[256,1024]{1,0:T(8,128)(2,1)S(1)} %collective-permute-done.12.refs_0_), custom_call_target="tpu_custom_call" | custom-call | flops 536870912 | bytes 2097152 | tf_op jit(solution)/shard_map/output_share/pallas_call | solution.py:233
  183.3 0.6 collective-permute-start.13
  183.8 5.1 %collective-permute-done.14.refs_0_ = bf16[256,1024]{1,0:T(8,128)(2,1)} collective-permute-done((bf16[256,1024]{1,0:T(8,128)(2,1)S(1)}, bf16[256,1024]{1,0:T(8,128)(2,1)}, u32[]{:S(2)}, u32[]{:S(2)}) %collective-permute-start.14) | collective-permute-done | bytes 524320 | tf_op jit(solution)/shard_map/ppermute | solution.py:30
  189.0 2.2 %output_share.15 = bf16[256,1024]{1,0:T(8,128)(2,1)S(1)} custom-call(s32[1]{0:T(128)} %bitcast.20.spot, bf16[256,1024]{1,0:T(8,128)(2,1)S(1)} %gated_rows.1.x_ref, bf16[1024,8192]{1,0:T(8,128)(2,1)} %w_ref.23, bf16[256,1024]{1,0:T(8,128)(2,1)} %collective-permute-done.14.refs_0_), custom_call_target="tpu_custom_call" | custom-call | flops 536870912 | bytes 2097152 | tf_op jit(solution)/shard_map/output_share/pallas_call | solution.py:233
  191.2 12.3 %collective-permute-done.11 = bf16[256,1024]{1,0:T(8,128)(2,1)} collective-permute-done((bf16[256,1024]{1,0:T(8,128)(2,1)}, bf16[256,1024]{1,0:T(8,128)(2,1)}, u32[]{:S(2)}, u32[]{:S(2)}) %collective-permute-start.11) | collective-permute-done | bytes 524320 | tf_op jit(solution)/shard_map/ppermute | solution.py:30
  203.5 2.4 %add_convert_fusion = bf16[256,1024]{1,0:T(8,128)(2,1)} fusion(bf16[256,1024]{1,0:T(8,128)(2,1)S(1)} %output_share.15, bf16[256,1024]{1,0:T(8,128)(2,1)S(1)} %collective-permute-done.13, bf16[256,1024]{1,0:T(8,128)(2,1)} %collective-permute-done.11, f32[256,1024]{1,0:T(8,128)S(1)} %copy-done.10, bf16[256,1024]{1,0:T(8,128)(2,1)} %collective-permute-done.9), kind=kLoop, calls=%fused_computation | loop fusion | flops 2359296 | bytes 3670016 | tf_op jit(solution)/shard_map/convert_element_type | solution.py:350
  (40 shorter events, 0.2 us)
Async XLA Ops:
  6.5 2.4 %copy-start = (bf16[512,1024]{1,0:T(8,128)(2,1)S(1)}, bf16[512,1024]{1,0:T(8,128)(2,1)}, u32[]{:S(2)}) copy-start(bf16[512,1024]{1,0:T(8,128)(2,1)} %param.10) | copy-start | bytes 3145732
  6.5 49.9 %all-gather.3.cloned.1.call-start = ((), (), s32[]{:S(2)}) async-start(), calls=%async_computation.2 | async-start | bytes 1179648 | tf_op jit(solution)/shard_map/all_gather | solution.py:258
  10.4 20.6 %collective-permute-start.6 = (bf16[256,1024]{1,0:T(8,128)(2,1)S(1)}, bf16[256,1024]{1,0:T(8,128)(2,1)S(1)}, u32[]{:S(2)}, u32[]{:S(2)}) collective-permute-start(bf16[256,1024]{1,0:T(8,128)(2,1)S(1)} %get-tuple-element.8.near), channel_id=1, source_target_pairs={{0,2},{2,0},{4,6},{6,4},{8,10},{10,8},{12,14},{14,12},{1,3},{3,1},... | collective-permute-start | bytes 1572872 | tf_op jit(solution)/shard_map/ppermute | solution.py:30
  11.9 17.8 %collective-permute-start = (bf16[256,1024]{1,0:T(8,128)(2,1)S(1)}, bf16[256,1024]{1,0:T(8,128)(2,1)S(1)}, u32[]{:S(2)}, u32[]{:S(2)}) collective-permute-start(bf16[256,1024]{1,0:T(8,128)(2,1)S(1)} %get-tuple-element.8.near), channel_id=1, source_target_pairs={{0,4},{2,6},{4,8},{6,10},{8,12},{10,14},{12,0},{14,2},{1,5},{3,7},... | collective-permute-start | bytes 1572872 | tf_op jit(solution)/shard_map/ppermute | solution.py:30
  14.8 14.8 %all-to-all-start = ((f32[8,10,128]{2,1,0:T(8,128)}), f32[8,10,128]{2,1,0:T(8,128)S(1)}, u32[]{:S(2)}, u32[]{:S(2)}) async-start(f32[8,10,128]{2,1,0:T(8,128)} %broadcast_in_dim.68), calls=%async_computation | async-start | bytes 131072 | tf_op jit(solution)/shard_map/all_to_all | solution.py:286
  29.7 13.6 %copy-start.6 = (bf16[256,1024]{1,0:T(8,128)(2,1)}, bf16[256,1024]{1,0:T(8,128)(2,1)S(1)}, u32[]{:S(2)}) copy-start(bf16[256,1024]{1,0:T(8,128)(2,1)S(1)} %collective-permute-done.near) | copy-start | bytes 1572868
  29.7 13.5 %collective-permute-start.5 = (bf16[256,1024]{1,0:T(8,128)(2,1)S(1)}, bf16[256,1024]{1,0:T(8,128)(2,1)S(1)}, u32[]{:S(2)}, u32[]{:S(2)}) collective-permute-start(bf16[256,1024]{1,0:T(8,128)(2,1)S(1)} %collective-permute-done.near), channel_id=1, source_target_pairs={{0,2},{2,0},{4,6},{6,4},{8,10},{10,8},{12,14},{14,12},{1,3},{3,1},... | collective-permute-start | bytes 1572872 | tf_op jit(solution)/shard_map/ppermute | solution.py:30
  43.3 1.0 copy-start.7
  44.3 12.2 %copy-start.11 = (s32[128]{0:T(128)S(1)}, s32[128]{0:T(128)}, u32[]{:S(2)}) copy-start(s32[128]{0:T(128)} %param.16) | copy-start | bytes 1540
  44.3 13.9 %copy-start.12 = (s32[64]{0:T(128)S(1)}, s32[64]{0:T(128)}, u32[]{:S(2)}) copy-start(s32[64]{0:T(128)} %param.17) | copy-start | bytes 772
  56.5 17.1 %collective-permute-start.7 = (bf16[8,512,128]{2,1,0:T(8,128)(2,1)}, bf16[8,512,128]{2,1,0:T(8,128)(2,1)}, u32[]{:S(2)}, u32[]{:S(2)}) collective-permute-start(bf16[8,512,128]{2,1,0:T(8,128)(2,1)} %bitcast.36), channel_id=1, source_target_pairs={{0,1},{1,0},{2,3},{3,2},{4,5},{5,4},{6,7},{7,6},{8,9},{9,8},{10,11... | collective-permute-start | bytes 3145736 | tf_op jit(solution)/shard_map/ppermute | solution.py:322
  56.7 15.1 %collective-permute-start.1 = (bf16[256,1024]{1,0:T(8,128)(2,1)}, bf16[256,1024]{1,0:T(8,128)(2,1)}, u32[]{:S(2)}, u32[]{:S(2)}) collective-permute-start(bf16[256,1024]{1,0:T(8,128)(2,1)} %copy-done.6), channel_id=1, source_target_pairs={{0,4},{2,6},{4,8},{6,10},{8,12},{10,14},{12,0},{14,2},{1,5},{3,7},... | collective-permute-start | bytes 1572872 | tf_op jit(solution)/shard_map/ppermute | solution.py:30
  71.8 36.9 %collective-permute-start.2 = (bf16[256,1024]{1,0:T(8,128)(2,1)}, bf16[256,1024]{1,0:T(8,128)(2,1)}, u32[]{:S(2)}, u32[]{:S(2)}) collective-permute-start(bf16[256,1024]{1,0:T(8,128)(2,1)} %collective-permute-done.1.near), channel_id=1, source_target_pairs={{0,4},{2,6},{4,8},{6,10},{8,12},{10,14},{12,0},{14,2},{1,5},{3,7},... | collective-permute-start | bytes 1572872 | tf_op jit(solution)/shard_map/ppermute | solution.py:30
  72.9 37.3 %collective-permute-start.4 = (bf16[256,1024]{1,0:T(8,128)(2,1)}, bf16[256,1024]{1,0:T(8,128)(2,1)}, u32[]{:S(2)}, u32[]{:S(2)}) collective-permute-start(bf16[256,1024]{1,0:T(8,128)(2,1)} %collective-permute-done.1.near), channel_id=1, source_target_pairs={{0,2},{2,0},{4,6},{6,4},{8,10},{10,8},{12,14},{14,12},{1,3},{3,1},... | collective-permute-start | bytes 1572872 | tf_op jit(solution)/shard_map/ppermute | solution.py:30
  73.7 1.2 copy-start.5
  94.2 0.8 copy-start.4
  95.0 30.0 %all-to-all-start.1 = ((bf16[8,4,8,1024]{3,2,1,0:T(8,128)(2,1)}), bf16[8,4,8,1024]{3,2,1,0:T(8,128)(2,1)}, u32[]{:S(2)}, u32[]{:S(2)}) async-start(bf16[8,4,8,1024]{3,2,1,0:T(8,128)(2,1)} %copy-done.4), calls=%async_computation.1 | async-start | bytes 1048576 | tf_op jit(solution)/shard_map/all_to_all | solution.py:325
  108.7 15.6 %collective-permute-start.3 = (bf16[256,1024]{1,0:T(8,128)(2,1)}, bf16[256,1024]{1,0:T(8,128)(2,1)S(1)}, u32[]{:S(2)}, u32[]{:S(2)}) collective-permute-start(bf16[256,1024]{1,0:T(8,128)(2,1)} %collective-permute-done.2.near), channel_id=1, source_target_pairs={{0,2},{2,0},{4,6},{6,4},{8,10},{10,8},{12,14},{14,12},{1,3},{3,1},... | collective-permute-start | bytes 1572872 | tf_op jit(solution)/shard_map/ppermute | solution.py:30
  122.6 1.6 copy-start.2
  124.2 0.8 copy-start.8
  125.0 1.9 copy-start.3
  126.9 1.0 copy-start.9
  142.9 15.0 %collective-permute-start.8 = (bf16[256,1024]{1,0:T(8,128)(2,1)S(1)}, bf16[256,1024]{1,0:T(8,128)(2,1)}, u32[]{:S(2)}, u32[]{:S(2)}) collective-permute-start(bf16[256,1024]{1,0:T(8,128)(2,1)S(1)} %output_share.8), channel_id=1, source_target_pairs={{0,2},{2,0},{4,6},{6,4},{8,10},{10,8},{12,14},{14,12},{1,3},{3,1},... | collective-permute-start | bytes 1572872 | tf_op jit(solution)/shard_map/ppermute | solution.py:30
  145.7 23.5 %collective-permute-start.10 = (bf16[256,1024]{1,0:T(8,128)(2,1)S(1)}, bf16[256,1024]{1,0:T(8,128)(2,1)}, u32[]{:S(2)}, u32[]{:S(2)}) collective-permute-start(bf16[256,1024]{1,0:T(8,128)(2,1)S(1)} %output_share.10), channel_id=1, source_target_pairs={{0,2},{2,0},{4,6},{6,4},{8,10},{10,8},{12,14},{14,12},{1,3},{3,1},... | collective-permute-start | bytes 1572872 | tf_op jit(solution)/shard_map/ppermute | solution.py:30
  149.4 30.9 %collective-permute-start.12 = (bf16[256,1024]{1,0:T(8,128)(2,1)S(1)}, bf16[256,1024]{1,0:T(8,128)(2,1)S(1)}, u32[]{:S(2)}, u32[]{:S(2)}) collective-permute-start(bf16[256,1024]{1,0:T(8,128)(2,1)S(1)} %output_share.12), channel_id=1, source_target_pairs={{0,2},{2,0},{4,6},{6,4},{8,10},{10,8},{12,14},{14,12},{1,3},{3,1},... | collective-permute-start | bytes 1572872 | tf_op jit(solution)/shard_map/ppermute | solution.py:30
  152.2 36.8 %collective-permute-start.14 = (bf16[256,1024]{1,0:T(8,128)(2,1)S(1)}, bf16[256,1024]{1,0:T(8,128)(2,1)}, u32[]{:S(2)}, u32[]{:S(2)}) collective-permute-start(bf16[256,1024]{1,0:T(8,128)(2,1)S(1)} %output_share.14), channel_id=1, source_target_pairs={{0,2},{2,0},{4,6},{6,4},{8,10},{10,8},{12,14},{14,12},{1,3},{3,1},... | collective-permute-start | bytes 1572872 | tf_op jit(solution)/shard_map/ppermute | solution.py:30
  160.2 31.0 %collective-permute-start.9 = (bf16[256,1024]{1,0:T(8,128)(2,1)S(1)}, bf16[256,1024]{1,0:T(8,128)(2,1)}, u32[]{:S(2)}, u32[]{:S(2)}) collective-permute-start(bf16[256,1024]{1,0:T(8,128)(2,1)S(1)} %output_share.9), channel_id=1, source_target_pairs={{0,8},{2,10},{4,12},{6,14},{8,0},{10,2},{12,4},{14,6},{1,9},{3,11}... | collective-permute-start | bytes 1572872 | tf_op jit(solution)/shard_map/ppermute | solution.py:30
  172.1 31.4 %collective-permute-start.11 = (bf16[256,1024]{1,0:T(8,128)(2,1)}, bf16[256,1024]{1,0:T(8,128)(2,1)}, u32[]{:S(2)}, u32[]{:S(2)}) collective-permute-start(bf16[256,1024]{1,0:T(8,128)(2,1)} %output_share.11), channel_id=1, source_target_pairs={{0,4},{2,6},{4,8},{6,10},{8,12},{10,14},{12,0},{14,2},{1,5},{3,7},... | collective-permute-start | bytes 1572872 | tf_op jit(solution)/shard_map/ppermute | solution.py:30
  180.3 25.6 %copy-start.1 = (bf16[512,1024]{1,0:T(8,128)(2,1)S(1)}, bf16[512,1024]{1,0:T(8,128)(2,1)}, u32[]{:S(2)}) copy-start(bf16[512,1024]{1,0:T(8,128)(2,1)} %param.10) | copy-start | bytes 3145732
  183.3 20.3 %collective-permute-start.13 = (bf16[256,1024]{1,0:T(8,128)(2,1)}, bf16[256,1024]{1,0:T(8,128)(2,1)S(1)}, u32[]{:S(2)}, u32[]{:S(2)}) collective-permute-start(bf16[256,1024]{1,0:T(8,128)(2,1)} %output_share.13), channel_id=1, source_target_pairs={{0,12},{2,14},{4,0},{6,2},{8,4},{10,6},{12,8},{14,10},{1,13},{3,15... | collective-permute-start | bytes 1572872 | tf_op jit(solution)/shard_map/ppermute | solution.py:30
  183.8 19.7 %copy-start.10 = (f32[256,1024]{1,0:T(8,128)S(1)}, f32[256,1024]{1,0:T(8,128)}, u32[]{:S(2)}) copy-start(f32[256,1024]{1,0:T(8,128)} %get-tuple-element.9) | copy-start | bytes 3145732
Sparse Core Ops, SparseCore 0:
  9.5 44.0 all-gather.2

commit v5 on v0

v5 whole, which is shorter than its diff:
```python
import functools

import jax
import jax.numpy as jnp
from jax import lax
from jax.experimental import pallas as pl
from jax.experimental.pallas import tpu as pltpu
from jax.sharding import PartitionSpec as P

D = 8192
EPSILON = 1e-05
LANES = 128
PACKED = 16
INNER = 2
DEPTH = 4
VMEM_LIMIT = 16 * 1024 * 1024
IN_SMEM = pl.BlockSpec(memory_space=pltpu.SMEM)
IN_VMEM = pl.BlockSpec(memory_space=pltpu.VMEM)
IN_HBM = pl.BlockSpec(memory_space=pltpu.HBM)


def moved(array, outer_by, flip):
    owners = lax.axis_size("tensor")
    outer_size = owners // INNER
    pairs = []
    for source in range(owners):
        outer, inner = source // INNER, source % INNER
        pairs.append((source, (outer + outer_by) % outer_size * INNER + (inner ^ flip)))
    return lax.ppermute(array, "tensor", pairs)


def spread(block):
    outer_size = lax.axis_size("tensor") // INNER
    blocks = []
    held = block
    for step in range(outer_size):
        if step:
            held = moved(held, 1, 0)
        blocks.append((held, moved(held, 0, 1)))
    return blocks


def kernel_call(kernel, name, spot, operands, outputs, aliases, scratch, flops, moved_bytes):
    specs, args = zip(*operands)
    args = [
        pltpu.with_memory_space_constraint(arg, pltpu.HBM) if spec is IN_HBM else arg
        for spec, arg in operands
    ]
    out_specs, out_shape = zip(*outputs)
    return pl.pallas_call(
        kernel,
        in_specs=[IN_SMEM, *specs],
        out_specs=list(out_specs),
        out_shape=list(out_shape),
        input_output_aliases=aliases,
        scratch_shapes=scratch,
        compiler_params=pltpu.CompilerParams(vmem_limit_bytes=VMEM_LIMIT),
        cost_estimate=pl.CostEstimate(flops=flops, bytes_accessed=moved_bytes, transcendentals=0),
        name=name,
    )(spot, *args)


def history_kernel(steps, first, spot, lengths_ref, near_ref, far_ref, cache_hbm, *refs):
    terms_ref, held, taps_scr, sems = refs if first else refs[1:]
    if not first:
        terms_ref[...] = refs[0][...]
    _, lags, rows, width = held.shape
    channels = near_ref.shape[1]
    parts = channels // width
    lengths = jnp.concatenate([lengths_ref[...]] * (width // LANES), axis=1)

    def owner_of(flip):
        return spot[0] * INNER + (spot[1] + flip) % INNER

    def fetch(index):
        start = (owner_of(index // parts) * parts + index % parts) * width
        columns = pl.ds(pl.multiple_of(start, width), width)
        return pltpu.make_async_copy(cache_hbm.at[:, :, columns], held.at[index], sems.at[index])

    for index in range(2 * parts):
        fetch(index).start()

    def one_part(index, carry):
        fetch(index).wait()
        flip = index // parts
        at = pl.ds(pl.multiple_of(index % parts * width, width), width)

        @pl.when(flip == 0)
        def _():
            taps_scr[...] = near_ref[pl.ds(0, lags + 1), at].astype(jnp.float32)

        @pl.when(flip == 1)
        def _():
            taps_scr[...] = far_ref[pl.ds(0, lags + 1), at].astype(jnp.float32)

        def tap(lag):
            return jnp.broadcast_to(taps_scr[pl.ds(lag, 1), :], (rows, width))

        taps = [tap(1 + step) for step in range(steps)]
        sums = [jnp.zeros((rows, width), jnp.float32) for _ in range(steps)]
        for lag in range(lags):
            values = jnp.where(lengths > lag, held[index, lag].astype(jnp.float32), 0.0)
            for step in range(min(steps, lags - lag)):
                sums[step] += values * taps[step]
            taps = taps[1:]
            if lag + 1 + steps <= lags:
                taps.append(tap(lag + 1 + steps))
        for step in range(steps):
            terms_ref[owner_of(flip), step, :, at] = sums[step].astype(terms_ref.dtype)
        return carry

    lax.fori_loop(0, 2 * parts, one_part, 0)


def history_terms(cache, near, far, lengths, spot, steps, earlier):
    lags, rows, total = cache.shape
    channels = near.shape[1]
    width = min(4 * LANES, channels)
    count = 2 * channels // width
    operands = [(IN_VMEM, lengths), (IN_VMEM, near), (IN_VMEM, far), (IN_HBM, cache)]
    aliases = {}
    if earlier is not None:
        aliases = {len(operands) + 1: 0}
        operands.append((IN_VMEM, earlier))
    shape = (total // channels, steps, rows, channels)
    return kernel_call(
        functools.partial(history_kernel, steps, earlier is None),
        "history_terms",
        spot,
        operands,
        [(IN_VMEM, jax.ShapeDtypeStruct(shape, jnp.bfloat16))],
        aliases,
        [
            pltpu.VMEM((count, lags, rows, width), jnp.bfloat16),
            pltpu.VMEM((lags + 1, width), jnp.float32),
            pltpu.SemaphoreType.DMA((count,)),
        ],
        2400 * steps * rows * lags * channels // 2,
        4 * rows * lags * channels,
    )[0]


def project_kernel(steps, first, last, gain_at, spot, near, far, near_gain, far_gain, inv_ref, w_hbm, *refs):
    refs = list(refs)
    earlier = None if first else refs.pop(0)
    taps_ref, place_ref, terms_ref = (refs.pop(0) for _ in range(3)) if last else (None,) * 3
    total_ref = refs.pop(0)
    gated_ref = refs.pop(0) if last else None
    normed, held, sems = refs
    rows, channels = near.shape
    slots, depth, block = held.shape
    chunks = 3 * channels // block
    in_rows = pl.ds(pl.multiple_of(spot[0] * depth, depth), depth)

    def fetch(chunk):
        columns = pl.ds(pl.multiple_of(chunk * block, block), block)
        slot = lax.rem(chunk, slots)
        return pltpu.make_async_copy(w_hbm.at[in_rows, columns], held.at[slot], sems.at[slot])

    for chunk in range(min(slots, chunks)):
        fetch(chunk).start()

    scale = inv_ref[:, :1]
    for flip, x_ref, gain_ref in ((0, near, near_gain), (1, far, far_gain)):
        inner = (spot[1] + flip) % INNER
        gain = gain_ref[pl.ds(gain_at, PACKED), :].astype(jnp.float32)[:1]
        normed[:, pl.ds(pl.multiple_of(inner * channels, channels), channels)] = (
            x_ref[...].astype(jnp.float32) * scale * gain
        ).astype(jnp.bfloat16)

    def one_chunk(chunk, carry):
        fetch(chunk).wait()
        columns = pl.ds(pl.multiple_of(chunk * block, block), block)
        term = jnp.dot(
            normed[...], held[lax.rem(chunk, slots)], preferred_element_type=jnp.float32
        )
        if first:
            total_ref[:, columns] = term
        else:
            total_ref[:, columns] = earlier[:, columns] + term

        @pl.when(chunk + slots < chunks)
        def _():
            fetch(chunk + slots).start()

        return carry

    lax.fori_loop(0, chunks, one_chunk, 0)
    if not last:
        return
    seqs = rows // steps

    def one_gate(chunk, carry):
        start = pl.multiple_of(chunk * block, block)
        at = pl.ds(start, block)
        history = jnp.dot(place_ref[...], terms_ref[:, at], preferred_element_type=jnp.float32)
        keys = total_ref[:, pl.ds(pl.multiple_of(channels + start, block), block)]
        values = total_ref[:, pl.ds(pl.multiple_of(2 * channels + start, block), block)]
        recent = (keys * values).astype(jnp.bfloat16).astype(jnp.float32)
        for step in range(steps):
            rows_at = pl.ds(step * seqs, seqs)
            filtered = history[step * seqs : (step + 1) * seqs]
            for back in range(step + 1):
                older = recent[(step - back) * seqs : (step - back + 1) * seqs]
                filtered += taps_ref[pl.ds(back, 1), at] * older
            gated_ref[rows_at, at] = (total_ref[rows_at, at] * filtered).astype(jnp.bfloat16)
        return carry

    lax.fori_loop(0, channels // block, one_gate, 0)


def projected(spot, pair, gains, gain_at, inv_rms, w_in, earlier, ends=None):
    near, far = pair
    rows, channels = near.shape
    block = min(256, channels)
    first, last = earlier is None, ends is not None
    operands = [(IN_VMEM, array) for array in (near, far, *gains, inv_rms)] + [(IN_HBM, w_in)]
    aliases = {}
    if not first:
        aliases = {len(operands) + 1: 0}
        operands.append((IN_VMEM, earlier))
    outputs = [(IN_VMEM, jax.ShapeDtypeStruct((rows, 3 * channels), jnp.float32))]
    steps = 1
    if last:
        steps, *arrays = ends
        operands += [(IN_VMEM, array) for array in arrays]
        outputs.append((IN_VMEM, jax.ShapeDtypeStruct((rows, channels), jnp.bfloat16)))
    return kernel_call(
        functools.partial(project_kernel, steps, first, last, gain_at),
        "gated_rows" if last else "projected_part",
        spot,
        operands,
        outputs,
        aliases,
        [
            pltpu.VMEM((rows, INNER * channels), jnp.bfloat16),
            pltpu.VMEM((DEPTH, INNER * channels, block), jnp.bfloat16),
            pltpu.SemaphoreType.DMA((DEPTH,)),
        ],
        4 * rows * INNER * channels * 3 * channels,
        4 * INNER * channels * 3 * channels,
    )[-1]


def share_kernel(spot, x_ref, w_hbm, *refs):
    *arrived, out_ref, held, sems = refs
    chunks, _, block = held.shape

    def fetch(chunk):
        start = pl.multiple_of((spot[0] * chunks + chunk) * block, block)
        return pltpu.make_async_copy(w_hbm.at[:, pl.ds(start, block)], held.at[chunk], sems.at[chunk])

    for chunk in range(chunks):
        fetch(chunk).start()
    for chunk in range(chunks):
        fetch(chunk).wait()
        columns = pl.ds(chunk * block, block)
        share = jnp.dot(x_ref[...], held[chunk], preferred_element_type=jnp.float32)
        if arrived:
            share += arrived[0][:, columns].astype(jnp.float32)
        out_ref[:, columns] = share.astype(out_ref.dtype)


def output_share(spot, gated, w_out, owners, arrived=None):
    rows, channels = gated.shape
    wide = w_out.shape[1] // owners
    block = min(256, wide)
    operands = [(IN_VMEM, gated), (IN_HBM, w_out)]
    if arrived is not None:
        operands.append((IN_VMEM, arrived))
    return kernel_call(
        share_kernel,
        "output_share",
        spot,
        operands,
        [(IN_VMEM, jax.ShapeDtypeStruct((rows, wide), jnp.bfloat16))],
        {},
        [
            pltpu.VMEM((wide // block, channels, block), jnp.bfloat16),
            pltpu.SemaphoreType.DMA((wide // block,)),
        ],
        2 * rows * channels * wide,
        2 * channels * wide,
    )[0]


def split_sums(values, channels):
    parts = []
    rest = values
    for _ in range(3):
        part = lax.reduce_precision(rest, 8, 7)
        parts.append(part.astype(jnp.bfloat16))
        rest = rest - part
    flat = jnp.concatenate(parts)
    count = -(-flat.shape[0] // channels)
    return jnp.pad(flat, (0, count * channels - flat.shape[0])).reshape(count, channels)


def after(array, earlier):
    return lax.optimization_barrier((array, earlier))[0]


def per_device(token_ids, embed, norm_gain, w_in, filters, w_out, cache_rows, owner, lengths):
    steps, seqs = token_ids.shape
    vocab, channels = embed.shape
    rows = cache_rows.shape[0]
    taps = filters.shape[1]
    tokens = steps * seqs
    owners = lax.axis_size("tensor")
    halves = lax.axis_size("batch")
    mine = lax.axis_index("tensor")
    half = lax.axis_index("batch")
    outer, inner, outer_size = mine // INNER, mine % INNER, owners // INNER

    onehot = token_ids.reshape(-1)[:, None] == jnp.arange(vocab, dtype=jnp.int32)[None, :]
    stream = jnp.dot(onehot.astype(jnp.bfloat16), embed, preferred_element_type=jnp.float32)
    squares = split_sums(jnp.sum(stream * stream, axis=1), channels)
    square_rows = squares.shape[0]
    filler = jnp.zeros((-(taps + 1 + square_rows) % PACKED, channels), jnp.bfloat16)
    small = jnp.concatenate([filters.T, norm_gain[None, :], squares, filler], axis=0)
    smalls = spread(small)
    streams = spread(stream.astype(jnp.bfloat16))

    def spot_at(back):
        return jnp.stack([(outer + back) % outer_size, inner]).astype(jnp.int32)

    owner_grid = owner.reshape(owners, halves, rows)
    arrived = lax.dynamic_index_in_dim(owner_grid, half, 1, keepdims=False) - half * seqs
    seq_index = jnp.arange(seqs, dtype=jnp.int32)
    own = lax.dynamic_index_in_dim(arrived, mine, 0, keepdims=False)
    row_lengths = jnp.sum(jnp.where(own[:, None] == seq_index[None, :], lengths[None, :], 0), axis=1)
    row_lengths = jnp.broadcast_to(row_lengths[:, None], (rows, LANES))
    step_index = jnp.arange(steps, dtype=jnp.int32)
    place = (
        (step_index[:, None, None, None, None] == step_index[None, None, None, :, None])
        & (seq_index[None, :, None, None, None] == arrived[None, None, :, None, :])
    ).reshape(tokens, owners * steps * rows)
    place = place.astype(jnp.bfloat16)

    cache = cache_rows.transpose(1, 0, 2)
    terms = None
    for back, (near, far) in enumerate(smalls):
        if 0 < back < outer_size - 1:
            near = after(near, streams[back][0])
        terms = history_terms(cache, near, far, row_lengths, spot_at(-back), steps, terms)
    terms = lax.all_to_all(terms, "tensor", 0, 0, tiled=True)

    total = 0.0
    for near, far in smalls:
        for block in (near, far):
            flat = block[taps + 1 : taps + 1 + square_rows].reshape(-1)[: 3 * tokens]
            total = total + jnp.sum(flat.astype(jnp.float32).reshape(3, tokens), axis=0)
    inv_rms = lax.rsqrt(total / D + EPSILON)
    inv_rms = jnp.broadcast_to(inv_rms[:, None], (tokens, LANES))

    near_taps = filters[:, : 2 * steps].T.astype(jnp.float32)
    sums = None
    for back in range(outer_size):
        ends = None
        if back == outer_size - 1:
            ends = (steps, near_taps, place, terms.reshape(owners * steps * rows, channels))
        sums = projected(spot_at(-back), streams[back], smalls[back], taps, inv_rms, w_in, sums, ends)
    gated = sums

    def spot_to(ahead, flip):
        return ((outer + ahead) % outer_size * INNER + (inner + flip) % INNER)[None].astype(jnp.int32)

    order = sorted(range(outer_size), key=lambda ahead: (ahead == 0, -min(ahead, outer_size - ahead)))
    across = {
        ahead: moved(output_share(spot_to(ahead, 1), gated, w_out, owners), 0, 1) for ahead in order
    }
    out = stream
    for ahead in order:
        share = output_share(spot_to(ahead, 0), gated, w_out, owners, across[ahead])
        out = out + (moved(share, ahead, 0) if ahead else share).astype(jnp.float32)
    return out.astype(jnp.bfloat16).reshape(steps, seqs, channels)


def solution(mesh):
    in_specs = (
        P(None, ("groups", "batch")),
        P(None, "tensor"),
        P("tensor"),
        P(None, "tensor"),
        P("tensor", None),
        P("tensor", None),
        P(("groups", "tensor", "batch"), None, None),
        P("groups"),
        P(("groups", "batch")),
    )
    out_specs = P(None, ("groups", "batch"), "tensor")
    return jax.shard_map(
        per_device, mesh=mesh, in_specs=in_specs, out_specs=out_specs, check_vma=False
    )
```

time: 877 us -> 184 us (0.21)
  blocking collectives: 369 us -> 0 us
  waiting for transfers between devices: 216 us -> 51.5 us
  matrix products: 154 us -> 1.45 us
  Pallas kernels: 0 us -> 83.2 us
  local copies, waits for them, and re-layouts: 92.9 us -> 12.9 us
  starting transfers between devices: 6.59 us -> 28.5 us
  other arithmetic: 20 us -> 3.64 us
  between operations: 13.9 us -> 0.57 us
    psum x1 -> x0, blocking collectives: 369 us -> none  [project_in(): squares = lax.psum(jnp.sum(stream * stream, axis=1), 'tensor')]
    reduce_scatter x4 -> x0, waiting for transfers between devices: 184 us -> none  [project_out(): lax.psum_scatter(lax.dot_general(w_out, gated_rows, (((0,), (1,)), ((), (...]
    dot_general x13 -> x1, matrix products: 154 us -> 1.45 us  [per_device(): jnp.dot(onehot.astype(jnp.bfloat16), embed, preferred_element_type=jnp.fl...]
    pallas_call x0 -> x16, Pallas kernels: none -> 83.2 us  [kernel_call(): pl.pallas_call(kernel, in_specs=[IN_SMEM, *specs], out_specs=list(out_spe...]
    ppermute x0 -> x21, waiting for transfers between devices: none -> 51.5 us  [moved(): return lax.ppermute(array, 'tensor', pairs)]
    all_gather x4 -> x0, waiting for transfers between devices: 30.4 us -> none  [project_in(): lax.all_gather(normed, 'tensor', axis=1, tiled=True)]
    all_to_all x1 -> x0, local copies, waits for them, and re-layouts: 25.9 us -> none  [per_device(): lax.all_to_all(cache_rows, 'tensor', split_axis=2, concat_axis=0, tiled=T...]
    select_n x1 -> x0, local copies, waits for them, and re-layouts: 23.3 us -> none  [prefill_terms(): jnp.where(in_range[:, :, None], cached, jnp.zeros((), jnp.bfloat16))]
  transfers between devices with their start and end apart: 9 -> 22, of which waited for: 4 -> 11; matrix products, arithmetic and copies ran while one was open for 28% -> 1% of each run, Pallas kernels for 0% -> 39%
where the time goes in v5:
time: 184 us; the launch traced here: 182 us
  Pallas kernels  83.2 us (45%)
  waiting for transfers between devices  51.5 us (28%)
  starting transfers between devices  28.5 us (15%)
  local copies, waits for them, and re-layouts  12.9 us (7%)
  other arithmetic  3.64 us (2%)
    pallas_call x16, Pallas kernels, kernel_call(): pl.pallas_call(kernel, in_specs=[IN_SMEM, *specs], out_specs=list(out_spe...  83.2 us
    ppermute x21, waiting for transfers between devices, moved(): return lax.ppermute(array, 'tensor', pairs)  51.5 us
    ppermute x21, starting transfers between devices, moved(): return lax.ppermute(array, 'tensor', pairs)  22.2 us
    unnamed x63, local copies, waits for them, and re-layouts  11.3 us
    all_to_all x1, starting transfers between devices, per_device(): terms = lax.all_to_all(terms, 'tensor', 0, 0, tiled=True)  6.26 us
  transfers between devices with their start and end apart: 22, of which 11 were waited for; matrix products, arithmetic and copies ran while one was open for 1% of the time, Pallas kernels for 39%

profile of v5, /device:TPU:18, one launch (start us, length us, event | category | flops | bytes accessed | tf_op | source)
XLA Modules:
  0.0 181.8 jit_solution(16468844080027392809)
XLA Ops:
  0.0 0.8 eq.92
  0.9 0.4 copy-done
  1.2 1.5 multiply_reduce_fusion
  2.7 1.2 copy.21
  4.2 1.6 collective-permute-start.8
  5.8 1.6 collective-permute-start.4
  7.4 0.2 collective-permute-start
  7.6 0.5 collective-permute-start.13
  9.4 6.3 %collective-permute-done.4.near_gain.near_ref = bf16[144,1024]{1,0:T(8,128)(2,1)S(1)} collective-permute-done((bf16[144,1024]{1,0:T(8,128)(2,1)S(1)}, bf16[144,1024]{1,0:T(8,128)(2,1)S(1)}, u32[]{:S(2)}, u32[]{:S(2)}) %collective-permute-start.4) | collective-permute-done | bytes 294944 | tf_op jit(solution)/shard_map/ppermute | solution.py:29
  15.9 0.6 collective-permute-start.9
  16.5 1.6 collective-permute-start.5
  18.1 5.8 %history_terms.4.refs_0_ = bf16[8,4,8,1024]{3,2,1,0:T(8,128)(2,1)} custom-call(s32[2]{0:T(128)S(1)} %pad_add_fusion.3.spot, s32[8,128]{1,0:T(8,128)S(1)} %broadcast_in_dim.68.lengths_ref, bf16[144,1024]{1,0:T(8,128)(2,1)S(1)} %maximum_maximum_fusion.near_gain.near_ref, bf16[144,1024]{1,0:T(8,128)(2,1)S(1)} %collective-permute-done.8.far_gain.far_ref, ...), custom_call_target="tpu_custom_call" | custom-call | flops 4993843200 | bytes 4161536 | tf_op jit(solution)/shard_map/history_terms/pallas_call | solution.py:50
  23.9 3.2 %collective-permute-done.near = bf16[256,1024]{1,0:T(8,128)(2,1)} collective-permute-done((bf16[256,1024]{1,0:T(8,128)(2,1)S(1)}, bf16[256,1024]{1,0:T(8,128)(2,1)}, u32[]{:S(2)}, u32[]{:S(2)}) %collective-permute-start) | collective-permute-done | bytes 524320 | tf_op jit(solution)/shard_map/ppermute | solution.py:29
  27.1 1.6 collective-permute-start.1
  28.7 0.5 collective-permute-start.12
  29.2 4.1 %collective-permute-done.5.near_gain.near_ref = bf16[144,1024]{1,0:T(8,128)(2,1)S(1)} collective-permute-done((bf16[144,1024]{1,0:T(8,128)(2,1)S(1)}, bf16[144,1024]{1,0:T(8,128)(2,1)S(1)}, u32[]{:S(2)}, u32[]{:S(2)}) %collective-permute-start.5) | collective-permute-done | bytes 294944 | tf_op jit(solution)/shard_map/ppermute | solution.py:29
  33.3 0.5 collective-permute-start.10
  33.8 1.6 collective-permute-start.6
  35.4 6.3 %history_terms.5.refs_0_ = bf16[8,4,8,1024]{3,2,1,0:T(8,128)(2,1)} custom-call(s32[2]{0:T(128)S(1)} %pad_add_fusion.2.spot, s32[8,128]{1,0:T(8,128)S(1)} %broadcast_in_dim.68.lengths_ref, bf16[144,1024]{1,0:T(8,128)(2,1)S(1)} %collective-permute-done.4.near_gain.near_ref, ...), custom_call_target="tpu_custom_call", output_to_operand_aliasing={{}: (5, {})} | custom-call | flops 4993843200 | bytes 4161536 | tf_op jit(solution)/shard_map/history_terms/pallas_call | solution.py:50
  41.8 7.6 %collective-permute-done.6.near_ref.near_gain = bf16[144,1024]{1,0:T(8,128)(2,1)S(1)} collective-permute-done((bf16[144,1024]{1,0:T(8,128)(2,1)S(1)}, bf16[144,1024]{1,0:T(8,128)(2,1)S(1)}, u32[]{:S(2)}, u32[]{:S(2)}) %collective-permute-start.6) | collective-permute-done | bytes 294944 | tf_op jit(solution)/shard_map/ppermute | solution.py:29
  49.5 0.6 collective-permute-start.7
  50.1 1.5 collective-permute-start.11
  51.6 1.6 collective-permute-start.2
  53.2 6.3 %history_terms.6.refs_0_ = bf16[8,4,8,1024]{3,2,1,0:T(8,128)(2,1)} custom-call(s32[2]{0:T(128)S(1)} %pad_add_fusion.1.spot, s32[8,128]{1,0:T(8,128)S(1)} %broadcast_in_dim.68.lengths_ref, bf16[144,1024]{1,0:T(8,128)(2,1)S(1)} %collective-permute-done.5.near_gain.near_ref, ...), custom_call_target="tpu_custom_call", output_to_operand_aliasing={{}: (5, {})} | custom-call | flops 4993843200 | bytes 4161536 | tf_op jit(solution)/shard_map/history_terms/pallas_call | solution.py:50
  59.5 6.4 %history_terms.7 = bf16[8,4,8,1024]{3,2,1,0:T(8,128)(2,1)} custom-call(s32[2]{0:T(128)S(1)} %pad_add_fusion.spot, s32[8,128]{1,0:T(8,128)S(1)} %broadcast_in_dim.68.lengths_ref, bf16[144,1024]{1,0:T(8,128)(2,1)S(1)} %collective-permute-done.6.near_ref.near_gain, ...), custom_call_target="tpu_custom_call", output_to_operand_aliasing={{}: (5, {})} | custom-call | flops 4993843200 | bytes 4161536 | tf_op jit(solution)/shard_map/history_terms/pallas_call | solution.py:50
  65.9 6.3 %all-to-all-start = ((bf16[8,4,8,1024]{3,2,1,0:T(8,128)(2,1)}), bf16[8,4,8,1024]{3,2,1,0:T(8,128)(2,1)}, u32[]{:S(2)}, u32[]{:S(2)}) async-start(bf16[8,4,8,1024]{3,2,1,0:T(8,128)(2,1)} %history_terms.7), calls=%async_computation | async-start | bytes 1048576 | tf_op jit(solution)/shard_map/all_to_all | solution.py:346
  72.3 0.8 copy-done.9
  73.2 1.0 copy-done.6
  74.2 1.0 copy-done.8
  75.2 1.0 copy-done.10
  76.2 1.0 copy-done.26
  77.2 7.1 %projected_part.3.refs_0_ = f32[256,3072]{1,0:T(8,128)S(1)} custom-call(s32[2]{0:T(128)S(1)} %pad_add_fusion.3.spot, bf16[256,1024]{1,0:T(8,128)(2,1)S(1)} %copy-done.6, bf16[256,1024]{1,0:T(8,128)(2,1)S(1)} %copy-done.10, bf16[144,1024]{1,0:T(8,128)(2,1)S(1)} %copy-done.8, bf16[144,1024]{1,0:T(8,128)(2,1)S(1)} %copy-done.26, ...), custom_call_target="tpu_custom_call" | custom-call | flops 6442450944 | bytes 25165824 | tf_op jit(solution)/shard_map/projected_part/pallas_call | solution.py:50
  84.4 7.8 %projected_part.4.refs_0_ = f32[256,3072]{1,0:T(8,128)S(1)} custom-call(s32[2]{0:T(128)S(1)} %pad_add_fusion.2.spot, bf16[256,1024]{1,0:T(8,128)(2,1)} %collective-permute-done.near, bf16[256,1024]{1,0:T(8,128)(2,1)} %collective-permute-done.12.far, bf16[144,1024]{1,0:T(8,128)(2,1)S(1)} %copy-done.14, ...), custom_call_target="tpu_custom_call", output_to_operand_aliasing={{}: (7, {})} | custom-call | flops 6442450944 | bytes 25165824 | tf_op jit(solution)/shard_map/projected_part/pallas_call | solution.py:50
  92.2 1.5 collective-permute-start.3
  93.8 7.8 %projected_part.5.refs_0_ = f32[256,3072]{1,0:T(8,128)S(1)} custom-call(s32[2]{0:T(128)S(1)} %pad_add_fusion.1.spot, bf16[256,1024]{1,0:T(8,128)(2,1)} %collective-permute-done.1.near, bf16[256,1024]{1,0:T(8,128)(2,1)} %collective-permute-done.11.far, bf16[144,1024]{1,0:T(8,128)(2,1)S(1)} %copy-done.16, ...), custom_call_target="tpu_custom_call", output_to_operand_aliasing={{}: (7, {})} | custom-call | flops 6442450944 | bytes 25165824 | tf_op jit(solution)/shard_map/projected_part/pallas_call | solution.py:50
  101.6 1.5 collective-permute-done.3.far
  103.1 0.8 copy-done.11
  103.9 1.0 copy-done.12
  104.9 1.0 copy-done.18
  105.9 1.0 copy-done.24
  106.8 8.6 %gated_rows.1 = (f32[256,3072]{1,0:T(8,128)S(1)}, bf16[256,1024]{1,0:T(8,128)(2,1)S(1)}) custom-call(s32[2]{0:T(128)S(1)} %pad_add_fusion.spot, bf16[256,1024]{1,0:T(8,128)(2,1)} %collective-permute-done.2.near, bf16[256,1024]{1,0:T(8,128)(2,1)S(1)} %copy-done.12, bf16[144,1024]{1,0:T(8,128)(2,1)S(1)} %copy-done.18, ...), custom_call_target="tpu_custom_call", output_to_operand_aliasing={{0}: (7, {})} | custom-call | flops 6442450944 | bytes 25165824 | tf_op jit(solution)/shard_map/gated_rows/pallas_call | solution.py:50
  115.5 3.0 %output_share.8 = bf16[256,1024]{1,0:T(8,128)(2,1)S(1)} custom-call(s32[1]{0:T(128)} %bitcast.12.spot, bf16[256,1024]{1,0:T(8,128)(2,1)S(1)} %get-tuple-element.10.x_ref, bf16[1024,8192]{1,0:T(8,128)(2,1)} %w_hbm.23), custom_call_target="tpu_custom_call" | custom-call | flops 536870912 | bytes 2097152 | tf_op jit(solution)/shard_map/output_share/pallas_call | solution.py:50
  118.5 1.5 collective-permute-start.14
  120.0 1.0 copy-done.3
  121.0 2.8 %output_share.10 = bf16[256,1024]{1,0:T(8,128)(2,1)S(1)} custom-call(s32[1]{0:T(128)} %bitcast.14.spot, bf16[256,1024]{1,0:T(8,128)(2,1)S(1)} %copy-done.3, bf16[1024,8192]{1,0:T(8,128)(2,1)} %w_hbm.23), custom_call_target="tpu_custom_call" | custom-call | flops 536870912 | bytes 2097152 | tf_op jit(solution)/shard_map/output_share/pallas_call | solution.py:50
  123.9 0.6 collective-permute-start.16
  124.5 2.8 %output_share.12 = bf16[256,1024]{1,0:T(8,128)(2,1)S(1)} custom-call(s32[1]{0:T(128)} %bitcast.16.spot, bf16[256,1024]{1,0:T(8,128)(2,1)S(1)} %copy-done.4, bf16[1024,8192]{1,0:T(8,128)(2,1)} %w_hbm.23), custom_call_target="tpu_custom_call" | custom-call | flops 536870912 | bytes 2097152 | tf_op jit(solution)/shard_map/output_share/pallas_call | solution.py:50
  127.3 1.5 collective-permute-start.18
  128.8 2.8 %output_share.14 = bf16[256,1024]{1,0:T(8,128)(2,1)S(1)} custom-call(s32[1]{0:T(128)} %bitcast.18.spot, bf16[256,1024]{1,0:T(8,128)(2,1)S(1)} %copy-done.4, bf16[1024,8192]{1,0:T(8,128)(2,1)} %w_hbm.23), custom_call_target="tpu_custom_call" | custom-call | flops 536870912 | bytes 2097152 | tf_op jit(solution)/shard_map/output_share/pallas_call | solution.py:50
  131.6 0.6 collective-permute-start.20
  132.2 1.3 collective-permute-done.14.refs_0_
  133.5 3.8 %output_share.9 = bf16[256,1024]{1,0:T(8,128)(2,1)S(1)} custom-call(s32[1]{0:T(128)} %bitcast.spot, bf16[256,1024]{1,0:T(8,128)(2,1)S(1)} %copy-done.4, bf16[1024,8192]{1,0:T(8,128)(2,1)} %w_hbm.23, bf16[256,1024]{1,0:T(8,128)(2,1)} %collective-permute-done.14.refs_0_), custom_call_target="tpu_custom_call" | custom-call | flops 536870912 | bytes 2097152 | tf_op jit(solution)/shard_map/output_share/pallas_call | solution.py:50
  137.3 0.4 collective-permute-start.15
  137.7 7.1 %collective-permute-done.16.refs_0_ = bf16[256,1024]{1,0:T(8,128)(2,1)} collective-permute-done((bf16[256,1024]{1,0:T(8,128)(2,1)S(1)}, bf16[256,1024]{1,0:T(8,128)(2,1)}, u32[]{:S(2)}, u32[]{:S(2)}) %collective-permute-start.16) | collective-permute-done | bytes 524320 | tf_op jit(solution)/shard_map/ppermute | solution.py:29
  144.7 4.6 %output_share.11 = bf16[256,1024]{1,0:T(8,128)(2,1)} custom-call(s32[1]{0:T(128)} %bitcast.13.spot, bf16[256,1024]{1,0:T(8,128)(2,1)S(1)} %copy-done.4, bf16[1024,8192]{1,0:T(8,128)(2,1)} %w_hbm.23, bf16[256,1024]{1,0:T(8,128)(2,1)} %collective-permute-done.16.refs_0_), custom_call_target="tpu_custom_call" | custom-call | flops 536870912 | bytes 2097152 | tf_op jit(solution)/shard_map/output_share/pallas_call | solution.py:50
  149.3 1.5 collective-permute-start.17
  150.9 5.0 %collective-permute-done.18.refs_0_ = bf16[256,1024]{1,0:T(8,128)(2,1)S(1)} collective-permute-done((bf16[256,1024]{1,0:T(8,128)(2,1)S(1)}, bf16[256,1024]{1,0:T(8,128)(2,1)S(1)}, u32[]{:S(2)}, u32[]{:S(2)}) %collective-permute-start.18) | collective-permute-done | bytes 524320 | tf_op jit(solution)/shard_map/ppermute | solution.py:29
  155.9 3.6 %output_share.13 = bf16[256,1024]{1,0:T(8,128)(2,1)} custom-call(s32[1]{0:T(128)} %bitcast.15.spot, bf16[256,1024]{1,0:T(8,128)(2,1)S(1)} %copy-done.4, bf16[1024,8192]{1,0:T(8,128)(2,1)} %w_hbm.23, bf16[256,1024]{1,0:T(8,128)(2,1)S(1)} %collective-permute-done.18.refs_0_), custom_call_target="tpu_custom_call" | custom-call | flops 536870912 | bytes 2097152 | tf_op jit(solution)/shard_map/output_share/pallas_call | solution.py:50
  159.4 0.6 collective-permute-start.19
  160.0 2.0 %collective-permute-done.20.refs_0_ = bf16[256,1024]{1,0:T(8,128)(2,1)} collective-permute-done((bf16[256,1024]{1,0:T(8,128)(2,1)S(1)}, bf16[256,1024]{1,0:T(8,128)(2,1)}, u32[]{:S(2)}, u32[]{:S(2)}) %collective-permute-start.20) | collective-permute-done | bytes 524320 | tf_op jit(solution)/shard_map/ppermute | solution.py:29
  162.0 4.0 %output_share.15 = bf16[256,1024]{1,0:T(8,128)(2,1)S(1)} custom-call(s32[1]{0:T(128)} %bitcast.17.spot, bf16[256,1024]{1,0:T(8,128)(2,1)S(1)} %copy-done.4, bf16[1024,8192]{1,0:T(8,128)(2,1)} %w_hbm.23, bf16[256,1024]{1,0:T(8,128)(2,1)} %collective-permute-done.20.refs_0_), custom_call_target="tpu_custom_call" | custom-call | flops 536870912 | bytes 2097152 | tf_op jit(solution)/shard_map/output_share/pallas_call | solution.py:50
  166.0 1.0 collective-permute-done.15
  166.9 12.4 %collective-permute-done.17 = bf16[256,1024]{1,0:T(8,128)(2,1)} collective-permute-done((bf16[256,1024]{1,0:T(8,128)(2,1)}, bf16[256,1024]{1,0:T(8,128)(2,1)}, u32[]{:S(2)}, u32[]{:S(2)}) %collective-permute-start.17) | collective-permute-done | bytes 524320 | tf_op jit(solution)/shard_map/ppermute | solution.py:29
  179.3 2.4 %add_convert_fusion = bf16[256,1024]{1,0:T(8,128)(2,1)} fusion(bf16[256,1024]{1,0:T(8,128)(2,1)S(1)} %output_share.15, bf16[256,1024]{1,0:T(8,128)(2,1)S(1)} %collective-permute-done.19, bf16[256,1024]{1,0:T(8,128)(2,1)} %collective-permute-done.17, f32[256,1024]{1,0:T(8,128)S(1)} %copy-done.27, bf16[256,1024]{1,0:T(8,128)(2,1)} %collective-permute-done.15), kind=kLoop, calls=%fused_computation | loop fusion | flops 2359296 | bytes 3670016 | tf_op jit(solution)/shard_map/convert_element_type | solution.py:376
  (110 shorter events, 2.1 us)
Async XLA Ops:
  0.0 1.2 copy-start
  0.0 4.0 %copy-start.28 = (bf16[1024]{0:T(1024)(128)(2,1)S(1)}, bf16[1024]{0:T(1024)(128)(2,1)}, u32[]{:S(2)}) copy-start(bf16[1024]{0:T(1024)(128)(2,1)} %param.11) | copy-start | bytes 6148
  0.0 8.1 %copy-start.29 = (s32[128]{0:T(128)S(1)}, s32[128]{0:T(128)}, u32[]{:S(2)}) copy-start(s32[128]{0:T(128)} %param.16) | copy-start | bytes 1540
  0.0 9.1 %copy-start.30 = (s32[64]{0:T(128)S(1)}, s32[64]{0:T(128)}, u32[]{:S(2)}) copy-start(s32[64]{0:T(128)} %param.17) | copy-start | bytes 772
  2.7 21.2 %copy-start.5 = (bf16[256,1024]{1,0:T(8,128)(2,1)}, bf16[256,1024]{1,0:T(8,128)(2,1)S(1)}, u32[]{:S(2)}) copy-start(bf16[256,1024]{1,0:T(8,128)(2,1)S(1)} %get-tuple-element.12.near) | copy-start | bytes 1572868
  4.2 19.6 %copy-start.7 = (bf16[144,1024]{1,0:T(8,128)(2,1)}, bf16[144,1024]{1,0:T(8,128)(2,1)S(1)}, u32[]{:S(2)}) copy-start(bf16[144,1024]{1,0:T(8,128)(2,1)S(1)} %maximum_maximum_fusion.near_gain.near_ref) | copy-start | bytes 884740
  4.2 11.5 %collective-permute-start.8 = (bf16[144,1024]{1,0:T(8,128)(2,1)S(1)}, bf16[144,1024]{1,0:T(8,128)(2,1)S(1)}, u32[]{:S(2)}, u32[]{:S(2)}) collective-permute-start(bf16[144,1024]{1,0:T(8,128)(2,1)S(1)} %maximum_maximum_fusion.near_gain.near_ref), channel_id=1, source_target_pairs={{0,2},{2,0},{4,6},{6,4},{8,10},{10,8},{12,14},{14,12},{1,3},{3,1},... | collective-permute-start | bytes 884744 | tf_op jit(solution)/shard_map/ppermute | solution.py:29
  5.8 9.9 %collective-permute-start.4 = (bf16[144,1024]{1,0:T(8,128)(2,1)S(1)}, bf16[144,1024]{1,0:T(8,128)(2,1)S(1)}, u32[]{:S(2)}, u32[]{:S(2)}) collective-permute-start(bf16[144,1024]{1,0:T(8,128)(2,1)S(1)} %maximum_maximum_fusion.near_gain.near_ref), channel_id=1, source_target_pairs={{0,4},{2,6},{4,8},{6,10},{8,12},{10,14},{12,0},{14,2},{1,5},{3,7},... | collective-permute-start | bytes 884744 | tf_op jit(solution)/shard_map/ppermute | solution.py:29
  7.4 19.7 %collective-permute-start = (bf16[256,1024]{1,0:T(8,128)(2,1)S(1)}, bf16[256,1024]{1,0:T(8,128)(2,1)}, u32[]{:S(2)}, u32[]{:S(2)}) collective-permute-start(bf16[256,1024]{1,0:T(8,128)(2,1)S(1)} %get-tuple-element.12.near), channel_id=1, source_target_pairs={{0,4},{2,6},{4,8},{6,10},{8,12},{10,14},{12,0},{14,2},{1,5},{3,7},... | collective-permute-start | bytes 1572872 | tf_op jit(solution)/shard_map/ppermute | solution.py:29
  7.6 64.6 %collective-permute-start.13 = (bf16[256,1024]{1,0:T(8,128)(2,1)S(1)}, bf16[256,1024]{1,0:T(8,128)(2,1)S(1)}, u32[]{:S(2)}, u32[]{:S(2)}) collective-permute-start(bf16[256,1024]{1,0:T(8,128)(2,1)S(1)} %get-tuple-element.12.near), channel_id=1, source_target_pairs={{0,2},{2,0},{4,6},{6,4},{8,10},{10,8},{12,14},{14,12},{1,3},{3,1},... | collective-permute-start | bytes 1572872 | tf_op jit(solution)/shard_map/ppermute | solution.py:29
  15.8 19.6 %copy-start.13 = (bf16[144,1024]{1,0:T(8,128)(2,1)}, bf16[144,1024]{1,0:T(8,128)(2,1)S(1)}, u32[]{:S(2)}) copy-start(bf16[144,1024]{1,0:T(8,128)(2,1)S(1)} %collective-permute-done.4.near_gain.near_ref) | copy-start | bytes 884740
  15.8 8.1 %copy-start.25 = (bf16[144,1024]{1,0:T(8,128)(2,1)}, bf16[144,1024]{1,0:T(8,128)(2,1)S(1)}, u32[]{:S(2)}) copy-start(bf16[144,1024]{1,0:T(8,128)(2,1)S(1)} %collective-permute-done.8.far_gain.far_ref) | copy-start | bytes 884740
  15.9 17.9 %collective-permute-start.9 = (bf16[144,1024]{1,0:T(8,128)(2,1)S(1)}, bf16[144,1024]{1,0:T(8,128)(2,1)S(1)}, u32[]{:S(2)}, u32[]{:S(2)}) collective-permute-start(bf16[144,1024]{1,0:T(8,128)(2,1)S(1)} %collective-permute-done.4.near_gain.near_ref), channel_id=1, source_target_pairs={{0,2},{2,0},{4,6},{6,4},{8,10},{10,8},{12,14},{14,12},{1,3},{3,1},... | collective-permute-start | bytes 884744 | tf_op jit(solution)/shard_map/ppermute | solution.py:29
  16.5 16.9 %collective-permute-start.5 = (bf16[144,1024]{1,0:T(8,128)(2,1)S(1)}, bf16[144,1024]{1,0:T(8,128)(2,1)S(1)}, u32[]{:S(2)}, u32[]{:S(2)}) collective-permute-start(bf16[144,1024]{1,0:T(8,128)(2,1)S(1)} %collective-permute-done.4.near_gain.near_ref), channel_id=1, source_target_pairs={{0,4},{2,6},{4,8},{6,10},{8,12},{10,14},{12,0},{14,2},{1,5},{3,7},... | collective-permute-start | bytes 884744 | tf_op jit(solution)/shard_map/ppermute | solution.py:29
  27.1 23.0 %collective-permute-start.1 = (bf16[256,1024]{1,0:T(8,128)(2,1)}, bf16[256,1024]{1,0:T(8,128)(2,1)}, u32[]{:S(2)}, u32[]{:S(2)}) collective-permute-start(bf16[256,1024]{1,0:T(8,128)(2,1)} %collective-permute-done.near), channel_id=1, source_target_pairs={{0,4},{2,6},{4,8},{6,10},{8,12},{10,14},{12,0},{14,2},{1,5},{3,7},... | collective-permute-start | bytes 1572872 | tf_op jit(solution)/shard_map/ppermute | solution.py:29
  28.7 55.7 %collective-permute-start.12 = (bf16[256,1024]{1,0:T(8,128)(2,1)}, bf16[256,1024]{1,0:T(8,128)(2,1)}, u32[]{:S(2)}, u32[]{:S(2)}) collective-permute-start(bf16[256,1024]{1,0:T(8,128)(2,1)} %collective-permute-done.near), channel_id=1, source_target_pairs={{0,2},{2,0},{4,6},{6,4},{8,10},{10,8},{12,14},{14,12},{1,3},{3,1},... | collective-permute-start | bytes 1572872 | tf_op jit(solution)/shard_map/ppermute | solution.py:29
  33.3 19.9 %copy-start.15 = (bf16[144,1024]{1,0:T(8,128)(2,1)}, bf16[144,1024]{1,0:T(8,128)(2,1)S(1)}, u32[]{:S(2)}) copy-start(bf16[144,1024]{1,0:T(8,128)(2,1)S(1)} %collective-permute-done.5.near_gain.near_ref) | copy-start | bytes 884740
  33.3 16.1 %collective-permute-start.10 = (bf16[144,1024]{1,0:T(8,128)(2,1)S(1)}, bf16[144,1024]{1,0:T(8,128)(2,1)S(1)}, u32[]{:S(2)}, u32[]{:S(2)}) collective-permute-start(bf16[144,1024]{1,0:T(8,128)(2,1)S(1)} %collective-permute-done.5.near_gain.near_ref), channel_id=1, source_target_pairs={{0,2},{2,0},{4,6},{6,4},{8,10},{10,8},{12,14},{14,12},{1,3},{3,1},... | collective-permute-start | bytes 884744 | tf_op jit(solution)/shard_map/ppermute | solution.py:29
  33.8 7.9 %copy-start.19 = (bf16[144,1024]{1,0:T(8,128)(2,1)}, bf16[144,1024]{1,0:T(8,128)(2,1)S(1)}, u32[]{:S(2)}) copy-start(bf16[144,1024]{1,0:T(8,128)(2,1)S(1)} %collective-permute-done.9.far_gain.far_ref) | copy-start | bytes 884740
  33.8 15.6 %collective-permute-start.6 = (bf16[144,1024]{1,0:T(8,128)(2,1)S(1)}, bf16[144,1024]{1,0:T(8,128)(2,1)S(1)}, u32[]{:S(2)}, u32[]{:S(2)}) collective-permute-start(bf16[144,1024]{1,0:T(8,128)(2,1)S(1)} %collective-permute-done.5.near_gain.near_ref), channel_id=1, source_target_pairs={{0,4},{2,6},{4,8},{6,10},{8,12},{10,14},{12,0},{14,2},{1,5},{3,7},... | collective-permute-start | bytes 884744 | tf_op jit(solution)/shard_map/ppermute | solution.py:29
  49.4 10.1 %copy-start.17 = (bf16[144,1024]{1,0:T(8,128)(2,1)}, bf16[144,1024]{1,0:T(8,128)(2,1)S(1)}, u32[]{:S(2)}) copy-start(bf16[144,1024]{1,0:T(8,128)(2,1)S(1)} %collective-permute-done.6.near_ref.near_gain) | copy-start | bytes 884740
  49.5 10.0 %copy-start.21 = (bf16[144,1024]{1,0:T(8,128)(2,1)}, bf16[144,1024]{1,0:T(8,128)(2,1)S(1)}, u32[]{:S(2)}) copy-start(bf16[144,1024]{1,0:T(8,128)(2,1)S(1)} %collective-permute-done.10.far_gain.far_ref) | copy-start | bytes 884740
  49.5 10.0 %collective-permute-start.7 = (bf16[144,1024]{1,0:T(8,128)(2,1)S(1)}, bf16[144,1024]{1,0:T(8,128)(2,1)S(1)}, u32[]{:S(2)}, u32[]{:S(2)}) collective-permute-start(bf16[144,1024]{1,0:T(8,128)(2,1)S(1)} %collective-permute-done.6.near_ref.near_gain), channel_id=1, source_target_pairs={{0,2},{2,0},{4,6},{6,4},{8,10},{10,8},{12,14},{14,12},{1,3},{3,1},... | collective-permute-start | bytes 884744 | tf_op jit(solution)/shard_map/ppermute | solution.py:29
  50.1 43.7 %collective-permute-start.11 = (bf16[256,1024]{1,0:T(8,128)(2,1)}, bf16[256,1024]{1,0:T(8,128)(2,1)}, u32[]{:S(2)}, u32[]{:S(2)}) collective-permute-start(bf16[256,1024]{1,0:T(8,128)(2,1)} %collective-permute-done.1.near), channel_id=1, source_target_pairs={{0,2},{2,0},{4,6},{6,4},{8,10},{10,8},{12,14},{14,12},{1,3},{3,1},... | collective-permute-start | bytes 1572872 | tf_op jit(solution)/shard_map/ppermute | solution.py:29
  51.6 40.6 %collective-permute-start.2 = (bf16[256,1024]{1,0:T(8,128)(2,1)}, bf16[256,1024]{1,0:T(8,128)(2,1)}, u32[]{:S(2)}, u32[]{:S(2)}) collective-permute-start(bf16[256,1024]{1,0:T(8,128)(2,1)} %collective-permute-done.1.near), channel_id=1, source_target_pairs={{0,4},{2,6},{4,8},{6,10},{8,12},{10,14},{12,0},{14,2},{1,5},{3,7},... | collective-permute-start | bytes 1572872 | tf_op jit(solution)/shard_map/ppermute | solution.py:29
  59.5 12.6 %copy-start.23 = (bf16[144,1024]{1,0:T(8,128)(2,1)}, bf16[144,1024]{1,0:T(8,128)(2,1)S(1)}, u32[]{:S(2)}) copy-start(bf16[144,1024]{1,0:T(8,128)(2,1)S(1)} %collective-permute-done.7.far_ref.far_gain) | copy-start | bytes 884740
  65.9 38.0 %all-to-all-start = ((bf16[8,4,8,1024]{3,2,1,0:T(8,128)(2,1)}), bf16[8,4,8,1024]{3,2,1,0:T(8,128)(2,1)}, u32[]{:S(2)}, u32[]{:S(2)}) async-start(bf16[8,4,8,1024]{3,2,1,0:T(8,128)(2,1)} %history_terms.7), calls=%async_computation | async-start | bytes 1048576 | tf_op jit(solution)/shard_map/all_to_all | solution.py:346
  72.3 0.8 copy-start.9
  73.2 1.0 copy-start.6
  74.2 1.0 copy-start.8
  75.2 1.0 copy-start.10
  76.2 1.0 copy-start.26
  77.2 7.2 %copy-start.14 = (bf16[144,1024]{1,0:T(8,128)(2,1)S(1)}, bf16[144,1024]{1,0:T(8,128)(2,1)}, u32[]{:S(2)}) copy-start(bf16[144,1024]{1,0:T(8,128)(2,1)} %copy-done.13) | copy-start | bytes 884740
  77.2 7.2 %copy-start.20 = (bf16[144,1024]{1,0:T(8,128)(2,1)S(1)}, bf16[144,1024]{1,0:T(8,128)(2,1)}, u32[]{:S(2)}) copy-start(bf16[144,1024]{1,0:T(8,128)(2,1)} %copy-done.19) | copy-start | bytes 884740
  84.3 9.5 %copy-start.16 = (bf16[144,1024]{1,0:T(8,128)(2,1)S(1)}, bf16[144,1024]{1,0:T(8,128)(2,1)}, u32[]{:S(2)}) copy-start(bf16[144,1024]{1,0:T(8,128)(2,1)} %copy-done.15) | copy-start | bytes 884740
  84.3 9.5 %copy-start.22 = (bf16[144,1024]{1,0:T(8,128)(2,1)S(1)}, bf16[144,1024]{1,0:T(8,128)(2,1)}, u32[]{:S(2)}) copy-start(bf16[144,1024]{1,0:T(8,128)(2,1)} %copy-done.21) | copy-start | bytes 884740
  92.2 10.9 %collective-permute-start.3 = (bf16[256,1024]{1,0:T(8,128)(2,1)}, bf16[256,1024]{1,0:T(8,128)(2,1)S(1)}, u32[]{:S(2)}, u32[]{:S(2)}) collective-permute-start(bf16[256,1024]{1,0:T(8,128)(2,1)} %collective-permute-done.2.near), channel_id=1, source_target_pairs={{0,2},{2,0},{4,6},{6,4},{8,10},{10,8},{12,14},{14,12},{1,3},{3,1},... | collective-permute-start | bytes 1572872 | tf_op jit(solution)/shard_map/ppermute | solution.py:29
  103.1 0.8 copy-start.11
  103.9 1.0 copy-start.12
  104.9 1.0 copy-start.18
  105.9 1.0 copy-start.24
  115.5 3.0 %copy-start.2 = (bf16[256,1024]{1,0:T(8,128)(2,1)}, bf16[256,1024]{1,0:T(8,128)(2,1)S(1)}, u32[]{:S(2)}) copy-start(bf16[256,1024]{1,0:T(8,128)(2,1)S(1)} %get-tuple-element.10.x_ref) | copy-start | bytes 1572868
  118.5 15.0 %collective-permute-start.14 = (bf16[256,1024]{1,0:T(8,128)(2,1)S(1)}, bf16[256,1024]{1,0:T(8,128)(2,1)}, u32[]{:S(2)}, u32[]{:S(2)}) collective-permute-start(bf16[256,1024]{1,0:T(8,128)(2,1)S(1)} %output_share.8), channel_id=1, source_target_pairs={{0,2},{2,0},{4,6},{6,4},{8,10},{10,8},{12,14},{14,12},{1,3},{3,1},... | collective-permute-start | bytes 1572872 | tf_op jit(solution)/shard_map/ppermute | solution.py:29
  120.0 1.0 copy-start.3
  121.0 3.4 %copy-start.4 = (bf16[256,1024]{1,0:T(8,128)(2,1)S(1)}, bf16[256,1024]{1,0:T(8,128)(2,1)}, u32[]{:S(2)}) copy-start(bf16[256,1024]{1,0:T(8,128)(2,1)} %copy-done.2) | copy-start | bytes 1572868
  123.9 20.9 %collective-permute-start.16 = (bf16[256,1024]{1,0:T(8,128)(2,1)S(1)}, bf16[256,1024]{1,0:T(8,128)(2,1)}, u32[]{:S(2)}, u32[]{:S(2)}) collective-permute-start(bf16[256,1024]{1,0:T(8,128)(2,1)S(1)} %output_share.10), channel_id=1, source_target_pairs={{0,2},{2,0},{4,6},{6,4},{8,10},{10,8},{12,14},{14,12},{1,3},{3,1},... | collective-permute-start | bytes 1572872 | tf_op jit(solution)/shard_map/ppermute | solution.py:29
  127.3 28.6 %collective-permute-start.18 = (bf16[256,1024]{1,0:T(8,128)(2,1)S(1)}, bf16[256,1024]{1,0:T(8,128)(2,1)S(1)}, u32[]{:S(2)}, u32[]{:S(2)}) collective-permute-start(bf16[256,1024]{1,0:T(8,128)(2,1)S(1)} %output_share.12), channel_id=1, source_target_pairs={{0,2},{2,0},{4,6},{6,4},{8,10},{10,8},{12,14},{14,12},{1,3},{3,1},... | collective-permute-start | bytes 1572872 | tf_op jit(solution)/shard_map/ppermute | solution.py:29
  131.6 30.5 %collective-permute-start.20 = (bf16[256,1024]{1,0:T(8,128)(2,1)S(1)}, bf16[256,1024]{1,0:T(8,128)(2,1)}, u32[]{:S(2)}, u32[]{:S(2)}) collective-permute-start(bf16[256,1024]{1,0:T(8,128)(2,1)S(1)} %output_share.14), channel_id=1, source_target_pairs={{0,2},{2,0},{4,6},{6,4},{8,10},{10,8},{12,14},{14,12},{1,3},{3,1},... | collective-permute-start | bytes 1572872 | tf_op jit(solution)/shard_map/ppermute | solution.py:29
  137.3 29.6 %collective-permute-start.15 = (bf16[256,1024]{1,0:T(8,128)(2,1)S(1)}, bf16[256,1024]{1,0:T(8,128)(2,1)}, u32[]{:S(2)}, u32[]{:S(2)}) collective-permute-start(bf16[256,1024]{1,0:T(8,128)(2,1)S(1)} %output_share.9), channel_id=1, source_target_pairs={{0,8},{2,10},{4,12},{6,14},{8,0},{10,2},{12,4},{14,6},{1,9},{3,11}... | collective-permute-start | bytes 1572872 | tf_op jit(solution)/shard_map/ppermute | solution.py:29
  149.3 30.0 %collective-permute-start.17 = (bf16[256,1024]{1,0:T(8,128)(2,1)}, bf16[256,1024]{1,0:T(8,128)(2,1)}, u32[]{:S(2)}, u32[]{:S(2)}) collective-permute-start(bf16[256,1024]{1,0:T(8,128)(2,1)} %output_share.11), channel_id=1, source_target_pairs={{0,4},{2,6},{4,8},{6,10},{8,12},{10,14},{12,0},{14,2},{1,5},{3,7},... | collective-permute-start | bytes 1572872 | tf_op jit(solution)/shard_map/ppermute | solution.py:29
  159.4 19.9 %collective-permute-start.19 = (bf16[256,1024]{1,0:T(8,128)(2,1)}, bf16[256,1024]{1,0:T(8,128)(2,1)S(1)}, u32[]{:S(2)}, u32[]{:S(2)}) collective-permute-start(bf16[256,1024]{1,0:T(8,128)(2,1)} %output_share.13), channel_id=1, source_target_pairs={{0,12},{2,14},{4,0},{6,2},{8,4},{10,6},{12,8},{14,10},{1,13},{3,15... | collective-permute-start | bytes 1572872 | tf_op jit(solution)/shard_map/ppermute | solution.py:29
  162.0 17.3 %copy-start.27 = (f32[256,1024]{1,0:T(8,128)S(1)}, f32[256,1024]{1,0:T(8,128)}, u32[]{:S(2)}) copy-start(f32[256,1024]{1,0:T(8,128)} %get-tuple-element.18) | copy-start | bytes 3145732
  162.0 19.8 %copy-start.1 = (bf16[512,1024]{1,0:T(8,128)(2,1)S(1)}, bf16[512,1024]{1,0:T(8,128)(2,1)}, u32[]{:S(2)}) copy-start(bf16[512,1024]{1,0:T(8,128)(2,1)} %param.10) | copy-start | bytes 3145732

commit v6 on v5

--- a/solution.py
+++ b/solution.py
@@ -10,13 +10,13 @@
 D = 8192
 EPSILON = 1e-05
 LANES = 128
-PACKED = 16
 INNER = 2
-DEPTH = 4
+DEPTH = 3
 VMEM_LIMIT = 16 * 1024 * 1024
 IN_SMEM = pl.BlockSpec(memory_space=pltpu.SMEM)
 IN_VMEM = pl.BlockSpec(memory_space=pltpu.VMEM)
 IN_HBM = pl.BlockSpec(memory_space=pltpu.HBM)
+ANYWHERE = pl.BlockSpec(memory_space=pl.ANY)
 
 
 def moved(array, outer_by, flip):
@@ -140,14 +140,16 @@
     )[0]
 
 
-def project_kernel(steps, first, last, gain_at, spot, near, far, near_gain, far_gain, inv_ref, w_hbm, *refs):
+def project_kernel(steps, first, last, ahead, spot, near, far, gain_ref, inv_ref, w_hbm, *refs):
     refs = list(refs)
     earlier = None if first else refs.pop(0)
-    taps_ref, place_ref, terms_ref = (refs.pop(0) for _ in range(3)) if last else (None,) * 3
+    taps_ref, place_ref, terms_any = (refs.pop(0) for _ in range(3)) if last else (None,) * 3
+    next_hbm = refs.pop(0) if ahead else None
     total_ref = refs.pop(0)
     gated_ref = refs.pop(0) if last else None
-    normed, held, sems = refs
-    rows, channels = near.shape
+    next_ref = refs.pop(0) if ahead else None
+    blocks, normed, held, sems, block_sems, extra_sem, *terms_scr = refs
+    _, rows, channels = blocks.shape
     slots, depth, block = held.shape
     chunks = 3 * channels // block
     in_rows = pl.ds(pl.multiple_of(spot[0] * depth, depth), depth)
@@ -157,15 +159,28 @@
         slot = lax.rem(chunk, slots)
         return pltpu.make_async_copy(w_hbm.at[in_rows, columns], held.at[slot], sems.at[slot])
 
+    copies = [
+        pltpu.make_async_copy(x_any, blocks.at[flip], block_sems.at[flip])
+        for flip, x_any in enumerate((near, far))
+    ]
+    for copy in copies:
+        copy.start()
     for chunk in range(min(slots, chunks)):
         fetch(chunk).start()
+    if last:
+        extra = pltpu.make_async_copy(terms_any, terms_scr[0], extra_sem.at[0])
+        extra.start()
+    if ahead:
+        extra = pltpu.make_async_copy(next_hbm, next_ref, extra_sem.at[0])
+        extra.start()
 
     scale = inv_ref[:, :1]
-    for flip, x_ref, gain_ref in ((0, near, near_gain), (1, far, far_gain)):
+    for flip, copy in enumerate(copies):
+        copy.wait()
         inner = (spot[1] + flip) % INNER
-        gain = gain_ref[pl.ds(gain_at, PACKED), :].astype(jnp.float32)[:1]
+        gain = gain_ref[pl.ds(spot[0] * INNER + inner, 1), :]
         normed[:, pl.ds(pl.multiple_of(inner * channels, channels), channels)] = (
-            x_ref[...].astype(jnp.float32) * scale * gain
+            blocks[flip].astype(jnp.float32) * scale * gain
         ).astype(jnp.bfloat16)
 
     def one_chunk(chunk, carry):
@@ -174,10 +189,7 @@
         term = jnp.dot(
             normed[...], held[lax.rem(chunk, slots)], preferred_element_type=jnp.float32
         )
-        if first:
-            total_ref[:, columns] = term
-        else:
-            total_ref[:, columns] = earlier[:, columns] + term
+        total_ref[:, columns] = term if first else earlier[:, columns] + term
 
         @pl.when(chunk + slots < chunks)
         def _():
@@ -186,16 +198,19 @@
         return carry
 
     lax.fori_loop(0, chunks, one_chunk, 0)
+    if last or ahead:
+        extra.wait()
     if not last:
         return
     seqs = rows // steps
+    wide = min(256, channels)
 
     def one_gate(chunk, carry):
-        start = pl.multiple_of(chunk * block, block)
-        at = pl.ds(start, block)
-        history = jnp.dot(place_ref[...], terms_ref[:, at], preferred_element_type=jnp.float32)
-        keys = total_ref[:, pl.ds(pl.multiple_of(channels + start, block), block)]
-        values = total_ref[:, pl.ds(pl.multiple_of(2 * channels + start, block), block)]
+        start = pl.multiple_of(chunk * wide, wide)
+        at = pl.ds(start, wide)
+        history = jnp.dot(place_ref[...], terms_scr[0][:, at], preferred_element_type=jnp.float32)
+        keys = total_ref[:, pl.ds(pl.multiple_of(channels + start, wide), wide)]
+        values = total_ref[:, pl.ds(pl.multiple_of(2 * channels + start, wide), wide)]
         recent = (keys * values).astype(jnp.bfloat16).astype(jnp.float32)
         for step in range(steps):
             rows_at = pl.ds(step * seqs, seqs)
@@ -206,68 +221,75 @@
             gated_ref[rows_at, at] = (total_ref[rows_at, at] * filtered).astype(jnp.bfloat16)
         return carry
 
-    lax.fori_loop(0, channels // block, one_gate, 0)
-
-
-def projected(spot, pair, gains, gain_at, inv_rms, w_in, earlier, ends=None):
+    lax.fori_loop(0, channels // wide, one_gate, 0)
+
+
+def projected(spot, pair, gains, inv_rms, w_in, earlier, ends=None, ahead=None):
     near, far = pair
     rows, channels = near.shape
-    block = min(256, channels)
+    block = min(512, channels)
     first, last = earlier is None, ends is not None
-    operands = [(IN_VMEM, array) for array in (near, far, *gains, inv_rms)] + [(IN_HBM, w_in)]
+    operands = [(ANYWHERE, near), (ANYWHERE, far), (IN_VMEM, gains), (IN_VMEM, inv_rms), (IN_HBM, w_in)]
     aliases = {}
     if not first:
         aliases = {len(operands) + 1: 0}
         operands.append((IN_VMEM, earlier))
     outputs = [(IN_VMEM, jax.ShapeDtypeStruct((rows, 3 * channels), jnp.float32))]
+    scratch = [
+        pltpu.VMEM((INNER, rows, channels), jnp.bfloat16),
+        pltpu.VMEM((rows, INNER * channels), jnp.bfloat16),
+        pltpu.VMEM((DEPTH, INNER * channels, block), jnp.bfloat16),
+        pltpu.SemaphoreType.DMA((DEPTH,)),
+        pltpu.SemaphoreType.DMA((INNER,)),
+        pltpu.SemaphoreType.DMA((1,)),
+    ]
     steps = 1
     if last:
-        steps, *arrays = ends
-        operands += [(IN_VMEM, array) for array in arrays]
+        steps, taps, place, terms = ends
+        operands += [(IN_VMEM, taps), (IN_VMEM, place), (ANYWHERE, terms)]
         outputs.append((IN_VMEM, jax.ShapeDtypeStruct((rows, channels), jnp.bfloat16)))
-    return kernel_call(
-        functools.partial(project_kernel, steps, first, last, gain_at),
+        scratch.append(pltpu.VMEM(terms.shape, jnp.bfloat16))
+    if ahead is not None:
+        operands.append((IN_HBM, ahead))
+        outputs.append((IN_VMEM, jax.ShapeDtypeStruct(ahead.shape, ahead.dtype)))
+    out = kernel_call(
+        functools.partial(project_kernel, steps, first, last, ahead is not None),
         "gated_rows" if last else "projected_part",
         spot,
         operands,
         outputs,
         aliases,
-        [
-            pltpu.VMEM((rows, INNER * channels), jnp.bfloat16),
-            pltpu.VMEM((DEPTH, INNER * channels, block), jnp.bfloat16),
-            pltpu.SemaphoreType.DMA((DEPTH,)),
-        ],
+        scratch,
         4 * rows * INNER * channels * 3 * channels,
         4 * INNER * channels * 3 * channels,
-    )[-1]
-
-
-def share_kernel(spot, x_ref, w_hbm, *refs):
-    *arrived, out_ref, held, sems = refs
-    chunks, _, block = held.shape
-
-    def fetch(chunk):
-        start = pl.multiple_of((spot[0] * chunks + chunk) * block, block)
-        return pltpu.make_async_copy(w_hbm.at[:, pl.ds(start, block)], held.at[chunk], sems.at[chunk])
-
-    for chunk in range(chunks):
-        fetch(chunk).start()
-    for chunk in range(chunks):
-        fetch(chunk).wait()
-        columns = pl.ds(chunk * block, block)
-        share = jnp.dot(x_ref[...], held[chunk], preferred_element_type=jnp.float32)
+    )
+    return (out[0], out[1]) if ahead is not None else out[-1]
+
+
+def share_kernel(spot, x_ref, w_ref, *refs):
+    *arrived, out_ref, held, sem = refs
+    wide = out_ref.shape[1]
+    block = min(512, wide)
+    if arrived:
+        copy = pltpu.make_async_copy(arrived[0], held, sem.at[0])
+        copy.start()
+    for start in range(0, wide, block):
+        columns = pl.ds(start, block)
+        in_columns = pl.ds(pl.multiple_of(spot[0] * wide + start, block), block)
+        share = jnp.dot(x_ref[...], w_ref[:, in_columns], preferred_element_type=jnp.float32)
         if arrived:
-            share += arrived[0][:, columns].astype(jnp.float32)
+            if start == 0:
+                copy.wait()
+            share += held[:, columns].astype(jnp.float32)
         out_ref[:, columns] = share.astype(out_ref.dtype)
 
 
 def output_share(spot, gated, w_out, owners, arrived=None):
     rows, channels = gated.shape
     wide = w_out.shape[1] // owners
-    block = min(256, wide)
-    operands = [(IN_VMEM, gated), (IN_HBM, w_out)]
+    operands = [(IN_VMEM, gated), (IN_VMEM, w_out)]
     if arrived is not None:
-        operands.append((IN_VMEM, arrived))
+        operands.append((ANYWHERE, arrived))
     return kernel_call(
         share_kernel,
         "output_share",
@@ -275,25 +297,10 @@
         operands,
         [(IN_VMEM, jax.ShapeDtypeStruct((rows, wide), jnp.bfloat16))],
         {},
-        [
-            pltpu.VMEM((wide // block, channels, block), jnp.bfloat16),
-            pltpu.SemaphoreType.DMA((wide // block,)),
-        ],
+        [pltpu.VMEM((rows, wide), jnp.bfloat16), pltpu.SemaphoreType.DMA((1,))],
         2 * rows * channels * wide,
         2 * channels * wide,
     )[0]
-
-
-def split_sums(values, channels):
-    parts = []
-    rest = values
-    for _ in range(3):
-        part = lax.reduce_precision(rest, 8, 7)
-        parts.append(part.astype(jnp.bfloat16))
-        rest = rest - part
-    flat = jnp.concatenate(parts)
-    count = -(-flat.shape[0] // channels)
-    return jnp.pad(flat, (0, count * channels - flat.shape[0])).reshape(count, channels)
 
 
 def after(array, earlier):
@@ -304,7 +311,6 @@
     steps, seqs = token_ids.shape
     vocab, channels = embed.shape
     rows = cache_rows.shape[0]
-    taps = filters.shape[1]
     tokens = steps * seqs
     owners = lax.axis_size("tensor")
     halves = lax.axis_size("batch")
@@ -314,11 +320,16 @@
 
     onehot = token_ids.reshape(-1)[:, None] == jnp.arange(vocab, dtype=jnp.int32)[None, :]
     stream = jnp.dot(onehot.astype(jnp.bfloat16), embed, preferred_element_type=jnp.float32)
-    squares = split_sums(jnp.sum(stream * stream, axis=1), channels)
-    square_rows = squares.shape[0]
-    filler = jnp.zeros((-(taps + 1 + square_rows) % PACKED, channels), jnp.bfloat16)
-    small = jnp.concatenate([filters.T, norm_gain[None, :], squares, filler], axis=0)
-    smalls = spread(small)
+    tiny = jnp.concatenate([norm_gain.astype(jnp.float32), jnp.sum(stream * stream, axis=1)])
+    tiny = tiny.reshape(-1, LANES)
+    tiny = lax.all_to_all(
+        jnp.broadcast_to(tiny[None], (owners, *tiny.shape)), "tensor", 0, 0, tiled=True
+    )
+    gain_rows = channels // LANES
+    gains = tiny[:, :gain_rows].reshape(owners, channels)
+    inv_rms = lax.rsqrt(jnp.sum(tiny[:, gain_rows:], axis=0).reshape(tokens) / D + EPSILON)
+    inv_rms = jnp.broadcast_to(inv_rms[:, None], (tokens, LANES))
+    lag_taps = spread(filters.T)
     streams = spread(stream.astype(jnp.bfloat16))
 
     def spot_at(back):
@@ -338,29 +349,21 @@
     place = place.astype(jnp.bfloat16)
 
     cache = cache_rows.transpose(1, 0, 2)
-    terms = None
-    for back, (near, far) in enumerate(smalls):
-        if 0 < back < outer_size - 1:
-            near = after(near, streams[back][0])
+    near_taps = filters[:, : 2 * steps].T.astype(jnp.float32)
+    terms = sums = None
+    for back, (near, far) in enumerate(lag_taps):
+        if 0 < back <= outer_size // 2:
+            sums = projected(spot_at(1 - back), streams[back - 1], gains, inv_rms, w_in, sums)
+            near = after(near, sums)
         terms = history_terms(cache, near, far, row_lengths, spot_at(-back), steps, terms)
     terms = lax.all_to_all(terms, "tensor", 0, 0, tiled=True)
-
-    total = 0.0
-    for near, far in smalls:
-        for block in (near, far):
-            flat = block[taps + 1 : taps + 1 + square_rows].reshape(-1)[: 3 * tokens]
-            total = total + jnp.sum(flat.astype(jnp.float32).reshape(3, tokens), axis=0)
-    inv_rms = lax.rsqrt(total / D + EPSILON)
-    inv_rms = jnp.broadcast_to(inv_rms[:, None], (tokens, LANES))
-
-    near_taps = filters[:, : 2 * steps].T.astype(jnp.float32)
-    sums = None
-    for back in range(outer_size):
-        ends = None
-        if back == outer_size - 1:
-            ends = (steps, near_taps, place, terms.reshape(owners * steps * rows, channels))
-        sums = projected(spot_at(-back), streams[back], smalls[back], taps, inv_rms, w_in, sums, ends)
-    gated = sums
+    terms = terms.reshape(owners * steps * rows, channels)
+    for back in range(outer_size // 2, outer_size - 1):
+        ahead = w_out if back == outer_size - 2 else None
+        sums = projected(spot_at(-back), streams[back], gains, inv_rms, w_in, sums, ahead=ahead)
+    sums, w_out = sums
+    ends = (steps, near_taps, place, terms)
+    gated = projected(spot_at(1 - outer_size), streams[-1], gains, inv_rms, w_in, sums, ends)
 
     def spot_to(ahead, flip):
         return ((outer + ahead) % outer_size * INNER + (inner + flip) % INNER)[None].astype(jnp.int32)

time: 184 us -> 198 us (1.076)
  local copies, waits for them, and re-layouts: 12.9 us -> 42.4 us
  Pallas kernels: 83.2 us -> 64 us
  starting transfers between devices: 28.5 us -> 37.3 us
  waiting for transfers between devices: 51.5 us -> 45.5 us
  other arithmetic: 3.64 us -> 5.99 us
    unnamed x63 -> x39, local copies, waits for them, and re-layouts: 11.3 us -> 37.2 us
    pallas_call x16, Pallas kernels: 83.2 us -> 64 us  [kernel_call(): pl.pallas_call(kernel, in_specs=[IN_SMEM, *specs], out_specs=list(out_spe...]
    ppermute x21, waiting for transfers between devices: 51.5 us -> 38.2 us  [moved(): return lax.ppermute(array, 'tensor', pairs)]
    all_to_all x0 -> x1, waiting for transfers between devices: none -> 7.3 us  [per_device(): lax.all_to_all(jnp.broadcast_to(tiny[None], (owners, *tiny.shape)), 'tens...]
    all_to_all x0 -> x1, starting transfers between devices: none -> 6.17 us  [per_device(): lax.all_to_all(jnp.broadcast_to(tiny[None], (owners, *tiny.shape)), 'tens...]
    convert_element_type x2, local copies, waits for them, and re-layouts: 0.31 us -> 2.84 us  [per_device(): place = place.astype(jnp.bfloat16)]
    ppermute x21, starting transfers between devices: 22.2 us -> 24.6 us  [moved(): return lax.ppermute(array, 'tensor', pairs)]
  transfers between devices with their start and end apart: 22 -> 23, of which waited for: 11 -> 6; matrix products, arithmetic and copies ran while one was open for 1% -> 5% of each run, Pallas kernels for 39% -> 28%
where the time goes in v6:
time: 198 us; the launch traced here: 197 us
  Pallas kernels  64 us (32%)
  waiting for transfers between devices  45.5 us (23%)
  local copies, waits for them, and re-layouts  42.4 us (21%)
  starting transfers between devices  37.3 us (19%)
  other arithmetic  5.99 us (3%)
    pallas_call x16, Pallas kernels, kernel_call(): pl.pallas_call(kernel, in_specs=[IN_SMEM, *specs], out_specs=list(out_spe...  64 us
    ppermute x21, waiting for transfers between devices, moved(): return lax.ppermute(array, 'tensor', pairs)  38.2 us
    unnamed x39, local copies, waits for them, and re-layouts  37.2 us
    ppermute x21, starting transfers between devices, moved(): return lax.ppermute(array, 'tensor', pairs)  24.6 us
    all_to_all x1, waiting for transfers between devices, per_device(): lax.all_to_all(jnp.broadcast_to(tiny[None], (owners, *tiny.shape)), 'tens...  7.3 us
    all_to_all x1, starting transfers between devices, per_device(): terms = lax.all_to_all(terms, 'tensor', 0, 0, tiled=True)  6.51 us
    all_to_all x1, starting transfers between devices, per_device(): lax.all_to_all(jnp.broadcast_to(tiny[None], (owners, *tiny.shape)), 'tens...  6.17 us
  transfers between devices with their start and end apart: 23, of which 6 were waited for; matrix products, arithmetic and copies ran while one was open for 5% of the time, Pallas kernels for 28%

profile of v6, /device:TPU:18, one launch (start us, length us, event | category | flops | bytes accessed | tf_op | source)
XLA Modules:
  0.0 197.0 jit_solution(7227027532320458922)
XLA Ops:
  0.0 0.8 eq.92
  1.2 1.5 multiply_reduce_fusion
  2.7 1.5 collective-permute-start.6
  4.2 1.6 collective-permute-start
  5.8 1.1 copy.24
  7.7 0.7 convert_element_type.33
  8.4 0.6 broadcast_in_dim.65
  9.0 6.2 %all-to-all-start = ((f32[8,10,128]{2,1,0:T(8,128)}), f32[8,10,128]{2,1,0:T(8,128)S(1)}, u32[]{:S(2)}, u32[]{:S(2)}) async-start(f32[8,10,128]{2,1,0:T(8,128)} %broadcast_in_dim.65), calls=%async_computation | async-start | bytes 131072 | tf_op jit(solution)/shard_map/all_to_all | solution.py:325
  15.4 0.7 reshape.69
  16.3 0.8 select_reduce_fusion
  17.2 7.3 %all-to-all-done = f32[8,10,128]{2,1,0:T(8,128)S(1)} async-done(((f32[8,10,128]{2,1,0:T(8,128)}), f32[8,10,128]{2,1,0:T(8,128)S(1)}, u32[]{:S(2)}, u32[]{:S(2)}) %all-to-all-start) | async-done | bytes 40992 | tf_op jit(solution)/shard_map/all_to_all | solution.py:325
  24.5 1.7 collective-permute-start.8
  26.2 1.4 collective-permute-start.12
  27.6 4.9 %history_terms.4.refs_0_ = bf16[8,4,8,1024]{3,2,1,0:T(8,128)(2,1)S(1)} custom-call(s32[2]{0:T(128)S(1)} %pad_add_fusion.3.spot, s32[8,128]{1,0:T(8,128)S(1)} %broadcast_in_dim.69.lengths_ref, bf16[128,1024]{1,0:T(8,128)(2,1)S(1)} %bitcast.40, bf16[128,1024]{1,0:T(8,128)(2,1)S(1)} %collective-permute-done.13.far_ref, bf16[127,8,8192]{2,1,0:T(8,128)(2,1)} %bitcast.42), custom_call_target="tpu_custom_call" | custom-call | flops 4993843200 | bytes 4161536 | tf_op jit(solution)/shard_map/history_terms/pallas_call | solution.py:50
  32.6 0.7 collective-permute-start.5
  33.3 0.8 copy-done.13
  34.3 1.0 copy-done.12
  35.3 1.0 copy-done.14
  36.3 6.7 %projected_part.3.refs_0_ = f32[256,3072]{1,0:T(8,128)S(1)} custom-call(s32[2]{0:T(128)S(1)} %pad_add_fusion.3.spot, bf16[256,1024]{1,0:T(8,128)(2,1)S(1)} %copy-done.12, bf16[256,1024]{1,0:T(8,128)(2,1)S(1)} %copy-done.14, f32[8,1024]{1,0:T(8,128)S(1)} %bitcast.34, f32[256,128]{1,0:T(8,128)S(1)} %broadcast_in_dim.66.inv_ref, bf16[8192,3072]{1,0:T(8,128)(2,1)} %w_hbm.7), custom_call_target="tpu_custom_call" | custom-call | flops 6442450944 | bytes 25165824 | tf_op jit(solution)/shard_map/projected_part/pallas_call | solution.py:50
  43.0 2.2 %collective-permute-start.1 = (bf16[256,1024]{1,0:T(8,128)(2,1)}, bf16[256,1024]{1,0:T(8,128)(2,1)}, u32[]{:S(2)}, u32[]{:S(2)}) collective-permute-start(bf16[256,1024]{1,0:T(8,128)(2,1)} %collective-permute-done.near), channel_id=1, source_target_pairs={{0,4},{2,6},{4,8},{6,10},{8,12},{10,14},{12,0},{14,2},{1,5},{3,7},... | collective-permute-start | bytes 1572872 | tf_op jit(solution)/shard_map/ppermute | solution.py:29
  45.3 1.4 collective-permute-start.11
  46.9 5.4 %history_terms.5.refs_0_ = bf16[8,4,8,1024]{3,2,1,0:T(8,128)(2,1)S(1)} custom-call(s32[2]{0:T(128)S(1)} %pad_add_fusion.2.spot, s32[8,128]{1,0:T(8,128)S(1)} %broadcast_in_dim.69.lengths_ref, bf16[128,1024]{1,0:T(8,128)(2,1)} %collective-permute-done.7.near_ref, ...), custom_call_target="tpu_custom_call", output_to_operand_aliasing={{}: (5, {})} | custom-call | flops 4993843200 | bytes 4161536 | tf_op jit(solution)/shard_map/history_terms/pallas_call | solution.py:50
  52.3 9.0 %collective-permute-done.9.near_ref = bf16[128,1024]{1,0:T(8,128)(2,1)S(1)} collective-permute-done((bf16[128,1024]{1,0:T(8,128)(2,1)S(1)}, bf16[128,1024]{1,0:T(8,128)(2,1)S(1)}, u32[]{:S(2)}, u32[]{:S(2)}) %collective-permute-start.9) | collective-permute-done | bytes 262176 | tf_op jit(solution)/shard_map/ppermute | solution.py:29
  61.3 1.3 collective-permute-start.10
  62.6 6.8 %projected_part.4.refs_0_ = f32[256,3072]{1,0:T(8,128)S(1)} custom-call(s32[2]{0:T(128)S(1)} %pad_add_fusion.2.spot, bf16[256,1024]{1,0:T(8,128)(2,1)} %collective-permute-done.near, bf16[256,1024]{1,0:T(8,128)(2,1)S(1)} %collective-permute-done.5.far, f32[8,1024]{1,0:T(8,128)S(1)} %bitcast.35, ...), custom_call_target="tpu_custom_call", output_to_operand_aliasing={{}: (6, {})} | custom-call | flops 6442450944 | bytes 25165824 | tf_op jit(solution)/shard_map/projected_part/pallas_call | solution.py:50
  69.4 0.8 collective-permute-start.4
  70.2 2.5 %collective-permute-start.2 = (bf16[256,1024]{1,0:T(8,128)(2,1)}, bf16[256,1024]{1,0:T(8,128)(2,1)}, u32[]{:S(2)}, u32[]{:S(2)}) collective-permute-start(bf16[256,1024]{1,0:T(8,128)(2,1)} %collective-permute-done.1.near), channel_id=1, source_target_pairs={{0,4},{2,6},{4,8},{6,10},{8,12},{10,14},{12,0},{14,2},{1,5},{3,7},... | collective-permute-start | bytes 1572872 | tf_op jit(solution)/shard_map/ppermute | solution.py:29
  72.7 5.0 %history_terms.6.refs_0_ = bf16[8,4,8,1024]{3,2,1,0:T(8,128)(2,1)S(1)} custom-call(s32[2]{0:T(128)S(1)} %pad_add_fusion.1.spot, s32[8,128]{1,0:T(8,128)S(1)} %broadcast_in_dim.69.lengths_ref, bf16[128,1024]{1,0:T(8,128)(2,1)S(1)} %collective-permute-done.8.near_ref, ...), custom_call_target="tpu_custom_call", output_to_operand_aliasing={{}: (5, {})} | custom-call | flops 4993843200 | bytes 4161536 | tf_op jit(solution)/shard_map/history_terms/pallas_call | solution.py:50
  77.7 5.0 %history_terms.7 = bf16[8,4,8,1024]{3,2,1,0:T(8,128)(2,1)S(1)} custom-call(s32[2]{0:T(128)S(1)} %pad_add_fusion.spot, s32[8,128]{1,0:T(8,128)S(1)} %broadcast_in_dim.69.lengths_ref, bf16[128,1024]{1,0:T(8,128)(2,1)S(1)} %collective-permute-done.9.near_ref, bf16[128,1024]{1,0:T(8,128)(2,1)S(1)} %collective-permute-done.10.far_ref, ...), custom_call_target="tpu_custom_call", output_to_operand_aliasing={{}: (5, {})} | custom-call | flops 4993843200 | bytes 4161536 | tf_op jit(solution)/shard_map/history_terms/pallas_call | solution.py:50
  82.6 0.8 copy-done.15
  83.4 6.5 %all-to-all-start.1 = ((bf16[8,4,8,1024]{3,2,1,0:T(8,128)(2,1)}), bf16[8,4,8,1024]{3,2,1,0:T(8,128)(2,1)}, u32[]{:S(2)}, u32[]{:S(2)}) async-start(bf16[8,4,8,1024]{3,2,1,0:T(8,128)(2,1)} %copy-done.15), calls=%async_computation.1 | async-start | bytes 1048576 | tf_op jit(solution)/shard_map/all_to_all | solution.py:359
  89.9 0.9 and_convert_fusion
  90.8 1.8 reshape.72
  92.6 1.0 copy.26.refs_2_
  93.7 0.7 convert_bitcast_fusion.refs_1_
  94.4 1.5 collective-permute-start.3
  95.9 11.5 %projected_part.5 = (f32[256,3072]{1,0:T(8,128)S(1)}, bf16[1024,8192]{1,0:T(8,128)(2,1)S(1)}) custom-call(s32[2]{0:T(128)S(1)} %pad_add_fusion.1.spot, bf16[256,1024]{1,0:T(8,128)(2,1)} %collective-permute-done.1.near, bf16[256,1024]{1,0:T(8,128)(2,1)} %collective-permute-done.4.far, f32[8,1024]{1,0:T(8,128)S(1)} %bitcast.36, ...), custom_call_target="tpu_custom_call", output_to_operand_aliasing={{0}: (6, {})} | custom-call | flops 6442450944 | bytes 25165824 | tf_op jit(solution)/shard_map/projected_part/pallas_call | solution.py:50
  107.4 5.7 %copy-done.2 = bf16[1024,8192]{1,0:T(8,128)(2,1)} copy-done((bf16[1024,8192]{1,0:T(8,128)(2,1)}, bf16[1024,8192]{1,0:T(8,128)(2,1)S(1)}, u32[]{:S(2)}) %copy-start.2) | copy-done | bytes 16777240
  113.2 8.0 %gated_rows.1 = (f32[256,3072]{1,0:T(8,128)S(1)}, bf16[256,1024]{1,0:T(8,128)(2,1)S(1)}) custom-call(s32[2]{0:T(128)S(1)} %pad_add_fusion.spot, bf16[256,1024]{1,0:T(8,128)(2,1)} %collective-permute-done.2.near, bf16[256,1024]{1,0:T(8,128)(2,1)} %collective-permute-done.3.far, f32[8,1024]{1,0:T(8,128)S(1)} %bitcast.37, ...), custom_call_target="tpu_custom_call", output_to_operand_aliasing={{0}: (6, {})} | custom-call | flops 6442450944 | bytes 25165824 | tf_op jit(solution)/shard_map/gated_rows/pallas_call | solution.py:50
  121.2 2.2 %copy-done.3 = bf16[1024,8192]{1,0:T(8,128)(2,1)S(1)} copy-done((bf16[1024,8192]{1,0:T(8,128)(2,1)S(1)}, bf16[1024,8192]{1,0:T(8,128)(2,1)}, u32[]{:S(2)}) %copy-start.3) | copy-done | bytes 16777240
  123.4 0.7 output_share.8
  124.1 0.6 collective-permute-start.14
  124.7 5.8 %copy-done.4 = bf16[1024,8192]{1,0:T(8,128)(2,1)S(1)} copy-done((bf16[1024,8192]{1,0:T(8,128)(2,1)S(1)}, bf16[1024,8192]{1,0:T(8,128)(2,1)}, u32[]{:S(2)}) %copy-start.4) | copy-done | bytes 16777240
  130.5 1.0 copy-done.9
  131.6 0.7 output_share.10
  132.3 1.5 collective-permute-start.16
  133.8 5.8 %copy-done.5 = bf16[1024,8192]{1,0:T(8,128)(2,1)S(1)} copy-done((bf16[1024,8192]{1,0:T(8,128)(2,1)S(1)}, bf16[1024,8192]{1,0:T(8,128)(2,1)}, u32[]{:S(2)}) %copy-start.5) | copy-done | bytes 16777240
  139.6 0.7 output_share.12
  140.3 0.6 collective-permute-start.18
  141.0 5.8 %copy-done.6 = bf16[1024,8192]{1,0:T(8,128)(2,1)S(1)} copy-done((bf16[1024,8192]{1,0:T(8,128)(2,1)S(1)}, bf16[1024,8192]{1,0:T(8,128)(2,1)}, u32[]{:S(2)}) %copy-start.6) | copy-done | bytes 16777240
  146.7 0.7 output_share.14
  147.5 1.5 collective-permute-start.20
  149.0 1.8 output_share.9
  150.8 0.6 collective-permute-start.15
  151.4 2.6 %output_share.11 = bf16[256,1024]{1,0:T(8,128)(2,1)} custom-call(s32[1]{0:T(128)} %bitcast.15.spot, bf16[256,1024]{1,0:T(8,128)(2,1)S(1)} %copy-done.10, bf16[1024,8192]{1,0:T(8,128)(2,1)S(1)} %copy-done.6, bf16[256,1024]{1,0:T(8,128)(2,1)} %collective-permute-done.16.refs_0_), custom_call_target="tpu_custom_call" | custom-call | flops 536870912 | bytes 2097152 | tf_op jit(solution)/shard_map/output_share/pallas_call | solution.py:50
  154.0 1.5 collective-permute-start.17
  155.5 4.5 %collective-permute-done.18.refs_0_ = bf16[256,1024]{1,0:T(8,128)(2,1)S(1)} collective-permute-done((bf16[256,1024]{1,0:T(8,128)(2,1)S(1)}, bf16[256,1024]{1,0:T(8,128)(2,1)S(1)}, u32[]{:S(2)}, u32[]{:S(2)}) %collective-permute-start.18) | collective-permute-done | bytes 524320 | tf_op jit(solution)/shard_map/ppermute | solution.py:29
  160.0 1.7 output_share.13
  162.3 5.8 %collective-permute-done.20.refs_0_ = bf16[256,1024]{1,0:T(8,128)(2,1)} collective-permute-done((bf16[256,1024]{1,0:T(8,128)(2,1)S(1)}, bf16[256,1024]{1,0:T(8,128)(2,1)}, u32[]{:S(2)}, u32[]{:S(2)}) %collective-permute-start.20) | collective-permute-done | bytes 524320 | tf_op jit(solution)/shard_map/ppermute | solution.py:29
  168.1 5.8 %copy-done.7 = bf16[1024,8192]{1,0:T(8,128)(2,1)S(1)} copy-done((bf16[1024,8192]{1,0:T(8,128)(2,1)S(1)}, bf16[1024,8192]{1,0:T(8,128)(2,1)}, u32[]{:S(2)}) %copy-start.7) | copy-done | bytes 16777240
  173.9 1.9 output_share.15
  175.7 5.8 %collective-permute-done.15 = bf16[256,1024]{1,0:T(8,128)(2,1)} collective-permute-done((bf16[256,1024]{1,0:T(8,128)(2,1)S(1)}, bf16[256,1024]{1,0:T(8,128)(2,1)}, u32[]{:S(2)}, u32[]{:S(2)}) %collective-permute-start.15) | collective-permute-done | bytes 524320 | tf_op jit(solution)/shard_map/ppermute | solution.py:29
  181.5 13.1 %collective-permute-done.17 = bf16[256,1024]{1,0:T(8,128)(2,1)} collective-permute-done((bf16[256,1024]{1,0:T(8,128)(2,1)}, bf16[256,1024]{1,0:T(8,128)(2,1)}, u32[]{:S(2)}, u32[]{:S(2)}) %collective-permute-start.17) | collective-permute-done | bytes 524320 | tf_op jit(solution)/shard_map/ppermute | solution.py:29
  194.6 2.4 %add_convert_fusion = bf16[256,1024]{1,0:T(8,128)(2,1)} fusion(bf16[256,1024]{1,0:T(8,128)(2,1)S(1)} %output_share.15, bf16[256,1024]{1,0:T(8,128)(2,1)S(1)} %collective-permute-done.19, bf16[256,1024]{1,0:T(8,128)(2,1)} %collective-permute-done.17, f32[256,1024]{1,0:T(8,128)S(1)} %copy-done.17, bf16[256,1024]{1,0:T(8,128)(2,1)} %collective-permute-done.15), kind=kLoop, calls=%fused_computation | loop fusion | flops 2359296 | bytes 3670016 | tf_op jit(solution)/shard_map/convert_element_type | solution.py:379
  (61 shorter events, 2.7 us)
Async XLA Ops:
  0.0 1.2 copy-start
  2.7 31.5 %copy-start.11 = (bf16[256,1024]{1,0:T(8,128)(2,1)}, bf16[256,1024]{1,0:T(8,128)(2,1)S(1)}, u32[]{:S(2)}) copy-start(bf16[256,1024]{1,0:T(8,128)(2,1)S(1)} %get-tuple-element.16.near) | copy-start | bytes 1572868
  2.7 30.6 %collective-permute-start.6 = (bf16[256,1024]{1,0:T(8,128)(2,1)S(1)}, bf16[256,1024]{1,0:T(8,128)(2,1)S(1)}, u32[]{:S(2)}, u32[]{:S(2)}) collective-permute-start(bf16[256,1024]{1,0:T(8,128)(2,1)S(1)} %get-tuple-element.16.near), channel_id=1, source_target_pairs={{0,2},{2,0},{4,6},{6,4},{8,10},{10,8},{12,14},{14,12},{1,3},{3,1},... | collective-permute-start | bytes 1572872 | tf_op jit(solution)/shard_map/ppermute | solution.py:29
  4.2 28.4 %collective-permute-start = (bf16[256,1024]{1,0:T(8,128)(2,1)S(1)}, bf16[256,1024]{1,0:T(8,128)(2,1)}, u32[]{:S(2)}, u32[]{:S(2)}) collective-permute-start(bf16[256,1024]{1,0:T(8,128)(2,1)S(1)} %get-tuple-element.16.near), channel_id=1, source_target_pairs={{0,4},{2,6},{4,8},{6,10},{8,12},{10,14},{12,0},{14,2},{1,5},{3,7},... | collective-permute-start | bytes 1572872 | tf_op jit(solution)/shard_map/ppermute | solution.py:29
  6.9 27.4 %copy-start.16 = (bf16[1024,128]{0,1:T(8,128)(2,1)}, bf16[1024,128]{0,1:T(8,128)(2,1)S(1)}, u32[]{:S(2)}) copy-start(bf16[1024,128]{0,1:T(8,128)(2,1)S(1)} %copy.24) | copy-start | bytes 786436
  6.9 17.6 %collective-permute-start.7 = (bf16[128,1024]{1,0:T(8,128)(2,1)S(1)}, bf16[128,1024]{1,0:T(8,128)(2,1)}, u32[]{:S(2)}, u32[]{:S(2)}) collective-permute-start(bf16[128,1024]{1,0:T(8,128)(2,1)S(1)} %bitcast.38), channel_id=1, source_target_pairs={{0,4},{2,6},{4,8},{6,10},{8,12},{10,14},{12,0},{14,2},{1,5},{3,7},... | collective-permute-start | bytes 786440 | tf_op jit(solution)/shard_map/ppermute | solution.py:29
  7.2 20.4 %collective-permute-start.13 = (bf16[128,1024]{1,0:T(8,128)(2,1)S(1)}, bf16[128,1024]{1,0:T(8,128)(2,1)S(1)}, u32[]{:S(2)}, u32[]{:S(2)}) collective-permute-start(bf16[128,1024]{1,0:T(8,128)(2,1)S(1)} %bitcast.39), channel_id=1, source_target_pairs={{0,2},{2,0},{4,6},{6,4},{8,10},{10,8},{12,14},{14,12},{1,3},{3,1},... | collective-permute-start | bytes 786440 | tf_op jit(solution)/shard_map/ppermute | solution.py:29
  9.0 15.5 %all-to-all-start = ((f32[8,10,128]{2,1,0:T(8,128)}), f32[8,10,128]{2,1,0:T(8,128)S(1)}, u32[]{:S(2)}, u32[]{:S(2)}) async-start(f32[8,10,128]{2,1,0:T(8,128)} %broadcast_in_dim.65), calls=%async_computation | async-start | bytes 131072 | tf_op jit(solution)/shard_map/all_to_all | solution.py:325
  24.5 20.7 %collective-permute-start.8 = (bf16[128,1024]{1,0:T(8,128)(2,1)}, bf16[128,1024]{1,0:T(8,128)(2,1)S(1)}, u32[]{:S(2)}, u32[]{:S(2)}) collective-permute-start(bf16[128,1024]{1,0:T(8,128)(2,1)} %collective-permute-done.7.near_ref), channel_id=1, source_target_pairs={{0,4},{2,6},{4,8},{6,10},{8,12},{10,14},{12,0},{14,2},{1,5},{3,7},... | collective-permute-start | bytes 786440 | tf_op jit(solution)/shard_map/ppermute | solution.py:29
  26.2 20.7 %collective-permute-start.12 = (bf16[128,1024]{1,0:T(8,128)(2,1)}, bf16[128,1024]{1,0:T(8,128)(2,1)S(1)}, u32[]{:S(2)}, u32[]{:S(2)}) collective-permute-start(bf16[128,1024]{1,0:T(8,128)(2,1)} %collective-permute-done.7.near_ref), channel_id=1, source_target_pairs={{0,2},{2,0},{4,6},{6,4},{8,10},{10,8},{12,14},{14,12},{1,3},{3,1},... | collective-permute-start | bytes 786440 | tf_op jit(solution)/shard_map/ppermute | solution.py:29
  32.6 30.0 %collective-permute-start.5 = (bf16[256,1024]{1,0:T(8,128)(2,1)}, bf16[256,1024]{1,0:T(8,128)(2,1)S(1)}, u32[]{:S(2)}, u32[]{:S(2)}) collective-permute-start(bf16[256,1024]{1,0:T(8,128)(2,1)} %collective-permute-done.near), channel_id=1, source_target_pairs={{0,2},{2,0},{4,6},{6,4},{8,10},{10,8},{12,14},{14,12},{1,3},{3,1},... | collective-permute-start | bytes 1572872 | tf_op jit(solution)/shard_map/ppermute | solution.py:29
  33.3 0.8 copy-start.13
  34.2 1.0 copy-start.12
  35.3 1.0 copy-start.14
  43.0 26.4 %collective-permute-start.1 = (bf16[256,1024]{1,0:T(8,128)(2,1)}, bf16[256,1024]{1,0:T(8,128)(2,1)}, u32[]{:S(2)}, u32[]{:S(2)}) collective-permute-start(bf16[256,1024]{1,0:T(8,128)(2,1)} %collective-permute-done.near), channel_id=1, source_target_pairs={{0,4},{2,6},{4,8},{6,10},{8,12},{10,14},{12,0},{14,2},{1,5},{3,7},... | collective-permute-start | bytes 1572872 | tf_op jit(solution)/shard_map/ppermute | solution.py:29
  45.3 27.4 %collective-permute-start.11 = (bf16[128,1024]{1,0:T(8,128)(2,1)S(1)}, bf16[128,1024]{1,0:T(8,128)(2,1)S(1)}, u32[]{:S(2)}, u32[]{:S(2)}) collective-permute-start(bf16[128,1024]{1,0:T(8,128)(2,1)S(1)} %collective-permute-done.8.near_ref), channel_id=1, source_target_pairs={{0,2},{2,0},{4,6},{6,4},{8,10},{10,8},{12,14},{14,12},{1,3},{3,1},... | collective-permute-start | bytes 786440 | tf_op jit(solution)/shard_map/ppermute | solution.py:29
  46.6 14.7 %collective-permute-start.9 = (bf16[128,1024]{1,0:T(8,128)(2,1)S(1)}, bf16[128,1024]{1,0:T(8,128)(2,1)S(1)}, u32[]{:S(2)}, u32[]{:S(2)}) collective-permute-start(bf16[128,1024]{1,0:T(8,128)(2,1)S(1)} %collective-permute-done.8.near_ref), channel_id=1, source_target_pairs={{0,4},{2,6},{4,8},{6,10},{8,12},{10,14},{12,0},{14,2},{1,5},{3,7},... | collective-permute-start | bytes 786440 | tf_op jit(solution)/shard_map/ppermute | solution.py:29
  61.3 16.3 %collective-permute-start.10 = (bf16[128,1024]{1,0:T(8,128)(2,1)S(1)}, bf16[128,1024]{1,0:T(8,128)(2,1)S(1)}, u32[]{:S(2)}, u32[]{:S(2)}) collective-permute-start(bf16[128,1024]{1,0:T(8,128)(2,1)S(1)} %collective-permute-done.9.near_ref), channel_id=1, source_target_pairs={{0,2},{2,0},{4,6},{6,4},{8,10},{10,8},{12,14},{14,12},{1,3},{3,1},... | collective-permute-start | bytes 786440 | tf_op jit(solution)/shard_map/ppermute | solution.py:29
  69.4 26.5 %collective-permute-start.4 = (bf16[256,1024]{1,0:T(8,128)(2,1)}, bf16[256,1024]{1,0:T(8,128)(2,1)}, u32[]{:S(2)}, u32[]{:S(2)}) collective-permute-start(bf16[256,1024]{1,0:T(8,128)(2,1)} %collective-permute-done.1.near), channel_id=1, source_target_pairs={{0,2},{2,0},{4,6},{6,4},{8,10},{10,8},{12,14},{14,12},{1,3},{3,1},... | collective-permute-start | bytes 1572872 | tf_op jit(solution)/shard_map/ppermute | solution.py:29
  70.2 24.2 %collective-permute-start.2 = (bf16[256,1024]{1,0:T(8,128)(2,1)}, bf16[256,1024]{1,0:T(8,128)(2,1)}, u32[]{:S(2)}, u32[]{:S(2)}) collective-permute-start(bf16[256,1024]{1,0:T(8,128)(2,1)} %collective-permute-done.1.near), channel_id=1, source_target_pairs={{0,4},{2,6},{4,8},{6,10},{8,12},{10,14},{12,0},{14,2},{1,5},{3,7},... | collective-permute-start | bytes 1572872 | tf_op jit(solution)/shard_map/ppermute | solution.py:29
  82.6 0.8 copy-start.15
  83.4 29.8 %all-to-all-start.1 = ((bf16[8,4,8,1024]{3,2,1,0:T(8,128)(2,1)}), bf16[8,4,8,1024]{3,2,1,0:T(8,128)(2,1)}, u32[]{:S(2)}, u32[]{:S(2)}) async-start(bf16[8,4,8,1024]{3,2,1,0:T(8,128)(2,1)} %copy-done.15), calls=%async_computation.1 | async-start | bytes 1048576 | tf_op jit(solution)/shard_map/all_to_all | solution.py:359
  94.4 18.8 %collective-permute-start.3 = (bf16[256,1024]{1,0:T(8,128)(2,1)}, bf16[256,1024]{1,0:T(8,128)(2,1)}, u32[]{:S(2)}, u32[]{:S(2)}) collective-permute-start(bf16[256,1024]{1,0:T(8,128)(2,1)} %collective-permute-done.2.near), channel_id=1, source_target_pairs={{0,2},{2,0},{4,6},{6,4},{8,10},{10,8},{12,14},{14,12},{1,3},{3,1},... | collective-permute-start | bytes 1572872 | tf_op jit(solution)/shard_map/ppermute | solution.py:29
  107.4 5.8 %copy-start.2 = (bf16[1024,8192]{1,0:T(8,128)(2,1)}, bf16[1024,8192]{1,0:T(8,128)(2,1)S(1)}, u32[]{:S(2)}) copy-start(bf16[1024,8192]{1,0:T(8,128)(2,1)S(1)} %get-tuple-element.14.w_ref) | copy-start | bytes 50331652
  113.2 10.2 %copy-start.3 = (bf16[1024,8192]{1,0:T(8,128)(2,1)S(1)}, bf16[1024,8192]{1,0:T(8,128)(2,1)}, u32[]{:S(2)}) copy-start(bf16[1024,8192]{1,0:T(8,128)(2,1)} %copy-done.2) | copy-start | bytes 50331652
  121.2 2.9 %copy-start.8 = (bf16[256,1024]{1,0:T(8,128)(2,1)}, bf16[256,1024]{1,0:T(8,128)(2,1)S(1)}, u32[]{:S(2)}) copy-start(bf16[256,1024]{1,0:T(8,128)(2,1)S(1)} %get-tuple-element.13.x_ref) | copy-start | bytes 1572868
  124.1 24.9 %collective-permute-start.14 = (bf16[256,1024]{1,0:T(8,128)(2,1)S(1)}, bf16[256,1024]{1,0:T(8,128)(2,1)}, u32[]{:S(2)}, u32[]{:S(2)}) collective-permute-start(bf16[256,1024]{1,0:T(8,128)(2,1)S(1)} %output_share.8), channel_id=1, source_target_pairs={{0,2},{2,0},{4,6},{6,4},{8,10},{10,8},{12,14},{14,12},{1,3},{3,1},... | collective-permute-start | bytes 1572872 | tf_op jit(solution)/shard_map/ppermute | solution.py:29
  124.7 5.8 %copy-start.4 = (bf16[1024,8192]{1,0:T(8,128)(2,1)S(1)}, bf16[1024,8192]{1,0:T(8,128)(2,1)}, u32[]{:S(2)}) copy-start(bf16[1024,8192]{1,0:T(8,128)(2,1)} %copy-done.2) | copy-start | bytes 50331652
  130.5 1.0 copy-start.9
  131.6 2.3 %copy-start.10 = (bf16[256,1024]{1,0:T(8,128)(2,1)S(1)}, bf16[256,1024]{1,0:T(8,128)(2,1)}, u32[]{:S(2)}) copy-start(bf16[256,1024]{1,0:T(8,128)(2,1)} %copy-done.8) | copy-start | bytes 1572868
  132.3 19.1 %collective-permute-start.16 = (bf16[256,1024]{1,0:T(8,128)(2,1)S(1)}, bf16[256,1024]{1,0:T(8,128)(2,1)}, u32[]{:S(2)}, u32[]{:S(2)}) collective-permute-start(bf16[256,1024]{1,0:T(8,128)(2,1)S(1)} %output_share.10), channel_id=1, source_target_pairs={{0,2},{2,0},{4,6},{6,4},{8,10},{10,8},{12,14},{14,12},{1,3},{3,1},... | collective-permute-start | bytes 1572872 | tf_op jit(solution)/shard_map/ppermute | solution.py:29
  133.8 5.8 %copy-start.5 = (bf16[1024,8192]{1,0:T(8,128)(2,1)S(1)}, bf16[1024,8192]{1,0:T(8,128)(2,1)}, u32[]{:S(2)}) copy-start(bf16[1024,8192]{1,0:T(8,128)(2,1)} %copy-done.2) | copy-start | bytes 50331652
  140.3 19.7 %collective-permute-start.18 = (bf16[256,1024]{1,0:T(8,128)(2,1)S(1)}, bf16[256,1024]{1,0:T(8,128)(2,1)S(1)}, u32[]{:S(2)}, u32[]{:S(2)}) collective-permute-start(bf16[256,1024]{1,0:T(8,128)(2,1)S(1)} %output_share.12), channel_id=1, source_target_pairs={{0,2},{2,0},{4,6},{6,4},{8,10},{10,8},{12,14},{14,12},{1,3},{3,1},... | collective-permute-start | bytes 1572872 | tf_op jit(solution)/shard_map/ppermute | solution.py:29
  141.0 5.8 %copy-start.6 = (bf16[1024,8192]{1,0:T(8,128)(2,1)S(1)}, bf16[1024,8192]{1,0:T(8,128)(2,1)}, u32[]{:S(2)}) copy-start(bf16[1024,8192]{1,0:T(8,128)(2,1)} %copy-done.2) | copy-start | bytes 50331652
  147.5 20.6 %collective-permute-start.20 = (bf16[256,1024]{1,0:T(8,128)(2,1)S(1)}, bf16[256,1024]{1,0:T(8,128)(2,1)}, u32[]{:S(2)}, u32[]{:S(2)}) collective-permute-start(bf16[256,1024]{1,0:T(8,128)(2,1)S(1)} %output_share.14), channel_id=1, source_target_pairs={{0,2},{2,0},{4,6},{6,4},{8,10},{10,8},{12,14},{14,12},{1,3},{3,1},... | collective-permute-start | bytes 1572872 | tf_op jit(solution)/shard_map/ppermute | solution.py:29
  150.8 30.7 %collective-permute-start.15 = (bf16[256,1024]{1,0:T(8,128)(2,1)S(1)}, bf16[256,1024]{1,0:T(8,128)(2,1)}, u32[]{:S(2)}, u32[]{:S(2)}) collective-permute-start(bf16[256,1024]{1,0:T(8,128)(2,1)S(1)} %output_share.9), channel_id=1, source_target_pairs={{0,8},{2,10},{4,12},{6,14},{8,0},{10,2},{12,4},{14,6},{1,9},{3,11}... | collective-permute-start | bytes 1572872 | tf_op jit(solution)/shard_map/ppermute | solution.py:29
  154.0 40.6 %collective-permute-start.17 = (bf16[256,1024]{1,0:T(8,128)(2,1)}, bf16[256,1024]{1,0:T(8,128)(2,1)}, u32[]{:S(2)}, u32[]{:S(2)}) collective-permute-start(bf16[256,1024]{1,0:T(8,128)(2,1)} %output_share.11), channel_id=1, source_target_pairs={{0,4},{2,6},{4,8},{6,10},{8,12},{10,14},{12,0},{14,2},{1,5},{3,7},... | collective-permute-start | bytes 1572872 | tf_op jit(solution)/shard_map/ppermute | solution.py:29
  160.0 37.0 %copy-start.1 = (bf16[512,1024]{1,0:T(8,128)(2,1)S(1)}, bf16[512,1024]{1,0:T(8,128)(2,1)}, u32[]{:S(2)}) copy-start(bf16[512,1024]{1,0:T(8,128)(2,1)} %param.10) | copy-start | bytes 3145732
  161.7 32.8 %collective-permute-start.19 = (bf16[256,1024]{1,0:T(8,128)(2,1)}, bf16[256,1024]{1,0:T(8,128)(2,1)S(1)}, u32[]{:S(2)}, u32[]{:S(2)}) collective-permute-start(bf16[256,1024]{1,0:T(8,128)(2,1)} %output_share.13), channel_id=1, source_target_pairs={{0,12},{2,14},{4,0},{6,2},{8,4},{10,6},{12,8},{14,10},{1,13},{3,15... | collective-permute-start | bytes 1572872 | tf_op jit(solution)/shard_map/ppermute | solution.py:29
  168.1 5.8 %copy-start.7 = (bf16[1024,8192]{1,0:T(8,128)(2,1)S(1)}, bf16[1024,8192]{1,0:T(8,128)(2,1)}, u32[]{:S(2)}) copy-start(bf16[1024,8192]{1,0:T(8,128)(2,1)} %copy-done.2) | copy-start | bytes 50331652
  173.9 20.7 %copy-start.17 = (f32[256,1024]{1,0:T(8,128)S(1)}, f32[256,1024]{1,0:T(8,128)}, u32[]{:S(2)}) copy-start(f32[256,1024]{1,0:T(8,128)} %get-tuple-element.17) | copy-start | bytes 3145732

commit v7 on v6

--- a/solution.py
+++ b/solution.py
@@ -16,7 +16,6 @@
 IN_SMEM = pl.BlockSpec(memory_space=pltpu.SMEM)
 IN_VMEM = pl.BlockSpec(memory_space=pltpu.VMEM)
 IN_HBM = pl.BlockSpec(memory_space=pltpu.HBM)
-ANYWHERE = pl.BlockSpec(memory_space=pl.ANY)
 
 
 def moved(array, outer_by, flip):
@@ -31,12 +30,14 @@
 
 def spread(block):
     outer_size = lax.axis_size("tensor") // INNER
-    blocks = []
-    held = block
-    for step in range(outer_size):
-        if step:
-            held = moved(held, 1, 0)
-        blocks.append((held, moved(held, 0, 1)))
+    forward = backward = block
+    blocks = [(0, block, moved(block, 0, 1))]
+    for step in range(1, outer_size // 2 + 1):
+        forward = moved(forward, 1, 0)
+        blocks.append((step, forward, moved(forward, 0, 1)))
+        if step < outer_size - step:
+            backward = moved(backward, -1, 0)
+            blocks.append((-step, backward, moved(backward, 0, 1)))
     return blocks
 
 
@@ -140,14 +141,12 @@
     )[0]
 
 
-def project_kernel(steps, first, last, ahead, spot, near, far, gain_ref, inv_ref, w_hbm, *refs):
+def project_kernel(steps, first, last, spot, near, far, gain_ref, inv_ref, w_hbm, *refs):
     refs = list(refs)
     earlier = None if first else refs.pop(0)
     taps_ref, place_ref, terms_any = (refs.pop(0) for _ in range(3)) if last else (None,) * 3
-    next_hbm = refs.pop(0) if ahead else None
     total_ref = refs.pop(0)
     gated_ref = refs.pop(0) if last else None
-    next_ref = refs.pop(0) if ahead else None
     blocks, normed, held, sems, block_sems, extra_sem, *terms_scr = refs
     _, rows, channels = blocks.shape
     slots, depth, block = held.shape
@@ -170,9 +169,6 @@
     if last:
         extra = pltpu.make_async_copy(terms_any, terms_scr[0], extra_sem.at[0])
         extra.start()
-    if ahead:
-        extra = pltpu.make_async_copy(next_hbm, next_ref, extra_sem.at[0])
-        extra.start()
 
     scale = inv_ref[:, :1]
     for flip, copy in enumerate(copies):
@@ -198,10 +194,9 @@
         return carry
 
     lax.fori_loop(0, chunks, one_chunk, 0)
-    if last or ahead:
-        extra.wait()
     if not last:
         return
+    extra.wait()
     seqs = rows // steps
     wide = min(256, channels)
 
@@ -224,12 +219,12 @@
     lax.fori_loop(0, channels // wide, one_gate, 0)
 
 
-def projected(spot, pair, gains, inv_rms, w_in, earlier, ends=None, ahead=None):
+def projected(spot, pair, gains, inv_rms, w_in, earlier, ends=None):
     near, far = pair
     rows, channels = near.shape
     block = min(512, channels)
     first, last = earlier is None, ends is not None
-    operands = [(ANYWHERE, near), (ANYWHERE, far), (IN_VMEM, gains), (IN_VMEM, inv_rms), (IN_HBM, w_in)]
+    operands = [(IN_HBM, near), (IN_HBM, far), (IN_VMEM, gains), (IN_VMEM, inv_rms), (IN_HBM, w_in)]
     aliases = {}
     if not first:
         aliases = {len(operands) + 1: 0}
@@ -246,14 +241,11 @@
     steps = 1
     if last:
         steps, taps, place, terms = ends
-        operands += [(IN_VMEM, taps), (IN_VMEM, place), (ANYWHERE, terms)]
+        operands += [(IN_VMEM, taps), (IN_VMEM, place), (IN_HBM, terms)]
         outputs.append((IN_VMEM, jax.ShapeDtypeStruct((rows, channels), jnp.bfloat16)))
         scratch.append(pltpu.VMEM(terms.shape, jnp.bfloat16))
-    if ahead is not None:
-        operands.append((IN_HBM, ahead))
-        outputs.append((IN_VMEM, jax.ShapeDtypeStruct(ahead.shape, ahead.dtype)))
-    out = kernel_call(
-        functools.partial(project_kernel, steps, first, last, ahead is not None),
+    return kernel_call(
+        functools.partial(project_kernel, steps, first, last),
         "gated_rows" if last else "projected_part",
         spot,
         operands,
@@ -262,45 +254,47 @@
         scratch,
         4 * rows * INNER * channels * 3 * channels,
         4 * INNER * channels * 3 * channels,
-    )
-    return (out[0], out[1]) if ahead is not None else out[-1]
-
-
-def share_kernel(spot, x_ref, w_ref, *refs):
-    *arrived, out_ref, held, sem = refs
-    wide = out_ref.shape[1]
-    block = min(512, wide)
-    if arrived:
-        copy = pltpu.make_async_copy(arrived[0], held, sem.at[0])
-        copy.start()
-    for start in range(0, wide, block):
-        columns = pl.ds(start, block)
-        in_columns = pl.ds(pl.multiple_of(spot[0] * wide + start, block), block)
-        share = jnp.dot(x_ref[...], w_ref[:, in_columns], preferred_element_type=jnp.float32)
-        if arrived:
-            if start == 0:
-                copy.wait()
-            share += held[:, columns].astype(jnp.float32)
-        out_ref[:, columns] = share.astype(out_ref.dtype)
-
-
-def output_share(spot, gated, w_out, owners, arrived=None):
+    )[-1]
+
+
+def share_kernel(spot, x_ref, w_hbm, *refs):
+    *outs, held, sems = refs
+    wide = outs[0].shape[1]
+    slots, _, block = held.shape
+    parts = wide // block
+    chunks = len(outs) * parts
+
+    def fetch(chunk):
+        start = pl.multiple_of(spot[chunk // parts] * wide + chunk % parts * block, block)
+        slot = chunk % slots
+        return pltpu.make_async_copy(w_hbm.at[:, pl.ds(start, block)], held.at[slot], sems.at[slot])
+
+    for chunk in range(min(slots, chunks)):
+        fetch(chunk).start()
+    for chunk in range(chunks):
+        fetch(chunk).wait()
+        out_ref = outs[chunk // parts]
+        share = jnp.dot(x_ref[...], held[chunk % slots], preferred_element_type=jnp.float32)
+        out_ref[:, pl.ds(chunk % parts * block, block)] = share.astype(out_ref.dtype)
+        if chunk + slots < chunks:
+            fetch(chunk + slots).start()
+
+
+def output_shares(targets, gated, w_out, owners):
     rows, channels = gated.shape
     wide = w_out.shape[1] // owners
-    operands = [(IN_VMEM, gated), (IN_VMEM, w_out)]
-    if arrived is not None:
-        operands.append((ANYWHERE, arrived))
+    block = min(512, wide)
     return kernel_call(
         share_kernel,
-        "output_share",
-        spot,
-        operands,
-        [(IN_VMEM, jax.ShapeDtypeStruct((rows, wide), jnp.bfloat16))],
+        "output_shares",
+        jnp.stack([which for which, _ in targets]).astype(jnp.int32),
+        [(IN_VMEM, gated), (IN_HBM, w_out)],
+        [(IN_VMEM, jax.ShapeDtypeStruct((rows, wide), kind)) for _, kind in targets],
         {},
-        [pltpu.VMEM((rows, wide), jnp.bfloat16), pltpu.SemaphoreType.DMA((1,))],
-        2 * rows * channels * wide,
-        2 * channels * wide,
-    )[0]
+        [pltpu.VMEM((DEPTH, channels, block), jnp.bfloat16), pltpu.SemaphoreType.DMA((DEPTH,))],
+        2 * rows * channels * wide * len(targets),
+        2 * channels * wide * len(targets),
+    )
 
 
 def after(array, earlier):
@@ -329,8 +323,9 @@
     gains = tiny[:, :gain_rows].reshape(owners, channels)
     inv_rms = lax.rsqrt(jnp.sum(tiny[:, gain_rows:], axis=0).reshape(tokens) / D + EPSILON)
     inv_rms = jnp.broadcast_to(inv_rms[:, None], (tokens, LANES))
-    lag_taps = spread(filters.T)
-    streams = spread(stream.astype(jnp.bfloat16))
+    own_taps = filters.T
+    lag_taps = spread(own_taps)
+    streams = spread(after(stream.astype(jnp.bfloat16), own_taps))
 
     def spot_at(back):
         return jnp.stack([(outer + back) % outer_size, inner]).astype(jnp.int32)
@@ -351,31 +346,38 @@
     cache = cache_rows.transpose(1, 0, 2)
     near_taps = filters[:, : 2 * steps].T.astype(jnp.float32)
     terms = sums = None
-    for back, (near, far) in enumerate(lag_taps):
-        if 0 < back <= outer_size // 2:
-            sums = projected(spot_at(1 - back), streams[back - 1], gains, inv_rms, w_in, sums)
+    parts = len(streams)
+    for index, (back, near, far) in enumerate(lag_taps):
+        if index:
             near = after(near, sums)
         terms = history_terms(cache, near, far, row_lengths, spot_at(-back), steps, terms)
+        if 2 * index < parts:
+            at, *pair = streams[index]
+            pair[0] = after(pair[0], terms)
+            sums = projected(spot_at(-at), pair, gains, inv_rms, w_in, sums)
     terms = lax.all_to_all(terms, "tensor", 0, 0, tiled=True)
     terms = terms.reshape(owners * steps * rows, channels)
-    for back in range(outer_size // 2, outer_size - 1):
-        ahead = w_out if back == outer_size - 2 else None
-        sums = projected(spot_at(-back), streams[back], gains, inv_rms, w_in, sums, ahead=ahead)
-    sums, w_out = sums
-    ends = (steps, near_taps, place, terms)
-    gated = projected(spot_at(1 - outer_size), streams[-1], gains, inv_rms, w_in, sums, ends)
-
-    def spot_to(ahead, flip):
-        return ((outer + ahead) % outer_size * INNER + (inner + flip) % INNER)[None].astype(jnp.int32)
+    for index in range((parts + 1) // 2, parts):
+        at, *pair = streams[index]
+        ends = (steps, near_taps, place, terms) if index == parts - 1 else None
+        sums = projected(spot_at(-at), pair, gains, inv_rms, w_in, sums, ends)
+    gated = sums
+
+    def owner_at(ahead, flip):
+        return (outer + ahead) % outer_size * INNER + (inner + flip) % INNER
 
     order = sorted(range(outer_size), key=lambda ahead: (ahead == 0, -min(ahead, outer_size - ahead)))
-    across = {
-        ahead: moved(output_share(spot_to(ahead, 1), gated, w_out, owners), 0, 1) for ahead in order
-    }
+    targets = [(owner_at(ahead, 1), jnp.bfloat16) for ahead in order]
+    targets += [(owner_at(ahead, 0), jnp.float32) for ahead in order]
+    shares = list(output_shares(targets[:2], gated, w_out, owners))
+    across = [moved(share, 0, 1) for share in shares]
+    for start in range(2, len(targets), 6):
+        shares += output_shares(targets[start : start + 6], gated, w_out, owners)
+    across += [moved(share, 0, 1) for share in shares[2:outer_size]]
     out = stream
-    for ahead in order:
-        share = output_share(spot_to(ahead, 0), gated, w_out, owners, across[ahead])
-        out = out + (moved(share, ahead, 0) if ahead else share).astype(jnp.float32)
+    for ahead, own_share, arrived_share in zip(order, shares[outer_size:], across):
+        share = own_share + arrived_share.astype(jnp.float32)
+        out = out + (moved(share.astype(jnp.bfloat16), ahead, 0) if ahead else share)
     return out.astype(jnp.bfloat16).reshape(steps, seqs, channels)
 
 

time: 198 us -> 174 us (0.88)
  local copies, waits for them, and re-layouts: 42.4 us -> 5.89 us
  waiting for transfers between devices: 45.5 us -> 60.3 us
  Pallas kernels: 64 us -> 60.8 us
  other arithmetic: 5.99 us -> 3.36 us
    unnamed x39 -> x27, local copies, waits for them, and re-layouts: 37.2 us -> 3.84 us
    ppermute x21, waiting for transfers between devices: 38.2 us -> 48.2 us  [moved(): return lax.ppermute(array, 'tensor', pairs)]
    all_to_all x1, waiting for transfers between devices: 7.3 us -> 12.1 us  [per_device(): lax.all_to_all(jnp.broadcast_to(tiny[None], (owners, *tiny.shape)), 'tens...]
    pallas_call x16 -> x10, Pallas kernels: 64 us -> 60.8 us  [kernel_call(): pl.pallas_call(kernel, in_specs=[IN_SMEM, *specs], out_specs=list(out_spe...]
    convert_element_type x2, local copies, waits for them, and re-layouts: 2.84 us -> 0.31 us  [per_device(): place = place.astype(jnp.bfloat16)]
    ppermute x21, starting transfers between devices: 24.6 us -> 26.7 us  [moved(): return lax.ppermute(array, 'tensor', pairs)]
  transfers between devices with their start and end apart: 23 -> 23, of which waited for: 6 -> 9; matrix products, arithmetic and copies ran while one was open for 5% -> 3% of each run, Pallas kernels for 28% -> 29%
where the time goes in v7:
time: 174 us; the launch traced here: 171 us
  Pallas kernels  60.8 us (35%)
  waiting for transfers between devices  60.3 us (35%)
  starting transfers between devices  38.9 us (22%)
  local copies, waits for them, and re-layouts  5.89 us (3%)
  other arithmetic  3.36 us (2%)
    pallas_call x10, Pallas kernels, kernel_call(): pl.pallas_call(kernel, in_specs=[IN_SMEM, *specs], out_specs=list(out_spe...  60.8 us
    ppermute x21, waiting for transfers between devices, moved(): return lax.ppermute(array, 'tensor', pairs)  48.2 us
    ppermute x21, starting transfers between devices, moved(): return lax.ppermute(array, 'tensor', pairs)  26.7 us
    all_to_all x1, waiting for transfers between devices, per_device(): lax.all_to_all(jnp.broadcast_to(tiny[None], (owners, *tiny.shape)), 'tens...  12.1 us
    all_to_all x1, starting transfers between devices, per_device(): terms = lax.all_to_all(terms, 'tensor', 0, 0, tiled=True)  6.74 us
    all_to_all x1, starting transfers between devices, per_device(): lax.all_to_all(jnp.broadcast_to(tiny[None], (owners, *tiny.shape)), 'tens...  5.4 us
    unnamed x27, local copies, waits for them, and re-layouts  3.84 us
  transfers between devices with their start and end apart: 23, of which 9 were waited for; matrix products, arithmetic and copies ran while one was open for 3% of the time, Pallas kernels for 29%

profile of v7, /device:TPU:18, one launch (start us, length us, event | category | flops | bytes accessed | tf_op | source)
XLA Modules:
  0.0 171.2 jit_solution(17786610443849034189)
XLA Ops:
  0.0 1.2 copy.24
  1.2 1.6 collective-permute-start.6
  2.8 1.6 collective-permute-start.5
  4.4 0.8 eq.92
  5.1 1.6 multiply_reduce_fusion
  6.8 0.5 collective-permute-start.7
  7.3 0.2 collective-permute-start
  7.5 1.8 %collective-permute-start.12 = (bf16[128,1024]{1,0:T(8,128)(2,1)S(1)}, bf16[128,1024]{1,0:T(8,128)(2,1)}, u32[]{:S(2)}, u32[]{:S(2)}) collective-permute-start(bf16[128,1024]{1,0:T(8,128)(2,1)S(1)} %bitcast.40), channel_id=1, source_target_pairs={{0,12},{2,14},{4,0},{6,2},{8,4},{10,6},{12,8},{14,10},{1,13},{3,15... | collective-permute-start | bytes 786440 | tf_op jit(solution)/shard_map/ppermute | solution.py:28
  9.3 0.6 broadcast_in_dim.21
  9.9 5.4 %all-to-all-start = ((f32[8,10,128]{2,1,0:T(8,128)}), f32[8,10,128]{2,1,0:T(8,128)S(1)}, u32[]{:S(2)}, u32[]{:S(2)}) async-start(f32[8,10,128]{2,1,0:T(8,128)} %broadcast_in_dim.21), calls=%async_computation | async-start | bytes 131072 | tf_op jit(solution)/shard_map/all_to_all | solution.py:319
  15.4 0.1 reshape.69
  15.5 0.1 pad_add_fusion.3.spot
  15.7 0.1 iota_compare_fusion.2
  15.8 0.2 and_convert_fusion
  16.0 0.2 reshape.72
  16.2 0.1 copy.26.refs_2_
  16.3 0.2 select_reduce_fusion
  16.5 0.1 pad_add_fusion.spot
  16.6 12.1 %all-to-all-done = f32[8,10,128]{2,1,0:T(8,128)S(1)} async-done(((f32[8,10,128]{2,1,0:T(8,128)}), f32[8,10,128]{2,1,0:T(8,128)S(1)}, u32[]{:S(2)}, u32[]{:S(2)}) %all-to-all-start) | async-done | bytes 40992 | tf_op jit(solution)/shard_map/all_to_all | solution.py:319
  28.7 1.3 collective-permute-start.3
  30.1 4.9 %history_terms.4.refs_0_ = bf16[8,4,8,1024]{3,2,1,0:T(8,128)(2,1)S(1)} custom-call(s32[2]{0:T(128)S(1)} %pad_add_fusion.3.spot, s32[8,128]{1,0:T(8,128)S(1)} %broadcast_in_dim.25.lengths_ref, bf16[128,1024]{1,0:T(8,128)(2,1)S(1)} %bitcast.41, bf16[128,1024]{1,0:T(8,128)(2,1)S(1)} %collective-permute-done.6.far_ref, bf16[127,8,8192]{2,1,0:T(8,128)(2,1)} %bitcast.43), custom_call_target="tpu_custom_call" | custom-call | flops 4993843200 | bytes 4161536 | tf_op jit(solution)/shard_map/history_terms/pallas_call | solution.py:51
  35.1 1.3 collective-permute-start.8
  36.4 0.9 collective-permute-start.10
  37.3 0.7 collective-permute-start.13
  38.0 1.3 collective-permute-start.9
  39.3 0.1 broadcast_in_dim.22.inv_ref
  39.4 6.9 %projected_part.3.refs_0_ = f32[256,3072]{1,0:T(8,128)S(1)} custom-call(s32[2]{0:T(128)S(1)} %pad_add_fusion.3.spot, bf16[256,1024]{1,0:T(8,128)(2,1)} %get-tuple-element.21.near, bf16[256,1024]{1,0:T(8,128)(2,1)} %copy-done.7, f32[8,1024]{1,0:T(8,128)S(1)} %bitcast.34, f32[256,128]{1,0:T(8,128)S(1)} %broadcast_in_dim.22.inv_ref, bf16[8192,3072]{1,0:T(8,128)(2,1)} %w_hbm.9), custom_call_target="tpu_custom_call" | custom-call | flops 6442450944 | bytes 25165824 | tf_op jit(solution)/shard_map/projected_part/pallas_call | solution.py:51
  46.3 5.4 %history_terms.5.refs_0_ = bf16[8,4,8,1024]{3,2,1,0:T(8,128)(2,1)S(1)} custom-call(s32[2]{0:T(128)S(1)} %pad_add_fusion.2.spot, s32[8,128]{1,0:T(8,128)S(1)} %broadcast_in_dim.25.lengths_ref, bf16[128,1024]{1,0:T(8,128)(2,1)} %collective-permute-done.5.near_ref, ...), custom_call_target="tpu_custom_call", output_to_operand_aliasing={{}: (5, {})} | custom-call | flops 4993843200 | bytes 4161536 | tf_op jit(solution)/shard_map/history_terms/pallas_call | solution.py:51
  51.7 3.5 %collective-permute-start.1 = (bf16[256,1024]{1,0:T(8,128)(2,1)}, bf16[256,1024]{1,0:T(8,128)(2,1)}, u32[]{:S(2)}, u32[]{:S(2)}) collective-permute-start(bf16[256,1024]{1,0:T(8,128)(2,1)} %collective-permute-done.near), channel_id=1, source_target_pairs={{0,4},{2,6},{4,8},{6,10},{8,12},{10,14},{12,0},{14,2},{1,5},{3,7},... | collective-permute-start | bytes 1572872 | tf_op jit(solution)/shard_map/ppermute | solution.py:28
  55.2 0.7 collective-permute-start.11
  55.9 1.4 collective-permute-start.4
  57.3 4.2 %collective-permute-done.9.far = bf16[256,1024]{1,0:T(8,128)(2,1)S(1)} collective-permute-done((bf16[256,1024]{1,0:T(8,128)(2,1)}, bf16[256,1024]{1,0:T(8,128)(2,1)S(1)}, u32[]{:S(2)}, u32[]{:S(2)}) %collective-permute-start.9) | collective-permute-done | bytes 524320 | tf_op jit(solution)/shard_map/ppermute | solution.py:28
  61.5 0.8 copy-done.8
  62.3 6.9 %projected_part.4.refs_0_ = f32[256,3072]{1,0:T(8,128)S(1)} custom-call(s32[2]{0:T(128)S(1)} %pad_add_fusion.2.spot, bf16[256,1024]{1,0:T(8,128)(2,1)} %collective-permute-done.near, bf16[256,1024]{1,0:T(8,128)(2,1)} %copy-done.8, f32[8,1024]{1,0:T(8,128)S(1)} %bitcast.35, f32[256,128]{1,0:T(8,128)S(1)} %broadcast_in_dim.22.inv_ref, ...), custom_call_target="tpu_custom_call", output_to_operand_aliasing={{}: (6, {})} | custom-call | flops 6442450944 | bytes 25165824 | tf_op jit(solution)/shard_map/projected_part/pallas_call | solution.py:51
  69.2 5.4 %history_terms.6.refs_0_ = bf16[8,4,8,1024]{3,2,1,0:T(8,128)(2,1)S(1)} custom-call(s32[2]{0:T(128)S(1)} %pad_add_fusion.1.spot, s32[8,128]{1,0:T(8,128)S(1)} %broadcast_in_dim.25.lengths_ref, bf16[128,1024]{1,0:T(8,128)(2,1)} %collective-permute-done.12.near_ref, ...), custom_call_target="tpu_custom_call", output_to_operand_aliasing={{}: (5, {})} | custom-call | flops 4993843200 | bytes 4161536 | tf_op jit(solution)/shard_map/history_terms/pallas_call | solution.py:51
  74.6 5.0 %history_terms.7 = bf16[8,4,8,1024]{3,2,1,0:T(8,128)(2,1)S(1)} custom-call(s32[2]{0:T(128)S(1)} %pad_add_fusion.spot, s32[8,128]{1,0:T(8,128)S(1)} %broadcast_in_dim.25.lengths_ref, bf16[128,1024]{1,0:T(8,128)(2,1)S(1)} %collective-permute-done.10.near_ref, bf16[128,1024]{1,0:T(8,128)(2,1)S(1)} %collective-permute-done.11.far_ref, ...), custom_call_target="tpu_custom_call", output_to_operand_aliasing={{}: (5, {})} | custom-call | flops 4993843200 | bytes 4161536 | tf_op jit(solution)/shard_map/history_terms/pallas_call | solution.py:51
  79.6 0.8 copy-done.4
  80.4 6.7 %all-to-all-start.1 = ((bf16[8,4,8,1024]{3,2,1,0:T(8,128)(2,1)}), bf16[8,4,8,1024]{3,2,1,0:T(8,128)(2,1)}, u32[]{:S(2)}, u32[]{:S(2)}) async-start(bf16[8,4,8,1024]{3,2,1,0:T(8,128)(2,1)} %copy-done.4), calls=%async_computation.1 | async-start | bytes 1048576 | tf_op jit(solution)/shard_map/all_to_all | solution.py:358
  87.2 0.7 convert_bitcast_fusion.refs_1_
  87.9 1.5 collective-permute-start.2
  89.4 6.9 %projected_part.5.refs_0_ = f32[256,3072]{1,0:T(8,128)S(1)} custom-call(s32[2]{0:T(128)S(1)} %pad_add_fusion.1.spot, bf16[256,1024]{1,0:T(8,128)(2,1)} %collective-permute-done.3.near, bf16[256,1024]{1,0:T(8,128)(2,1)} %collective-permute-done.4.far, f32[8,1024]{1,0:T(8,128)S(1)} %bitcast.36, ...), custom_call_target="tpu_custom_call", output_to_operand_aliasing={{}: (6, {})} | custom-call | flops 6442450944 | bytes 25165824 | tf_op jit(solution)/shard_map/projected_part/pallas_call | solution.py:51
  96.3 5.0 %collective-permute-done.2.far = bf16[256,1024]{1,0:T(8,128)(2,1)} collective-permute-done((bf16[256,1024]{1,0:T(8,128)(2,1)}, bf16[256,1024]{1,0:T(8,128)(2,1)}, u32[]{:S(2)}, u32[]{:S(2)}) %collective-permute-start.2) | collective-permute-done | bytes 524320 | tf_op jit(solution)/shard_map/ppermute | solution.py:28
  101.3 7.8 %gated_rows.1 = (f32[256,3072]{1,0:T(8,128)S(1)}, bf16[256,1024]{1,0:T(8,128)(2,1)S(1)}) custom-call(s32[2]{0:T(128)S(1)} %pad_add_fusion.spot, bf16[256,1024]{1,0:T(8,128)(2,1)} %collective-permute-done.1.near, bf16[256,1024]{1,0:T(8,128)(2,1)} %collective-permute-done.2.far, f32[8,1024]{1,0:T(8,128)S(1)} %bitcast.37, ...), custom_call_target="tpu_custom_call", output_to_operand_aliasing={{0}: (6, {})} | custom-call | flops 6442450944 | bytes 25165824 | tf_op jit(solution)/shard_map/gated_rows/pallas_call | solution.py:51
  109.1 3.8 %output_shares.3 = (bf16[256,1024]{1,0:T(8,128)(2,1)S(1)}, bf16[256,1024]{1,0:T(8,128)(2,1)S(1)}) custom-call(s32[2]{0:T(128)S(1)} %pad_add_fusion.4.spot, bf16[256,1024]{1,0:T(8,128)(2,1)S(1)} %get-tuple-element.26.x_ref, bf16[1024,8192]{1,0:T(8,128)(2,1)} %w_hbm.11), custom_call_target="tpu_custom_call" | custom-call | flops 1073741824 | bytes 4194304 | tf_op jit(solution)/shard_map/output_shares/pallas_call | solution.py:51
  112.9 0.9 collective-permute-start.14
  113.8 0.1 stack.78.spot
  113.9 1.2 collective-permute-start.16
  115.1 1.0 copy-done.3
  116.1 7.9 %output_shares.2 = (bf16[256,1024]{1,0:T(8,128)(2,1)S(1)}, bf16[256,1024]{1,0:T(8,128)(2,1)S(1)}, f32[256,1024]{1,0:T(8,128)S(1)}, f32[256,1024]{1,0:T(8,128)S(1...) custom-call(s32[6]{0:T(128)S(1)} %stack.78.spot, bf16[256,1024]{1,0:T(8,128)(2,1)S(1)} %copy-done.3, ...), custom_call_target="tpu_custom_call" | custom-call | flops 3221225472 | bytes 12582912 | tf_op jit(solution)/shard_map/output_shares/pallas_call | solution.py:51
  124.0 0.9 collective-permute-start.18
  124.9 1.2 collective-permute-start.20
  126.1 1.8 %collective-permute-done.14 = bf16[256,1024]{1,0:T(8,128)(2,1)S(1)} collective-permute-done((bf16[256,1024]{1,0:T(8,128)(2,1)S(1)}, bf16[256,1024]{1,0:T(8,128)(2,1)S(1)}, u32[]{:S(2)}, u32[]{:S(2)}) %collective-permute-start.14) | collective-permute-done | bytes 524320 | tf_op jit(solution)/shard_map/ppermute | solution.py:28
  127.8 0.1 add_convert_fusion.3
  128.0 0.7 collective-permute-start.15
  128.7 10.3 %collective-permute-done.16 = bf16[256,1024]{1,0:T(8,128)(2,1)S(1)} collective-permute-done((bf16[256,1024]{1,0:T(8,128)(2,1)S(1)}, bf16[256,1024]{1,0:T(8,128)(2,1)S(1)}, u32[]{:S(2)}, u32[]{:S(2)}) %collective-permute-start.16) | collective-permute-done | bytes 524320 | tf_op jit(solution)/shard_map/ppermute | solution.py:28
  139.0 0.1 add_convert_fusion.2
  139.2 1.8 %collective-permute-start.17 = (bf16[256,1024]{1,0:T(8,128)(2,1)S(1)}, bf16[256,1024]{1,0:T(8,128)(2,1)S(1)}, u32[]{:S(2)}, u32[]{:S(2)}) collective-permute-start(bf16[256,1024]{1,0:T(8,128)(2,1)S(1)} %add_convert_fusion.2), channel_id=1, source_target_pairs={{0,4},{2,6},{4,8},{6,10},{8,12},{10,14},{12,0},{14,2},{1,5},{3,7},... | collective-permute-start | bytes 1572872 | tf_op jit(solution)/shard_map/ppermute | solution.py:28
  141.0 9.3 %collective-permute-done.18 = bf16[256,1024]{1,0:T(8,128)(2,1)S(1)} collective-permute-done((bf16[256,1024]{1,0:T(8,128)(2,1)S(1)}, bf16[256,1024]{1,0:T(8,128)(2,1)S(1)}, u32[]{:S(2)}, u32[]{:S(2)}) %collective-permute-start.18) | collective-permute-done | bytes 524320 | tf_op jit(solution)/shard_map/ppermute | solution.py:28
  150.3 0.2 add_convert_fusion.1
  150.5 1.8 %collective-permute-start.19 = (bf16[256,1024]{1,0:T(8,128)(2,1)S(1)}, bf16[256,1024]{1,0:T(8,128)(2,1)S(1)}, u32[]{:S(2)}, u32[]{:S(2)}) collective-permute-start(bf16[256,1024]{1,0:T(8,128)(2,1)S(1)} %add_convert_fusion.1), channel_id=1, source_target_pairs={{0,12},{2,14},{4,0},{6,2},{8,4},{10,6},{12,8},{14,10},{1,13},{3,15... | collective-permute-start | bytes 1572872 | tf_op jit(solution)/shard_map/ppermute | solution.py:28
  152.3 4.4 %collective-permute-done.20 = bf16[256,1024]{1,0:T(8,128)(2,1)S(1)} collective-permute-done((bf16[256,1024]{1,0:T(8,128)(2,1)S(1)}, bf16[256,1024]{1,0:T(8,128)(2,1)S(1)}, u32[]{:S(2)}, u32[]{:S(2)}) %collective-permute-start.20) | collective-permute-done | bytes 524320 | tf_op jit(solution)/shard_map/ppermute | solution.py:28
  156.7 2.6 %collective-permute-done.15 = bf16[256,1024]{1,0:T(8,128)(2,1)S(1)} collective-permute-done((bf16[256,1024]{1,0:T(8,128)(2,1)S(1)}, bf16[256,1024]{1,0:T(8,128)(2,1)S(1)}, u32[]{:S(2)}, u32[]{:S(2)}) %collective-permute-start.15) | collective-permute-done | bytes 524320 | tf_op jit(solution)/shard_map/ppermute | solution.py:28
  159.3 10.6 %collective-permute-done.17 = bf16[256,1024]{1,0:T(8,128)(2,1)S(1)} collective-permute-done((bf16[256,1024]{1,0:T(8,128)(2,1)S(1)}, bf16[256,1024]{1,0:T(8,128)(2,1)S(1)}, u32[]{:S(2)}, u32[]{:S(2)}) %collective-permute-start.17) | collective-permute-done | bytes 524320 | tf_op jit(solution)/shard_map/ppermute | solution.py:28
  169.8 1.3 add_convert_fusion
  (48 shorter events, 0.4 us)
Async XLA Ops:
  0.0 5.1 %copy-start = (bf16[512,1024]{1,0:T(8,128)(2,1)S(1)}, bf16[512,1024]{1,0:T(8,128)(2,1)}, u32[]{:S(2)}) copy-start(bf16[512,1024]{1,0:T(8,128)(2,1)} %param.10) | copy-start | bytes 3145732
  0.0 9.3 %copy-start.9 = (bf16[1024]{0:T(1024)(128)(2,1)S(1)}, bf16[1024]{0:T(1024)(128)(2,1)}, u32[]{:S(2)}) copy-start(bf16[1024]{0:T(1024)(128)(2,1)} %param.11) | copy-start | bytes 6148
  0.0 15.3 %copy-start.10 = (s32[128]{0:T(128)S(1)}, s32[128]{0:T(128)}, u32[]{:S(2)}) copy-start(s32[128]{0:T(128)} %param.16) | copy-start | bytes 1540
  0.0 16.3 %copy-start.11 = (s32[64]{0:T(128)S(1)}, s32[64]{0:T(128)}, u32[]{:S(2)}) copy-start(s32[64]{0:T(128)} %param.17) | copy-start | bytes 772
  1.2 33.9 %copy-start.5 = (bf16[1024,128]{0,1:T(8,128)(2,1)}, bf16[1024,128]{0,1:T(8,128)(2,1)S(1)}, u32[]{:S(2)}) copy-start(bf16[1024,128]{0,1:T(8,128)(2,1)S(1)} %copy.24) | copy-start | bytes 786436
  1.2 27.5 %collective-permute-start.6 = (bf16[128,1024]{1,0:T(8,128)(2,1)S(1)}, bf16[128,1024]{1,0:T(8,128)(2,1)S(1)}, u32[]{:S(2)}, u32[]{:S(2)}) collective-permute-start(bf16[128,1024]{1,0:T(8,128)(2,1)S(1)} %bitcast.38), channel_id=1, source_target_pairs={{0,2},{2,0},{4,6},{6,4},{8,10},{10,8},{12,14},{14,12},{1,3},{3,1},... | collective-permute-start | bytes 786440 | tf_op jit(solution)/shard_map/ppermute | solution.py:28
  2.8 32.3 %collective-permute-start.5 = (bf16[128,1024]{1,0:T(8,128)(2,1)S(1)}, bf16[128,1024]{1,0:T(8,128)(2,1)}, u32[]{:S(2)}, u32[]{:S(2)}) collective-permute-start(bf16[128,1024]{1,0:T(8,128)(2,1)S(1)} %bitcast.39), channel_id=1, source_target_pairs={{0,4},{2,6},{4,8},{6,10},{8,12},{10,14},{12,0},{14,2},{1,5},{3,7},... | collective-permute-start | bytes 786440 | tf_op jit(solution)/shard_map/ppermute | solution.py:28
  6.8 30.5 %collective-permute-start.7 = (bf16[256,1024]{1,0:T(8,128)(2,1)}, bf16[256,1024]{1,0:T(8,128)(2,1)S(1)}, u32[]{:S(2)}, u32[]{:S(2)}) collective-permute-start(bf16[256,1024]{1,0:T(8,128)(2,1)} %get-tuple-element.21.near), channel_id=1, source_target_pairs={{0,2},{2,0},{4,6},{6,4},{8,10},{10,8},{12,14},{14,12},{1,3},{3,1},... | collective-permute-start | bytes 1572872 | tf_op jit(solution)/shard_map/ppermute | solution.py:28
  7.3 30.7 %collective-permute-start = (bf16[256,1024]{1,0:T(8,128)(2,1)}, bf16[256,1024]{1,0:T(8,128)(2,1)}, u32[]{:S(2)}, u32[]{:S(2)}) collective-permute-start(bf16[256,1024]{1,0:T(8,128)(2,1)} %get-tuple-element.21.near), channel_id=1, source_target_pairs={{0,4},{2,6},{4,8},{6,10},{8,12},{10,14},{12,0},{14,2},{1,5},{3,7},... | collective-permute-start | bytes 1572872 | tf_op jit(solution)/shard_map/ppermute | solution.py:28
  7.5 28.9 %collective-permute-start.12 = (bf16[128,1024]{1,0:T(8,128)(2,1)S(1)}, bf16[128,1024]{1,0:T(8,128)(2,1)}, u32[]{:S(2)}, u32[]{:S(2)}) collective-permute-start(bf16[128,1024]{1,0:T(8,128)(2,1)S(1)} %bitcast.40), channel_id=1, source_target_pairs={{0,12},{2,14},{4,0},{6,2},{8,4},{10,6},{12,8},{14,10},{1,13},{3,15... | collective-permute-start | bytes 786440 | tf_op jit(solution)/shard_map/ppermute | solution.py:28
  9.9 18.7 %all-to-all-start = ((f32[8,10,128]{2,1,0:T(8,128)}), f32[8,10,128]{2,1,0:T(8,128)S(1)}, u32[]{:S(2)}, u32[]{:S(2)}) async-start(f32[8,10,128]{2,1,0:T(8,128)} %broadcast_in_dim.21), calls=%async_computation | async-start | bytes 131072 | tf_op jit(solution)/shard_map/all_to_all | solution.py:319
  28.7 27.1 %collective-permute-start.3 = (bf16[256,1024]{1,0:T(8,128)(2,1)}, bf16[256,1024]{1,0:T(8,128)(2,1)}, u32[]{:S(2)}, u32[]{:S(2)}) collective-permute-start(bf16[256,1024]{1,0:T(8,128)(2,1)} %get-tuple-element.21.near), channel_id=1, source_target_pairs={{0,12},{2,14},{4,0},{6,2},{8,4},{10,6},{12,8},{14,10},{1,13},{3,15... | collective-permute-start | bytes 1572872 | tf_op jit(solution)/shard_map/ppermute | solution.py:28
  35.1 11.2 %collective-permute-start.8 = (bf16[128,1024]{1,0:T(8,128)(2,1)}, bf16[128,1024]{1,0:T(8,128)(2,1)S(1)}, u32[]{:S(2)}, u32[]{:S(2)}) collective-permute-start(bf16[128,1024]{1,0:T(8,128)(2,1)} %collective-permute-done.5.near_ref), channel_id=1, source_target_pairs={{0,2},{2,0},{4,6},{6,4},{8,10},{10,8},{12,14},{14,12},{1,3},{3,1},... | collective-permute-start | bytes 786440 | tf_op jit(solution)/shard_map/ppermute | solution.py:28
  36.4 18.8 %collective-permute-start.10 = (bf16[128,1024]{1,0:T(8,128)(2,1)}, bf16[128,1024]{1,0:T(8,128)(2,1)S(1)}, u32[]{:S(2)}, u32[]{:S(2)}) collective-permute-start(bf16[128,1024]{1,0:T(8,128)(2,1)} %collective-permute-done.5.near_ref), channel_id=1, source_target_pairs={{0,4},{2,6},{4,8},{6,10},{8,12},{10,14},{12,0},{14,2},{1,5},{3,7},... | collective-permute-start | bytes 786440 | tf_op jit(solution)/shard_map/ppermute | solution.py:28
  37.3 2.1 %copy-start.7 = (bf16[256,1024]{1,0:T(8,128)(2,1)}, bf16[256,1024]{1,0:T(8,128)(2,1)S(1)}, u32[]{:S(2)}) copy-start(bf16[256,1024]{1,0:T(8,128)(2,1)S(1)} %collective-permute-done.7.far) | copy-start | bytes 1572868
  37.3 31.9 %collective-permute-start.13 = (bf16[128,1024]{1,0:T(8,128)(2,1)}, bf16[128,1024]{1,0:T(8,128)(2,1)S(1)}, u32[]{:S(2)}, u32[]{:S(2)}) collective-permute-start(bf16[128,1024]{1,0:T(8,128)(2,1)} %collective-permute-done.12.near_ref), channel_id=1, source_target_pairs={{0,2},{2,0},{4,6},{6,4},{8,10},{10,8},{12,14},{14,12},{1,3},{3,1},... | collective-permute-start | bytes 786440 | tf_op jit(solution)/shard_map/ppermute | solution.py:28
  38.0 23.5 %collective-permute-start.9 = (bf16[256,1024]{1,0:T(8,128)(2,1)}, bf16[256,1024]{1,0:T(8,128)(2,1)S(1)}, u32[]{:S(2)}, u32[]{:S(2)}) collective-permute-start(bf16[256,1024]{1,0:T(8,128)(2,1)} %collective-permute-done.near), channel_id=1, source_target_pairs={{0,2},{2,0},{4,6},{6,4},{8,10},{10,8},{12,14},{14,12},{1,3},{3,1},... | collective-permute-start | bytes 1572872 | tf_op jit(solution)/shard_map/ppermute | solution.py:28
  51.7 36.2 %collective-permute-start.1 = (bf16[256,1024]{1,0:T(8,128)(2,1)}, bf16[256,1024]{1,0:T(8,128)(2,1)}, u32[]{:S(2)}, u32[]{:S(2)}) collective-permute-start(bf16[256,1024]{1,0:T(8,128)(2,1)} %collective-permute-done.near), channel_id=1, source_target_pairs={{0,4},{2,6},{4,8},{6,10},{8,12},{10,14},{12,0},{14,2},{1,5},{3,7},... | collective-permute-start | bytes 1572872 | tf_op jit(solution)/shard_map/ppermute | solution.py:28
  55.2 19.4 %collective-permute-start.11 = (bf16[128,1024]{1,0:T(8,128)(2,1)S(1)}, bf16[128,1024]{1,0:T(8,128)(2,1)S(1)}, u32[]{:S(2)}, u32[]{:S(2)}) collective-permute-start(bf16[128,1024]{1,0:T(8,128)(2,1)S(1)} %collective-permute-done.10.near_ref), channel_id=1, source_target_pairs={{0,2},{2,0},{4,6},{6,4},{8,10},{10,8},{12,14},{14,12},{1,3},{3,1},... | collective-permute-start | bytes 786440 | tf_op jit(solution)/shard_map/ppermute | solution.py:28
  55.9 33.5 %collective-permute-start.4 = (bf16[256,1024]{1,0:T(8,128)(2,1)}, bf16[256,1024]{1,0:T(8,128)(2,1)}, u32[]{:S(2)}, u32[]{:S(2)}) collective-permute-start(bf16[256,1024]{1,0:T(8,128)(2,1)} %collective-permute-done.3.near), channel_id=1, source_target_pairs={{0,2},{2,0},{4,6},{6,4},{8,10},{10,8},{12,14},{14,12},{1,3},{3,1},... | collective-permute-start | bytes 1572872 | tf_op jit(solution)/shard_map/ppermute | solution.py:28
  61.5 0.8 copy-start.8
  79.6 0.8 copy-start.4
  80.4 21.0 %all-to-all-start.1 = ((bf16[8,4,8,1024]{3,2,1,0:T(8,128)(2,1)}), bf16[8,4,8,1024]{3,2,1,0:T(8,128)(2,1)}, u32[]{:S(2)}, u32[]{:S(2)}) async-start(bf16[8,4,8,1024]{3,2,1,0:T(8,128)(2,1)} %copy-done.4), calls=%async_computation.1 | async-start | bytes 1048576 | tf_op jit(solution)/shard_map/all_to_all | solution.py:358
  87.9 13.4 %collective-permute-start.2 = (bf16[256,1024]{1,0:T(8,128)(2,1)}, bf16[256,1024]{1,0:T(8,128)(2,1)}, u32[]{:S(2)}, u32[]{:S(2)}) collective-permute-start(bf16[256,1024]{1,0:T(8,128)(2,1)} %collective-permute-done.1.near), channel_id=1, source_target_pairs={{0,2},{2,0},{4,6},{6,4},{8,10},{10,8},{12,14},{14,12},{1,3},{3,1},... | collective-permute-start | bytes 1572872 | tf_op jit(solution)/shard_map/ppermute | solution.py:28
  109.1 3.8 %copy-start.2 = (bf16[256,1024]{1,0:T(8,128)(2,1)}, bf16[256,1024]{1,0:T(8,128)(2,1)S(1)}, u32[]{:S(2)}) copy-start(bf16[256,1024]{1,0:T(8,128)(2,1)S(1)} %get-tuple-element.26.x_ref) | copy-start | bytes 1572868
  112.9 14.9 %collective-permute-start.14 = (bf16[256,1024]{1,0:T(8,128)(2,1)S(1)}, bf16[256,1024]{1,0:T(8,128)(2,1)S(1)}, u32[]{:S(2)}, u32[]{:S(2)}) collective-permute-start(bf16[256,1024]{1,0:T(8,128)(2,1)S(1)} %get-tuple-element.28), channel_id=1, source_target_pairs={{0,2},{2,0},{4,6},{6,4},{8,10},{10,8},{12,14},{14,12},{1,3},{3,1},... | collective-permute-start | bytes 1572872 | tf_op jit(solution)/shard_map/ppermute | solution.py:28
  113.9 25.1 %collective-permute-start.16 = (bf16[256,1024]{1,0:T(8,128)(2,1)S(1)}, bf16[256,1024]{1,0:T(8,128)(2,1)S(1)}, u32[]{:S(2)}, u32[]{:S(2)}) collective-permute-start(bf16[256,1024]{1,0:T(8,128)(2,1)S(1)} %get-tuple-element.30), channel_id=1, source_target_pairs={{0,2},{2,0},{4,6},{6,4},{8,10},{10,8},{12,14},{14,12},{1,3},{3,1},... | collective-permute-start | bytes 1572872 | tf_op jit(solution)/shard_map/ppermute | solution.py:28
  115.1 1.0 copy-start.3
  124.0 26.3 %collective-permute-start.18 = (bf16[256,1024]{1,0:T(8,128)(2,1)S(1)}, bf16[256,1024]{1,0:T(8,128)(2,1)S(1)}, u32[]{:S(2)}, u32[]{:S(2)}) collective-permute-start(bf16[256,1024]{1,0:T(8,128)(2,1)S(1)} %get-tuple-element.32), channel_id=1, source_target_pairs={{0,2},{2,0},{4,6},{6,4},{8,10},{10,8},{12,14},{14,12},{1,3},{3,1},... | collective-permute-start | bytes 1572872 | tf_op jit(solution)/shard_map/ppermute | solution.py:28
  124.9 31.8 %collective-permute-start.20 = (bf16[256,1024]{1,0:T(8,128)(2,1)S(1)}, bf16[256,1024]{1,0:T(8,128)(2,1)S(1)}, u32[]{:S(2)}, u32[]{:S(2)}) collective-permute-start(bf16[256,1024]{1,0:T(8,128)(2,1)S(1)} %get-tuple-element.34), channel_id=1, source_target_pairs={{0,2},{2,0},{4,6},{6,4},{8,10},{10,8},{12,14},{14,12},{1,3},{3,1},... | collective-permute-start | bytes 1572872 | tf_op jit(solution)/shard_map/ppermute | solution.py:28
  127.8 42.0 %copy-start.6 = (f32[256,1024]{1,0:T(8,128)S(1)}, f32[256,1024]{1,0:T(8,128)}, u32[]{:S(2)}) copy-start(f32[256,1024]{1,0:T(8,128)} %get-tuple-element.37) | copy-start | bytes 3145732
  128.0 31.3 %collective-permute-start.15 = (bf16[256,1024]{1,0:T(8,128)(2,1)S(1)}, bf16[256,1024]{1,0:T(8,128)(2,1)S(1)}, u32[]{:S(2)}, u32[]{:S(2)}) collective-permute-start(bf16[256,1024]{1,0:T(8,128)(2,1)S(1)} %add_convert_fusion.3), channel_id=1, source_target_pairs={{0,8},{2,10},{4,12},{6,14},{8,0},{10,2},{12,4},{14,6},{1,9},{3,11}... | collective-permute-start | bytes 1572872 | tf_op jit(solution)/shard_map/ppermute | solution.py:28
  139.2 30.6 %collective-permute-start.17 = (bf16[256,1024]{1,0:T(8,128)(2,1)S(1)}, bf16[256,1024]{1,0:T(8,128)(2,1)S(1)}, u32[]{:S(2)}, u32[]{:S(2)}) collective-permute-start(bf16[256,1024]{1,0:T(8,128)(2,1)S(1)} %add_convert_fusion.2), channel_id=1, source_target_pairs={{0,4},{2,6},{4,8},{6,10},{8,12},{10,14},{12,0},{14,2},{1,5},{3,7},... | collective-permute-start | bytes 1572872 | tf_op jit(solution)/shard_map/ppermute | solution.py:28
  150.3 20.9 %copy-start.1 = (bf16[512,1024]{1,0:T(8,128)(2,1)S(1)}, bf16[512,1024]{1,0:T(8,128)(2,1)}, u32[]{:S(2)}) copy-start(bf16[512,1024]{1,0:T(8,128)(2,1)} %param.10) | copy-start | bytes 3145732
  150.5 19.4 %collective-permute-start.19 = (bf16[256,1024]{1,0:T(8,128)(2,1)S(1)}, bf16[256,1024]{1,0:T(8,128)(2,1)S(1)}, u32[]{:S(2)}, u32[]{:S(2)}) collective-permute-start(bf16[256,1024]{1,0:T(8,128)(2,1)S(1)} %add_convert_fusion.1), channel_id=1, source_target_pairs={{0,12},{2,14},{4,0},{6,2},{8,4},{10,6},{12,8},{14,10},{1,13},{3,15... | collective-permute-start | bytes 1572872 | tf_op jit(solution)/shard_map/ppermute | solution.py:28

commit v8 on v7

--- a/solution.py
+++ b/solution.py
@@ -13,6 +13,7 @@
 INNER = 2
 DEPTH = 3
 VMEM_LIMIT = 16 * 1024 * 1024
+LARGE_LIMIT = 30 * 1024 * 1024
 IN_SMEM = pl.BlockSpec(memory_space=pltpu.SMEM)
 IN_VMEM = pl.BlockSpec(memory_space=pltpu.VMEM)
 IN_HBM = pl.BlockSpec(memory_space=pltpu.HBM)
@@ -41,7 +42,7 @@
     return blocks
 
 
-def kernel_call(kernel, name, spot, operands, outputs, aliases, scratch, flops, moved_bytes):
+def kernel_call(kernel, name, spot, operands, outputs, aliases, scratch, flops, moved_bytes, limit=VMEM_LIMIT):
     specs, args = zip(*operands)
     args = [
         pltpu.with_memory_space_constraint(arg, pltpu.HBM) if spec is IN_HBM else arg
@@ -55,7 +56,7 @@
         out_shape=list(out_shape),
         input_output_aliases=aliases,
         scratch_shapes=scratch,
-        compiler_params=pltpu.CompilerParams(vmem_limit_bytes=VMEM_LIMIT),
+        compiler_params=pltpu.CompilerParams(vmem_limit_bytes=limit),
         cost_estimate=pl.CostEstimate(flops=flops, bytes_accessed=moved_bytes, transcendentals=0),
         name=name,
     )(spot, *args)
@@ -144,10 +145,15 @@
 def project_kernel(steps, first, last, spot, near, far, gain_ref, inv_ref, w_hbm, *refs):
     refs = list(refs)
     earlier = None if first else refs.pop(0)
-    taps_ref, place_ref, terms_any = (refs.pop(0) for _ in range(3)) if last else (None,) * 3
+    taps_ref, place_ref, terms_hbm, out_hbm = (refs.pop(0) for _ in range(4)) if last else (None,) * 4
     total_ref = refs.pop(0)
     gated_ref = refs.pop(0) if last else None
-    blocks, normed, held, sems, block_sems, extra_sem, *terms_scr = refs
+    shares = []
+    while last and len(refs) > 9:
+        shares.append(refs.pop(0))
+    blocks, normed, held, sems, block_sems, *last_scr = refs
+    if last:
+        terms_ref, out_held, terms_sem, out_sems = last_scr
     _, rows, channels = blocks.shape
     slots, depth, block = held.shape
     chunks = 3 * channels // block
@@ -167,8 +173,14 @@
     for chunk in range(min(slots, chunks)):
         fetch(chunk).start()
     if last:
-        extra = pltpu.make_async_copy(terms_any, terms_scr[0], extra_sem.at[0])
-        extra.start()
+        terms_copy = pltpu.make_async_copy(terms_hbm, terms_ref, terms_sem.at[0])
+        terms_copy.start()
+
+    def fetch_out(index):
+        start = pl.multiple_of(spot[2 + index] * shares[0].shape[1], shares[0].shape[1])
+        columns = pl.ds(start, shares[0].shape[1])
+        return pltpu.make_async_copy(out_hbm.at[:, columns], out_held.at[index], out_sems.at[index])
+
 
     scale = inv_ref[:, :1]
     for flip, copy in enumerate(copies):
@@ -191,19 +203,25 @@
         def _():
             fetch(chunk + slots).start()
 
+        for index in range(len(shares)):
+
+            @pl.when(chunk == index % chunks)
+            def _():
+                fetch_out(index).start()
+
         return carry
 
     lax.fori_loop(0, chunks, one_chunk, 0)
     if not last:
         return
-    extra.wait()
+    terms_copy.wait()
     seqs = rows // steps
     wide = min(256, channels)
 
     def one_gate(chunk, carry):
         start = pl.multiple_of(chunk * wide, wide)
         at = pl.ds(start, wide)
-        history = jnp.dot(place_ref[...], terms_scr[0][:, at], preferred_element_type=jnp.float32)
+        history = jnp.dot(place_ref[...], terms_ref[:, at], preferred_element_type=jnp.float32)
         keys = total_ref[:, pl.ds(pl.multiple_of(channels + start, wide), wide)]
         values = total_ref[:, pl.ds(pl.multiple_of(2 * channels + start, wide), wide)]
         recent = (keys * values).astype(jnp.bfloat16).astype(jnp.float32)
@@ -217,6 +235,15 @@
         return carry
 
     lax.fori_loop(0, channels // wide, one_gate, 0)
+    for index, share_ref in enumerate(shares):
+        fetch_out(index).wait()
+        width = share_ref.shape[1]
+        for start in range(0, width, block):
+            columns = pl.ds(start, min(block, width))
+            share = jnp.dot(
+                gated_ref[...], out_held[index, :, columns], preferred_element_type=jnp.float32
+            )
+            share_ref[:, columns] = share.astype(share_ref.dtype)
 
 
 def projected(spot, pair, gains, inv_rms, w_in, earlier, ends=None):
@@ -236,15 +263,22 @@
         pltpu.VMEM((DEPTH, INNER * channels, block), jnp.bfloat16),
         pltpu.SemaphoreType.DMA((DEPTH,)),
         pltpu.SemaphoreType.DMA((INNER,)),
-        pltpu.SemaphoreType.DMA((1,)),
     ]
     steps = 1
     if last:
-        steps, taps, place, terms = ends
-        operands += [(IN_VMEM, taps), (IN_VMEM, place), (IN_HBM, terms)]
+        steps, taps, place, terms, w_out, targets = ends
+        operands += [(IN_VMEM, taps), (IN_VMEM, place), (IN_HBM, terms), (IN_HBM, w_out)]
         outputs.append((IN_VMEM, jax.ShapeDtypeStruct((rows, channels), jnp.bfloat16)))
-        scratch.append(pltpu.VMEM(terms.shape, jnp.bfloat16))
-    return kernel_call(
+        wide = w_out.shape[1] * channels // w_in.shape[0]
+        outputs += [(IN_VMEM, jax.ShapeDtypeStruct((rows, wide), jnp.bfloat16)) for _ in targets]
+        spot = jnp.concatenate([spot, jnp.stack(targets).astype(jnp.int32)])
+        scratch += [
+            pltpu.VMEM(terms.shape, jnp.bfloat16),
+            pltpu.VMEM((len(targets), channels, wide), jnp.bfloat16),
+            pltpu.SemaphoreType.DMA((1,)),
+            pltpu.SemaphoreType.DMA((len(targets),)),
+        ]
+    out = kernel_call(
         functools.partial(project_kernel, steps, first, last),
         "gated_rows" if last else "projected_part",
         spot,
@@ -254,7 +288,9 @@
         scratch,
         4 * rows * INNER * channels * 3 * channels,
         4 * INNER * channels * 3 * channels,
-    )[-1]
+        LARGE_LIMIT if last else VMEM_LIMIT,
+    )
+    return out[1:] if last else out[0]
 
 
 def share_kernel(spot, x_ref, w_hbm, *refs):
@@ -287,9 +323,9 @@
     return kernel_call(
         share_kernel,
         "output_shares",
-        jnp.stack([which for which, _ in targets]).astype(jnp.int32),
+        jnp.stack(targets).astype(jnp.int32),
         [(IN_VMEM, gated), (IN_HBM, w_out)],
-        [(IN_VMEM, jax.ShapeDtypeStruct((rows, wide), kind)) for _, kind in targets],
+        [(IN_VMEM, jax.ShapeDtypeStruct((rows, wide), jnp.float32)) for _ in targets],
         {},
         [pltpu.VMEM((DEPTH, channels, block), jnp.bfloat16), pltpu.SemaphoreType.DMA((DEPTH,))],
         2 * rows * channels * wide * len(targets),
@@ -319,10 +355,6 @@
     tiny = lax.all_to_all(
         jnp.broadcast_to(tiny[None], (owners, *tiny.shape)), "tensor", 0, 0, tiled=True
     )
-    gain_rows = channels // LANES
-    gains = tiny[:, :gain_rows].reshape(owners, channels)
-    inv_rms = lax.rsqrt(jnp.sum(tiny[:, gain_rows:], axis=0).reshape(tokens) / D + EPSILON)
-    inv_rms = jnp.broadcast_to(inv_rms[:, None], (tokens, LANES))
     own_taps = filters.T
     lag_taps = spread(own_taps)
     streams = spread(after(stream.astype(jnp.bfloat16), own_taps))
@@ -345,12 +377,23 @@
 
     cache = cache_rows.transpose(1, 0, 2)
     near_taps = filters[:, : 2 * steps].T.astype(jnp.float32)
-    terms = sums = None
+    def owner_at(ahead, flip):
+        return (outer + ahead) % outer_size * INNER + (inner + flip) % INNER
+
+    order = sorted(range(outer_size), key=lambda ahead: (ahead == 0, -min(ahead, outer_size - ahead)))
+    first_terms = history_terms(cache, *lag_taps[0][1:], row_lengths, spot_at(0), steps, None)
+    tiny = after(tiny, first_terms)
+    gain_rows = channels // LANES
+    gains = tiny[:, :gain_rows].reshape(owners, channels)
+    inv_rms = lax.rsqrt(jnp.sum(tiny[:, gain_rows:], axis=0).reshape(tokens) / D + EPSILON)
+    inv_rms = jnp.broadcast_to(inv_rms[:, None], (tokens, LANES))
+
+    terms, sums = first_terms, None
     parts = len(streams)
     for index, (back, near, far) in enumerate(lag_taps):
         if index:
             near = after(near, sums)
-        terms = history_terms(cache, near, far, row_lengths, spot_at(-back), steps, terms)
+            terms = history_terms(cache, near, far, row_lengths, spot_at(-back), steps, terms)
         if 2 * index < parts:
             at, *pair = streams[index]
             pair[0] = after(pair[0], terms)
@@ -359,23 +402,17 @@
     terms = terms.reshape(owners * steps * rows, channels)
     for index in range((parts + 1) // 2, parts):
         at, *pair = streams[index]
-        ends = (steps, near_taps, place, terms) if index == parts - 1 else None
+        ends = None
+        if index == parts - 1:
+            targets = [owner_at(ahead, 1) for ahead in order]
+            ends = (steps, near_taps, place, terms, w_out, targets)
         sums = projected(spot_at(-at), pair, gains, inv_rms, w_in, sums, ends)
-    gated = sums
-
-    def owner_at(ahead, flip):
-        return (outer + ahead) % outer_size * INNER + (inner + flip) % INNER
-
-    order = sorted(range(outer_size), key=lambda ahead: (ahead == 0, -min(ahead, outer_size - ahead)))
-    targets = [(owner_at(ahead, 1), jnp.bfloat16) for ahead in order]
-    targets += [(owner_at(ahead, 0), jnp.float32) for ahead in order]
-    shares = list(output_shares(targets[:2], gated, w_out, owners))
-    across = [moved(share, 0, 1) for share in shares]
-    for start in range(2, len(targets), 6):
-        shares += output_shares(targets[start : start + 6], gated, w_out, owners)
-    across += [moved(share, 0, 1) for share in shares[2:outer_size]]
+    gated, *across = sums
+
+    across = [moved(share, 0, 1) for share in across]
+    own_shares = output_shares([owner_at(ahead, 0) for ahead in order], gated, w_out, owners)
     out = stream
-    for ahead, own_share, arrived_share in zip(order, shares[outer_size:], across):
+    for ahead, own_share, arrived_share in zip(order, own_shares, across):
         share = own_share + arrived_share.astype(jnp.float32)
         out = out + (moved(share.astype(jnp.bfloat16), ahead, 0) if ahead else share)
     return out.astype(jnp.bfloat16).reshape(steps, seqs, channels)

time: 174 us -> 189 us (1.086)
  the two profiles are of different devices: /device:TPU:18 before, /device:TPU:0 now
where the time goes in v8:
time: 189 us; the launch traced here: 188 us
  waiting for transfers between devices  69.3 us (37%)
  Pallas kernels  59.6 us (32%)
  starting transfers between devices  40.9 us (22%)
  local copies, waits for them, and re-layouts  12.4 us (7%)
  other arithmetic  4.11 us (2%)
    ppermute x21, waiting for transfers between devices, moved(): return lax.ppermute(array, 'tensor', pairs)  64.5 us
    pallas_call x9, Pallas kernels, kernel_call(): pl.pallas_call(kernel, in_specs=[IN_SMEM, *specs], out_specs=list(out_spe...  59.6 us
    ppermute x21, starting transfers between devices, moved(): return lax.ppermute(array, 'tensor', pairs)  29.9 us
    unnamed x37, local copies, waits for them, and re-layouts  7.79 us
    all_to_all x1, starting transfers between devices, per_device(): lax.all_to_all(jnp.broadcast_to(tiny[None], (owners, *tiny.shape)), 'tens...  6.61 us
    all_to_all x1, waiting for transfers between devices, per_device(): lax.all_to_all(jnp.broadcast_to(tiny[None], (owners, *tiny.shape)), 'tens...  4.78 us
    all_to_all x1, starting transfers between devices, per_device(): terms = lax.all_to_all(terms, 'tensor', 0, 0, tiled=True)  4.33 us
  transfers between devices with their start and end apart: 23, of which 8 were waited for; matrix products, arithmetic and copies ran while one was open for 5% of the time, Pallas kernels for 25%

profile of v8, /device:TPU:0, one launch (start us, length us, event | category | flops | bytes accessed | tf_op | source)
XLA Modules:
  0.0 188.2 jit_solution(1607965302804865915)
XLA Ops:
  0.0 1.2 copy.24
  1.2 3.0 %collective-permute-start.3 = (bf16[128,1024]{1,0:T(8,128)(2,1)S(1)}, bf16[128,1024]{1,0:T(8,128)(2,1)S(1)}, u32[]{:S(2)}, u32[]{:S(2)}) collective-permute-start(bf16[128,1024]{1,0:T(8,128)(2,1)S(1)} %bitcast.38), channel_id=1, source_target_pairs={{0,2},{2,0},{4,6},{6,4},{8,10},{10,8},{12,14},{14,12},{1,3},{3,1},... | collective-permute-start | bytes 786440 | tf_op jit(solution)/shard_map/ppermute | solution.py:29
  4.2 3.6 %collective-permute-start.12 = (bf16[128,1024]{1,0:T(8,128)(2,1)S(1)}, bf16[128,1024]{1,0:T(8,128)(2,1)}, u32[]{:S(2)}, u32[]{:S(2)}) collective-permute-start(bf16[128,1024]{1,0:T(8,128)(2,1)S(1)} %bitcast.39), channel_id=1, source_target_pairs={{0,12},{2,14},{4,0},{6,2},{8,4},{10,6},{12,8},{14,10},{1,13},{3,15... | collective-permute-start | bytes 786440 | tf_op jit(solution)/shard_map/ppermute | solution.py:29
  7.8 0.8 eq.92
  8.6 1.6 multiply_reduce_fusion
  10.2 0.5 collective-permute-start.7
  10.8 0.6 broadcast_in_dim.21
  11.4 6.6 %all-to-all-start = ((f32[8,10,128]{2,1,0:T(8,128)}), f32[8,10,128]{2,1,0:T(8,128)S(1)}, u32[]{:S(2)}, u32[]{:S(2)}) async-start(f32[8,10,128]{2,1,0:T(8,128)} %broadcast_in_dim.21), calls=%async_computation | async-start | bytes 131072 | tf_op jit(solution)/shard_map/all_to_all | solution.py:355
  18.0 0.1 reshape.68
  18.1 0.1 pad_add_fusion.1.spot
  18.4 0.2 select_reduce_fusion
  18.8 3.9 %collective-permute-start.4 = (bf16[256,1024]{1,0:T(8,128)(2,1)}, bf16[256,1024]{1,0:T(8,128)(2,1)}, u32[]{:S(2)}, u32[]{:S(2)}) collective-permute-start(bf16[256,1024]{1,0:T(8,128)(2,1)} %get-tuple-element.23.near), channel_id=1, source_target_pairs={{0,12},{2,14},{4,0},{6,2},{8,4},{10,6},{12,8},{14,10},{1,13},{3,15... | collective-permute-start | bytes 1572872 | tf_op jit(solution)/shard_map/ppermute | solution.py:29
  22.7 4.9 %history_terms.4.refs_0_ = bf16[8,4,8,1024]{3,2,1,0:T(8,128)(2,1)S(1)} custom-call(s32[2]{0:T(128)S(1)} %pad_add_fusion.1.spot, s32[8,128]{1,0:T(8,128)S(1)} %broadcast_in_dim.24.lengths_ref, bf16[128,1024]{1,0:T(8,128)(2,1)S(1)} %bitcast.41, bf16[128,1024]{1,0:T(8,128)(2,1)S(1)} %collective-permute-done.3.far_ref, bf16[127,8,8192]{2,1,0:T(8,128)(2,1)} %bitcast.43), custom_call_target="tpu_custom_call" | custom-call | flops 4993843200 | bytes 4161536 | tf_op jit(solution)/shard_map/history_terms/pallas_call | solution.py:52
  27.7 0.8 copy-done.4
  28.5 4.8 %all-to-all-done = f32[8,10,128]{2,1,0:T(8,128)S(1)} async-done(((f32[8,10,128]{2,1,0:T(8,128)}), f32[8,10,128]{2,1,0:T(8,128)S(1)}, u32[]{:S(2)}, u32[]{:S(2)}) %all-to-all-start) | async-done | bytes 40992 | tf_op jit(solution)/shard_map/all_to_all | solution.py:355
  33.3 1.0 collective-permute-start.8
  34.3 1.5 collective-permute-start.10
  35.9 1.0 collective-permute-start.13
  36.9 1.0 collective-permute-start.9
  37.9 0.1 broadcast_in_dim.25.inv_ref
  38.0 6.9 %projected_part.3.refs_0_ = f32[256,3072]{1,0:T(8,128)S(1)} custom-call(s32[2]{0:T(128)S(1)} %pad_add_fusion.1.spot, bf16[256,1024]{1,0:T(8,128)(2,1)} %get-tuple-element.23.near, bf16[256,1024]{1,0:T(8,128)(2,1)} %copy-done.12, f32[8,1024]{1,0:T(8,128)S(1)} %bitcast.34, f32[256,128]{1,0:T(8,128)S(1)} %broadcast_in_dim.25.inv_ref, bf16[8192,3072]{1,0:T(8,128)(2,1)} %w_hbm.8), custom_call_target="tpu_custom_call" | custom-call | flops 6442450944 | bytes 25165824 | tf_op jit(solution)/shard_map/projected_part/pallas_call | solution.py:52
  45.0 5.4 %history_terms.5.refs_0_ = bf16[8,4,8,1024]{3,2,1,0:T(8,128)(2,1)S(1)} custom-call(s32[2]{0:T(128)S(1)} %pad_add_fusion.3.spot, s32[8,128]{1,0:T(8,128)S(1)} %broadcast_in_dim.24.lengths_ref, bf16[128,1024]{1,0:T(8,128)(2,1)} %collective-permute-done.6.near_ref, ...), custom_call_target="tpu_custom_call", output_to_operand_aliasing={{}: (5, {})} | custom-call | flops 4993843200 | bytes 4161536 | tf_op jit(solution)/shard_map/history_terms/pallas_call | solution.py:52
  50.3 2.0 %collective-permute-start.1 = (bf16[256,1024]{1,0:T(8,128)(2,1)}, bf16[256,1024]{1,0:T(8,128)(2,1)}, u32[]{:S(2)}, u32[]{:S(2)}) collective-permute-start(bf16[256,1024]{1,0:T(8,128)(2,1)} %collective-permute-done.near), channel_id=1, source_target_pairs={{0,4},{2,6},{4,8},{6,10},{8,12},{10,14},{12,0},{14,2},{1,5},{3,7},... | collective-permute-start | bytes 1572872 | tf_op jit(solution)/shard_map/ppermute | solution.py:29
  52.4 0.8 collective-permute-start.5
  53.2 1.2 collective-permute-start.11
  54.4 5.3 %collective-permute-done.9.far = bf16[256,1024]{1,0:T(8,128)(2,1)S(1)} collective-permute-done((bf16[256,1024]{1,0:T(8,128)(2,1)}, bf16[256,1024]{1,0:T(8,128)(2,1)S(1)}, u32[]{:S(2)}, u32[]{:S(2)}) %collective-permute-start.9) | collective-permute-done | bytes 524320 | tf_op jit(solution)/shard_map/ppermute | solution.py:29
  59.7 0.8 copy-done.13
  60.5 6.9 %projected_part.4.refs_0_ = f32[256,3072]{1,0:T(8,128)S(1)} custom-call(s32[2]{0:T(128)S(1)} %pad_add_fusion.3.spot, bf16[256,1024]{1,0:T(8,128)(2,1)} %collective-permute-done.near, bf16[256,1024]{1,0:T(8,128)(2,1)} %copy-done.13, f32[8,1024]{1,0:T(8,128)S(1)} %bitcast.35, f32[256,128]{1,0:T(8,128)S(1)} %broadcast_in_dim.25.inv_ref, ...), custom_call_target="tpu_custom_call", output_to_operand_aliasing={{}: (6, {})} | custom-call | flops 6442450944 | bytes 25165824 | tf_op jit(solution)/shard_map/projected_part/pallas_call | solution.py:52
  67.4 5.4 %history_terms.6.refs_0_ = bf16[8,4,8,1024]{3,2,1,0:T(8,128)(2,1)S(1)} custom-call(s32[2]{0:T(128)S(1)} %pad_add_fusion.2.spot, s32[8,128]{1,0:T(8,128)S(1)} %broadcast_in_dim.24.lengths_ref, bf16[128,1024]{1,0:T(8,128)(2,1)} %collective-permute-done.12.near_ref, ...), custom_call_target="tpu_custom_call", output_to_operand_aliasing={{}: (5, {})} | custom-call | flops 4993843200 | bytes 4161536 | tf_op jit(solution)/shard_map/history_terms/pallas_call | solution.py:52
  72.8 1.0 collective-permute-done.11.far_ref
  73.7 5.0 %history_terms.7 = bf16[8,4,8,1024]{3,2,1,0:T(8,128)(2,1)S(1)} custom-call(s32[2]{0:T(128)S(1)} %pad_add_fusion.4.spot, s32[8,128]{1,0:T(8,128)S(1)} %broadcast_in_dim.24.lengths_ref, bf16[128,1024]{1,0:T(8,128)(2,1)S(1)} %collective-permute-done.10.near_ref, bf16[128,1024]{1,0:T(8,128)(2,1)S(1)} %collective-permute-done.11.far_ref, ...), custom_call_target="tpu_custom_call", output_to_operand_aliasing={{}: (5, {})} | custom-call | flops 4993843200 | bytes 4161536 | tf_op jit(solution)/shard_map/history_terms/pallas_call | solution.py:52
  78.7 0.8 copy-done.6
  79.5 4.3 %all-to-all-start.1 = ((bf16[8,4,8,1024]{3,2,1,0:T(8,128)(2,1)}), bf16[8,4,8,1024]{3,2,1,0:T(8,128)(2,1)}, u32[]{:S(2)}, u32[]{:S(2)}) async-start(bf16[8,4,8,1024]{3,2,1,0:T(8,128)(2,1)} %copy-done.6), calls=%async_computation.1 | async-start | bytes 1048576 | tf_op jit(solution)/shard_map/all_to_all | solution.py:401
  83.8 0.9 and_convert_fusion
  84.7 1.8 reshape.72
  86.6 1.0 copy.26.refs_2_
  87.6 0.1 concatenate.6.spot
  87.7 0.7 convert_bitcast_fusion.refs_1_
  88.4 1.7 collective-permute-start.2
  90.1 6.9 %projected_part.5.refs_0_ = f32[256,3072]{1,0:T(8,128)S(1)} custom-call(s32[2]{0:T(128)S(1)} %pad_add_fusion.2.spot, bf16[256,1024]{1,0:T(8,128)(2,1)} %collective-permute-done.4.near, bf16[256,1024]{1,0:T(8,128)(2,1)} %collective-permute-done.5.far, f32[8,1024]{1,0:T(8,128)S(1)} %bitcast.36, ...), custom_call_target="tpu_custom_call", output_to_operand_aliasing={{}: (6, {})} | custom-call | flops 6442450944 | bytes 25165824 | tf_op jit(solution)/shard_map/projected_part/pallas_call | solution.py:52
  97.0 5.7 %collective-permute-done.2.far = bf16[256,1024]{1,0:T(8,128)(2,1)} collective-permute-done((bf16[256,1024]{1,0:T(8,128)(2,1)}, bf16[256,1024]{1,0:T(8,128)(2,1)}, u32[]{:S(2)}, u32[]{:S(2)}) %collective-permute-start.2) | collective-permute-done | bytes 524320 | tf_op jit(solution)/shard_map/ppermute | solution.py:29
  102.7 12.4 %gated_rows.1 = (f32[256,3072]{1,0:T(8,128)S(1)}, bf16[256,1024]{1,0:T(8,128)(2,1)S(1)}, bf16[256,1024]{1,0:T(8,128)(2,1)S(1)}, bf16[256,1024]{1,0:T(8,128)(2,1)...) custom-call(s32[6]{0:T(128)S(1)} %concatenate.6.spot, ...), custom_call_target="tpu_custom_call", output_to_operand_aliasing={{0}: (6, {})} | custom-call | flops 6442450944 | bytes 25165824 | tf_op jit(solution)/shard_map/gated_rows/pallas_call | solution.py:52
  115.1 0.8 copy-done.2
  115.9 0.8 copy-done.8
  116.7 0.8 copy-done.9
  117.5 0.8 copy-done.10
  118.3 0.6 collective-permute-start.18
  118.9 1.4 collective-permute-start.16
  120.3 0.1 pad_add_fusion.spot
  120.4 0.6 collective-permute-start.20
  121.0 1.4 collective-permute-start.14
  122.4 1.0 copy-done.3
  123.5 5.8 %output_shares.1 = (f32[256,1024]{1,0:T(8,128)S(1)}, f32[256,1024]{1,0:T(8,128)S(1)}, f32[256,1024]{1,0:T(8,128)S(1)}, f32[256,1024]{1,0:T(8,128)S(1)}) custom-call(s32[4]{0:T(128)S(1)} %pad_add_fusion.spot, bf16[256,1024]{1,0:T(8,128)(2,1)S(1)} %copy-done.3, bf16[1024,8192]{1,0:T(8,128)(2,1)} %w_hbm.9), custom_call_target="tpu_custom_call" | custom-call | flops 2147483648 | bytes 8388608 | tf_op jit(solution)/shard_map/output_shares/pallas_call | solution.py:52
  129.3 4.1 %collective-permute-done.18 = bf16[256,1024]{1,0:T(8,128)(2,1)S(1)} collective-permute-done((bf16[256,1024]{1,0:T(8,128)(2,1)}, bf16[256,1024]{1,0:T(8,128)(2,1)S(1)}, u32[]{:S(2)}, u32[]{:S(2)}) %collective-permute-start.18) | collective-permute-done | bytes 524320 | tf_op jit(solution)/shard_map/ppermute | solution.py:29
  133.4 0.2 add_convert_fusion.1
  133.5 2.1 %collective-permute-start.19 = (bf16[256,1024]{1,0:T(8,128)(2,1)S(1)}, bf16[256,1024]{1,0:T(8,128)(2,1)S(1)}, u32[]{:S(2)}, u32[]{:S(2)}) collective-permute-start(bf16[256,1024]{1,0:T(8,128)(2,1)S(1)} %add_convert_fusion.1), channel_id=1, source_target_pairs={{0,12},{2,14},{4,0},{6,2},{8,4},{10,6},{12,8},{14,10},{1,13},{3,15... | collective-permute-start | bytes 1572872 | tf_op jit(solution)/shard_map/ppermute | solution.py:29
  135.6 9.0 %collective-permute-done.16 = bf16[256,1024]{1,0:T(8,128)(2,1)S(1)} collective-permute-done((bf16[256,1024]{1,0:T(8,128)(2,1)}, bf16[256,1024]{1,0:T(8,128)(2,1)S(1)}, u32[]{:S(2)}, u32[]{:S(2)}) %collective-permute-start.16) | collective-permute-done | bytes 524320 | tf_op jit(solution)/shard_map/ppermute | solution.py:29
  144.6 0.2 add_convert_fusion.2
  144.8 0.8 collective-permute-start.17
  145.6 18.7 %collective-permute-done.14 = bf16[256,1024]{1,0:T(8,128)(2,1)S(1)} collective-permute-done((bf16[256,1024]{1,0:T(8,128)(2,1)}, bf16[256,1024]{1,0:T(8,128)(2,1)S(1)}, u32[]{:S(2)}, u32[]{:S(2)}) %collective-permute-start.14) | collective-permute-done | bytes 524320 | tf_op jit(solution)/shard_map/ppermute | solution.py:29
  164.3 0.2 add_convert_fusion.3
  164.5 1.6 collective-permute-start.15
  166.1 20.8 %collective-permute-done.15 = bf16[256,1024]{1,0:T(8,128)(2,1)S(1)} collective-permute-done((bf16[256,1024]{1,0:T(8,128)(2,1)S(1)}, bf16[256,1024]{1,0:T(8,128)(2,1)S(1)}, u32[]{:S(2)}, u32[]{:S(2)}) %collective-permute-start.15) | collective-permute-done | bytes 524320 | tf_op jit(solution)/shard_map/ppermute | solution.py:29
  186.9 1.3 add_convert_fusion
  (57 shorter events, 0.5 us)
Async XLA Ops:
  0.0 8.6 %copy-start = (bf16[512,1024]{1,0:T(8,128)(2,1)S(1)}, bf16[512,1024]{1,0:T(8,128)(2,1)}, u32[]{:S(2)}) copy-start(bf16[512,1024]{1,0:T(8,128)(2,1)} %param.10) | copy-start | bytes 3145732
  0.0 10.7 %copy-start.14 = (bf16[1024]{0:T(1024)(128)(2,1)S(1)}, bf16[1024]{0:T(1024)(128)(2,1)}, u32[]{:S(2)}) copy-start(bf16[1024]{0:T(1024)(128)(2,1)} %param.11) | copy-start | bytes 6148
  0.0 18.0 %copy-start.15 = (s32[128]{0:T(128)S(1)}, s32[128]{0:T(128)}, u32[]{:S(2)}) copy-start(s32[128]{0:T(128)} %param.16) | copy-start | bytes 1540
  0.0 18.4 %copy-start.16 = (s32[64]{0:T(128)S(1)}, s32[64]{0:T(128)}, u32[]{:S(2)}) copy-start(s32[64]{0:T(128)} %param.17) | copy-start | bytes 772
  1.2 26.5 %copy-start.7 = (bf16[1024,128]{0,1:T(8,128)(2,1)}, bf16[1024,128]{0,1:T(8,128)(2,1)S(1)}, u32[]{:S(2)}) copy-start(bf16[1024,128]{0,1:T(8,128)(2,1)S(1)} %copy.24) | copy-start | bytes 786436
  1.2 17.5 %collective-permute-start.3 = (bf16[128,1024]{1,0:T(8,128)(2,1)S(1)}, bf16[128,1024]{1,0:T(8,128)(2,1)S(1)}, u32[]{:S(2)}, u32[]{:S(2)}) collective-permute-start(bf16[128,1024]{1,0:T(8,128)(2,1)S(1)} %bitcast.38), channel_id=1, source_target_pairs={{0,2},{2,0},{4,6},{6,4},{8,10},{10,8},{12,14},{14,12},{1,3},{3,1},... | collective-permute-start | bytes 786440 | tf_op jit(solution)/shard_map/ppermute | solution.py:29
  4.2 30.1 %collective-permute-start.12 = (bf16[128,1024]{1,0:T(8,128)(2,1)S(1)}, bf16[128,1024]{1,0:T(8,128)(2,1)}, u32[]{:S(2)}, u32[]{:S(2)}) collective-permute-start(bf16[128,1024]{1,0:T(8,128)(2,1)S(1)} %bitcast.39), channel_id=1, source_target_pairs={{0,12},{2,14},{4,0},{6,2},{8,4},{10,6},{12,8},{14,10},{1,13},{3,15... | collective-permute-start | bytes 786440 | tf_op jit(solution)/shard_map/ppermute | solution.py:29
  7.8 25.4 %collective-permute-start.6 = (bf16[128,1024]{1,0:T(8,128)(2,1)S(1)}, bf16[128,1024]{1,0:T(8,128)(2,1)}, u32[]{:S(2)}, u32[]{:S(2)}) collective-permute-start(bf16[128,1024]{1,0:T(8,128)(2,1)S(1)} %bitcast.40), channel_id=1, source_target_pairs={{0,4},{2,6},{4,8},{6,10},{8,12},{10,14},{12,0},{14,2},{1,5},{3,7},... | collective-permute-start | bytes 786440 | tf_op jit(solution)/shard_map/ppermute | solution.py:29
  10.2 25.6 %collective-permute-start = (bf16[256,1024]{1,0:T(8,128)(2,1)}, bf16[256,1024]{1,0:T(8,128)(2,1)}, u32[]{:S(2)}, u32[]{:S(2)}) collective-permute-start(bf16[256,1024]{1,0:T(8,128)(2,1)} %get-tuple-element.23.near), channel_id=1, source_target_pairs={{0,4},{2,6},{4,8},{6,10},{8,12},{10,14},{12,0},{14,2},{1,5},{3,7},... | collective-permute-start | bytes 1572872 | tf_op jit(solution)/shard_map/ppermute | solution.py:29
  10.2 26.7 %collective-permute-start.7 = (bf16[256,1024]{1,0:T(8,128)(2,1)}, bf16[256,1024]{1,0:T(8,128)(2,1)S(1)}, u32[]{:S(2)}, u32[]{:S(2)}) collective-permute-start(bf16[256,1024]{1,0:T(8,128)(2,1)} %get-tuple-element.23.near), channel_id=1, source_target_pairs={{0,2},{2,0},{4,6},{6,4},{8,10},{10,8},{12,14},{14,12},{1,3},{3,1},... | collective-permute-start | bytes 1572872 | tf_op jit(solution)/shard_map/ppermute | solution.py:29
  11.4 21.9 %all-to-all-start = ((f32[8,10,128]{2,1,0:T(8,128)}), f32[8,10,128]{2,1,0:T(8,128)S(1)}, u32[]{:S(2)}, u32[]{:S(2)}) async-start(f32[8,10,128]{2,1,0:T(8,128)} %broadcast_in_dim.21), calls=%async_computation | async-start | bytes 131072 | tf_op jit(solution)/shard_map/all_to_all | solution.py:355
  18.8 33.6 %collective-permute-start.4 = (bf16[256,1024]{1,0:T(8,128)(2,1)}, bf16[256,1024]{1,0:T(8,128)(2,1)}, u32[]{:S(2)}, u32[]{:S(2)}) collective-permute-start(bf16[256,1024]{1,0:T(8,128)(2,1)} %get-tuple-element.23.near), channel_id=1, source_target_pairs={{0,12},{2,14},{4,0},{6,2},{8,4},{10,6},{12,8},{14,10},{1,13},{3,15... | collective-permute-start | bytes 1572872 | tf_op jit(solution)/shard_map/ppermute | solution.py:29
  27.7 0.8 copy-start.4
  33.3 11.6 %collective-permute-start.8 = (bf16[128,1024]{1,0:T(8,128)(2,1)}, bf16[128,1024]{1,0:T(8,128)(2,1)S(1)}, u32[]{:S(2)}, u32[]{:S(2)}) collective-permute-start(bf16[128,1024]{1,0:T(8,128)(2,1)} %collective-permute-done.6.near_ref), channel_id=1, source_target_pairs={{0,2},{2,0},{4,6},{6,4},{8,10},{10,8},{12,14},{14,12},{1,3},{3,1},... | collective-permute-start | bytes 786440 | tf_op jit(solution)/shard_map/ppermute | solution.py:29
  34.3 18.8 %collective-permute-start.10 = (bf16[128,1024]{1,0:T(8,128)(2,1)}, bf16[128,1024]{1,0:T(8,128)(2,1)S(1)}, u32[]{:S(2)}, u32[]{:S(2)}) collective-permute-start(bf16[128,1024]{1,0:T(8,128)(2,1)} %collective-permute-done.6.near_ref), channel_id=1, source_target_pairs={{0,4},{2,6},{4,8},{6,10},{8,12},{10,14},{12,0},{14,2},{1,5},{3,7},... | collective-permute-start | bytes 786440 | tf_op jit(solution)/shard_map/ppermute | solution.py:29
  35.9 31.5 %collective-permute-start.13 = (bf16[128,1024]{1,0:T(8,128)(2,1)}, bf16[128,1024]{1,0:T(8,128)(2,1)S(1)}, u32[]{:S(2)}, u32[]{:S(2)}) collective-permute-start(bf16[128,1024]{1,0:T(8,128)(2,1)} %collective-permute-done.12.near_ref), channel_id=1, source_target_pairs={{0,2},{2,0},{4,6},{6,4},{8,10},{10,8},{12,14},{14,12},{1,3},{3,1},... | collective-permute-start | bytes 786440 | tf_op jit(solution)/shard_map/ppermute | solution.py:29
  36.9 1.0 copy-start.12
  36.9 22.8 %collective-permute-start.9 = (bf16[256,1024]{1,0:T(8,128)(2,1)}, bf16[256,1024]{1,0:T(8,128)(2,1)S(1)}, u32[]{:S(2)}, u32[]{:S(2)}) collective-permute-start(bf16[256,1024]{1,0:T(8,128)(2,1)} %collective-permute-done.near), channel_id=1, source_target_pairs={{0,2},{2,0},{4,6},{6,4},{8,10},{10,8},{12,14},{14,12},{1,3},{3,1},... | collective-permute-start | bytes 1572872 | tf_op jit(solution)/shard_map/ppermute | solution.py:29
  38.0 6.9 %copy-start.5 = (bf16[8,4,8,1024]{3,2,1,0:T(8,128)(2,1)S(1)}, bf16[8,4,8,1024]{3,2,1,0:T(8,128)(2,1)}, u32[]{:S(2)}) copy-start(bf16[8,4,8,1024]{3,2,1,0:T(8,128)(2,1)} %copy-done.4) | copy-start | bytes 1572868
  50.3 38.1 %collective-permute-start.1 = (bf16[256,1024]{1,0:T(8,128)(2,1)}, bf16[256,1024]{1,0:T(8,128)(2,1)}, u32[]{:S(2)}, u32[]{:S(2)}) collective-permute-start(bf16[256,1024]{1,0:T(8,128)(2,1)} %collective-permute-done.near), channel_id=1, source_target_pairs={{0,4},{2,6},{4,8},{6,10},{8,12},{10,14},{12,0},{14,2},{1,5},{3,7},... | collective-permute-start | bytes 1572872 | tf_op jit(solution)/shard_map/ppermute | solution.py:29
  52.4 37.7 %collective-permute-start.5 = (bf16[256,1024]{1,0:T(8,128)(2,1)}, bf16[256,1024]{1,0:T(8,128)(2,1)}, u32[]{:S(2)}, u32[]{:S(2)}) collective-permute-start(bf16[256,1024]{1,0:T(8,128)(2,1)} %collective-permute-done.4.near), channel_id=1, source_target_pairs={{0,2},{2,0},{4,6},{6,4},{8,10},{10,8},{12,14},{14,12},{1,3},{3,1},... | collective-permute-start | bytes 1572872 | tf_op jit(solution)/shard_map/ppermute | solution.py:29
  53.2 20.6 %collective-permute-start.11 = (bf16[128,1024]{1,0:T(8,128)(2,1)S(1)}, bf16[128,1024]{1,0:T(8,128)(2,1)S(1)}, u32[]{:S(2)}, u32[]{:S(2)}) collective-permute-start(bf16[128,1024]{1,0:T(8,128)(2,1)S(1)} %collective-permute-done.10.near_ref), channel_id=1, source_target_pairs={{0,2},{2,0},{4,6},{6,4},{8,10},{10,8},{12,14},{14,12},{1,3},{3,1},... | collective-permute-start | bytes 786440 | tf_op jit(solution)/shard_map/ppermute | solution.py:29
  59.7 0.8 copy-start.13
  78.7 0.8 copy-start.6
  79.5 23.2 %all-to-all-start.1 = ((bf16[8,4,8,1024]{3,2,1,0:T(8,128)(2,1)}), bf16[8,4,8,1024]{3,2,1,0:T(8,128)(2,1)}, u32[]{:S(2)}, u32[]{:S(2)}) async-start(bf16[8,4,8,1024]{3,2,1,0:T(8,128)(2,1)} %copy-done.6), calls=%async_computation.1 | async-start | bytes 1048576 | tf_op jit(solution)/shard_map/all_to_all | solution.py:401
  88.4 14.3 %collective-permute-start.2 = (bf16[256,1024]{1,0:T(8,128)(2,1)}, bf16[256,1024]{1,0:T(8,128)(2,1)}, u32[]{:S(2)}, u32[]{:S(2)}) collective-permute-start(bf16[256,1024]{1,0:T(8,128)(2,1)} %collective-permute-done.1.near), channel_id=1, source_target_pairs={{0,2},{2,0},{4,6},{6,4},{8,10},{10,8},{12,14},{14,12},{1,3},{3,1},... | collective-permute-start | bytes 1572872 | tf_op jit(solution)/shard_map/ppermute | solution.py:29
  115.1 0.8 copy-start.2
  115.9 0.8 copy-start.8
  116.7 0.8 copy-start.9
  117.5 0.8 copy-start.10
  118.3 15.1 %collective-permute-start.18 = (bf16[256,1024]{1,0:T(8,128)(2,1)}, bf16[256,1024]{1,0:T(8,128)(2,1)S(1)}, u32[]{:S(2)}, u32[]{:S(2)}) collective-permute-start(bf16[256,1024]{1,0:T(8,128)(2,1)} %get-tuple-element.34), channel_id=1, source_target_pairs={{0,2},{2,0},{4,6},{6,4},{8,10},{10,8},{12,14},{14,12},{1,3},{3,1},... | collective-permute-start | bytes 1572872 | tf_op jit(solution)/shard_map/ppermute | solution.py:29
  118.9 25.7 %collective-permute-start.16 = (bf16[256,1024]{1,0:T(8,128)(2,1)}, bf16[256,1024]{1,0:T(8,128)(2,1)S(1)}, u32[]{:S(2)}, u32[]{:S(2)}) collective-permute-start(bf16[256,1024]{1,0:T(8,128)(2,1)} %copy-done.10), channel_id=1, source_target_pairs={{0,2},{2,0},{4,6},{6,4},{8,10},{10,8},{12,14},{14,12},{1,3},{3,1},... | collective-permute-start | bytes 1572872 | tf_op jit(solution)/shard_map/ppermute | solution.py:29
  120.4 45.7 %collective-permute-start.20 = (bf16[256,1024]{1,0:T(8,128)(2,1)}, bf16[256,1024]{1,0:T(8,128)(2,1)S(1)}, u32[]{:S(2)}, u32[]{:S(2)}) collective-permute-start(bf16[256,1024]{1,0:T(8,128)(2,1)} %copy-done.8), channel_id=1, source_target_pairs={{0,2},{2,0},{4,6},{6,4},{8,10},{10,8},{12,14},{14,12},{1,3},{3,1},... | collective-permute-start | bytes 1572872 | tf_op jit(solution)/shard_map/ppermute | solution.py:29
  121.0 43.3 %collective-permute-start.14 = (bf16[256,1024]{1,0:T(8,128)(2,1)}, bf16[256,1024]{1,0:T(8,128)(2,1)S(1)}, u32[]{:S(2)}, u32[]{:S(2)}) collective-permute-start(bf16[256,1024]{1,0:T(8,128)(2,1)} %copy-done.9), channel_id=1, source_target_pairs={{0,2},{2,0},{4,6},{6,4},{8,10},{10,8},{12,14},{14,12},{1,3},{3,1},... | collective-permute-start | bytes 1572872 | tf_op jit(solution)/shard_map/ppermute | solution.py:29
  122.4 1.0 copy-start.3
  133.4 53.5 %copy-start.11 = (f32[256,1024]{1,0:T(8,128)S(1)}, f32[256,1024]{1,0:T(8,128)}, u32[]{:S(2)}) copy-start(f32[256,1024]{1,0:T(8,128)} %get-tuple-element.39) | copy-start | bytes 3145732
  133.5 32.5 %collective-permute-start.19 = (bf16[256,1024]{1,0:T(8,128)(2,1)S(1)}, bf16[256,1024]{1,0:T(8,128)(2,1)S(1)}, u32[]{:S(2)}, u32[]{:S(2)}) collective-permute-start(bf16[256,1024]{1,0:T(8,128)(2,1)S(1)} %add_convert_fusion.1), channel_id=1, source_target_pairs={{0,12},{2,14},{4,0},{6,2},{8,4},{10,6},{12,8},{14,10},{1,13},{3,15... | collective-permute-start | bytes 1572872 | tf_op jit(solution)/shard_map/ppermute | solution.py:29
  144.8 21.3 %collective-permute-start.17 = (bf16[256,1024]{1,0:T(8,128)(2,1)S(1)}, bf16[256,1024]{1,0:T(8,128)(2,1)S(1)}, u32[]{:S(2)}, u32[]{:S(2)}) collective-permute-start(bf16[256,1024]{1,0:T(8,128)(2,1)S(1)} %add_convert_fusion.2), channel_id=1, source_target_pairs={{0,4},{2,6},{4,8},{6,10},{8,12},{10,14},{12,0},{14,2},{1,5},{3,7},... | collective-permute-start | bytes 1572872 | tf_op jit(solution)/shard_map/ppermute | solution.py:29
  164.3 23.8 %copy-start.1 = (bf16[512,1024]{1,0:T(8,128)(2,1)S(1)}, bf16[512,1024]{1,0:T(8,128)(2,1)}, u32[]{:S(2)}) copy-start(bf16[512,1024]{1,0:T(8,128)(2,1)} %param.10) | copy-start | bytes 3145732
  164.5 22.3 %collective-permute-start.15 = (bf16[256,1024]{1,0:T(8,128)(2,1)S(1)}, bf16[256,1024]{1,0:T(8,128)(2,1)S(1)}, u32[]{:S(2)}, u32[]{:S(2)}) collective-permute-start(bf16[256,1024]{1,0:T(8,128)(2,1)S(1)} %add_convert_fusion.3), channel_id=1, source_target_pairs={{0,8},{2,10},{4,12},{6,14},{8,0},{10,2},{12,4},{14,6},{1,9},{3,11}... | collective-permute-start | bytes 1572872 | tf_op jit(solution)/shard_map/ppermute | solution.py:29

commit v9 on v7

--- a/solution.py
+++ b/solution.py
@@ -13,6 +13,7 @@
 INNER = 2
 DEPTH = 3
 VMEM_LIMIT = 16 * 1024 * 1024
+SHARE_LIMIT = 28 * 1024 * 1024
 IN_SMEM = pl.BlockSpec(memory_space=pltpu.SMEM)
 IN_VMEM = pl.BlockSpec(memory_space=pltpu.VMEM)
 IN_HBM = pl.BlockSpec(memory_space=pltpu.HBM)
@@ -257,44 +258,43 @@
     )[-1]
 
 
-def share_kernel(spot, x_ref, w_hbm, *refs):
-    *outs, held, sems = refs
-    wide = outs[0].shape[1]
-    slots, _, block = held.shape
-    parts = wide // block
-    chunks = len(outs) * parts
-
-    def fetch(chunk):
-        start = pl.multiple_of(spot[chunk // parts] * wide + chunk % parts * block, block)
-        slot = chunk % slots
-        return pltpu.make_async_copy(w_hbm.at[:, pl.ds(start, block)], held.at[slot], sems.at[slot])
-
-    for chunk in range(min(slots, chunks)):
-        fetch(chunk).start()
-    for chunk in range(chunks):
-        fetch(chunk).wait()
-        out_ref = outs[chunk // parts]
-        share = jnp.dot(x_ref[...], held[chunk % slots], preferred_element_type=jnp.float32)
-        out_ref[:, pl.ds(chunk % parts * block, block)] = share.astype(out_ref.dtype)
-        if chunk + slots < chunks:
-            fetch(chunk + slots).start()
-
-
-def output_shares(targets, gated, w_out, owners):
+def share_kernel(spot, x_ref, w_ref, *refs):
+    share = jnp.dot(x_ref[...], w_ref[...], preferred_element_type=jnp.float32)
+    if len(refs) > 1:
+        share += refs[0][...].astype(jnp.float32)
+    refs[-1][...] = share.astype(refs[-1].dtype)
+
+
+def output_share(spot, gated, w_out, owners, arrived=None):
     rows, channels = gated.shape
     wide = w_out.shape[1] // owners
     block = min(512, wide)
-    return kernel_call(
+    blocks = wide // block
+    specs = [
+        pl.BlockSpec((rows, channels), lambda c, _: (0, 0)),
+        pl.BlockSpec((channels, block), lambda c, spot: (0, spot[0] * blocks + c)),
+    ]
+    args = [gated, w_out]
+    if arrived is not None:
+        specs.append(pl.BlockSpec((rows, block), lambda c, _: (0, c)))
+        args.append(arrived)
+    return pl.pallas_call(
         share_kernel,
-        "output_shares",
-        jnp.stack([which for which, _ in targets]).astype(jnp.int32),
-        [(IN_VMEM, gated), (IN_HBM, w_out)],
-        [(IN_VMEM, jax.ShapeDtypeStruct((rows, wide), kind)) for _, kind in targets],
-        {},
-        [pltpu.VMEM((DEPTH, channels, block), jnp.bfloat16), pltpu.SemaphoreType.DMA((DEPTH,))],
-        2 * rows * channels * wide * len(targets),
-        2 * channels * wide * len(targets),
-    )
+        grid_spec=pltpu.PrefetchScalarGridSpec(
+            num_scalar_prefetch=1,
+            grid=(blocks,),
+            in_specs=specs,
+            out_specs=pl.BlockSpec((rows, block), lambda c, _: (0, c)),
+        ),
+        out_shape=jax.ShapeDtypeStruct((rows, wide), jnp.bfloat16),
+        compiler_params=pltpu.CompilerParams(vmem_limit_bytes=SHARE_LIMIT),
+        cost_estimate=pl.CostEstimate(
+            flops=2 * rows * channels * wide,
+            bytes_accessed=2 * channels * wide,
+            transcendentals=0,
+        ),
+        name="output_share",
+    )(spot, *args)
 
 
 def after(array, earlier):
@@ -319,10 +319,6 @@
     tiny = lax.all_to_all(
         jnp.broadcast_to(tiny[None], (owners, *tiny.shape)), "tensor", 0, 0, tiled=True
     )
-    gain_rows = channels // LANES
-    gains = tiny[:, :gain_rows].reshape(owners, channels)
-    inv_rms = lax.rsqrt(jnp.sum(tiny[:, gain_rows:], axis=0).reshape(tokens) / D + EPSILON)
-    inv_rms = jnp.broadcast_to(inv_rms[:, None], (tokens, LANES))
     own_taps = filters.T
     lag_taps = spread(own_taps)
     streams = spread(after(stream.astype(jnp.bfloat16), own_taps))
@@ -345,12 +341,19 @@
 
     cache = cache_rows.transpose(1, 0, 2)
     near_taps = filters[:, : 2 * steps].T.astype(jnp.float32)
-    terms = sums = None
+    first_terms = history_terms(cache, *lag_taps[0][1:], row_lengths, spot_at(0), steps, None)
+    tiny = after(tiny, first_terms)
+    gain_rows = channels // LANES
+    gains = tiny[:, :gain_rows].reshape(owners, channels)
+    inv_rms = lax.rsqrt(jnp.sum(tiny[:, gain_rows:], axis=0).reshape(tokens) / D + EPSILON)
+    inv_rms = jnp.broadcast_to(inv_rms[:, None], (tokens, LANES))
+
+    terms, sums = first_terms, None
     parts = len(streams)
     for index, (back, near, far) in enumerate(lag_taps):
         if index:
             near = after(near, sums)
-        terms = history_terms(cache, near, far, row_lengths, spot_at(-back), steps, terms)
+            terms = history_terms(cache, near, far, row_lengths, spot_at(-back), steps, terms)
         if 2 * index < parts:
             at, *pair = streams[index]
             pair[0] = after(pair[0], terms)
@@ -363,21 +366,17 @@
         sums = projected(spot_at(-at), pair, gains, inv_rms, w_in, sums, ends)
     gated = sums
 
-    def owner_at(ahead, flip):
-        return (outer + ahead) % outer_size * INNER + (inner + flip) % INNER
+    def spot_to(ahead, flip):
+        return ((outer + ahead) % outer_size * INNER + (inner + flip) % INNER)[None].astype(jnp.int32)
 
     order = sorted(range(outer_size), key=lambda ahead: (ahead == 0, -min(ahead, outer_size - ahead)))
-    targets = [(owner_at(ahead, 1), jnp.bfloat16) for ahead in order]
-    targets += [(owner_at(ahead, 0), jnp.float32) for ahead in order]
-    shares = list(output_shares(targets[:2], gated, w_out, owners))
-    across = [moved(share, 0, 1) for share in shares]
-    for start in range(2, len(targets), 6):
-        shares += output_shares(targets[start : start + 6], gated, w_out, owners)
-    across += [moved(share, 0, 1) for share in shares[2:outer_size]]
+    across = {
+        ahead: moved(output_share(spot_to(ahead, 1), gated, w_out, owners), 0, 1) for ahead in order
+    }
     out = stream
-    for ahead, own_share, arrived_share in zip(order, shares[outer_size:], across):
-        share = own_share + arrived_share.astype(jnp.float32)
-        out = out + (moved(share.astype(jnp.bfloat16), ahead, 0) if ahead else share)
+    for ahead in order:
+        share = output_share(spot_to(ahead, 0), gated, w_out, owners, across[ahead])
+        out = out + (moved(share, ahead, 0) if ahead else share).astype(jnp.float32)
     return out.astype(jnp.bfloat16).reshape(steps, seqs, channels)
 
 

time: 174 us -> 182 us (1.046); the launches traced: 171 us -> 181 us
  local copies, waits for them, and re-layouts: 5.89 us -> 39.4 us
  waiting for transfers between devices: 60.3 us -> 36.9 us
  starting transfers between devices: 38.9 us -> 35.2 us
  Pallas kernels: 60.8 us -> 63.2 us
    unnamed x27 -> x51, local copies, waits for them, and re-layouts: 3.84 us -> 34.9 us
    ppermute x21, waiting for transfers between devices: 48.2 us -> 20.3 us  [moved(): return lax.ppermute(array, 'tensor', pairs)]
    pallas_call x0 -> x8, Pallas kernels: none -> 12.9 us  [output_share(): pl.pallas_call(share_kernel, grid_spec=pltpu.PrefetchScalarGridSpec(num_s...]
    pallas_call x10 -> x8, Pallas kernels: 60.8 us -> 50.3 us  [kernel_call(): pl.pallas_call(kernel, in_specs=[IN_SMEM, *specs], out_specs=list(out_spe...]
    all_to_all x1, waiting for transfers between devices: 12.1 us -> 16.6 us  [per_device(): lax.all_to_all(jnp.broadcast_to(tiny[None], (owners, *tiny.shape)), 'tens...]
    ppermute x21, starting transfers between devices: 26.7 us -> 22.4 us  [moved(): return lax.ppermute(array, 'tensor', pairs)]
    convert_element_type x2, local copies, waits for them, and re-layouts: 0.31 us -> 2.85 us  [per_device(): place = place.astype(jnp.bfloat16)]
  transfers between devices with their start and end apart: 23 -> 23, of which waited for: 9 -> 5; matrix products, arithmetic and copies ran while one was open for 3% -> 5% of each run, Pallas kernels for 29% -> 29%
where the time goes in v9:
time: 182 us; the launch traced here: 181 us
  Pallas kernels  63.2 us (35%)
  local copies, waits for them, and re-layouts  39.4 us (22%)
  waiting for transfers between devices  36.9 us (20%)
  starting transfers between devices  35.2 us (19%)
  other arithmetic  4.67 us (3%)
    pallas_call x8, Pallas kernels, kernel_call(): pl.pallas_call(kernel, in_specs=[IN_SMEM, *specs], out_specs=list(out_spe...  50.3 us
    unnamed x51, local copies, waits for them, and re-layouts  34.9 us
    ppermute x21, starting transfers between devices, moved(): return lax.ppermute(array, 'tensor', pairs)  22.4 us
    ppermute x21, waiting for transfers between devices, moved(): return lax.ppermute(array, 'tensor', pairs)  20.3 us
    all_to_all x1, waiting for transfers between devices, per_device(): lax.all_to_all(jnp.broadcast_to(tiny[None], (owners, *tiny.shape)), 'tens...  16.6 us
    pallas_call x8, Pallas kernels, output_share(): pl.pallas_call(share_kernel, grid_spec=pltpu.PrefetchScalarGridSpec(num_s...  12.9 us
    all_to_all x1, starting transfers between devices, per_device(): terms = lax.all_to_all(terms, 'tensor', 0, 0, tiled=True)  7.34 us
    all_to_all x1, starting transfers between devices, per_device(): lax.all_to_all(jnp.broadcast_to(tiny[None], (owners, *tiny.shape)), 'tens...  5.4 us
  transfers between devices with their start and end apart: 23, of which 5 were waited for; matrix products, arithmetic and copies ran while one was open for 5% of the time, Pallas kernels for 29%

profile of v9, /device:TPU:18, one launch (start us, length us, event | category | flops | bytes accessed | tf_op | source)
XLA Modules:
  0.0 181.3 jit_solution(4139875588347717803)
XLA Ops:
  0.0 1.2 copy.24
  1.2 1.6 collective-permute-start.3
  2.8 1.6 collective-permute-start.6
  4.4 0.8 eq.92
  5.1 1.6 multiply_reduce_fusion
  6.8 0.5 collective-permute-start.7
  7.3 0.2 collective-permute-start
  7.5 1.8 collective-permute-start.12
  9.3 0.6 broadcast_in_dim.65
  10.0 5.4 %all-to-all-start = ((f32[8,10,128]{2,1,0:T(8,128)}), f32[8,10,128]{2,1,0:T(8,128)S(1)}, u32[]{:S(2)}, u32[]{:S(2)}) async-start(f32[8,10,128]{2,1,0:T(8,128)} %broadcast_in_dim.65), calls=%async_computation | async-start | bytes 131072 | tf_op jit(solution)/shard_map/all_to_all | solution.py:319
  15.7 0.2 select_reduce_fusion
  16.1 0.6 collective-permute-start.4
  16.8 4.9 %history_terms.4.refs_0_ = bf16[8,4,8,1024]{3,2,1,0:T(8,128)(2,1)S(1)} custom-call(s32[2]{0:T(128)S(1)} %pad_add_fusion.1.spot, s32[8,128]{1,0:T(8,128)S(1)} %broadcast_in_dim.68.lengths_ref, bf16[128,1024]{1,0:T(8,128)(2,1)S(1)} %bitcast.43, bf16[128,1024]{1,0:T(8,128)(2,1)S(1)} %collective-permute-done.3.far_ref, bf16[127,8,8192]{2,1,0:T(8,128)(2,1)} %bitcast.45), custom_call_target="tpu_custom_call" | custom-call | flops 4993843200 | bytes 4161536 | tf_op jit(solution)/shard_map/history_terms/pallas_call | solution.py:52
  21.7 0.8 copy-done.10
  22.5 16.6 %all-to-all-done = f32[8,10,128]{2,1,0:T(8,128)S(1)} async-done(((f32[8,10,128]{2,1,0:T(8,128)}), f32[8,10,128]{2,1,0:T(8,128)S(1)}, u32[]{:S(2)}, u32[]{:S(2)}) %all-to-all-start) | async-done | bytes 40992 | tf_op jit(solution)/shard_map/all_to_all | solution.py:319
  39.1 1.0 collective-permute-start.8
  40.1 2.2 %collective-permute-start.10 = (bf16[128,1024]{1,0:T(8,128)(2,1)}, bf16[128,1024]{1,0:T(8,128)(2,1)S(1)}, u32[]{:S(2)}, u32[]{:S(2)}) collective-permute-start(bf16[128,1024]{1,0:T(8,128)(2,1)} %collective-permute-done.6.near_ref), channel_id=1, source_target_pairs={{0,4},{2,6},{4,8},{6,10},{8,12},{10,14},{12,0},{14,2},{1,5},{3,7},... | collective-permute-start | bytes 786440 | tf_op jit(solution)/shard_map/ppermute | solution.py:29
  42.3 0.9 collective-permute-start.13
  43.2 1.1 collective-permute-start.9
  44.5 6.9 %projected_part.3.refs_0_ = f32[256,3072]{1,0:T(8,128)S(1)} custom-call(s32[2]{0:T(128)S(1)} %pad_add_fusion.1.spot, bf16[256,1024]{1,0:T(8,128)(2,1)} %get-tuple-element.15.near, bf16[256,1024]{1,0:T(8,128)(2,1)} %copy-done.15, f32[8,1024]{1,0:T(8,128)S(1)} %bitcast.36, f32[256,128]{1,0:T(8,128)S(1)} %broadcast_in_dim.69.inv_ref, bf16[8192,3072]{1,0:T(8,128)(2,1)} %w_hbm.7), custom_call_target="tpu_custom_call" | custom-call | flops 6442450944 | bytes 25165824 | tf_op jit(solution)/shard_map/projected_part/pallas_call | solution.py:52
  51.4 5.4 %history_terms.5.refs_0_ = bf16[8,4,8,1024]{3,2,1,0:T(8,128)(2,1)S(1)} custom-call(s32[2]{0:T(128)S(1)} %pad_add_fusion.3.spot, s32[8,128]{1,0:T(8,128)S(1)} %broadcast_in_dim.68.lengths_ref, bf16[128,1024]{1,0:T(8,128)(2,1)} %collective-permute-done.6.near_ref, ...), custom_call_target="tpu_custom_call", output_to_operand_aliasing={{}: (5, {})} | custom-call | flops 4993843200 | bytes 4161536 | tf_op jit(solution)/shard_map/history_terms/pallas_call | solution.py:52
  56.8 0.1 collective-permute-start.1
  56.9 0.9 collective-permute-start.11
  57.8 1.1 collective-permute-start.5
  59.0 1.0 collective-permute-done.9.far
  60.0 0.8 copy-done.16
  60.8 6.9 %projected_part.4.refs_0_ = f32[256,3072]{1,0:T(8,128)S(1)} custom-call(s32[2]{0:T(128)S(1)} %pad_add_fusion.3.spot, bf16[256,1024]{1,0:T(8,128)(2,1)} %collective-permute-done.near, bf16[256,1024]{1,0:T(8,128)(2,1)} %copy-done.16, f32[8,1024]{1,0:T(8,128)S(1)} %bitcast.37, f32[256,128]{1,0:T(8,128)S(1)} %broadcast_in_dim.69.inv_ref, ...), custom_call_target="tpu_custom_call", output_to_operand_aliasing={{}: (6, {})} | custom-call | flops 6442450944 | bytes 25165824 | tf_op jit(solution)/shard_map/projected_part/pallas_call | solution.py:52
  67.7 5.4 %history_terms.6.refs_0_ = bf16[8,4,8,1024]{3,2,1,0:T(8,128)(2,1)S(1)} custom-call(s32[2]{0:T(128)S(1)} %pad_add_fusion.2.spot, s32[8,128]{1,0:T(8,128)S(1)} %broadcast_in_dim.68.lengths_ref, bf16[128,1024]{1,0:T(8,128)(2,1)} %collective-permute-done.12.near_ref, ...), custom_call_target="tpu_custom_call", output_to_operand_aliasing={{}: (5, {})} | custom-call | flops 4993843200 | bytes 4161536 | tf_op jit(solution)/shard_map/history_terms/pallas_call | solution.py:52
  73.1 5.0 %history_terms.7 = bf16[8,4,8,1024]{3,2,1,0:T(8,128)(2,1)S(1)} custom-call(s32[2]{0:T(128)S(1)} %pad_add_fusion.spot, s32[8,128]{1,0:T(8,128)S(1)} %broadcast_in_dim.68.lengths_ref, bf16[128,1024]{1,0:T(8,128)(2,1)S(1)} %collective-permute-done.10.near_ref, bf16[128,1024]{1,0:T(8,128)(2,1)S(1)} %collective-permute-done.11.far_ref, ...), custom_call_target="tpu_custom_call", output_to_operand_aliasing={{}: (5, {})} | custom-call | flops 4993843200 | bytes 4161536 | tf_op jit(solution)/shard_map/history_terms/pallas_call | solution.py:52
  78.1 0.8 copy-done.12
  78.8 7.3 %all-to-all-start.1 = ((bf16[8,4,8,1024]{3,2,1,0:T(8,128)(2,1)}), bf16[8,4,8,1024]{3,2,1,0:T(8,128)(2,1)}, u32[]{:S(2)}, u32[]{:S(2)}) async-start(bf16[8,4,8,1024]{3,2,1,0:T(8,128)(2,1)} %copy-done.12), calls=%async_computation.1 | async-start | bytes 1048576 | tf_op jit(solution)/shard_map/all_to_all | solution.py:361
  86.2 0.9 and_convert_fusion
  87.1 1.9 %reshape.72 = bf16[256,256]{0,1:T(8,128)(2,1)} reshape(bf16[4,64,8,4,8]{1,0,4,3,2:T(4,128)(2,1)} %and_convert_fusion) | data formatting | bytes 262144 | tf_op jit(solution)/shard_map/convert_element_type | solution.py:340
  88.9 1.0 copy.26.refs_2_
  90.0 0.7 convert_bitcast_fusion.refs_1_
  90.7 1.5 collective-permute-start.2
  92.2 6.9 %projected_part.5.refs_0_ = f32[256,3072]{1,0:T(8,128)S(1)} custom-call(s32[2]{0:T(128)S(1)} %pad_add_fusion.2.spot, bf16[256,1024]{1,0:T(8,128)(2,1)} %collective-permute-done.4.near, bf16[256,1024]{1,0:T(8,128)(2,1)} %collective-permute-done.5.far, f32[8,1024]{1,0:T(8,128)S(1)} %bitcast.38, ...), custom_call_target="tpu_custom_call", output_to_operand_aliasing={{}: (6, {})} | custom-call | flops 6442450944 | bytes 25165824 | tf_op jit(solution)/shard_map/projected_part/pallas_call | solution.py:52
  99.1 1.1 collective-permute-done.2.far
  100.2 8.8 %gated_rows.1 = (f32[256,3072]{1,0:T(8,128)S(1)}, bf16[256,1024]{1,0:T(8,128)(2,1)S(1)}) custom-call(s32[2]{0:T(128)S(1)} %pad_add_fusion.spot, bf16[256,1024]{1,0:T(8,128)(2,1)} %collective-permute-done.1.near, bf16[256,1024]{1,0:T(8,128)(2,1)} %collective-permute-done.2.far, f32[8,1024]{1,0:T(8,128)S(1)} %bitcast.39, ...), custom_call_target="tpu_custom_call", output_to_operand_aliasing={{0}: (6, {})} | custom-call | flops 6442450944 | bytes 25165824 | tf_op jit(solution)/shard_map/gated_rows/pallas_call | solution.py:52
  109.1 1.3 slice-done.3
  110.5 1.1 output_share.8
  111.6 1.5 collective-permute-start.14
  113.1 5.8 %copy-done.2 = bf16[1024,8192]{1,0:T(8,128)(2,1)S(1)} copy-done((bf16[1024,8192]{1,0:T(8,128)(2,1)S(1)}, bf16[1024,8192]{1,0:T(8,128)(2,1)}, u32[]{:S(2)}) %copy-start.2) | copy-done | bytes 16777240
  118.9 1.0 copy-done.8
  119.9 1.1 output_share.10
  121.0 0.6 collective-permute-start.16
  121.7 5.8 %copy-done.3 = bf16[1024,8192]{1,0:T(8,128)(2,1)S(1)} copy-done((bf16[1024,8192]{1,0:T(8,128)(2,1)S(1)}, bf16[1024,8192]{1,0:T(8,128)(2,1)}, u32[]{:S(2)}) %copy-start.3) | copy-done | bytes 16777240
  127.4 1.1 output_share.12
  128.5 1.5 collective-permute-start.18
  130.1 5.8 %copy-done.4 = bf16[1024,8192]{1,0:T(8,128)(2,1)S(1)} copy-done((bf16[1024,8192]{1,0:T(8,128)(2,1)S(1)}, bf16[1024,8192]{1,0:T(8,128)(2,1)}, u32[]{:S(2)}) %copy-start.4) | copy-done | bytes 16777240
  135.8 1.1 output_share.14
  137.0 0.6 collective-permute-start.20
  137.6 5.8 %copy-done.5 = bf16[1024,8192]{1,0:T(8,128)(2,1)S(1)} copy-done((bf16[1024,8192]{1,0:T(8,128)(2,1)S(1)}, bf16[1024,8192]{1,0:T(8,128)(2,1)}, u32[]{:S(2)}) %copy-start.5) | copy-done | bytes 16777240
  143.4 2.0 %output_share.9 = bf16[256,1024]{1,0:T(8,128)(2,1)S(1)} custom-call(s32[1]{0:T(128)} %bitcast.spot, bf16[256,1024]{1,0:T(8,128)(2,1)S(1)} %copy-done.9, bf16[1024,8192]{1,0:T(8,128)(2,1)S(1)} %copy-done.5, bf16[256,1024]{1,0:T(8,128)(2,1)} %collective-permute-done.14.refs_0_), custom_call_target="tpu_custom_call" | custom-call | flops 536870912 | bytes 2097152 | tf_op jit(solution)/shard_map/output_share/pallas_call | solution.py:281
  145.3 0.8 collective-permute-start.15
  146.1 2.6 %output_share.11 = bf16[256,1024]{1,0:T(8,128)(2,1)} custom-call(s32[1]{0:T(128)} %bitcast.15.spot, bf16[256,1024]{1,0:T(8,128)(2,1)S(1)} %copy-done.9, bf16[1024,8192]{1,0:T(8,128)(2,1)S(1)} %copy-done.5, bf16[256,1024]{1,0:T(8,128)(2,1)} %collective-permute-done.16.refs_0_), custom_call_target="tpu_custom_call" | custom-call | flops 536870912 | bytes 2097152 | tf_op jit(solution)/shard_map/output_share/pallas_call | solution.py:281
  148.8 1.3 collective-permute-start.17
  150.1 1.8 %output_share.13 = bf16[256,1024]{1,0:T(8,128)(2,1)} custom-call(s32[1]{0:T(128)} %bitcast.17.spot, bf16[256,1024]{1,0:T(8,128)(2,1)S(1)} %copy-done.9, bf16[1024,8192]{1,0:T(8,128)(2,1)S(1)} %copy-done.5, bf16[256,1024]{1,0:T(8,128)(2,1)S(1)} %collective-permute-done.18.refs_0_), custom_call_target="tpu_custom_call" | custom-call | flops 536870912 | bytes 2097152 | tf_op jit(solution)/shard_map/output_share/pallas_call | solution.py:281
  151.9 0.9 collective-permute-start.19
  152.8 5.8 %copy-done.6 = bf16[1024,8192]{1,0:T(8,128)(2,1)S(1)} copy-done((bf16[1024,8192]{1,0:T(8,128)(2,1)S(1)}, bf16[1024,8192]{1,0:T(8,128)(2,1)}, u32[]{:S(2)}) %copy-start.6) | copy-done | bytes 16777240
  158.6 2.1 %output_share.15 = bf16[256,1024]{1,0:T(8,128)(2,1)S(1)} custom-call(s32[1]{0:T(128)} %bitcast.19.spot, bf16[256,1024]{1,0:T(8,128)(2,1)S(1)} %copy-done.9, bf16[1024,8192]{1,0:T(8,128)(2,1)S(1)} %copy-done.6, bf16[256,1024]{1,0:T(8,128)(2,1)} %collective-permute-done.20.refs_0_), custom_call_target="tpu_custom_call" | custom-call | flops 536870912 | bytes 2097152 | tf_op jit(solution)/shard_map/output_share/pallas_call | solution.py:281
  160.7 9.1 %collective-permute-done.15 = bf16[256,1024]{1,0:T(8,128)(2,1)} collective-permute-done((bf16[256,1024]{1,0:T(8,128)(2,1)S(1)}, bf16[256,1024]{1,0:T(8,128)(2,1)}, u32[]{:S(2)}, u32[]{:S(2)}) %collective-permute-start.15) | collective-permute-done | bytes 524320 | tf_op jit(solution)/shard_map/ppermute | solution.py:29
  169.8 9.1 %collective-permute-done.17 = bf16[256,1024]{1,0:T(8,128)(2,1)} collective-permute-done((bf16[256,1024]{1,0:T(8,128)(2,1)}, bf16[256,1024]{1,0:T(8,128)(2,1)}, u32[]{:S(2)}, u32[]{:S(2)}) %collective-permute-start.17) | collective-permute-done | bytes 524320 | tf_op jit(solution)/shard_map/ppermute | solution.py:29
  178.9 2.4 %add_convert_fusion = bf16[256,1024]{1,0:T(8,128)(2,1)} fusion(bf16[256,1024]{1,0:T(8,128)(2,1)S(1)} %output_share.15, bf16[256,1024]{1,0:T(8,128)(2,1)S(1)} %collective-permute-done.19, bf16[256,1024]{1,0:T(8,128)(2,1)} %collective-permute-done.17, f32[256,1024]{1,0:T(8,128)S(1)} %copy-done.14, bf16[256,1024]{1,0:T(8,128)(2,1)} %collective-permute-done.15), kind=kLoop, calls=%fused_computation | loop fusion | flops 2359296 | bytes 3670016 | tf_op jit(solution)/shard_map/convert_element_type | solution.py:380
  (74 shorter events, 0.8 us)
Async XLA Ops:
  0.0 5.1 %copy-start = (bf16[512,1024]{1,0:T(8,128)(2,1)S(1)}, bf16[512,1024]{1,0:T(8,128)(2,1)}, u32[]{:S(2)}) copy-start(bf16[512,1024]{1,0:T(8,128)(2,1)} %param.10) | copy-start | bytes 3145732
  0.0 9.3 %copy-start.17 = (bf16[1024]{0:T(1024)(128)(2,1)S(1)}, bf16[1024]{0:T(1024)(128)(2,1)}, u32[]{:S(2)}) copy-start(bf16[1024]{0:T(1024)(128)(2,1)} %param.11) | copy-start | bytes 6148
  0.0 15.4 %copy-start.18 = (s32[128]{0:T(128)S(1)}, s32[128]{0:T(128)}, u32[]{:S(2)}) copy-start(s32[128]{0:T(128)} %param.16) | copy-start | bytes 1540
  0.0 15.7 %copy-start.19 = (s32[64]{0:T(128)S(1)}, s32[64]{0:T(128)}, u32[]{:S(2)}) copy-start(s32[64]{0:T(128)} %param.17) | copy-start | bytes 772
  1.2 20.5 %copy-start.13 = (bf16[1024,128]{0,1:T(8,128)(2,1)}, bf16[1024,128]{0,1:T(8,128)(2,1)S(1)}, u32[]{:S(2)}) copy-start(bf16[1024,128]{0,1:T(8,128)(2,1)S(1)} %copy.24) | copy-start | bytes 786436
  1.2 14.9 %collective-permute-start.3 = (bf16[128,1024]{1,0:T(8,128)(2,1)S(1)}, bf16[128,1024]{1,0:T(8,128)(2,1)S(1)}, u32[]{:S(2)}, u32[]{:S(2)}) collective-permute-start(bf16[128,1024]{1,0:T(8,128)(2,1)S(1)} %bitcast.40), channel_id=1, source_target_pairs={{0,2},{2,0},{4,6},{6,4},{8,10},{10,8},{12,14},{14,12},{1,3},{3,1},... | collective-permute-start | bytes 786440 | tf_op jit(solution)/shard_map/ppermute | solution.py:29
  2.8 36.3 %collective-permute-start.6 = (bf16[128,1024]{1,0:T(8,128)(2,1)S(1)}, bf16[128,1024]{1,0:T(8,128)(2,1)}, u32[]{:S(2)}, u32[]{:S(2)}) collective-permute-start(bf16[128,1024]{1,0:T(8,128)(2,1)S(1)} %bitcast.41), channel_id=1, source_target_pairs={{0,4},{2,6},{4,8},{6,10},{8,12},{10,14},{12,0},{14,2},{1,5},{3,7},... | collective-permute-start | bytes 786440 | tf_op jit(solution)/shard_map/ppermute | solution.py:29
  6.8 35.5 %collective-permute-start.7 = (bf16[256,1024]{1,0:T(8,128)(2,1)}, bf16[256,1024]{1,0:T(8,128)(2,1)S(1)}, u32[]{:S(2)}, u32[]{:S(2)}) collective-permute-start(bf16[256,1024]{1,0:T(8,128)(2,1)} %get-tuple-element.15.near), channel_id=1, source_target_pairs={{0,2},{2,0},{4,6},{6,4},{8,10},{10,8},{12,14},{14,12},{1,3},{3,1},... | collective-permute-start | bytes 1572872 | tf_op jit(solution)/shard_map/ppermute | solution.py:29
  7.3 36.0 %collective-permute-start = (bf16[256,1024]{1,0:T(8,128)(2,1)}, bf16[256,1024]{1,0:T(8,128)(2,1)}, u32[]{:S(2)}, u32[]{:S(2)}) collective-permute-start(bf16[256,1024]{1,0:T(8,128)(2,1)} %get-tuple-element.15.near), channel_id=1, source_target_pairs={{0,4},{2,6},{4,8},{6,10},{8,12},{10,14},{12,0},{14,2},{1,5},{3,7},... | collective-permute-start | bytes 1572872 | tf_op jit(solution)/shard_map/ppermute | solution.py:29
  7.5 32.6 %collective-permute-start.12 = (bf16[128,1024]{1,0:T(8,128)(2,1)S(1)}, bf16[128,1024]{1,0:T(8,128)(2,1)}, u32[]{:S(2)}, u32[]{:S(2)}) collective-permute-start(bf16[128,1024]{1,0:T(8,128)(2,1)S(1)} %bitcast.42), channel_id=1, source_target_pairs={{0,12},{2,14},{4,0},{6,2},{8,4},{10,6},{12,8},{14,10},{1,13},{3,15... | collective-permute-start | bytes 786440 | tf_op jit(solution)/shard_map/ppermute | solution.py:29
  10.0 29.2 %all-to-all-start = ((f32[8,10,128]{2,1,0:T(8,128)}), f32[8,10,128]{2,1,0:T(8,128)S(1)}, u32[]{:S(2)}, u32[]{:S(2)}) async-start(f32[8,10,128]{2,1,0:T(8,128)} %broadcast_in_dim.65), calls=%async_computation | async-start | bytes 131072 | tf_op jit(solution)/shard_map/all_to_all | solution.py:319
  16.1 41.8 %collective-permute-start.4 = (bf16[256,1024]{1,0:T(8,128)(2,1)}, bf16[256,1024]{1,0:T(8,128)(2,1)}, u32[]{:S(2)}, u32[]{:S(2)}) collective-permute-start(bf16[256,1024]{1,0:T(8,128)(2,1)} %get-tuple-element.15.near), channel_id=1, source_target_pairs={{0,12},{2,14},{4,0},{6,2},{8,4},{10,6},{12,8},{14,10},{1,13},{3,15... | collective-permute-start | bytes 1572872 | tf_op jit(solution)/shard_map/ppermute | solution.py:29
  21.7 0.8 copy-start.10
  39.1 12.2 %collective-permute-start.8 = (bf16[128,1024]{1,0:T(8,128)(2,1)}, bf16[128,1024]{1,0:T(8,128)(2,1)S(1)}, u32[]{:S(2)}, u32[]{:S(2)}) collective-permute-start(bf16[128,1024]{1,0:T(8,128)(2,1)} %collective-permute-done.6.near_ref), channel_id=1, source_target_pairs={{0,2},{2,0},{4,6},{6,4},{8,10},{10,8},{12,14},{14,12},{1,3},{3,1},... | collective-permute-start | bytes 786440 | tf_op jit(solution)/shard_map/ppermute | solution.py:29
  40.1 16.8 %collective-permute-start.10 = (bf16[128,1024]{1,0:T(8,128)(2,1)}, bf16[128,1024]{1,0:T(8,128)(2,1)S(1)}, u32[]{:S(2)}, u32[]{:S(2)}) collective-permute-start(bf16[128,1024]{1,0:T(8,128)(2,1)} %collective-permute-done.6.near_ref), channel_id=1, source_target_pairs={{0,4},{2,6},{4,8},{6,10},{8,12},{10,14},{12,0},{14,2},{1,5},{3,7},... | collective-permute-start | bytes 786440 | tf_op jit(solution)/shard_map/ppermute | solution.py:29
  42.3 2.1 %copy-start.15 = (bf16[256,1024]{1,0:T(8,128)(2,1)}, bf16[256,1024]{1,0:T(8,128)(2,1)S(1)}, u32[]{:S(2)}) copy-start(bf16[256,1024]{1,0:T(8,128)(2,1)S(1)} %collective-permute-done.7.far) | copy-start | bytes 1572868
  42.3 25.4 %collective-permute-start.13 = (bf16[128,1024]{1,0:T(8,128)(2,1)}, bf16[128,1024]{1,0:T(8,128)(2,1)S(1)}, u32[]{:S(2)}, u32[]{:S(2)}) collective-permute-start(bf16[128,1024]{1,0:T(8,128)(2,1)} %collective-permute-done.12.near_ref), channel_id=1, source_target_pairs={{0,2},{2,0},{4,6},{6,4},{8,10},{10,8},{12,14},{14,12},{1,3},{3,1},... | collective-permute-start | bytes 786440 | tf_op jit(solution)/shard_map/ppermute | solution.py:29
  43.2 16.7 %collective-permute-start.9 = (bf16[256,1024]{1,0:T(8,128)(2,1)}, bf16[256,1024]{1,0:T(8,128)(2,1)S(1)}, u32[]{:S(2)}, u32[]{:S(2)}) collective-permute-start(bf16[256,1024]{1,0:T(8,128)(2,1)} %collective-permute-done.near), channel_id=1, source_target_pairs={{0,2},{2,0},{4,6},{6,4},{8,10},{10,8},{12,14},{14,12},{1,3},{3,1},... | collective-permute-start | bytes 1572872 | tf_op jit(solution)/shard_map/ppermute | solution.py:29
  44.4 7.0 %copy-start.11 = (bf16[8,4,8,1024]{3,2,1,0:T(8,128)(2,1)S(1)}, bf16[8,4,8,1024]{3,2,1,0:T(8,128)(2,1)}, u32[]{:S(2)}) copy-start(bf16[8,4,8,1024]{3,2,1,0:T(8,128)(2,1)} %copy-done.10) | copy-start | bytes 1572868
  56.8 33.9 %collective-permute-start.1 = (bf16[256,1024]{1,0:T(8,128)(2,1)}, bf16[256,1024]{1,0:T(8,128)(2,1)}, u32[]{:S(2)}, u32[]{:S(2)}) collective-permute-start(bf16[256,1024]{1,0:T(8,128)(2,1)} %collective-permute-done.near), channel_id=1, source_target_pairs={{0,4},{2,6},{4,8},{6,10},{8,12},{10,14},{12,0},{14,2},{1,5},{3,7},... | collective-permute-start | bytes 1572872 | tf_op jit(solution)/shard_map/ppermute | solution.py:29
  56.9 16.2 %collective-permute-start.11 = (bf16[128,1024]{1,0:T(8,128)(2,1)S(1)}, bf16[128,1024]{1,0:T(8,128)(2,1)S(1)}, u32[]{:S(2)}, u32[]{:S(2)}) collective-permute-start(bf16[128,1024]{1,0:T(8,128)(2,1)S(1)} %collective-permute-done.10.near_ref), channel_id=1, source_target_pairs={{0,2},{2,0},{4,6},{6,4},{8,10},{10,8},{12,14},{14,12},{1,3},{3,1},... | collective-permute-start | bytes 786440 | tf_op jit(solution)/shard_map/ppermute | solution.py:29
  57.8 34.3 %collective-permute-start.5 = (bf16[256,1024]{1,0:T(8,128)(2,1)}, bf16[256,1024]{1,0:T(8,128)(2,1)}, u32[]{:S(2)}, u32[]{:S(2)}) collective-permute-start(bf16[256,1024]{1,0:T(8,128)(2,1)} %collective-permute-done.4.near), channel_id=1, source_target_pairs={{0,2},{2,0},{4,6},{6,4},{8,10},{10,8},{12,14},{14,12},{1,3},{3,1},... | collective-permute-start | bytes 1572872 | tf_op jit(solution)/shard_map/ppermute | solution.py:29
  60.0 0.8 copy-start.16
  78.1 0.8 copy-start.12
  78.8 21.4 %all-to-all-start.1 = ((bf16[8,4,8,1024]{3,2,1,0:T(8,128)(2,1)}), bf16[8,4,8,1024]{3,2,1,0:T(8,128)(2,1)}, u32[]{:S(2)}, u32[]{:S(2)}) async-start(bf16[8,4,8,1024]{3,2,1,0:T(8,128)(2,1)} %copy-done.12), calls=%async_computation.1 | async-start | bytes 1048576 | tf_op jit(solution)/shard_map/all_to_all | solution.py:361
  90.7 9.5 %collective-permute-start.2 = (bf16[256,1024]{1,0:T(8,128)(2,1)}, bf16[256,1024]{1,0:T(8,128)(2,1)}, u32[]{:S(2)}, u32[]{:S(2)}) collective-permute-start(bf16[256,1024]{1,0:T(8,128)(2,1)} %collective-permute-done.1.near), channel_id=1, source_target_pairs={{0,2},{2,0},{4,6},{6,4},{8,10},{10,8},{12,14},{14,12},{1,3},{3,1},... | collective-permute-start | bytes 1572872 | tf_op jit(solution)/shard_map/ppermute | solution.py:29
  100.2 8.9 %slice-start = ((s8[16777216]{0:T(1024)(128)(4,1)}), s8[4194304]{0:T(1024)(128)(4,1)S(1)}, s32[]{:S(2)}) async-start(s8[16777216]{0:T(1024)(128)(4,1)} %bitcast.34), calls=%async_computation.2 | async-start | bytes 8388608
  100.2 8.9 %slice-start.1 = ((s8[16777216]{0:T(1024)(128)(4,1)}), s8[4194304]{0:T(1024)(128)(4,1)S(1)}, s32[]{:S(2)}) async-start(s8[16777216]{0:T(1024)(128)(4,1)} %bitcast.34), calls=%async_computation.3 | async-start | bytes 8388608
  100.2 8.9 %slice-start.2 = ((s8[16777216]{0:T(1024)(128)(4,1)}), s8[4194304]{0:T(1024)(128)(4,1)S(1)}, s32[]{:S(2)}) async-start(s8[16777216]{0:T(1024)(128)(4,1)} %bitcast.34), calls=%async_computation.4 | async-start | bytes 8388608
  100.2 10.2 %slice-start.3 = ((s8[16777216]{0:T(1024)(128)(4,1)}), s8[4194304]{0:T(1024)(128)(4,1)S(1)}, s32[]{:S(2)}) async-start(s8[16777216]{0:T(1024)(128)(4,1)} %bitcast.34), calls=%async_computation.5 | async-start | bytes 8388608
  109.1 2.5 %copy-start.7 = (bf16[256,1024]{1,0:T(8,128)(2,1)}, bf16[256,1024]{1,0:T(8,128)(2,1)S(1)}, u32[]{:S(2)}) copy-start(bf16[256,1024]{1,0:T(8,128)(2,1)S(1)} %get-tuple-element.20.x_ref) | copy-start | bytes 1572868
  111.6 26.0 %collective-permute-start.14 = (bf16[256,1024]{1,0:T(8,128)(2,1)S(1)}, bf16[256,1024]{1,0:T(8,128)(2,1)}, u32[]{:S(2)}, u32[]{:S(2)}) collective-permute-start(bf16[256,1024]{1,0:T(8,128)(2,1)S(1)} %output_share.8), channel_id=1, source_target_pairs={{0,2},{2,0},{4,6},{6,4},{8,10},{10,8},{12,14},{14,12},{1,3},{3,1},... | collective-permute-start | bytes 1572872 | tf_op jit(solution)/shard_map/ppermute | solution.py:29
  113.1 5.8 %copy-start.2 = (bf16[1024,8192]{1,0:T(8,128)(2,1)S(1)}, bf16[1024,8192]{1,0:T(8,128)(2,1)}, u32[]{:S(2)}) copy-start(bf16[1024,8192]{1,0:T(8,128)(2,1)} %w_ref.15) | copy-start | bytes 50331652
  118.9 1.0 copy-start.8
  119.9 1.7 copy-start.9
  121.0 25.1 %collective-permute-start.16 = (bf16[256,1024]{1,0:T(8,128)(2,1)S(1)}, bf16[256,1024]{1,0:T(8,128)(2,1)}, u32[]{:S(2)}, u32[]{:S(2)}) collective-permute-start(bf16[256,1024]{1,0:T(8,128)(2,1)S(1)} %output_share.10), channel_id=1, source_target_pairs={{0,2},{2,0},{4,6},{6,4},{8,10},{10,8},{12,14},{14,12},{1,3},{3,1},... | collective-permute-start | bytes 1572872 | tf_op jit(solution)/shard_map/ppermute | solution.py:29
  121.7 5.8 %copy-start.3 = (bf16[1024,8192]{1,0:T(8,128)(2,1)S(1)}, bf16[1024,8192]{1,0:T(8,128)(2,1)}, u32[]{:S(2)}) copy-start(bf16[1024,8192]{1,0:T(8,128)(2,1)} %w_ref.15) | copy-start | bytes 50331652
  128.5 21.5 %collective-permute-start.18 = (bf16[256,1024]{1,0:T(8,128)(2,1)S(1)}, bf16[256,1024]{1,0:T(8,128)(2,1)S(1)}, u32[]{:S(2)}, u32[]{:S(2)}) collective-permute-start(bf16[256,1024]{1,0:T(8,128)(2,1)S(1)} %output_share.12), channel_id=1, source_target_pairs={{0,2},{2,0},{4,6},{6,4},{8,10},{10,8},{12,14},{14,12},{1,3},{3,1},... | collective-permute-start | bytes 1572872 | tf_op jit(solution)/shard_map/ppermute | solution.py:29
  130.1 5.8 %copy-start.4 = (bf16[1024,8192]{1,0:T(8,128)(2,1)S(1)}, bf16[1024,8192]{1,0:T(8,128)(2,1)}, u32[]{:S(2)}) copy-start(bf16[1024,8192]{1,0:T(8,128)(2,1)} %w_ref.15) | copy-start | bytes 50331652
  137.0 15.9 %collective-permute-start.20 = (bf16[256,1024]{1,0:T(8,128)(2,1)S(1)}, bf16[256,1024]{1,0:T(8,128)(2,1)}, u32[]{:S(2)}, u32[]{:S(2)}) collective-permute-start(bf16[256,1024]{1,0:T(8,128)(2,1)S(1)} %output_share.14), channel_id=1, source_target_pairs={{0,2},{2,0},{4,6},{6,4},{8,10},{10,8},{12,14},{14,12},{1,3},{3,1},... | collective-permute-start | bytes 1572872 | tf_op jit(solution)/shard_map/ppermute | solution.py:29
  137.6 5.8 %copy-start.5 = (bf16[1024,8192]{1,0:T(8,128)(2,1)S(1)}, bf16[1024,8192]{1,0:T(8,128)(2,1)}, u32[]{:S(2)}) copy-start(bf16[1024,8192]{1,0:T(8,128)(2,1)} %w_ref.15) | copy-start | bytes 50331652
  145.3 24.4 %collective-permute-start.15 = (bf16[256,1024]{1,0:T(8,128)(2,1)S(1)}, bf16[256,1024]{1,0:T(8,128)(2,1)}, u32[]{:S(2)}, u32[]{:S(2)}) collective-permute-start(bf16[256,1024]{1,0:T(8,128)(2,1)S(1)} %output_share.9), channel_id=1, source_target_pairs={{0,8},{2,10},{4,12},{6,14},{8,0},{10,2},{12,4},{14,6},{1,9},{3,11}... | collective-permute-start | bytes 1572872 | tf_op jit(solution)/shard_map/ppermute | solution.py:29
  148.8 30.1 %collective-permute-start.17 = (bf16[256,1024]{1,0:T(8,128)(2,1)}, bf16[256,1024]{1,0:T(8,128)(2,1)}, u32[]{:S(2)}, u32[]{:S(2)}) collective-permute-start(bf16[256,1024]{1,0:T(8,128)(2,1)} %output_share.11), channel_id=1, source_target_pairs={{0,4},{2,6},{4,8},{6,10},{8,12},{10,14},{12,0},{14,2},{1,5},{3,7},... | collective-permute-start | bytes 1572872 | tf_op jit(solution)/shard_map/ppermute | solution.py:29
  151.9 27.0 %collective-permute-start.19 = (bf16[256,1024]{1,0:T(8,128)(2,1)}, bf16[256,1024]{1,0:T(8,128)(2,1)S(1)}, u32[]{:S(2)}, u32[]{:S(2)}) collective-permute-start(bf16[256,1024]{1,0:T(8,128)(2,1)} %output_share.13), channel_id=1, source_target_pairs={{0,12},{2,14},{4,0},{6,2},{8,4},{10,6},{12,8},{14,10},{1,13},{3,15... | collective-permute-start | bytes 1572872 | tf_op jit(solution)/shard_map/ppermute | solution.py:29
  152.8 5.8 %copy-start.6 = (bf16[1024,8192]{1,0:T(8,128)(2,1)S(1)}, bf16[1024,8192]{1,0:T(8,128)(2,1)}, u32[]{:S(2)}) copy-start(bf16[1024,8192]{1,0:T(8,128)(2,1)} %w_ref.15) | copy-start | bytes 50331652
  158.6 20.3 %copy-start.14 = (f32[256,1024]{1,0:T(8,128)S(1)}, f32[256,1024]{1,0:T(8,128)}, u32[]{:S(2)}) copy-start(f32[256,1024]{1,0:T(8,128)} %get-tuple-element.23) | copy-start | bytes 3145732
  158.6 22.7 %copy-start.1 = (bf16[512,1024]{1,0:T(8,128)(2,1)S(1)}, bf16[512,1024]{1,0:T(8,128)(2,1)}, u32[]{:S(2)}) copy-start(bf16[512,1024]{1,0:T(8,128)(2,1)} %param.10) | copy-start | bytes 3145732

commit v10 on v7

--- a/solution.py
+++ b/solution.py
@@ -257,41 +257,27 @@
     )[-1]
 
 
-def share_kernel(spot, x_ref, w_hbm, *refs):
-    *outs, held, sems = refs
+def share_kernel(spot, x_ref, w_ref, *outs):
     wide = outs[0].shape[1]
-    slots, _, block = held.shape
-    parts = wide // block
-    chunks = len(outs) * parts
-
-    def fetch(chunk):
-        start = pl.multiple_of(spot[chunk // parts] * wide + chunk % parts * block, block)
-        slot = chunk % slots
-        return pltpu.make_async_copy(w_hbm.at[:, pl.ds(start, block)], held.at[slot], sems.at[slot])
-
-    for chunk in range(min(slots, chunks)):
-        fetch(chunk).start()
-    for chunk in range(chunks):
-        fetch(chunk).wait()
-        out_ref = outs[chunk // parts]
-        share = jnp.dot(x_ref[...], held[chunk % slots], preferred_element_type=jnp.float32)
-        out_ref[:, pl.ds(chunk % parts * block, block)] = share.astype(out_ref.dtype)
-        if chunk + slots < chunks:
-            fetch(chunk + slots).start()
+    block = min(512, wide)
+    for index, out_ref in enumerate(outs):
+        for start in range(0, wide, block):
+            columns = pl.ds(pl.multiple_of(spot[index] * wide + start, block), block)
+            share = jnp.dot(x_ref[...], w_ref[:, columns], preferred_element_type=jnp.float32)
+            out_ref[:, pl.ds(start, block)] = share.astype(out_ref.dtype)
 
 
 def output_shares(targets, gated, w_out, owners):
     rows, channels = gated.shape
     wide = w_out.shape[1] // owners
-    block = min(512, wide)
     return kernel_call(
         share_kernel,
         "output_shares",
         jnp.stack([which for which, _ in targets]).astype(jnp.int32),
-        [(IN_VMEM, gated), (IN_HBM, w_out)],
+        [(IN_VMEM, gated), (IN_VMEM, w_out)],
         [(IN_VMEM, jax.ShapeDtypeStruct((rows, wide), kind)) for _, kind in targets],
         {},
-        [pltpu.VMEM((DEPTH, channels, block), jnp.bfloat16), pltpu.SemaphoreType.DMA((DEPTH,))],
+        [],
         2 * rows * channels * wide * len(targets),
         2 * channels * wide * len(targets),
     )
@@ -319,10 +305,6 @@
     tiny = lax.all_to_all(
         jnp.broadcast_to(tiny[None], (owners, *tiny.shape)), "tensor", 0, 0, tiled=True
     )
-    gain_rows = channels // LANES
-    gains = tiny[:, :gain_rows].reshape(owners, channels)
-    inv_rms = lax.rsqrt(jnp.sum(tiny[:, gain_rows:], axis=0).reshape(tokens) / D + EPSILON)
-    inv_rms = jnp.broadcast_to(inv_rms[:, None], (tokens, LANES))
     own_taps = filters.T
     lag_taps = spread(own_taps)
     streams = spread(after(stream.astype(jnp.bfloat16), own_taps))
@@ -344,13 +326,20 @@
     place = place.astype(jnp.bfloat16)
 
     cache = cache_rows.transpose(1, 0, 2)
+    first_terms = history_terms(cache, *lag_taps[0][1:], row_lengths, spot_at(0), steps, None)
     near_taps = filters[:, : 2 * steps].T.astype(jnp.float32)
-    terms = sums = None
+    tiny = after(tiny, (first_terms, place, near_taps))
+    gain_rows = channels // LANES
+    gains = tiny[:, :gain_rows].reshape(owners, channels)
+    inv_rms = lax.rsqrt(jnp.sum(tiny[:, gain_rows:], axis=0).reshape(tokens) / D + EPSILON)
+    inv_rms = jnp.broadcast_to(inv_rms[:, None], (tokens, LANES))
+
+    terms, sums = first_terms, None
     parts = len(streams)
     for index, (back, near, far) in enumerate(lag_taps):
         if index:
             near = after(near, sums)
-        terms = history_terms(cache, near, far, row_lengths, spot_at(-back), steps, terms)
+            terms = history_terms(cache, near, far, row_lengths, spot_at(-back), steps, terms)
         if 2 * index < parts:
             at, *pair = streams[index]
             pair[0] = after(pair[0], terms)
@@ -369,15 +358,14 @@
     order = sorted(range(outer_size), key=lambda ahead: (ahead == 0, -min(ahead, outer_size - ahead)))
     targets = [(owner_at(ahead, 1), jnp.bfloat16) for ahead in order]
     targets += [(owner_at(ahead, 0), jnp.float32) for ahead in order]
-    shares = list(output_shares(targets[:2], gated, w_out, owners))
-    across = [moved(share, 0, 1) for share in shares]
-    for start in range(2, len(targets), 6):
-        shares += output_shares(targets[start : start + 6], gated, w_out, owners)
-    across += [moved(share, 0, 1) for share in shares[2:outer_size]]
+    shares = output_shares(targets, gated, w_out, owners)
+    across = [moved(share, 0, 1) for share in shares[:outer_size]]
     out = stream
     for ahead, own_share, arrived_share in zip(order, shares[outer_size:], across):
         share = own_share + arrived_share.astype(jnp.float32)
-        out = out + (moved(share.astype(jnp.bfloat16), ahead, 0) if ahead else share)
+        if ahead:
+            share = share.astype(jnp.bfloat16)
+        out = out + (moved(share, ahead, 0) if ahead else share).astype(jnp.float32)
     return out.astype(jnp.bfloat16).reshape(steps, seqs, channels)
 
 

time: 174 us -> 164 us (0.943)
  waiting for transfers between devices: 60.3 us -> 53.2 us
  local copies, waits for them, and re-layouts: 5.89 us -> 12.9 us
  Pallas kernels: 60.8 us -> 54.3 us
  starting transfers between devices: 38.9 us -> 36.2 us
    ppermute x21, waiting for transfers between devices: 48.2 us -> 37.6 us  [moved(): return lax.ppermute(array, 'tensor', pairs)]
    pallas_call x10 -> x9, Pallas kernels: 60.8 us -> 54.3 us  [kernel_call(): pl.pallas_call(kernel, in_specs=[IN_SMEM, *specs], out_specs=list(out_spe...]
    unnamed x27, local copies, waits for them, and re-layouts: 3.84 us -> 9.36 us
    all_to_all x1, waiting for transfers between devices: 12.1 us -> 15.6 us  [per_device(): lax.all_to_all(jnp.broadcast_to(tiny[None], (owners, *tiny.shape)), 'tens...]
    ppermute x21, starting transfers between devices: 26.7 us -> 23.4 us  [moved(): return lax.ppermute(array, 'tensor', pairs)]
  transfers between devices with their start and end apart: 23 -> 23, of which waited for: 9 -> 9; matrix products, arithmetic and copies ran while one was open for 3% -> 4% of each run, Pallas kernels for 29% -> 26%
where the time goes in v10:
time: 164 us; the launch traced here: 161 us
  Pallas kernels  54.3 us (33%)
  waiting for transfers between devices  53.2 us (32%)
  starting transfers between devices  36.2 us (22%)
  local copies, waits for them, and re-layouts  12.9 us (8%)
  other arithmetic  2.61 us (2%)
    pallas_call x9, Pallas kernels, kernel_call(): pl.pallas_call(kernel, in_specs=[IN_SMEM, *specs], out_specs=list(out_spe...  54.3 us
    ppermute x21, waiting for transfers between devices, moved(): return lax.ppermute(array, 'tensor', pairs)  37.6 us
    ppermute x21, starting transfers between devices, moved(): return lax.ppermute(array, 'tensor', pairs)  23.4 us
    all_to_all x1, waiting for transfers between devices, per_device(): lax.all_to_all(jnp.broadcast_to(tiny[None], (owners, *tiny.shape)), 'tens...  15.6 us
    unnamed x27, local copies, waits for them, and re-layouts  9.36 us
    all_to_all x1, starting transfers between devices, per_device(): terms = lax.all_to_all(terms, 'tensor', 0, 0, tiled=True)  7.34 us
    all_to_all x1, starting transfers between devices, per_device(): lax.all_to_all(jnp.broadcast_to(tiny[None], (owners, *tiny.shape)), 'tens...  5.41 us
  transfers between devices with their start and end apart: 23, of which 9 were waited for; matrix products, arithmetic and copies ran while one was open for 4% of the time, Pallas kernels for 26%

profile of v10, /device:TPU:18, one launch (start us, length us, event | category | flops | bytes accessed | tf_op | source)
XLA Modules:
  0.0 161.2 jit_solution(13402624934882033052)
XLA Ops:
  0.0 1.2 copy.24
  1.2 1.6 collective-permute-start.3
  2.8 1.6 collective-permute-start.6
  4.4 0.8 eq.92
  5.1 1.6 %multiply_reduce_fusion = (f32[256]{0:T(256)S(1)}, bf16[256,1024]{1,0:T(8,128)(2,1)}, f32[256,1024]{1,0:T(8,128)}) fusion(bf16[512,1024]{1,0:T(8,128)(2,1)S(1)} %copy-done, s32[256]{0:T(256)S(1)} %eq.92), kind=kOutput, calls=%fused_computation.4 | convolution fusion | flops 269352704 | bytes 2623488 | tf_op jit(solution)/shard_map/dot_general | solution.py:302
  6.7 0.5 collective-permute-start.7
  7.3 0.2 collective-permute-start
  7.5 1.8 %collective-permute-start.12 = (bf16[128,1024]{1,0:T(8,128)(2,1)S(1)}, bf16[128,1024]{1,0:T(8,128)(2,1)}, u32[]{:S(2)}, u32[]{:S(2)}) collective-permute-start(bf16[128,1024]{1,0:T(8,128)(2,1)S(1)} %bitcast.40), channel_id=1, source_target_pairs={{0,12},{2,14},{4,0},{6,2},{8,4},{10,6},{12,8},{14,10},{1,13},{3,15... | collective-permute-start | bytes 786440 | tf_op jit(solution)/shard_map/ppermute | solution.py:28
  9.3 0.6 broadcast_in_dim.21
  9.9 5.4 %all-to-all-start = ((f32[8,10,128]{2,1,0:T(8,128)}), f32[8,10,128]{2,1,0:T(8,128)S(1)}, u32[]{:S(2)}, u32[]{:S(2)}) async-start(f32[8,10,128]{2,1,0:T(8,128)} %broadcast_in_dim.21), calls=%async_computation | async-start | bytes 131072 | tf_op jit(solution)/shard_map/all_to_all | solution.py:305
  15.3 0.1 reshape.68
  15.5 0.1 iota_compare_fusion.2
  15.5 0.1 pad_add_fusion.1.spot
  15.7 0.1 pad_add_fusion.2.spot
  15.8 0.2 select_reduce_fusion
  16.0 0.2 and_convert_fusion
  16.2 0.1 pad_add_fusion.spot
  16.2 0.9 reshape.72
  17.1 0.6 collective-permute-start.4
  17.8 4.9 %history_terms.4.refs_0_ = bf16[8,4,8,1024]{3,2,1,0:T(8,128)(2,1)S(1)} custom-call(s32[2]{0:T(128)S(1)} %pad_add_fusion.1.spot, s32[8,128]{1,0:T(8,128)S(1)} %broadcast_in_dim.24.lengths_ref, bf16[128,1024]{1,0:T(8,128)(2,1)S(1)} %bitcast.41, bf16[128,1024]{1,0:T(8,128)(2,1)S(1)} %collective-permute-done.3.far_ref, bf16[127,8,8192]{2,1,0:T(8,128)(2,1)} %bitcast.43), custom_call_target="tpu_custom_call" | custom-call | flops 4993843200 | bytes 4161536 | tf_op jit(solution)/shard_map/history_terms/pallas_call | solution.py:51
  22.7 0.8 copy-done.3
  23.5 15.6 %all-to-all-done = f32[8,10,128]{2,1,0:T(8,128)S(1)} async-done(((f32[8,10,128]{2,1,0:T(8,128)}), f32[8,10,128]{2,1,0:T(8,128)S(1)}, u32[]{:S(2)}, u32[]{:S(2)}) %all-to-all-start) | async-done | bytes 40992 | tf_op jit(solution)/shard_map/all_to_all | solution.py:305
  39.1 1.0 collective-permute-start.8
  40.1 2.2 %collective-permute-start.10 = (bf16[128,1024]{1,0:T(8,128)(2,1)}, bf16[128,1024]{1,0:T(8,128)(2,1)S(1)}, u32[]{:S(2)}, u32[]{:S(2)}) collective-permute-start(bf16[128,1024]{1,0:T(8,128)(2,1)} %collective-permute-done.6.near_ref), channel_id=1, source_target_pairs={{0,4},{2,6},{4,8},{6,10},{8,12},{10,14},{12,0},{14,2},{1,5},{3,7},... | collective-permute-start | bytes 786440 | tf_op jit(solution)/shard_map/ppermute | solution.py:28
  42.3 0.9 collective-permute-start.13
  43.2 1.1 collective-permute-start.9
  44.3 0.1 broadcast_in_dim.25.inv_ref
  44.4 6.9 %projected_part.3.refs_0_ = f32[256,3072]{1,0:T(8,128)S(1)} custom-call(s32[2]{0:T(128)S(1)} %pad_add_fusion.1.spot, bf16[256,1024]{1,0:T(8,128)(2,1)} %get-tuple-element.23.near, bf16[256,1024]{1,0:T(8,128)(2,1)} %copy-done.7, f32[8,1024]{1,0:T(8,128)S(1)} %bitcast.34, f32[256,128]{1,0:T(8,128)S(1)} %broadcast_in_dim.25.inv_ref, bf16[8192,3072]{1,0:T(8,128)(2,1)} %w_hbm.7), custom_call_target="tpu_custom_call" | custom-call | flops 6442450944 | bytes 25165824 | tf_op jit(solution)/shard_map/projected_part/pallas_call | solution.py:51
  51.4 5.4 %history_terms.5.refs_0_ = bf16[8,4,8,1024]{3,2,1,0:T(8,128)(2,1)S(1)} custom-call(s32[2]{0:T(128)S(1)} %pad_add_fusion.3.spot, s32[8,128]{1,0:T(8,128)S(1)} %broadcast_in_dim.24.lengths_ref, bf16[128,1024]{1,0:T(8,128)(2,1)} %collective-permute-done.6.near_ref, ...), custom_call_target="tpu_custom_call", output_to_operand_aliasing={{}: (5, {})} | custom-call | flops 4993843200 | bytes 4161536 | tf_op jit(solution)/shard_map/history_terms/pallas_call | solution.py:51
  56.8 0.1 collective-permute-start.1
  56.9 0.9 collective-permute-start.11
  57.8 1.1 collective-permute-start.5
  58.9 1.0 collective-permute-done.9.far
  60.0 0.8 copy-done.8
  60.7 6.9 %projected_part.4.refs_0_ = f32[256,3072]{1,0:T(8,128)S(1)} custom-call(s32[2]{0:T(128)S(1)} %pad_add_fusion.3.spot, bf16[256,1024]{1,0:T(8,128)(2,1)} %collective-permute-done.near, bf16[256,1024]{1,0:T(8,128)(2,1)} %copy-done.8, f32[8,1024]{1,0:T(8,128)S(1)} %bitcast.35, f32[256,128]{1,0:T(8,128)S(1)} %broadcast_in_dim.25.inv_ref, ...), custom_call_target="tpu_custom_call", output_to_operand_aliasing={{}: (6, {})} | custom-call | flops 6442450944 | bytes 25165824 | tf_op jit(solution)/shard_map/projected_part/pallas_call | solution.py:51
  67.7 5.4 %history_terms.6.refs_0_ = bf16[8,4,8,1024]{3,2,1,0:T(8,128)(2,1)S(1)} custom-call(s32[2]{0:T(128)S(1)} %pad_add_fusion.2.spot, s32[8,128]{1,0:T(8,128)S(1)} %broadcast_in_dim.24.lengths_ref, bf16[128,1024]{1,0:T(8,128)(2,1)} %collective-permute-done.12.near_ref, ...), custom_call_target="tpu_custom_call", output_to_operand_aliasing={{}: (5, {})} | custom-call | flops 4993843200 | bytes 4161536 | tf_op jit(solution)/shard_map/history_terms/pallas_call | solution.py:51
  73.1 5.0 %history_terms.7 = bf16[8,4,8,1024]{3,2,1,0:T(8,128)(2,1)S(1)} custom-call(s32[2]{0:T(128)S(1)} %pad_add_fusion.spot, s32[8,128]{1,0:T(8,128)S(1)} %broadcast_in_dim.24.lengths_ref, bf16[128,1024]{1,0:T(8,128)(2,1)S(1)} %collective-permute-done.10.near_ref, bf16[128,1024]{1,0:T(8,128)(2,1)S(1)} %collective-permute-done.11.far_ref, ...), custom_call_target="tpu_custom_call", output_to_operand_aliasing={{}: (5, {})} | custom-call | flops 4993843200 | bytes 4161536 | tf_op jit(solution)/shard_map/history_terms/pallas_call | solution.py:51
  78.1 0.8 copy-done.5
  78.8 7.3 %all-to-all-start.1 = ((bf16[8,4,8,1024]{3,2,1,0:T(8,128)(2,1)}), bf16[8,4,8,1024]{3,2,1,0:T(8,128)(2,1)}, u32[]{:S(2)}, u32[]{:S(2)}) async-start(bf16[8,4,8,1024]{3,2,1,0:T(8,128)(2,1)} %copy-done.5), calls=%async_computation.1 | async-start | bytes 1048576 | tf_op jit(solution)/shard_map/all_to_all | solution.py:347
  86.2 1.0 copy.26.refs_2_
  87.3 0.1 stack.77.spot
  87.3 1.5 collective-permute-start.2
  88.9 6.9 %projected_part.5.refs_0_ = f32[256,3072]{1,0:T(8,128)S(1)} custom-call(s32[2]{0:T(128)S(1)} %pad_add_fusion.2.spot, bf16[256,1024]{1,0:T(8,128)(2,1)} %collective-permute-done.4.near, bf16[256,1024]{1,0:T(8,128)(2,1)} %collective-permute-done.5.far, f32[8,1024]{1,0:T(8,128)S(1)} %bitcast.36, ...), custom_call_target="tpu_custom_call", output_to_operand_aliasing={{}: (6, {})} | custom-call | flops 6442450944 | bytes 25165824 | tf_op jit(solution)/shard_map/projected_part/pallas_call | solution.py:51
  95.8 2.5 %collective-permute-done.2.far = bf16[256,1024]{1,0:T(8,128)(2,1)} collective-permute-done((bf16[256,1024]{1,0:T(8,128)(2,1)}, bf16[256,1024]{1,0:T(8,128)(2,1)}, u32[]{:S(2)}, u32[]{:S(2)}) %collective-permute-start.2) | collective-permute-done | bytes 524320 | tf_op jit(solution)/shard_map/ppermute | solution.py:28
  98.3 7.8 %gated_rows.1 = (f32[256,3072]{1,0:T(8,128)S(1)}, bf16[256,1024]{1,0:T(8,128)(2,1)S(1)}) custom-call(s32[2]{0:T(128)S(1)} %pad_add_fusion.spot, bf16[256,1024]{1,0:T(8,128)(2,1)} %collective-permute-done.1.near, bf16[256,1024]{1,0:T(8,128)(2,1)} %collective-permute-done.2.far, f32[8,1024]{1,0:T(8,128)S(1)} %bitcast.37, ...), custom_call_target="tpu_custom_call", output_to_operand_aliasing={{0}: (6, {})} | custom-call | flops 6442450944 | bytes 25165824 | tf_op jit(solution)/shard_map/gated_rows/pallas_call | solution.py:51
  106.1 5.8 %copy-done.2 = bf16[1024,8192]{1,0:T(8,128)(2,1)S(1)} copy-done((bf16[1024,8192]{1,0:T(8,128)(2,1)S(1)}, bf16[1024,8192]{1,0:T(8,128)(2,1)}, u32[]{:S(2)}) %copy-start.2) | copy-done | bytes 16777240
  111.9 5.1 %output_shares.1 = (bf16[256,1024]{1,0:T(8,128)(2,1)S(1)}, bf16[256,1024]{1,0:T(8,128)(2,1)S(1)}, bf16[256,1024]{1,0:T(8,128)(2,1)S(1)}, bf16[256,1024]{1,0:T(8,...) custom-call(s32[8]{0:T(128)S(1)} %stack.77.spot, ...), custom_call_target="tpu_custom_call" | custom-call | flops 4294967296 | bytes 16777216 | tf_op jit(solution)/shard_map/output_shares/pallas_call | solution.py:51
  117.0 0.5 collective-permute-start.14
  117.5 1.6 %collective-permute-start.16 = (bf16[256,1024]{1,0:T(8,128)(2,1)S(1)}, bf16[256,1024]{1,0:T(8,128)(2,1)S(1)}, u32[]{:S(2)}, u32[]{:S(2)}) collective-permute-start(bf16[256,1024]{1,0:T(8,128)(2,1)S(1)} %get-tuple-element.32), channel_id=1, source_target_pairs={{0,2},{2,0},{4,6},{6,4},{8,10},{10,8},{12,14},{14,12},{1,3},{3,1},... | collective-permute-start | bytes 1572872 | tf_op jit(solution)/shard_map/ppermute | solution.py:28
  119.1 0.4 collective-permute-start.18
  119.5 1.6 %collective-permute-start.20 = (bf16[256,1024]{1,0:T(8,128)(2,1)S(1)}, bf16[256,1024]{1,0:T(8,128)(2,1)S(1)}, u32[]{:S(2)}, u32[]{:S(2)}) collective-permute-start(bf16[256,1024]{1,0:T(8,128)(2,1)S(1)} %get-tuple-element.36), channel_id=1, source_target_pairs={{0,2},{2,0},{4,6},{6,4},{8,10},{10,8},{12,14},{14,12},{1,3},{3,1},... | collective-permute-start | bytes 1572872 | tf_op jit(solution)/shard_map/ppermute | solution.py:28
  121.1 10.8 %collective-permute-done.14 = bf16[256,1024]{1,0:T(8,128)(2,1)S(1)} collective-permute-done((bf16[256,1024]{1,0:T(8,128)(2,1)S(1)}, bf16[256,1024]{1,0:T(8,128)(2,1)S(1)}, u32[]{:S(2)}, u32[]{:S(2)}) %collective-permute-start.14) | collective-permute-done | bytes 524320 | tf_op jit(solution)/shard_map/ppermute | solution.py:28
  131.9 0.2 add_convert_fusion.3
  132.1 0.8 collective-permute-start.15
  132.9 6.5 %collective-permute-done.16 = bf16[256,1024]{1,0:T(8,128)(2,1)S(1)} collective-permute-done((bf16[256,1024]{1,0:T(8,128)(2,1)S(1)}, bf16[256,1024]{1,0:T(8,128)(2,1)S(1)}, u32[]{:S(2)}, u32[]{:S(2)}) %collective-permute-start.16) | collective-permute-done | bytes 524320 | tf_op jit(solution)/shard_map/ppermute | solution.py:28
  139.4 0.2 add_convert_fusion.2
  139.6 2.1 %collective-permute-start.17 = (bf16[256,1024]{1,0:T(8,128)(2,1)S(1)}, bf16[256,1024]{1,0:T(8,128)(2,1)S(1)}, u32[]{:S(2)}, u32[]{:S(2)}) collective-permute-start(bf16[256,1024]{1,0:T(8,128)(2,1)S(1)} %add_convert_fusion.2), channel_id=1, source_target_pairs={{0,4},{2,6},{4,8},{6,10},{8,12},{10,14},{12,0},{14,2},{1,5},{3,7},... | collective-permute-start | bytes 1572872 | tf_op jit(solution)/shard_map/ppermute | solution.py:28
  141.6 3.4 %collective-permute-done.18 = bf16[256,1024]{1,0:T(8,128)(2,1)S(1)} collective-permute-done((bf16[256,1024]{1,0:T(8,128)(2,1)S(1)}, bf16[256,1024]{1,0:T(8,128)(2,1)S(1)}, u32[]{:S(2)}, u32[]{:S(2)}) %collective-permute-start.18) | collective-permute-done | bytes 524320 | tf_op jit(solution)/shard_map/ppermute | solution.py:28
  145.0 0.2 add_convert_fusion.1
  145.2 1.3 collective-permute-start.19
  146.5 4.1 %collective-permute-done.20 = bf16[256,1024]{1,0:T(8,128)(2,1)S(1)} collective-permute-done((bf16[256,1024]{1,0:T(8,128)(2,1)S(1)}, bf16[256,1024]{1,0:T(8,128)(2,1)S(1)}, u32[]{:S(2)}, u32[]{:S(2)}) %collective-permute-start.20) | collective-permute-done | bytes 524320 | tf_op jit(solution)/shard_map/ppermute | solution.py:28
  150.6 1.5 collective-permute-done.15
  152.2 7.7 %collective-permute-done.17 = bf16[256,1024]{1,0:T(8,128)(2,1)S(1)} collective-permute-done((bf16[256,1024]{1,0:T(8,128)(2,1)S(1)}, bf16[256,1024]{1,0:T(8,128)(2,1)S(1)}, u32[]{:S(2)}, u32[]{:S(2)}) %collective-permute-start.17) | collective-permute-done | bytes 524320 | tf_op jit(solution)/shard_map/ppermute | solution.py:28
  159.9 1.3 add_convert_fusion
  (46 shorter events, 0.3 us)
Async XLA Ops:
  0.0 5.1 %copy-start = (bf16[512,1024]{1,0:T(8,128)(2,1)S(1)}, bf16[512,1024]{1,0:T(8,128)(2,1)}, u32[]{:S(2)}) copy-start(bf16[512,1024]{1,0:T(8,128)(2,1)} %param.10) | copy-start | bytes 3145732
  0.0 9.3 %copy-start.9 = (bf16[1024]{0:T(1024)(128)(2,1)S(1)}, bf16[1024]{0:T(1024)(128)(2,1)}, u32[]{:S(2)}) copy-start(bf16[1024]{0:T(1024)(128)(2,1)} %param.11) | copy-start | bytes 6148
  0.0 15.3 %copy-start.10 = (s32[128]{0:T(128)S(1)}, s32[128]{0:T(128)}, u32[]{:S(2)}) copy-start(s32[128]{0:T(128)} %param.16) | copy-start | bytes 1540
  0.0 15.8 %copy-start.11 = (s32[64]{0:T(128)S(1)}, s32[64]{0:T(128)}, u32[]{:S(2)}) copy-start(s32[64]{0:T(128)} %param.17) | copy-start | bytes 772
  1.2 15.9 %collective-permute-start.3 = (bf16[128,1024]{1,0:T(8,128)(2,1)S(1)}, bf16[128,1024]{1,0:T(8,128)(2,1)S(1)}, u32[]{:S(2)}, u32[]{:S(2)}) collective-permute-start(bf16[128,1024]{1,0:T(8,128)(2,1)S(1)} %bitcast.38), channel_id=1, source_target_pairs={{0,2},{2,0},{4,6},{6,4},{8,10},{10,8},{12,14},{14,12},{1,3},{3,1},... | collective-permute-start | bytes 786440 | tf_op jit(solution)/shard_map/ppermute | solution.py:28
  2.8 36.3 %collective-permute-start.6 = (bf16[128,1024]{1,0:T(8,128)(2,1)S(1)}, bf16[128,1024]{1,0:T(8,128)(2,1)}, u32[]{:S(2)}, u32[]{:S(2)}) collective-permute-start(bf16[128,1024]{1,0:T(8,128)(2,1)S(1)} %bitcast.39), channel_id=1, source_target_pairs={{0,4},{2,6},{4,8},{6,10},{8,12},{10,14},{12,0},{14,2},{1,5},{3,7},... | collective-permute-start | bytes 786440 | tf_op jit(solution)/shard_map/ppermute | solution.py:28
  6.7 35.5 %collective-permute-start.7 = (bf16[256,1024]{1,0:T(8,128)(2,1)}, bf16[256,1024]{1,0:T(8,128)(2,1)S(1)}, u32[]{:S(2)}, u32[]{:S(2)}) collective-permute-start(bf16[256,1024]{1,0:T(8,128)(2,1)} %get-tuple-element.23.near), channel_id=1, source_target_pairs={{0,2},{2,0},{4,6},{6,4},{8,10},{10,8},{12,14},{14,12},{1,3},{3,1},... | collective-permute-start | bytes 1572872 | tf_op jit(solution)/shard_map/ppermute | solution.py:28
  7.3 36.0 %collective-permute-start = (bf16[256,1024]{1,0:T(8,128)(2,1)}, bf16[256,1024]{1,0:T(8,128)(2,1)}, u32[]{:S(2)}, u32[]{:S(2)}) collective-permute-start(bf16[256,1024]{1,0:T(8,128)(2,1)} %get-tuple-element.23.near), channel_id=1, source_target_pairs={{0,4},{2,6},{4,8},{6,10},{8,12},{10,14},{12,0},{14,2},{1,5},{3,7},... | collective-permute-start | bytes 1572872 | tf_op jit(solution)/shard_map/ppermute | solution.py:28
  7.5 32.6 %collective-permute-start.12 = (bf16[128,1024]{1,0:T(8,128)(2,1)S(1)}, bf16[128,1024]{1,0:T(8,128)(2,1)}, u32[]{:S(2)}, u32[]{:S(2)}) collective-permute-start(bf16[128,1024]{1,0:T(8,128)(2,1)S(1)} %bitcast.40), channel_id=1, source_target_pairs={{0,12},{2,14},{4,0},{6,2},{8,4},{10,6},{12,8},{14,10},{1,13},{3,15... | collective-permute-start | bytes 786440 | tf_op jit(solution)/shard_map/ppermute | solution.py:28
  9.9 29.2 %all-to-all-start = ((f32[8,10,128]{2,1,0:T(8,128)}), f32[8,10,128]{2,1,0:T(8,128)S(1)}, u32[]{:S(2)}, u32[]{:S(2)}) async-start(f32[8,10,128]{2,1,0:T(8,128)} %broadcast_in_dim.21), calls=%async_computation | async-start | bytes 131072 | tf_op jit(solution)/shard_map/all_to_all | solution.py:305
  17.1 40.7 %collective-permute-start.4 = (bf16[256,1024]{1,0:T(8,128)(2,1)}, bf16[256,1024]{1,0:T(8,128)(2,1)}, u32[]{:S(2)}, u32[]{:S(2)}) collective-permute-start(bf16[256,1024]{1,0:T(8,128)(2,1)} %get-tuple-element.23.near), channel_id=1, source_target_pairs={{0,12},{2,14},{4,0},{6,2},{8,4},{10,6},{12,8},{14,10},{1,13},{3,15... | collective-permute-start | bytes 1572872 | tf_op jit(solution)/shard_map/ppermute | solution.py:28
  22.7 0.8 copy-start.3
  39.1 12.2 %collective-permute-start.8 = (bf16[128,1024]{1,0:T(8,128)(2,1)}, bf16[128,1024]{1,0:T(8,128)(2,1)S(1)}, u32[]{:S(2)}, u32[]{:S(2)}) collective-permute-start(bf16[128,1024]{1,0:T(8,128)(2,1)} %collective-permute-done.6.near_ref), channel_id=1, source_target_pairs={{0,2},{2,0},{4,6},{6,4},{8,10},{10,8},{12,14},{14,12},{1,3},{3,1},... | collective-permute-start | bytes 786440 | tf_op jit(solution)/shard_map/ppermute | solution.py:28
  40.1 16.8 %collective-permute-start.10 = (bf16[128,1024]{1,0:T(8,128)(2,1)}, bf16[128,1024]{1,0:T(8,128)(2,1)S(1)}, u32[]{:S(2)}, u32[]{:S(2)}) collective-permute-start(bf16[128,1024]{1,0:T(8,128)(2,1)} %collective-permute-done.6.near_ref), channel_id=1, source_target_pairs={{0,4},{2,6},{4,8},{6,10},{8,12},{10,14},{12,0},{14,2},{1,5},{3,7},... | collective-permute-start | bytes 786440 | tf_op jit(solution)/shard_map/ppermute | solution.py:28
  42.3 2.1 %copy-start.7 = (bf16[256,1024]{1,0:T(8,128)(2,1)}, bf16[256,1024]{1,0:T(8,128)(2,1)S(1)}, u32[]{:S(2)}) copy-start(bf16[256,1024]{1,0:T(8,128)(2,1)S(1)} %collective-permute-done.7.far) | copy-start | bytes 1572868
  42.3 25.4 %collective-permute-start.13 = (bf16[128,1024]{1,0:T(8,128)(2,1)}, bf16[128,1024]{1,0:T(8,128)(2,1)S(1)}, u32[]{:S(2)}, u32[]{:S(2)}) collective-permute-start(bf16[128,1024]{1,0:T(8,128)(2,1)} %collective-permute-done.12.near_ref), channel_id=1, source_target_pairs={{0,2},{2,0},{4,6},{6,4},{8,10},{10,8},{12,14},{14,12},{1,3},{3,1},... | collective-permute-start | bytes 786440 | tf_op jit(solution)/shard_map/ppermute | solution.py:28
  43.2 16.7 %collective-permute-start.9 = (bf16[256,1024]{1,0:T(8,128)(2,1)}, bf16[256,1024]{1,0:T(8,128)(2,1)S(1)}, u32[]{:S(2)}, u32[]{:S(2)}) collective-permute-start(bf16[256,1024]{1,0:T(8,128)(2,1)} %collective-permute-done.near), channel_id=1, source_target_pairs={{0,2},{2,0},{4,6},{6,4},{8,10},{10,8},{12,14},{14,12},{1,3},{3,1},... | collective-permute-start | bytes 1572872 | tf_op jit(solution)/shard_map/ppermute | solution.py:28
  44.4 7.0 %copy-start.4 = (bf16[8,4,8,1024]{3,2,1,0:T(8,128)(2,1)S(1)}, bf16[8,4,8,1024]{3,2,1,0:T(8,128)(2,1)}, u32[]{:S(2)}) copy-start(bf16[8,4,8,1024]{3,2,1,0:T(8,128)(2,1)} %copy-done.3) | copy-start | bytes 1572868
  56.8 30.6 %collective-permute-start.1 = (bf16[256,1024]{1,0:T(8,128)(2,1)}, bf16[256,1024]{1,0:T(8,128)(2,1)}, u32[]{:S(2)}, u32[]{:S(2)}) collective-permute-start(bf16[256,1024]{1,0:T(8,128)(2,1)} %collective-permute-done.near), channel_id=1, source_target_pairs={{0,4},{2,6},{4,8},{6,10},{8,12},{10,14},{12,0},{14,2},{1,5},{3,7},... | collective-permute-start | bytes 1572872 | tf_op jit(solution)/shard_map/ppermute | solution.py:28
  56.9 16.2 %collective-permute-start.11 = (bf16[128,1024]{1,0:T(8,128)(2,1)S(1)}, bf16[128,1024]{1,0:T(8,128)(2,1)S(1)}, u32[]{:S(2)}, u32[]{:S(2)}) collective-permute-start(bf16[128,1024]{1,0:T(8,128)(2,1)S(1)} %collective-permute-done.10.near_ref), channel_id=1, source_target_pairs={{0,2},{2,0},{4,6},{6,4},{8,10},{10,8},{12,14},{14,12},{1,3},{3,1},... | collective-permute-start | bytes 786440 | tf_op jit(solution)/shard_map/ppermute | solution.py:28
  57.8 31.0 %collective-permute-start.5 = (bf16[256,1024]{1,0:T(8,128)(2,1)}, bf16[256,1024]{1,0:T(8,128)(2,1)}, u32[]{:S(2)}, u32[]{:S(2)}) collective-permute-start(bf16[256,1024]{1,0:T(8,128)(2,1)} %collective-permute-done.4.near), channel_id=1, source_target_pairs={{0,2},{2,0},{4,6},{6,4},{8,10},{10,8},{12,14},{14,12},{1,3},{3,1},... | collective-permute-start | bytes 1572872 | tf_op jit(solution)/shard_map/ppermute | solution.py:28
  60.0 0.8 copy-start.8
  78.0 0.8 copy-start.5
  78.8 19.5 %all-to-all-start.1 = ((bf16[8,4,8,1024]{3,2,1,0:T(8,128)(2,1)}), bf16[8,4,8,1024]{3,2,1,0:T(8,128)(2,1)}, u32[]{:S(2)}, u32[]{:S(2)}) async-start(bf16[8,4,8,1024]{3,2,1,0:T(8,128)(2,1)} %copy-done.5), calls=%async_computation.1 | async-start | bytes 1048576 | tf_op jit(solution)/shard_map/all_to_all | solution.py:347
  87.3 11.0 %collective-permute-start.2 = (bf16[256,1024]{1,0:T(8,128)(2,1)}, bf16[256,1024]{1,0:T(8,128)(2,1)}, u32[]{:S(2)}, u32[]{:S(2)}) collective-permute-start(bf16[256,1024]{1,0:T(8,128)(2,1)} %collective-permute-done.1.near), channel_id=1, source_target_pairs={{0,2},{2,0},{4,6},{6,4},{8,10},{10,8},{12,14},{14,12},{1,3},{3,1},... | collective-permute-start | bytes 1572872 | tf_op jit(solution)/shard_map/ppermute | solution.py:28
  106.1 5.8 %copy-start.2 = (bf16[1024,8192]{1,0:T(8,128)(2,1)S(1)}, bf16[1024,8192]{1,0:T(8,128)(2,1)}, u32[]{:S(2)}) copy-start(bf16[1024,8192]{1,0:T(8,128)(2,1)} %w_ref.1) | copy-start | bytes 50331652
  117.0 14.9 %collective-permute-start.14 = (bf16[256,1024]{1,0:T(8,128)(2,1)S(1)}, bf16[256,1024]{1,0:T(8,128)(2,1)S(1)}, u32[]{:S(2)}, u32[]{:S(2)}) collective-permute-start(bf16[256,1024]{1,0:T(8,128)(2,1)S(1)} %get-tuple-element.30), channel_id=1, source_target_pairs={{0,2},{2,0},{4,6},{6,4},{8,10},{10,8},{12,14},{14,12},{1,3},{3,1},... | collective-permute-start | bytes 1572872 | tf_op jit(solution)/shard_map/ppermute | solution.py:28
  117.5 21.9 %collective-permute-start.16 = (bf16[256,1024]{1,0:T(8,128)(2,1)S(1)}, bf16[256,1024]{1,0:T(8,128)(2,1)S(1)}, u32[]{:S(2)}, u32[]{:S(2)}) collective-permute-start(bf16[256,1024]{1,0:T(8,128)(2,1)S(1)} %get-tuple-element.32), channel_id=1, source_target_pairs={{0,2},{2,0},{4,6},{6,4},{8,10},{10,8},{12,14},{14,12},{1,3},{3,1},... | collective-permute-start | bytes 1572872 | tf_op jit(solution)/shard_map/ppermute | solution.py:28
  119.1 25.9 %collective-permute-start.18 = (bf16[256,1024]{1,0:T(8,128)(2,1)S(1)}, bf16[256,1024]{1,0:T(8,128)(2,1)S(1)}, u32[]{:S(2)}, u32[]{:S(2)}) collective-permute-start(bf16[256,1024]{1,0:T(8,128)(2,1)S(1)} %get-tuple-element.34), channel_id=1, source_target_pairs={{0,2},{2,0},{4,6},{6,4},{8,10},{10,8},{12,14},{14,12},{1,3},{3,1},... | collective-permute-start | bytes 1572872 | tf_op jit(solution)/shard_map/ppermute | solution.py:28
  119.5 31.1 %collective-permute-start.20 = (bf16[256,1024]{1,0:T(8,128)(2,1)S(1)}, bf16[256,1024]{1,0:T(8,128)(2,1)S(1)}, u32[]{:S(2)}, u32[]{:S(2)}) collective-permute-start(bf16[256,1024]{1,0:T(8,128)(2,1)S(1)} %get-tuple-element.36), channel_id=1, source_target_pairs={{0,2},{2,0},{4,6},{6,4},{8,10},{10,8},{12,14},{14,12},{1,3},{3,1},... | collective-permute-start | bytes 1572872 | tf_op jit(solution)/shard_map/ppermute | solution.py:28
  131.9 27.9 %copy-start.6 = (f32[256,1024]{1,0:T(8,128)S(1)}, f32[256,1024]{1,0:T(8,128)}, u32[]{:S(2)}) copy-start(f32[256,1024]{1,0:T(8,128)} %get-tuple-element.39) | copy-start | bytes 3145732
  132.1 20.0 %collective-permute-start.15 = (bf16[256,1024]{1,0:T(8,128)(2,1)S(1)}, bf16[256,1024]{1,0:T(8,128)(2,1)S(1)}, u32[]{:S(2)}, u32[]{:S(2)}) collective-permute-start(bf16[256,1024]{1,0:T(8,128)(2,1)S(1)} %add_convert_fusion.3), channel_id=1, source_target_pairs={{0,8},{2,10},{4,12},{6,14},{8,0},{10,2},{12,4},{14,6},{1,9},{3,11}... | collective-permute-start | bytes 1572872 | tf_op jit(solution)/shard_map/ppermute | solution.py:28
  139.6 20.3 %collective-permute-start.17 = (bf16[256,1024]{1,0:T(8,128)(2,1)S(1)}, bf16[256,1024]{1,0:T(8,128)(2,1)S(1)}, u32[]{:S(2)}, u32[]{:S(2)}) collective-permute-start(bf16[256,1024]{1,0:T(8,128)(2,1)S(1)} %add_convert_fusion.2), channel_id=1, source_target_pairs={{0,4},{2,6},{4,8},{6,10},{8,12},{10,14},{12,0},{14,2},{1,5},{3,7},... | collective-permute-start | bytes 1572872 | tf_op jit(solution)/shard_map/ppermute | solution.py:28
  145.0 16.2 %copy-start.1 = (bf16[512,1024]{1,0:T(8,128)(2,1)S(1)}, bf16[512,1024]{1,0:T(8,128)(2,1)}, u32[]{:S(2)}) copy-start(bf16[512,1024]{1,0:T(8,128)(2,1)} %param.10) | copy-start | bytes 3145732
  145.2 14.7 %collective-permute-start.19 = (bf16[256,1024]{1,0:T(8,128)(2,1)S(1)}, bf16[256,1024]{1,0:T(8,128)(2,1)S(1)}, u32[]{:S(2)}, u32[]{:S(2)}) collective-permute-start(bf16[256,1024]{1,0:T(8,128)(2,1)S(1)} %add_convert_fusion.1), channel_id=1, source_target_pairs={{0,12},{2,14},{4,0},{6,2},{8,4},{10,6},{12,8},{14,10},{1,13},{3,15... | collective-permute-start | bytes 1572872 | tf_op jit(solution)/shard_map/ppermute | solution.py:28

commit v11 on v7

--- a/solution.py
+++ b/solution.py
@@ -16,6 +16,7 @@
 IN_SMEM = pl.BlockSpec(memory_space=pltpu.SMEM)
 IN_VMEM = pl.BlockSpec(memory_space=pltpu.VMEM)
 IN_HBM = pl.BlockSpec(memory_space=pltpu.HBM)
+ANYWHERE = pl.BlockSpec(memory_space=pl.ANY)
 
 
 def moved(array, outer_by, flip):
@@ -61,38 +62,31 @@
     )(spot, *args)
 
 
-def history_kernel(steps, first, spot, lengths_ref, near_ref, far_ref, cache_hbm, *refs):
-    terms_ref, held, taps_scr, sems = refs if first else refs[1:]
+def history_kernel(steps, count, first, spot, lengths_ref, *refs):
+    tap_refs, cache_hbm = refs[:count], refs[count]
+    terms_ref, held, taps_scr, sems = refs[-4:]
     if not first:
-        terms_ref[...] = refs[0][...]
-    _, lags, rows, width = held.shape
-    channels = near_ref.shape[1]
-    parts = channels // width
+        terms_ref[...] = refs[count + 1][...]
+    slots, lags, rows, width = held.shape
+    owners, _, channels = tap_refs[0].shape
+    per_owner = terms_ref.shape[3] // width
+    at = pl.ds(pl.multiple_of(spot[0] * width, width), width)
     lengths = jnp.concatenate([lengths_ref[...]] * (width // LANES), axis=1)
 
-    def owner_of(flip):
-        return spot[0] * INNER + (spot[1] + flip) % INNER
-
-    def fetch(index):
-        start = (owner_of(index // parts) * parts + index % parts) * width
-        columns = pl.ds(pl.multiple_of(start, width), width)
-        return pltpu.make_async_copy(cache_hbm.at[:, :, columns], held.at[index], sems.at[index])
-
-    for index in range(2 * parts):
-        fetch(index).start()
-
-    def one_part(index, carry):
-        fetch(index).wait()
-        flip = index // parts
-        at = pl.ds(pl.multiple_of(index % parts * width, width), width)
-
-        @pl.when(flip == 0)
-        def _():
-            taps_scr[...] = near_ref[pl.ds(0, lags + 1), at].astype(jnp.float32)
-
-        @pl.when(flip == 1)
-        def _():
-            taps_scr[...] = far_ref[pl.ds(0, lags + 1), at].astype(jnp.float32)
+    def fetch(owner):
+        columns = pl.ds(pl.multiple_of((owner * per_owner + spot[0]) * width, width), width)
+        slot = lax.rem(owner, slots)
+        return pltpu.make_async_copy(cache_hbm.at[:, :, columns], held.at[slot], sems.at[slot])
+
+    for owner in range(min(slots, owners)):
+        fetch(owner).start()
+
+    def one_owner(owner, carry):
+        for index, tap_ref in enumerate(tap_refs):
+            start = pl.multiple_of((spot[1] + index) % count * channels, channels)
+            taps_scr[:, pl.ds(start, channels)] = tap_ref[owner].astype(jnp.float32)
+        fetch(owner).wait()
+        slot = lax.rem(owner, slots)
 
         def tap(lag):
             return jnp.broadcast_to(taps_scr[pl.ds(lag, 1), :], (rows, width))
@@ -100,44 +94,50 @@
         taps = [tap(1 + step) for step in range(steps)]
         sums = [jnp.zeros((rows, width), jnp.float32) for _ in range(steps)]
         for lag in range(lags):
-            values = jnp.where(lengths > lag, held[index, lag].astype(jnp.float32), 0.0)
+            values = jnp.where(lengths > lag, held[slot, lag].astype(jnp.float32), 0.0)
             for step in range(min(steps, lags - lag)):
                 sums[step] += values * taps[step]
             taps = taps[1:]
             if lag + 1 + steps <= lags:
                 taps.append(tap(lag + 1 + steps))
         for step in range(steps):
-            terms_ref[owner_of(flip), step, :, at] = sums[step].astype(terms_ref.dtype)
+            terms_ref[owner, step, :, at] = sums[step].astype(terms_ref.dtype)
+
+        @pl.when(owner + slots < owners)
+        def _():
+            fetch(owner + slots).start()
+
         return carry
 
-    lax.fori_loop(0, 2 * parts, one_part, 0)
-
-
-def history_terms(cache, near, far, lengths, spot, steps, earlier):
+    lax.fori_loop(0, owners, one_owner, 0)
+
+
+def history_terms(cache, tap_parts, lengths, spot, steps, earlier):
     lags, rows, total = cache.shape
-    channels = near.shape[1]
-    width = min(4 * LANES, channels)
-    count = 2 * channels // width
-    operands = [(IN_VMEM, lengths), (IN_VMEM, near), (IN_VMEM, far), (IN_HBM, cache)]
+    owners, tap_rows, channels = tap_parts[0].shape
+    count = len(tap_parts)
+    width = count * channels
+    operands = [(IN_VMEM, lengths), *[(IN_VMEM, taps) for taps in tap_parts], (IN_HBM, cache)]
     aliases = {}
     if earlier is not None:
         aliases = {len(operands) + 1: 0}
         operands.append((IN_VMEM, earlier))
-    shape = (total // channels, steps, rows, channels)
+    shape = (owners, steps, rows, total // owners)
+    slots = min(DEPTH, owners)
     return kernel_call(
-        functools.partial(history_kernel, steps, earlier is None),
+        functools.partial(history_kernel, steps, count, earlier is None),
         "history_terms",
         spot,
         operands,
         [(IN_VMEM, jax.ShapeDtypeStruct(shape, jnp.bfloat16))],
         aliases,
         [
-            pltpu.VMEM((count, lags, rows, width), jnp.bfloat16),
-            pltpu.VMEM((lags + 1, width), jnp.float32),
-            pltpu.SemaphoreType.DMA((count,)),
+            pltpu.VMEM((slots, lags, rows, width), jnp.bfloat16),
+            pltpu.VMEM((tap_rows, width), jnp.float32),
+            pltpu.SemaphoreType.DMA((slots,)),
         ],
-        2400 * steps * rows * lags * channels // 2,
-        4 * rows * lags * channels,
+        1200 * steps * rows * lags * owners * width // 2,
+        2 * rows * lags * owners * width,
     )[0]
 
 
@@ -257,7 +257,7 @@
     )[-1]
 
 
-def share_kernel(spot, x_ref, w_hbm, *refs):
+def share_kernel(spot, x_ref, w_any, *refs):
     *outs, held, sems = refs
     wide = outs[0].shape[1]
     slots, _, block = held.shape
@@ -267,7 +267,7 @@
     def fetch(chunk):
         start = pl.multiple_of(spot[chunk // parts] * wide + chunk % parts * block, block)
         slot = chunk % slots
-        return pltpu.make_async_copy(w_hbm.at[:, pl.ds(start, block)], held.at[slot], sems.at[slot])
+        return pltpu.make_async_copy(w_any.at[:, pl.ds(start, block)], held.at[slot], sems.at[slot])
 
     for chunk in range(min(slots, chunks)):
         fetch(chunk).start()
@@ -288,13 +288,31 @@
         share_kernel,
         "output_shares",
         jnp.stack([which for which, _ in targets]).astype(jnp.int32),
-        [(IN_VMEM, gated), (IN_HBM, w_out)],
+        [(IN_VMEM, gated), (ANYWHERE, w_out)],
         [(IN_VMEM, jax.ShapeDtypeStruct((rows, wide), kind)) for _, kind in targets],
         {},
-        [pltpu.VMEM((DEPTH, channels, block), jnp.bfloat16), pltpu.SemaphoreType.DMA((DEPTH,))],
+        [pltpu.VMEM((4, channels, block), jnp.bfloat16), pltpu.SemaphoreType.DMA((4,))],
         2 * rows * channels * wide * len(targets),
         2 * channels * wide * len(targets),
     )
+
+
+def gathered_taps(filters):
+    owners = lax.axis_size("tensor")
+    channels = filters.shape[0]
+    if lax.axis_size("groups") != 2 or lax.axis_size("batch") != 2 or channels % (4 * LANES):
+        return [(0, 0, [lax.all_gather(filters.T, "tensor")])]
+    group, half = lax.axis_index("groups"), lax.axis_index("batch")
+    quarter = channels // 4
+    own = lax.dynamic_slice_in_dim(filters, (group * 2 + half) * quarter, quarter, 0).T
+    own = jnp.broadcast_to(own[None], (owners, *own.shape))
+    own = lax.all_to_all(own, "tensor", 0, 0, tiled=True)
+    swap = [(0, 1), (1, 0)]
+    across = lax.ppermute(own, "groups", swap)
+    return [
+        (group, half, [own, lax.ppermute(own, "batch", swap)]),
+        (1 - group, half, [across, lax.ppermute(across, "batch", swap)]),
+    ]
 
 
 def after(array, earlier):
@@ -319,13 +337,8 @@
     tiny = lax.all_to_all(
         jnp.broadcast_to(tiny[None], (owners, *tiny.shape)), "tensor", 0, 0, tiled=True
     )
-    gain_rows = channels // LANES
-    gains = tiny[:, :gain_rows].reshape(owners, channels)
-    inv_rms = lax.rsqrt(jnp.sum(tiny[:, gain_rows:], axis=0).reshape(tokens) / D + EPSILON)
-    inv_rms = jnp.broadcast_to(inv_rms[:, None], (tokens, LANES))
-    own_taps = filters.T
-    lag_taps = spread(own_taps)
-    streams = spread(after(stream.astype(jnp.bfloat16), own_taps))
+    lag_taps = gathered_taps(filters)
+    streams = spread(stream.astype(jnp.bfloat16))
 
     def spot_at(back):
         return jnp.stack([(outer + back) % outer_size, inner]).astype(jnp.int32)
@@ -344,22 +357,34 @@
     place = place.astype(jnp.bfloat16)
 
     cache = cache_rows.transpose(1, 0, 2)
+    def history_part(part, after_these, earlier):
+        place_at, first, parts = part
+        if after_these is not None:
+            parts = [after(parts[0], after_these), *parts[1:]]
+        spot = jnp.stack([jnp.int32(place_at), jnp.int32(first)])
+        return history_terms(cache, parts, row_lengths, spot, steps, earlier)
+
+    first_terms = history_part(lag_taps[0], None, None)
     near_taps = filters[:, : 2 * steps].T.astype(jnp.float32)
-    terms = sums = None
-    parts = len(streams)
-    for index, (back, near, far) in enumerate(lag_taps):
-        if index:
-            near = after(near, sums)
-        terms = history_terms(cache, near, far, row_lengths, spot_at(-back), steps, terms)
-        if 2 * index < parts:
-            at, *pair = streams[index]
-            pair[0] = after(pair[0], terms)
-            sums = projected(spot_at(-at), pair, gains, inv_rms, w_in, sums)
-    terms = lax.all_to_all(terms, "tensor", 0, 0, tiled=True)
-    terms = terms.reshape(owners * steps * rows, channels)
-    for index in range((parts + 1) // 2, parts):
+    tiny = after(tiny, (first_terms, place, near_taps))
+    gain_rows = channels // LANES
+    gains = tiny[:, :gain_rows].reshape(owners, channels)
+    inv_rms = lax.rsqrt(jnp.sum(tiny[:, gain_rows:], axis=0).reshape(tokens) / D + EPSILON)
+    inv_rms = jnp.broadcast_to(inv_rms[:, None], (tokens, LANES))
+
+    at, *pair = streams[0]
+    pair[0] = after(pair[0], first_terms)
+    sums = projected(spot_at(-at), pair, gains, inv_rms, w_in, None)
+    terms = first_terms
+    for part in lag_taps[1:]:
+        terms = history_part(part, (sums, streams[1][1]), terms)
+    sent = lax.all_to_all(terms, "tensor", 0, 0, tiled=True)
+    sent = sent.reshape(owners * steps * rows, channels)
+    for index in range(1, len(streams)):
         at, *pair = streams[index]
-        ends = (steps, near_taps, place, terms) if index == parts - 1 else None
+        if index == 1:
+            pair[0] = after(pair[0], (terms, streams[-1][1]))
+        ends = (steps, near_taps, place, sent) if index == len(streams) - 1 else None
         sums = projected(spot_at(-at), pair, gains, inv_rms, w_in, sums, ends)
     gated = sums
 
@@ -369,15 +394,14 @@
     order = sorted(range(outer_size), key=lambda ahead: (ahead == 0, -min(ahead, outer_size - ahead)))
     targets = [(owner_at(ahead, 1), jnp.bfloat16) for ahead in order]
     targets += [(owner_at(ahead, 0), jnp.float32) for ahead in order]
-    shares = list(output_shares(targets[:2], gated, w_out, owners))
-    across = [moved(share, 0, 1) for share in shares]
-    for start in range(2, len(targets), 6):
-        shares += output_shares(targets[start : start + 6], gated, w_out, owners)
-    across += [moved(share, 0, 1) for share in shares[2:outer_size]]
+    shares = output_shares(targets, gated, w_out, owners)
+    across = [moved(share, 0, 1) for share in shares[:outer_size]]
     out = stream
     for ahead, own_share, arrived_share in zip(order, shares[outer_size:], across):
         share = own_share + arrived_share.astype(jnp.float32)
-        out = out + (moved(share.astype(jnp.bfloat16), ahead, 0) if ahead else share)
+        if ahead:
+            share = share.astype(jnp.bfloat16)
+        out = out + (moved(share, ahead, 0) if ahead else share).astype(jnp.float32)
     return out.astype(jnp.bfloat16).reshape(steps, seqs, channels)
 
 

time: 174 us -> 200 us (1.15)
  waiting for transfers between devices: 60.3 us -> 88.8 us
  local copies, waits for them, and re-layouts: 5.89 us -> 12.6 us
  Pallas kernels: 60.8 us -> 56.7 us
  starting transfers between devices: 38.9 us -> 35.4 us
    ppermute x21 -> x14, waiting for transfers between devices: 48.2 us -> 70.8 us  [moved(): return lax.ppermute(array, 'tensor', pairs)]
    all_to_all x1 -> x2, waiting for transfers between devices: 0.01 us -> 15.9 us  [the longest x1 15.9 us: gathered_taps(): own = lax.all_to_all(own, 'tensor', 0, 0, tiled=True)]
    all_to_all x1, waiting for transfers between devices: 12.1 us -> 0.01 us  [per_device(): lax.all_to_all(jnp.broadcast_to(tiny[None], (owners, *tiny.shape)), 'tens...]
    ppermute x21 -> x14, starting transfers between devices: 26.7 us -> 16.8 us  [moved(): return lax.ppermute(array, 'tensor', pairs)]
    all_to_all x1 -> x2, starting transfers between devices: 6.74 us -> 11.6 us  [the longest x1 6.02 us: per_device(): sent = lax.all_to_all(terms, 'tensor', 0, 0, tiled=True)]
    unnamed x27 -> x29, local copies, waits for them, and re-layouts: 3.84 us -> 8.6 us
    pallas_call x10 -> x7, Pallas kernels: 60.8 us -> 56.7 us  [kernel_call(): pl.pallas_call(kernel, in_specs=[IN_SMEM, *specs], out_specs=list(out_spe...]
    ppermute x0 -> x3, waiting for transfers between devices: none -> 2.06 us  [the longest x1 2.06 us: gathered_taps(): across = lax.ppermute(own, 'groups', swap)]
  transfers between devices with their start and end apart: 23 -> 20, of which waited for: 9 -> 9; matrix products, arithmetic and copies ran while one was open for 3% -> 2% of each run, Pallas kernels for 29% -> 20%
where the time goes in v11:
time: 200 us; the launch traced here: 198 us
  waiting for transfers between devices  88.8 us (44%)
  Pallas kernels  56.7 us (28%)
  starting transfers between devices  35.4 us (18%)
  local copies, waits for them, and re-layouts  12.6 us (6%)
  other arithmetic  2.75 us (1%)
    ppermute x14, waiting for transfers between devices, moved(): return lax.ppermute(array, 'tensor', pairs)  70.8 us
    pallas_call x7, Pallas kernels, kernel_call(): pl.pallas_call(kernel, in_specs=[IN_SMEM, *specs], out_specs=list(out_spe...  56.7 us
    ppermute x14, starting transfers between devices, moved(): return lax.ppermute(array, 'tensor', pairs)  16.8 us
    all_to_all x1, waiting for transfers between devices, gathered_taps(): own = lax.all_to_all(own, 'tensor', 0, 0, tiled=True)  15.9 us
    unnamed x29, local copies, waits for them, and re-layouts  8.6 us
    all_to_all x1, starting transfers between devices, per_device(): lax.all_to_all(jnp.broadcast_to(tiny[None], (owners, *tiny.shape)), 'tens...  6.55 us
    all_to_all x1, starting transfers between devices, per_device(): sent = lax.all_to_all(terms, 'tensor', 0, 0, tiled=True)  6.02 us
    all_to_all x1, starting transfers between devices, gathered_taps(): own = lax.all_to_all(own, 'tensor', 0, 0, tiled=True)  5.54 us
  transfers between devices with their start and end apart: 20, of which 9 were waited for; matrix products, arithmetic and copies ran while one was open for 2% of the time, Pallas kernels for 20%

profile of v11, /device:TPU:18, one launch (start us, length us, event | category | flops | bytes accessed | tf_op | source)
XLA Modules:
  0.0 198.1 jit_solution(5767358205114129954)
XLA Ops:
  0.0 0.9 eq.88
  0.9 0.4 copy-done
  1.3 1.5 multiply_reduce_fusion
  2.8 1.5 collective-permute-start.7
  4.3 1.6 collective-permute-start
  5.8 0.4 collective-permute-start.4
  6.3 0.8 dynamic-slice_bitcast_fusion
  7.1 0.1 copy.22
  7.3 0.8 broadcast_in_dim.27
  8.1 5.5 %all-to-all-start.1 = ((bf16[8,128,256]{2,1,0:T(8,128)(2,1)}), bf16[8,128,256]{2,1,0:T(8,128)(2,1)S(1)}, u32[]{:S(2)}, u32[]{:S(2)}) async-start(bf16[8,128,256]{2,1,0:T(8,128)(2,1)} %broadcast_in_dim.27), calls=%async_computation.1 | async-start | bytes 1048576 | tf_op jit(solution)/shard_map/all_to_all | solution.py:309
  13.7 0.1 reshape.69
  13.8 0.1 iota_compare_fusion.2
  14.0 0.2 and_convert_fusion
  14.2 0.2 reshape.73
  14.4 0.1 copy.25
  14.5 0.1 copy.24.refs_2_
  14.7 0.1 stack.81.spot
  14.8 0.1 pad_add_fusion.1.spot
  14.8 0.1 pad_add_fusion.4.spot
  14.9 0.1 pad_add_fusion.5.spot
  15.0 0.1 pad_add_fusion.3.spot
  15.1 17.5 %collective-permute-done.near = bf16[256,1024]{1,0:T(8,128)(2,1)} collective-permute-done((bf16[256,1024]{1,0:T(8,128)(2,1)S(1)}, bf16[256,1024]{1,0:T(8,128)(2,1)}, u32[]{:S(2)}, u32[]{:S(2)}) %collective-permute-start) | collective-permute-done | bytes 524320 | tf_op jit(solution)/shard_map/ppermute | solution.py:29
  32.6 1.8 collective-permute-start.1
  34.4 15.9 %all-to-all-done.1.refs_0_ = bf16[8,128,256]{2,1,0:T(8,128)(2,1)S(1)} async-done(((bf16[8,128,256]{2,1,0:T(8,128)(2,1)}), bf16[8,128,256]{2,1,0:T(8,128)(2,1)S(1)}, u32[]{:S(2)}, u32[]{:S(2)}) %all-to-all-start.1) | async-done | bytes 524320 | tf_op jit(solution)/shard_map/all_to_all | solution.py:309
  50.3 0.6 broadcast_in_dim.23
  50.9 6.5 %all-to-all-start = ((f32[8,10,128]{2,1,0:T(8,128)}), f32[8,10,128]{2,1,0:T(8,128)S(1)}, u32[]{:S(2)}, u32[]{:S(2)}) async-start(f32[8,10,128]{2,1,0:T(8,128)} %broadcast_in_dim.23), calls=%async_computation | async-start | bytes 131072 | tf_op jit(solution)/shard_map/all_to_all | solution.py:337
  57.5 0.1 pad_add_fusion.2.spot
  57.5 0.1 pad_add_fusion.spot
  57.6 0.2 select_reduce_fusion
  57.8 1.5 collective-permute-start.9
  59.3 0.6 collective-permute-start.5
  59.9 0.5 collective-permute-start.6
  60.4 1.5 collective-permute-start.2
  62.0 8.9 %history_terms.2.refs_3_ = bf16[8,4,8,1024]{3,2,1,0:T(8,128)(2,1)S(1)} custom-call(s32[2]{0:T(128)S(1)} %pad_add_fusion.1.spot, s32[8,128]{1,0:T(8,128)S(1)} %broadcast_in_dim.26.lengths_ref, bf16[8,128,256]{2,1,0:T(8,128)(2,1)S(1)} %all-to-all-done.1.refs_0_, bf16[8,128,256]{2,1,0:T(8,128)(2,1)S(1)} %collective-permute-done.3.refs_1_, ...), custom_call_target="tpu_custom_call" | custom-call | flops 9987686400 | bytes 8323072 | tf_op jit(solution)/shard_map/history_terms/pallas_call | solution.py:52
  70.9 0.8 copy-done.3
  71.7 2.1 %collective-permute-done.6.refs_0_ = bf16[8,128,256]{2,1,0:T(8,128)(2,1)} collective-permute-done((bf16[8,128,256]{2,1,0:T(8,128)(2,1)S(1)}, bf16[8,128,256]{2,1,0:T(8,128)(2,1)}, u32[]{:S(2)}, u32[]{:S(2)}) %collective-permute-start.6) | collective-permute-done | bytes 524320 | tf_op jit(solution)/shard_map/ppermute | solution.py:311
  73.8 0.1 broadcast_in_dim.28.inv_ref
  73.9 0.7 copy-done.8
  74.6 6.9 %projected_part.3.refs_0_ = f32[256,3072]{1,0:T(8,128)S(1)} custom-call(s32[2]{0:T(128)S(1)} %pad_add_fusion.5.spot, bf16[256,1024]{1,0:T(8,128)(2,1)} %copy-done.7, bf16[256,1024]{1,0:T(8,128)(2,1)} %copy-done.8, f32[8,1024]{1,0:T(8,128)S(1)} %bitcast.39, f32[256,128]{1,0:T(8,128)S(1)} %broadcast_in_dim.28.inv_ref, bf16[8192,3072]{1,0:T(8,128)(2,1)} %w_hbm.7), custom_call_target="tpu_custom_call" | custom-call | flops 6442450944 | bytes 25165824 | tf_op jit(solution)/shard_map/projected_part/pallas_call | solution.py:52
  81.6 9.4 %history_terms.3 = bf16[8,4,8,1024]{3,2,1,0:T(8,128)(2,1)S(1)} custom-call(s32[2]{0:T(128)S(1)} %pad_add_fusion.4.spot, s32[8,128]{1,0:T(8,128)S(1)} %broadcast_in_dim.26.lengths_ref, bf16[8,128,256]{2,1,0:T(8,128)(2,1)} %collective-permute-done.6.refs_0_, bf16[8,128,256]{2,1,0:T(8,128)(2,1)S(1)} %collective-permute-done.8.refs_1_, ...), custom_call_target="tpu_custom_call", output_to_operand_aliasing={{}: (5, {})} | custom-call | flops 9987686400 | bytes 8323072 | tf_op jit(solution)/shard_map/history_terms/pallas_call | solution.py:52
  91.0 0.8 copy-done.5
  91.8 6.0 %all-to-all-start.2 = ((bf16[8,4,8,1024]{3,2,1,0:T(8,128)(2,1)}), bf16[8,4,8,1024]{3,2,1,0:T(8,128)(2,1)}, u32[]{:S(2)}, u32[]{:S(2)}) async-start(bf16[8,4,8,1024]{3,2,1,0:T(8,128)(2,1)} %copy-done.5), calls=%async_computation.2 | async-start | bytes 1048576 | tf_op jit(solution)/shard_map/all_to_all | solution.py:381
  97.8 6.9 %projected_part.4.refs_0_ = f32[256,3072]{1,0:T(8,128)S(1)} custom-call(s32[2]{0:T(128)S(1)} %pad_add_fusion.3.spot, bf16[256,1024]{1,0:T(8,128)(2,1)} %collective-permute-done.near, bf16[256,1024]{1,0:T(8,128)(2,1)} %collective-permute-done.9.far, f32[8,1024]{1,0:T(8,128)S(1)} %bitcast.40, ...), custom_call_target="tpu_custom_call", output_to_operand_aliasing={{}: (6, {})} | custom-call | flops 6442450944 | bytes 25165824 | tf_op jit(solution)/shard_map/projected_part/pallas_call | solution.py:52
  104.8 6.9 %projected_part.5.refs_0_ = f32[256,3072]{1,0:T(8,128)S(1)} custom-call(s32[2]{0:T(128)S(1)} %pad_add_fusion.2.spot, bf16[256,1024]{1,0:T(8,128)(2,1)} %collective-permute-done.4.near, bf16[256,1024]{1,0:T(8,128)(2,1)} %collective-permute-done.5.far, f32[8,1024]{1,0:T(8,128)S(1)} %bitcast.41, ...), custom_call_target="tpu_custom_call", output_to_operand_aliasing={{}: (6, {})} | custom-call | flops 6442450944 | bytes 25165824 | tf_op jit(solution)/shard_map/projected_part/pallas_call | solution.py:52
  111.7 7.8 %gated_rows.1 = (f32[256,3072]{1,0:T(8,128)S(1)}, bf16[256,1024]{1,0:T(8,128)(2,1)S(1)}) custom-call(s32[2]{0:T(128)S(1)} %pad_add_fusion.spot, bf16[256,1024]{1,0:T(8,128)(2,1)} %collective-permute-done.1.near, bf16[256,1024]{1,0:T(8,128)(2,1)} %collective-permute-done.2.far, f32[8,1024]{1,0:T(8,128)S(1)} %bitcast.42, ...), custom_call_target="tpu_custom_call", output_to_operand_aliasing={{0}: (6, {})} | custom-call | flops 6442450944 | bytes 25165824 | tf_op jit(solution)/shard_map/gated_rows/pallas_call | solution.py:52
  119.5 5.8 %copy-done.2 = bf16[1024,8192]{1,0:T(8,128)(2,1)S(1)} copy-done((bf16[1024,8192]{1,0:T(8,128)(2,1)S(1)}, bf16[1024,8192]{1,0:T(8,128)(2,1)}, u32[]{:S(2)}) %copy-start.2) | copy-done | bytes 16777240
  125.3 9.8 %output_shares.1 = (bf16[256,1024]{1,0:T(8,128)(2,1)S(1)}, bf16[256,1024]{1,0:T(8,128)(2,1)S(1)}, bf16[256,1024]{1,0:T(8,128)(2,1)S(1)}, bf16[256,1024]{1,0:T(8,...) custom-call(s32[8]{0:T(128)S(1)} %stack.81.spot, ...), custom_call_target="tpu_custom_call" | custom-call | flops 4294967296 | bytes 16777216 | tf_op jit(solution)/shard_map/output_shares/pallas_call | solution.py:52
  135.1 1.5 collective-permute-start.10
  136.6 0.6 collective-permute-start.12
  137.2 1.5 collective-permute-start.14
  138.6 0.6 collective-permute-start.16
  139.2 10.7 %collective-permute-done.10 = bf16[256,1024]{1,0:T(8,128)(2,1)S(1)} collective-permute-done((bf16[256,1024]{1,0:T(8,128)(2,1)S(1)}, bf16[256,1024]{1,0:T(8,128)(2,1)S(1)}, u32[]{:S(2)}, u32[]{:S(2)}) %collective-permute-start.10) | collective-permute-done | bytes 524320 | tf_op jit(solution)/shard_map/ppermute | solution.py:29
  149.9 0.2 add_convert_fusion.3
  150.1 1.5 collective-permute-start.11
  151.6 9.6 %collective-permute-done.12 = bf16[256,1024]{1,0:T(8,128)(2,1)S(1)} collective-permute-done((bf16[256,1024]{1,0:T(8,128)(2,1)S(1)}, bf16[256,1024]{1,0:T(8,128)(2,1)S(1)}, u32[]{:S(2)}, u32[]{:S(2)}) %collective-permute-start.12) | collective-permute-done | bytes 524320 | tf_op jit(solution)/shard_map/ppermute | solution.py:29
  161.2 0.2 add_convert_fusion.2
  161.3 1.5 collective-permute-start.13
  162.9 9.6 %collective-permute-done.14 = bf16[256,1024]{1,0:T(8,128)(2,1)S(1)} collective-permute-done((bf16[256,1024]{1,0:T(8,128)(2,1)S(1)}, bf16[256,1024]{1,0:T(8,128)(2,1)S(1)}, u32[]{:S(2)}, u32[]{:S(2)}) %collective-permute-start.14) | collective-permute-done | bytes 524320 | tf_op jit(solution)/shard_map/ppermute | solution.py:29
  172.4 0.2 add_convert_fusion.1
  172.6 0.7 collective-permute-start.15
  173.3 9.3 %collective-permute-done.16 = bf16[256,1024]{1,0:T(8,128)(2,1)S(1)} collective-permute-done((bf16[256,1024]{1,0:T(8,128)(2,1)S(1)}, bf16[256,1024]{1,0:T(8,128)(2,1)S(1)}, u32[]{:S(2)}, u32[]{:S(2)}) %collective-permute-start.16) | collective-permute-done | bytes 524320 | tf_op jit(solution)/shard_map/ppermute | solution.py:29
  182.6 1.0 collective-permute-done.11
  183.6 13.1 %collective-permute-done.13 = bf16[256,1024]{1,0:T(8,128)(2,1)S(1)} collective-permute-done((bf16[256,1024]{1,0:T(8,128)(2,1)S(1)}, bf16[256,1024]{1,0:T(8,128)(2,1)S(1)}, u32[]{:S(2)}, u32[]{:S(2)}) %collective-permute-start.13) | collective-permute-done | bytes 524320 | tf_op jit(solution)/shard_map/ppermute | solution.py:29
  196.7 1.3 add_convert_fusion
  (45 shorter events, 0.2 us)
Async XLA Ops:
  0.0 1.3 copy-start
  0.0 14.4 %copy-start.9 = (bf16[1024,128]{1,0:T(8,128)(2,1)S(1)}, bf16[1024,128]{1,0:T(8,128)(2,1)}, u32[]{:S(2)}) copy-start(bf16[1024,128]{1,0:T(8,128)(2,1)} %param.13) | copy-start | bytes 786436
  0.0 13.6 %copy-start.11 = (s32[128]{0:T(128)S(1)}, s32[128]{0:T(128)}, u32[]{:S(2)}) copy-start(s32[128]{0:T(128)} %param.16) | copy-start | bytes 1540
  0.0 14.4 %copy-start.10 = (bf16[1024]{0:T(1024)(128)(2,1)S(1)}, bf16[1024]{0:T(1024)(128)(2,1)}, u32[]{:S(2)}) copy-start(bf16[1024]{0:T(1024)(128)(2,1)} %param.11) | copy-start | bytes 6148
  1.3 56.3 %copy-start.12 = (s32[64]{0:T(128)S(1)}, s32[64]{0:T(128)}, u32[]{:S(2)}) copy-start(s32[64]{0:T(128)} %param.17) | copy-start | bytes 772
  2.7 68.1 %copy-start.7 = (bf16[256,1024]{1,0:T(8,128)(2,1)}, bf16[256,1024]{1,0:T(8,128)(2,1)S(1)}, u32[]{:S(2)}) copy-start(bf16[256,1024]{1,0:T(8,128)(2,1)S(1)} %get-tuple-element.19.near) | copy-start | bytes 1572868
  2.8 71.1 %collective-permute-start.7 = (bf16[256,1024]{1,0:T(8,128)(2,1)S(1)}, bf16[256,1024]{1,0:T(8,128)(2,1)S(1)}, u32[]{:S(2)}, u32[]{:S(2)}) collective-permute-start(bf16[256,1024]{1,0:T(8,128)(2,1)S(1)} %get-tuple-element.19.near), channel_id=1, source_target_pairs={{0,2},{2,0},{4,6},{6,4},{8,10},{10,8},{12,14},{14,12},{1,3},{3,1},... | collective-permute-start | bytes 1572872 | tf_op jit(solution)/shard_map/ppermute | solution.py:29
  4.3 28.3 %collective-permute-start = (bf16[256,1024]{1,0:T(8,128)(2,1)S(1)}, bf16[256,1024]{1,0:T(8,128)(2,1)}, u32[]{:S(2)}, u32[]{:S(2)}) collective-permute-start(bf16[256,1024]{1,0:T(8,128)(2,1)S(1)} %get-tuple-element.19.near), channel_id=1, source_target_pairs={{0,4},{2,6},{4,8},{6,10},{8,12},{10,14},{12,0},{14,2},{1,5},{3,7},... | collective-permute-start | bytes 1572872 | tf_op jit(solution)/shard_map/ppermute | solution.py:29
  5.8 53.5 %collective-permute-start.4 = (bf16[256,1024]{1,0:T(8,128)(2,1)S(1)}, bf16[256,1024]{1,0:T(8,128)(2,1)}, u32[]{:S(2)}, u32[]{:S(2)}) collective-permute-start(bf16[256,1024]{1,0:T(8,128)(2,1)S(1)} %get-tuple-element.19.near), channel_id=1, source_target_pairs={{0,12},{2,14},{4,0},{6,2},{8,4},{10,6},{12,8},{14,10},{1,13},{3,15... | collective-permute-start | bytes 1572872 | tf_op jit(solution)/shard_map/ppermute | solution.py:29
  8.1 42.2 %all-to-all-start.1 = ((bf16[8,128,256]{2,1,0:T(8,128)(2,1)}), bf16[8,128,256]{2,1,0:T(8,128)(2,1)S(1)}, u32[]{:S(2)}, u32[]{:S(2)}) async-start(bf16[8,128,256]{2,1,0:T(8,128)(2,1)} %broadcast_in_dim.27), calls=%async_computation.1 | async-start | bytes 1048576 | tf_op jit(solution)/shard_map/all_to_all | solution.py:309
  32.6 27.3 %collective-permute-start.1 = (bf16[256,1024]{1,0:T(8,128)(2,1)}, bf16[256,1024]{1,0:T(8,128)(2,1)}, u32[]{:S(2)}, u32[]{:S(2)}) collective-permute-start(bf16[256,1024]{1,0:T(8,128)(2,1)} %collective-permute-done.near), channel_id=1, source_target_pairs={{0,4},{2,6},{4,8},{6,10},{8,12},{10,14},{12,0},{14,2},{1,5},{3,7},... | collective-permute-start | bytes 1572872 | tf_op jit(solution)/shard_map/ppermute | solution.py:29
  50.9 20.8 %all-to-all-start = ((f32[8,10,128]{2,1,0:T(8,128)}), f32[8,10,128]{2,1,0:T(8,128)S(1)}, u32[]{:S(2)}, u32[]{:S(2)}) async-start(f32[8,10,128]{2,1,0:T(8,128)} %broadcast_in_dim.23), calls=%async_computation | async-start | bytes 131072 | tf_op jit(solution)/shard_map/all_to_all | solution.py:337
  57.5 3.0 %collective-permute-start.3 = (bf16[8,128,256]{2,1,0:T(8,128)(2,1)S(1)}, bf16[8,128,256]{2,1,0:T(8,128)(2,1)S(1)}, u32[]{:S(2)}, u32[]{:S(2)}) collective-permute-start(bf16[8,128,256]{2,1,0:T(8,128)(2,1)S(1)} %all-to-all-done.1.refs_0_), channel_id=1, source_target_pairs={{0,1},{1,0},{2,3},{3,2},{4,5},{5,4},{6,7},{7,6},{8,9},{9,8},{10,11... | collective-permute-start | bytes 1572872 | tf_op jit(solution)/shard_map/ppermute | solution.py:313
  57.8 40.0 %collective-permute-start.9 = (bf16[256,1024]{1,0:T(8,128)(2,1)}, bf16[256,1024]{1,0:T(8,128)(2,1)}, u32[]{:S(2)}, u32[]{:S(2)}) collective-permute-start(bf16[256,1024]{1,0:T(8,128)(2,1)} %collective-permute-done.near), channel_id=1, source_target_pairs={{0,2},{2,0},{4,6},{6,4},{8,10},{10,8},{12,14},{14,12},{1,3},{3,1},... | collective-permute-start | bytes 1572872 | tf_op jit(solution)/shard_map/ppermute | solution.py:29
  59.3 45.4 %collective-permute-start.5 = (bf16[256,1024]{1,0:T(8,128)(2,1)}, bf16[256,1024]{1,0:T(8,128)(2,1)}, u32[]{:S(2)}, u32[]{:S(2)}) collective-permute-start(bf16[256,1024]{1,0:T(8,128)(2,1)} %collective-permute-done.4.near), channel_id=1, source_target_pairs={{0,2},{2,0},{4,6},{6,4},{8,10},{10,8},{12,14},{14,12},{1,3},{3,1},... | collective-permute-start | bytes 1572872 | tf_op jit(solution)/shard_map/ppermute | solution.py:29
  59.9 13.9 %collective-permute-start.6 = (bf16[8,128,256]{2,1,0:T(8,128)(2,1)S(1)}, bf16[8,128,256]{2,1,0:T(8,128)(2,1)}, u32[]{:S(2)}, u32[]{:S(2)}) collective-permute-start(bf16[8,128,256]{2,1,0:T(8,128)(2,1)S(1)} %all-to-all-done.1.refs_0_), channel_id=1, source_target_pairs={{0,16},{16,0},{1,17},{17,1},{2,18},{18,2},{3,19},{19,3},{4,20},{20... | collective-permute-start | bytes 1572872 | tf_op jit(solution)/shard_map/ppermute | solution.py:311
  60.4 51.2 %collective-permute-start.2 = (bf16[256,1024]{1,0:T(8,128)(2,1)}, bf16[256,1024]{1,0:T(8,128)(2,1)}, u32[]{:S(2)}, u32[]{:S(2)}) collective-permute-start(bf16[256,1024]{1,0:T(8,128)(2,1)} %collective-permute-done.1.near), channel_id=1, source_target_pairs={{0,2},{2,0},{4,6},{6,4},{8,10},{10,8},{12,14},{14,12},{1,3},{3,1},... | collective-permute-start | bytes 1572872 | tf_op jit(solution)/shard_map/ppermute | solution.py:29
  70.9 0.8 copy-start.3
  73.8 7.8 %collective-permute-start.8 = (bf16[8,128,256]{2,1,0:T(8,128)(2,1)}, bf16[8,128,256]{2,1,0:T(8,128)(2,1)S(1)}, u32[]{:S(2)}, u32[]{:S(2)}) collective-permute-start(bf16[8,128,256]{2,1,0:T(8,128)(2,1)} %collective-permute-done.6.refs_0_), channel_id=1, source_target_pairs={{0,1},{1,0},{2,3},{3,2},{4,5},{5,4},{6,7},{7,6},{8,9},{9,8},{10,11... | collective-permute-start | bytes 1572872 | tf_op jit(solution)/shard_map/ppermute | solution.py:314
  73.8 0.8 copy-start.8
  74.6 6.9 %copy-start.4 = (bf16[8,4,8,1024]{3,2,1,0:T(8,128)(2,1)S(1)}, bf16[8,4,8,1024]{3,2,1,0:T(8,128)(2,1)}, u32[]{:S(2)}) copy-start(bf16[8,4,8,1024]{3,2,1,0:T(8,128)(2,1)} %copy-done.3) | copy-start | bytes 1572868
  91.0 0.8 copy-start.5
  91.8 19.9 %all-to-all-start.2 = ((bf16[8,4,8,1024]{3,2,1,0:T(8,128)(2,1)}), bf16[8,4,8,1024]{3,2,1,0:T(8,128)(2,1)}, u32[]{:S(2)}, u32[]{:S(2)}) async-start(bf16[8,4,8,1024]{3,2,1,0:T(8,128)(2,1)} %copy-done.5), calls=%async_computation.2 | async-start | bytes 1048576 | tf_op jit(solution)/shard_map/all_to_all | solution.py:381
  119.5 5.8 %copy-start.2 = (bf16[1024,8192]{1,0:T(8,128)(2,1)S(1)}, bf16[1024,8192]{1,0:T(8,128)(2,1)}, u32[]{:S(2)}) copy-start(bf16[1024,8192]{1,0:T(8,128)(2,1)} %w_any.1) | copy-start | bytes 50331652
  135.1 14.9 %collective-permute-start.10 = (bf16[256,1024]{1,0:T(8,128)(2,1)S(1)}, bf16[256,1024]{1,0:T(8,128)(2,1)S(1)}, u32[]{:S(2)}, u32[]{:S(2)}) collective-permute-start(bf16[256,1024]{1,0:T(8,128)(2,1)S(1)} %get-tuple-element.24), channel_id=1, source_target_pairs={{0,2},{2,0},{4,6},{6,4},{8,10},{10,8},{12,14},{14,12},{1,3},{3,1},... | collective-permute-start | bytes 1572872 | tf_op jit(solution)/shard_map/ppermute | solution.py:29
  136.6 24.6 %collective-permute-start.12 = (bf16[256,1024]{1,0:T(8,128)(2,1)S(1)}, bf16[256,1024]{1,0:T(8,128)(2,1)S(1)}, u32[]{:S(2)}, u32[]{:S(2)}) collective-permute-start(bf16[256,1024]{1,0:T(8,128)(2,1)S(1)} %get-tuple-element.26), channel_id=1, source_target_pairs={{0,2},{2,0},{4,6},{6,4},{8,10},{10,8},{12,14},{14,12},{1,3},{3,1},... | collective-permute-start | bytes 1572872 | tf_op jit(solution)/shard_map/ppermute | solution.py:29
  137.2 35.2 %collective-permute-start.14 = (bf16[256,1024]{1,0:T(8,128)(2,1)S(1)}, bf16[256,1024]{1,0:T(8,128)(2,1)S(1)}, u32[]{:S(2)}, u32[]{:S(2)}) collective-permute-start(bf16[256,1024]{1,0:T(8,128)(2,1)S(1)} %get-tuple-element.28), channel_id=1, source_target_pairs={{0,2},{2,0},{4,6},{6,4},{8,10},{10,8},{12,14},{14,12},{1,3},{3,1},... | collective-permute-start | bytes 1572872 | tf_op jit(solution)/shard_map/ppermute | solution.py:29
  138.6 44.0 %collective-permute-start.16 = (bf16[256,1024]{1,0:T(8,128)(2,1)S(1)}, bf16[256,1024]{1,0:T(8,128)(2,1)S(1)}, u32[]{:S(2)}, u32[]{:S(2)}) collective-permute-start(bf16[256,1024]{1,0:T(8,128)(2,1)S(1)} %get-tuple-element.30), channel_id=1, source_target_pairs={{0,2},{2,0},{4,6},{6,4},{8,10},{10,8},{12,14},{14,12},{1,3},{3,1},... | collective-permute-start | bytes 1572872 | tf_op jit(solution)/shard_map/ppermute | solution.py:29
  149.9 46.8 %copy-start.6 = (f32[256,1024]{1,0:T(8,128)S(1)}, f32[256,1024]{1,0:T(8,128)}, u32[]{:S(2)}) copy-start(f32[256,1024]{1,0:T(8,128)} %get-tuple-element.33) | copy-start | bytes 3145732
  150.1 33.5 %collective-permute-start.11 = (bf16[256,1024]{1,0:T(8,128)(2,1)S(1)}, bf16[256,1024]{1,0:T(8,128)(2,1)S(1)}, u32[]{:S(2)}, u32[]{:S(2)}) collective-permute-start(bf16[256,1024]{1,0:T(8,128)(2,1)S(1)} %add_convert_fusion.3), channel_id=1, source_target_pairs={{0,8},{2,10},{4,12},{6,14},{8,0},{10,2},{12,4},{14,6},{1,9},{3,11}... | collective-permute-start | bytes 1572872 | tf_op jit(solution)/shard_map/ppermute | solution.py:29
  161.3 35.4 %collective-permute-start.13 = (bf16[256,1024]{1,0:T(8,128)(2,1)S(1)}, bf16[256,1024]{1,0:T(8,128)(2,1)S(1)}, u32[]{:S(2)}, u32[]{:S(2)}) collective-permute-start(bf16[256,1024]{1,0:T(8,128)(2,1)S(1)} %add_convert_fusion.2), channel_id=1, source_target_pairs={{0,4},{2,6},{4,8},{6,10},{8,12},{10,14},{12,0},{14,2},{1,5},{3,7},... | collective-permute-start | bytes 1572872 | tf_op jit(solution)/shard_map/ppermute | solution.py:29
  172.4 25.7 %copy-start.1 = (bf16[512,1024]{1,0:T(8,128)(2,1)S(1)}, bf16[512,1024]{1,0:T(8,128)(2,1)}, u32[]{:S(2)}) copy-start(bf16[512,1024]{1,0:T(8,128)(2,1)} %param.10) | copy-start | bytes 3145732
  172.6 24.1 %collective-permute-start.15 = (bf16[256,1024]{1,0:T(8,128)(2,1)S(1)}, bf16[256,1024]{1,0:T(8,128)(2,1)S(1)}, u32[]{:S(2)}, u32[]{:S(2)}) collective-permute-start(bf16[256,1024]{1,0:T(8,128)(2,1)S(1)} %add_convert_fusion.1), channel_id=1, source_target_pairs={{0,12},{2,14},{4,0},{6,2},{8,4},{10,6},{12,8},{14,10},{1,13},{3,15... | collective-permute-start | bytes 1572872 | tf_op jit(solution)/shard_map/ppermute | solution.py:29

commit v12 on v11

--- a/solution.py
+++ b/solution.py
@@ -16,7 +16,6 @@
 IN_SMEM = pl.BlockSpec(memory_space=pltpu.SMEM)
 IN_VMEM = pl.BlockSpec(memory_space=pltpu.VMEM)
 IN_HBM = pl.BlockSpec(memory_space=pltpu.HBM)
-ANYWHERE = pl.BlockSpec(memory_space=pl.ANY)
 
 
 def moved(array, outer_by, flip):
@@ -257,41 +256,27 @@
     )[-1]
 
 
-def share_kernel(spot, x_ref, w_any, *refs):
-    *outs, held, sems = refs
+def share_kernel(spot, x_ref, w_ref, *outs):
     wide = outs[0].shape[1]
-    slots, _, block = held.shape
-    parts = wide // block
-    chunks = len(outs) * parts
-
-    def fetch(chunk):
-        start = pl.multiple_of(spot[chunk // parts] * wide + chunk % parts * block, block)
-        slot = chunk % slots
-        return pltpu.make_async_copy(w_any.at[:, pl.ds(start, block)], held.at[slot], sems.at[slot])
-
-    for chunk in range(min(slots, chunks)):
-        fetch(chunk).start()
-    for chunk in range(chunks):
-        fetch(chunk).wait()
-        out_ref = outs[chunk // parts]
-        share = jnp.dot(x_ref[...], held[chunk % slots], preferred_element_type=jnp.float32)
-        out_ref[:, pl.ds(chunk % parts * block, block)] = share.astype(out_ref.dtype)
-        if chunk + slots < chunks:
-            fetch(chunk + slots).start()
+    block = min(512, wide)
+    for index, out_ref in enumerate(outs):
+        for start in range(0, wide, block):
+            columns = pl.ds(pl.multiple_of(spot[index] * wide + start, block), block)
+            share = jnp.dot(x_ref[...], w_ref[:, columns], preferred_element_type=jnp.float32)
+            out_ref[:, pl.ds(start, block)] = share.astype(out_ref.dtype)
 
 
 def output_shares(targets, gated, w_out, owners):
     rows, channels = gated.shape
     wide = w_out.shape[1] // owners
-    block = min(512, wide)
     return kernel_call(
         share_kernel,
         "output_shares",
         jnp.stack([which for which, _ in targets]).astype(jnp.int32),
-        [(IN_VMEM, gated), (ANYWHERE, w_out)],
+        [(IN_VMEM, gated), (IN_VMEM, w_out)],
         [(IN_VMEM, jax.ShapeDtypeStruct((rows, wide), kind)) for _, kind in targets],
         {},
-        [pltpu.VMEM((4, channels, block), jnp.bfloat16), pltpu.SemaphoreType.DMA((4,))],
+        [],
         2 * rows * channels * wide * len(targets),
         2 * channels * wide * len(targets),
     )
@@ -338,7 +323,7 @@
         jnp.broadcast_to(tiny[None], (owners, *tiny.shape)), "tensor", 0, 0, tiled=True
     )
     lag_taps = gathered_taps(filters)
-    streams = spread(stream.astype(jnp.bfloat16))
+    streams = spread(after(stream.astype(jnp.bfloat16), (lag_taps[0][2][0], tiny)))
 
     def spot_at(back):
         return jnp.stack([(outer + back) % outer_size, inner]).astype(jnp.int32)

time: 200 us -> 183 us (0.915)
  the two profiles are of different devices: /device:TPU:18 before, /device:TPU:0 now
where the time goes in v12:
time: 183 us; the launch traced here: 182 us
  waiting for transfers between devices  77.2 us (42%)
  Pallas kernels  51.5 us (28%)
  starting transfers between devices  35.4 us (19%)
  local copies, waits for them, and re-layouts  12.9 us (7%)
  other arithmetic  3.44 us (2%)
    ppermute x14, waiting for transfers between devices, moved(): return lax.ppermute(array, 'tensor', pairs)  61.2 us
    pallas_call x7, Pallas kernels, kernel_call(): pl.pallas_call(kernel, in_specs=[IN_SMEM, *specs], out_specs=list(out_spe...  51.5 us
    ppermute x14, starting transfers between devices, moved(): return lax.ppermute(array, 'tensor', pairs)  16.8 us
    all_to_all x1, waiting for transfers between devices, gathered_taps(): own = lax.all_to_all(own, 'tensor', 0, 0, tiled=True)  8.44 us
    unnamed x17, local copies, waits for them, and re-layouts  8.33 us
    all_to_all x1, starting transfers between devices, gathered_taps(): own = lax.all_to_all(own, 'tensor', 0, 0, tiled=True)  7.28 us
    all_to_all x1, waiting for transfers between devices, per_device(): lax.all_to_all(jnp.broadcast_to(tiny[None], (owners, *tiny.shape)), 'tens...  6.55 us
    all_to_all x1, starting transfers between devices, per_device(): sent = lax.all_to_all(terms, 'tensor', 0, 0, tiled=True)  6.11 us
  transfers between devices with their start and end apart: 20, of which 11 were waited for; matrix products, arithmetic and copies ran while one was open for 4% of the time, Pallas kernels for 21%

profile of v12, /device:TPU:0, one launch (start us, length us, event | category | flops | bytes accessed | tf_op | source)
XLA Modules:
  0.0 182.4 jit_solution(16895094666549976067)
XLA Ops:
  0.0 0.9 dynamic-slice_bitcast_fusion
  0.9 0.1 copy.22
  1.1 0.8 broadcast_in_dim.22
  1.9 7.3 %all-to-all-start = ((bf16[8,128,256]{2,1,0:T(8,128)(2,1)}), bf16[8,128,256]{2,1,0:T(8,128)(2,1)S(1)}, u32[]{:S(2)}, u32[]{:S(2)}) async-start(bf16[8,128,256]{2,1,0:T(8,128)(2,1)} %broadcast_in_dim.22), calls=%async_computation | async-start | bytes 1048576 | tf_op jit(solution)/shard_map/all_to_all | solution.py:294
  9.3 0.7 reshape.69
  10.1 0.8 eq.88
  10.8 0.7 convert_element_type.51
  11.5 0.1 iota_compare_fusion.2
  11.6 0.2 and_convert_fusion
  11.8 0.2 reshape.73
  12.0 1.0 copy.25
  13.0 0.1 copy.24.refs_2_
  13.2 0.1 stack.81.spot
  13.3 0.1 pad_add_fusion.1.spot
  13.3 0.1 pad_add_fusion.4.spot
  13.4 0.1 pad_add_fusion.5.spot
  13.5 0.1 pad_add_fusion.3.spot
  13.6 1.6 multiply_reduce_fusion
  15.2 8.4 %all-to-all-done.refs_0_ = bf16[8,128,256]{2,1,0:T(8,128)(2,1)S(1)} async-done(((bf16[8,128,256]{2,1,0:T(8,128)(2,1)}), bf16[8,128,256]{2,1,0:T(8,128)(2,1)S(1)}, u32[]{:S(2)}, u32[]{:S(2)}) %all-to-all-start) | async-done | bytes 524320 | tf_op jit(solution)/shard_map/all_to_all | solution.py:294
  23.6 0.6 broadcast_in_dim.24
  24.3 3.6 %all-to-all-start.1 = ((f32[8,10,128]{2,1,0:T(8,128)}), f32[8,10,128]{2,1,0:T(8,128)S(1)}, u32[]{:S(2)}, u32[]{:S(2)}) async-start(f32[8,10,128]{2,1,0:T(8,128)} %broadcast_in_dim.24), calls=%async_computation.1 | async-start | bytes 131072 | tf_op jit(solution)/shard_map/all_to_all | solution.py:322
  27.9 0.1 pad_add_fusion.2.spot
  28.0 0.2 select_reduce_fusion
  28.2 0.1 pad_add_fusion.spot
  28.3 6.6 %all-to-all-done.1 = f32[8,10,128]{2,1,0:T(8,128)S(1)} async-done(((f32[8,10,128]{2,1,0:T(8,128)}), f32[8,10,128]{2,1,0:T(8,128)S(1)}, u32[]{:S(2)}, u32[]{:S(2)}) %all-to-all-start.1) | async-done | bytes 40992 | tf_op jit(solution)/shard_map/all_to_all | solution.py:322
  34.8 0.4 collective-permute-start.7
  35.2 0.8 collective-permute-start
  36.0 3.0 %collective-permute-start.4 = (bf16[256,1024]{1,0:T(8,128)(2,1)}, bf16[256,1024]{1,0:T(8,128)(2,1)}, u32[]{:S(2)}, u32[]{:S(2)}) collective-permute-start(bf16[256,1024]{1,0:T(8,128)(2,1)} %get-tuple-element.21.near), channel_id=1, source_target_pairs={{0,12},{2,14},{4,0},{6,2},{8,4},{10,6},{12,8},{14,10},{1,13},{3,15... | collective-permute-start | bytes 1572872 | tf_op jit(solution)/shard_map/ppermute | solution.py:28
  39.0 1.5 collective-permute-start.6
  40.5 0.1 broadcast_in_dim.27.lengths_ref
  40.6 8.9 %history_terms.2.refs_3_ = bf16[8,4,8,1024]{3,2,1,0:T(8,128)(2,1)S(1)} custom-call(s32[2]{0:T(128)S(1)} %pad_add_fusion.1.spot, s32[8,128]{1,0:T(8,128)S(1)} %broadcast_in_dim.27.lengths_ref, bf16[8,128,256]{2,1,0:T(8,128)(2,1)S(1)} %all-to-all-done.refs_0_, bf16[8,128,256]{2,1,0:T(8,128)(2,1)S(1)} %collective-permute-done.3.refs_1_, ...), custom_call_target="tpu_custom_call" | custom-call | flops 9987686400 | bytes 8323072 | tf_op jit(solution)/shard_map/history_terms/pallas_call | solution.py:51
  49.5 1.1 collective-permute-done.6.refs_0_
  50.7 0.1 broadcast_in_dim.28.inv_ref
  50.7 0.7 copy-done.5
  51.4 6.9 %projected_part.3.refs_0_ = f32[256,3072]{1,0:T(8,128)S(1)} custom-call(s32[2]{0:T(128)S(1)} %pad_add_fusion.5.spot, bf16[256,1024]{1,0:T(8,128)(2,1)} %get-tuple-element.21.near, bf16[256,1024]{1,0:T(8,128)(2,1)} %copy-done.5, f32[8,1024]{1,0:T(8,128)S(1)} %bitcast.39, f32[256,128]{1,0:T(8,128)S(1)} %broadcast_in_dim.28.inv_ref, bf16[8192,3072]{1,0:T(8,128)(2,1)} %w_hbm.7), custom_call_target="tpu_custom_call" | custom-call | flops 6442450944 | bytes 25165824 | tf_op jit(solution)/shard_map/projected_part/pallas_call | solution.py:51
  58.4 1.8 collective-permute-start.9
  60.3 0.4 collective-permute-start.5
  60.6 8.9 %history_terms.3 = bf16[8,4,8,1024]{3,2,1,0:T(8,128)(2,1)S(1)} custom-call(s32[2]{0:T(128)S(1)} %pad_add_fusion.4.spot, s32[8,128]{1,0:T(8,128)S(1)} %broadcast_in_dim.27.lengths_ref, bf16[8,128,256]{2,1,0:T(8,128)(2,1)S(1)} %collective-permute-done.6.refs_0_, ...), custom_call_target="tpu_custom_call", output_to_operand_aliasing={{}: (5, {})} | custom-call | flops 9987686400 | bytes 8323072 | tf_op jit(solution)/shard_map/history_terms/pallas_call | solution.py:51
  69.6 0.8 copy-done.3
  70.3 6.1 %all-to-all-start.2 = ((bf16[8,4,8,1024]{3,2,1,0:T(8,128)(2,1)}), bf16[8,4,8,1024]{3,2,1,0:T(8,128)(2,1)}, u32[]{:S(2)}, u32[]{:S(2)}) async-start(bf16[8,4,8,1024]{3,2,1,0:T(8,128)(2,1)} %copy-done.3), calls=%async_computation.2 | async-start | bytes 1048576 | tf_op jit(solution)/shard_map/all_to_all | solution.py:366
  76.4 2.0 %collective-permute-start.2 = (bf16[256,1024]{1,0:T(8,128)(2,1)}, bf16[256,1024]{1,0:T(8,128)(2,1)}, u32[]{:S(2)}, u32[]{:S(2)}) collective-permute-start(bf16[256,1024]{1,0:T(8,128)(2,1)} %collective-permute-done.1.near), channel_id=1, source_target_pairs={{0,2},{2,0},{4,6},{6,4},{8,10},{10,8},{12,14},{14,12},{1,3},{3,1},... | collective-permute-start | bytes 1572872 | tf_op jit(solution)/shard_map/ppermute | solution.py:28
  78.5 6.9 %projected_part.4.refs_0_ = f32[256,3072]{1,0:T(8,128)S(1)} custom-call(s32[2]{0:T(128)S(1)} %pad_add_fusion.3.spot, bf16[256,1024]{1,0:T(8,128)(2,1)} %collective-permute-done.near, bf16[256,1024]{1,0:T(8,128)(2,1)} %collective-permute-done.9.far, f32[8,1024]{1,0:T(8,128)S(1)} %bitcast.40, ...), custom_call_target="tpu_custom_call", output_to_operand_aliasing={{}: (6, {})} | custom-call | flops 6442450944 | bytes 25165824 | tf_op jit(solution)/shard_map/projected_part/pallas_call | solution.py:51
  85.4 2.9 %collective-permute-done.5.far = bf16[256,1024]{1,0:T(8,128)(2,1)} collective-permute-done((bf16[256,1024]{1,0:T(8,128)(2,1)}, bf16[256,1024]{1,0:T(8,128)(2,1)}, u32[]{:S(2)}, u32[]{:S(2)}) %collective-permute-start.5) | collective-permute-done | bytes 524320 | tf_op jit(solution)/shard_map/ppermute | solution.py:28
  88.3 6.9 %projected_part.5.refs_0_ = f32[256,3072]{1,0:T(8,128)S(1)} custom-call(s32[2]{0:T(128)S(1)} %pad_add_fusion.2.spot, bf16[256,1024]{1,0:T(8,128)(2,1)} %collective-permute-done.4.near, bf16[256,1024]{1,0:T(8,128)(2,1)} %collective-permute-done.5.far, f32[8,1024]{1,0:T(8,128)S(1)} %bitcast.41, ...), custom_call_target="tpu_custom_call", output_to_operand_aliasing={{}: (6, {})} | custom-call | flops 6442450944 | bytes 25165824 | tf_op jit(solution)/shard_map/projected_part/pallas_call | solution.py:51
  95.2 6.0 %collective-permute-done.2.far = bf16[256,1024]{1,0:T(8,128)(2,1)} collective-permute-done((bf16[256,1024]{1,0:T(8,128)(2,1)}, bf16[256,1024]{1,0:T(8,128)(2,1)}, u32[]{:S(2)}, u32[]{:S(2)}) %collective-permute-start.2) | collective-permute-done | bytes 524320 | tf_op jit(solution)/shard_map/ppermute | solution.py:28
  101.3 7.8 %gated_rows.1 = (f32[256,3072]{1,0:T(8,128)S(1)}, bf16[256,1024]{1,0:T(8,128)(2,1)S(1)}) custom-call(s32[2]{0:T(128)S(1)} %pad_add_fusion.spot, bf16[256,1024]{1,0:T(8,128)(2,1)} %collective-permute-done.1.near, bf16[256,1024]{1,0:T(8,128)(2,1)} %collective-permute-done.2.far, f32[8,1024]{1,0:T(8,128)S(1)} %bitcast.42, ...), custom_call_target="tpu_custom_call", output_to_operand_aliasing={{0}: (6, {})} | custom-call | flops 6442450944 | bytes 25165824 | tf_op jit(solution)/shard_map/gated_rows/pallas_call | solution.py:51
  109.0 5.8 %copy-done.2 = bf16[1024,8192]{1,0:T(8,128)(2,1)S(1)} copy-done((bf16[1024,8192]{1,0:T(8,128)(2,1)S(1)}, bf16[1024,8192]{1,0:T(8,128)(2,1)}, u32[]{:S(2)}) %copy-start.2) | copy-done | bytes 16777240
  114.8 5.1 %output_shares.1 = (bf16[256,1024]{1,0:T(8,128)(2,1)S(1)}, bf16[256,1024]{1,0:T(8,128)(2,1)S(1)}, bf16[256,1024]{1,0:T(8,128)(2,1)S(1)}, bf16[256,1024]{1,0:T(8,...) custom-call(s32[8]{0:T(128)S(1)} %stack.81.spot, ...), custom_call_target="tpu_custom_call" | custom-call | flops 4294967296 | bytes 16777216 | tf_op jit(solution)/shard_map/output_shares/pallas_call | solution.py:51
  120.0 1.8 collective-permute-start.10
  121.8 0.3 collective-permute-start.12
  122.0 1.7 collective-permute-start.14
  123.8 0.3 collective-permute-start.16
  124.1 10.8 %collective-permute-done.10 = bf16[256,1024]{1,0:T(8,128)(2,1)S(1)} collective-permute-done((bf16[256,1024]{1,0:T(8,128)(2,1)S(1)}, bf16[256,1024]{1,0:T(8,128)(2,1)S(1)}, u32[]{:S(2)}, u32[]{:S(2)}) %collective-permute-start.10) | collective-permute-done | bytes 524320 | tf_op jit(solution)/shard_map/ppermute | solution.py:28
  134.9 0.2 add_convert_fusion.3
  135.0 0.6 collective-permute-start.11
  135.6 10.5 %collective-permute-done.12 = bf16[256,1024]{1,0:T(8,128)(2,1)S(1)} collective-permute-done((bf16[256,1024]{1,0:T(8,128)(2,1)S(1)}, bf16[256,1024]{1,0:T(8,128)(2,1)S(1)}, u32[]{:S(2)}, u32[]{:S(2)}) %collective-permute-start.12) | collective-permute-done | bytes 524320 | tf_op jit(solution)/shard_map/ppermute | solution.py:28
  146.1 0.2 add_convert_fusion.2
  146.3 11.0 %collective-permute-done.14 = bf16[256,1024]{1,0:T(8,128)(2,1)S(1)} collective-permute-done((bf16[256,1024]{1,0:T(8,128)(2,1)S(1)}, bf16[256,1024]{1,0:T(8,128)(2,1)S(1)}, u32[]{:S(2)}, u32[]{:S(2)}) %collective-permute-start.14) | collective-permute-done | bytes 524320 | tf_op jit(solution)/shard_map/ppermute | solution.py:28
  157.3 0.2 add_convert_fusion.1
  157.5 3.6 %collective-permute-start.15 = (bf16[256,1024]{1,0:T(8,128)(2,1)S(1)}, bf16[256,1024]{1,0:T(8,128)(2,1)S(1)}, u32[]{:S(2)}, u32[]{:S(2)}) collective-permute-start(bf16[256,1024]{1,0:T(8,128)(2,1)S(1)} %add_convert_fusion.1), channel_id=1, source_target_pairs={{0,12},{2,14},{4,0},{6,2},{8,4},{10,6},{12,8},{14,10},{1,13},{3,15... | collective-permute-start | bytes 1572872 | tf_op jit(solution)/shard_map/ppermute | solution.py:28
  161.1 6.2 %collective-permute-done.16 = bf16[256,1024]{1,0:T(8,128)(2,1)S(1)} collective-permute-done((bf16[256,1024]{1,0:T(8,128)(2,1)S(1)}, bf16[256,1024]{1,0:T(8,128)(2,1)S(1)}, u32[]{:S(2)}, u32[]{:S(2)}) %collective-permute-start.16) | collective-permute-done | bytes 524320 | tf_op jit(solution)/shard_map/ppermute | solution.py:28
  167.3 3.0 %collective-permute-done.11 = bf16[256,1024]{1,0:T(8,128)(2,1)S(1)} collective-permute-done((bf16[256,1024]{1,0:T(8,128)(2,1)S(1)}, bf16[256,1024]{1,0:T(8,128)(2,1)S(1)}, u32[]{:S(2)}, u32[]{:S(2)}) %collective-permute-start.11) | collective-permute-done | bytes 524320 | tf_op jit(solution)/shard_map/ppermute | solution.py:28
  170.3 10.8 %collective-permute-done.15 = bf16[256,1024]{1,0:T(8,128)(2,1)S(1)} collective-permute-done((bf16[256,1024]{1,0:T(8,128)(2,1)S(1)}, bf16[256,1024]{1,0:T(8,128)(2,1)S(1)}, u32[]{:S(2)}, u32[]{:S(2)}) %collective-permute-start.15) | collective-permute-done | bytes 524320 | tf_op jit(solution)/shard_map/ppermute | solution.py:28
  181.1 1.3 add_convert_fusion
  (33 shorter events, 0.2 us)
Async XLA Ops:
  0.0 13.6 %copy-start = (bf16[512,1024]{1,0:T(8,128)(2,1)S(1)}, bf16[512,1024]{1,0:T(8,128)(2,1)}, u32[]{:S(2)}) copy-start(bf16[512,1024]{1,0:T(8,128)(2,1)} %param.10) | copy-start | bytes 3145732
  0.0 28.0 %copy-start.6 = (s32[64]{0:T(128)S(1)}, s32[64]{0:T(128)}, u32[]{:S(2)}) copy-start(s32[64]{0:T(128)} %param.17) | copy-start | bytes 772
  1.9 21.8 %all-to-all-start = ((bf16[8,128,256]{2,1,0:T(8,128)(2,1)}), bf16[8,128,256]{2,1,0:T(8,128)(2,1)S(1)}, u32[]{:S(2)}, u32[]{:S(2)}) async-start(bf16[8,128,256]{2,1,0:T(8,128)(2,1)} %broadcast_in_dim.22), calls=%async_computation | async-start | bytes 1048576 | tf_op jit(solution)/shard_map/all_to_all | solution.py:294
  24.3 10.5 %all-to-all-start.1 = ((f32[8,10,128]{2,1,0:T(8,128)}), f32[8,10,128]{2,1,0:T(8,128)S(1)}, u32[]{:S(2)}, u32[]{:S(2)}) async-start(f32[8,10,128]{2,1,0:T(8,128)} %broadcast_in_dim.24), calls=%async_computation.1 | async-start | bytes 131072 | tf_op jit(solution)/shard_map/all_to_all | solution.py:322
  27.9 12.6 %collective-permute-start.3 = (bf16[8,128,256]{2,1,0:T(8,128)(2,1)S(1)}, bf16[8,128,256]{2,1,0:T(8,128)(2,1)S(1)}, u32[]{:S(2)}, u32[]{:S(2)}) collective-permute-start(bf16[8,128,256]{2,1,0:T(8,128)(2,1)S(1)} %all-to-all-done.refs_0_), channel_id=1, source_target_pairs={{0,1},{1,0},{2,3},{3,2},{4,5},{5,4},{6,7},{7,6},{8,9},{9,8},{10,11... | collective-permute-start | bytes 1572872 | tf_op jit(solution)/shard_map/ppermute | solution.py:298
  34.8 15.8 %collective-permute-start.7 = (bf16[256,1024]{1,0:T(8,128)(2,1)}, bf16[256,1024]{1,0:T(8,128)(2,1)S(1)}, u32[]{:S(2)}, u32[]{:S(2)}) collective-permute-start(bf16[256,1024]{1,0:T(8,128)(2,1)} %get-tuple-element.21.near), channel_id=1, source_target_pairs={{0,2},{2,0},{4,6},{6,4},{8,10},{10,8},{12,14},{14,12},{1,3},{3,1},... | collective-permute-start | bytes 1572872 | tf_op jit(solution)/shard_map/ppermute | solution.py:28
  35.2 23.2 %collective-permute-start = (bf16[256,1024]{1,0:T(8,128)(2,1)}, bf16[256,1024]{1,0:T(8,128)(2,1)}, u32[]{:S(2)}, u32[]{:S(2)}) collective-permute-start(bf16[256,1024]{1,0:T(8,128)(2,1)} %get-tuple-element.21.near), channel_id=1, source_target_pairs={{0,4},{2,6},{4,8},{6,10},{8,12},{10,14},{12,0},{14,2},{1,5},{3,7},... | collective-permute-start | bytes 1572872 | tf_op jit(solution)/shard_map/ppermute | solution.py:28
  36.0 24.2 %collective-permute-start.4 = (bf16[256,1024]{1,0:T(8,128)(2,1)}, bf16[256,1024]{1,0:T(8,128)(2,1)}, u32[]{:S(2)}, u32[]{:S(2)}) collective-permute-start(bf16[256,1024]{1,0:T(8,128)(2,1)} %get-tuple-element.21.near), channel_id=1, source_target_pairs={{0,12},{2,14},{4,0},{6,2},{8,4},{10,6},{12,8},{14,10},{1,13},{3,15... | collective-permute-start | bytes 1572872 | tf_op jit(solution)/shard_map/ppermute | solution.py:28
  39.0 11.6 %collective-permute-start.6 = (bf16[8,128,256]{2,1,0:T(8,128)(2,1)S(1)}, bf16[8,128,256]{2,1,0:T(8,128)(2,1)S(1)}, u32[]{:S(2)}, u32[]{:S(2)}) collective-permute-start(bf16[8,128,256]{2,1,0:T(8,128)(2,1)S(1)} %all-to-all-done.refs_0_), channel_id=1, source_target_pairs={{0,16},{16,0},{1,17},{17,1},{2,18},{18,2},{3,19},{19,3},{4,20},{20... | collective-permute-start | bytes 1572872 | tf_op jit(solution)/shard_map/ppermute | solution.py:296
  50.6 10.0 %collective-permute-start.8 = (bf16[8,128,256]{2,1,0:T(8,128)(2,1)S(1)}, bf16[8,128,256]{2,1,0:T(8,128)(2,1)S(1)}, u32[]{:S(2)}, u32[]{:S(2)}) collective-permute-start(bf16[8,128,256]{2,1,0:T(8,128)(2,1)S(1)} %collective-permute-done.6.refs_0_), channel_id=1, source_target_pairs={{0,1},{1,0},{2,3},{3,2},{4,5},{5,4},{6,7},{7,6},{8,9},{9,8},{10,11... | collective-permute-start | bytes 1572872 | tf_op jit(solution)/shard_map/ppermute | solution.py:299
  50.6 0.8 copy-start.5
  58.4 18.1 %collective-permute-start.1 = (bf16[256,1024]{1,0:T(8,128)(2,1)}, bf16[256,1024]{1,0:T(8,128)(2,1)}, u32[]{:S(2)}, u32[]{:S(2)}) collective-permute-start(bf16[256,1024]{1,0:T(8,128)(2,1)} %collective-permute-done.near), channel_id=1, source_target_pairs={{0,4},{2,6},{4,8},{6,10},{8,12},{10,14},{12,0},{14,2},{1,5},{3,7},... | collective-permute-start | bytes 1572872 | tf_op jit(solution)/shard_map/ppermute | solution.py:28
  58.4 20.0 %collective-permute-start.9 = (bf16[256,1024]{1,0:T(8,128)(2,1)}, bf16[256,1024]{1,0:T(8,128)(2,1)}, u32[]{:S(2)}, u32[]{:S(2)}) collective-permute-start(bf16[256,1024]{1,0:T(8,128)(2,1)} %collective-permute-done.near), channel_id=1, source_target_pairs={{0,2},{2,0},{4,6},{6,4},{8,10},{10,8},{12,14},{14,12},{1,3},{3,1},... | collective-permute-start | bytes 1572872 | tf_op jit(solution)/shard_map/ppermute | solution.py:28
  60.3 28.0 %collective-permute-start.5 = (bf16[256,1024]{1,0:T(8,128)(2,1)}, bf16[256,1024]{1,0:T(8,128)(2,1)}, u32[]{:S(2)}, u32[]{:S(2)}) collective-permute-start(bf16[256,1024]{1,0:T(8,128)(2,1)} %collective-permute-done.4.near), channel_id=1, source_target_pairs={{0,2},{2,0},{4,6},{6,4},{8,10},{10,8},{12,14},{14,12},{1,3},{3,1},... | collective-permute-start | bytes 1572872 | tf_op jit(solution)/shard_map/ppermute | solution.py:28
  69.5 0.8 copy-start.3
  70.3 30.9 %all-to-all-start.2 = ((bf16[8,4,8,1024]{3,2,1,0:T(8,128)(2,1)}), bf16[8,4,8,1024]{3,2,1,0:T(8,128)(2,1)}, u32[]{:S(2)}, u32[]{:S(2)}) async-start(bf16[8,4,8,1024]{3,2,1,0:T(8,128)(2,1)} %copy-done.3), calls=%async_computation.2 | async-start | bytes 1048576 | tf_op jit(solution)/shard_map/all_to_all | solution.py:366
  76.4 24.8 %collective-permute-start.2 = (bf16[256,1024]{1,0:T(8,128)(2,1)}, bf16[256,1024]{1,0:T(8,128)(2,1)}, u32[]{:S(2)}, u32[]{:S(2)}) collective-permute-start(bf16[256,1024]{1,0:T(8,128)(2,1)} %collective-permute-done.1.near), channel_id=1, source_target_pairs={{0,2},{2,0},{4,6},{6,4},{8,10},{10,8},{12,14},{14,12},{1,3},{3,1},... | collective-permute-start | bytes 1572872 | tf_op jit(solution)/shard_map/ppermute | solution.py:28
  109.0 5.8 %copy-start.2 = (bf16[1024,8192]{1,0:T(8,128)(2,1)S(1)}, bf16[1024,8192]{1,0:T(8,128)(2,1)}, u32[]{:S(2)}) copy-start(bf16[1024,8192]{1,0:T(8,128)(2,1)} %w_ref.1) | copy-start | bytes 50331652
  120.0 14.9 %collective-permute-start.10 = (bf16[256,1024]{1,0:T(8,128)(2,1)S(1)}, bf16[256,1024]{1,0:T(8,128)(2,1)S(1)}, u32[]{:S(2)}, u32[]{:S(2)}) collective-permute-start(bf16[256,1024]{1,0:T(8,128)(2,1)S(1)} %get-tuple-element.26), channel_id=1, source_target_pairs={{0,2},{2,0},{4,6},{6,4},{8,10},{10,8},{12,14},{14,12},{1,3},{3,1},... | collective-permute-start | bytes 1572872 | tf_op jit(solution)/shard_map/ppermute | solution.py:28
  121.8 24.3 %collective-permute-start.12 = (bf16[256,1024]{1,0:T(8,128)(2,1)S(1)}, bf16[256,1024]{1,0:T(8,128)(2,1)S(1)}, u32[]{:S(2)}, u32[]{:S(2)}) collective-permute-start(bf16[256,1024]{1,0:T(8,128)(2,1)S(1)} %get-tuple-element.28), channel_id=1, source_target_pairs={{0,2},{2,0},{4,6},{6,4},{8,10},{10,8},{12,14},{14,12},{1,3},{3,1},... | collective-permute-start | bytes 1572872 | tf_op jit(solution)/shard_map/ppermute | solution.py:28
  122.0 35.3 %collective-permute-start.14 = (bf16[256,1024]{1,0:T(8,128)(2,1)S(1)}, bf16[256,1024]{1,0:T(8,128)(2,1)S(1)}, u32[]{:S(2)}, u32[]{:S(2)}) collective-permute-start(bf16[256,1024]{1,0:T(8,128)(2,1)S(1)} %get-tuple-element.30), channel_id=1, source_target_pairs={{0,2},{2,0},{4,6},{6,4},{8,10},{10,8},{12,14},{14,12},{1,3},{3,1},... | collective-permute-start | bytes 1572872 | tf_op jit(solution)/shard_map/ppermute | solution.py:28
  123.8 43.5 %collective-permute-start.16 = (bf16[256,1024]{1,0:T(8,128)(2,1)S(1)}, bf16[256,1024]{1,0:T(8,128)(2,1)S(1)}, u32[]{:S(2)}, u32[]{:S(2)}) collective-permute-start(bf16[256,1024]{1,0:T(8,128)(2,1)S(1)} %get-tuple-element.32), channel_id=1, source_target_pairs={{0,2},{2,0},{4,6},{6,4},{8,10},{10,8},{12,14},{14,12},{1,3},{3,1},... | collective-permute-start | bytes 1572872 | tf_op jit(solution)/shard_map/ppermute | solution.py:28
  134.9 46.2 %copy-start.4 = (f32[256,1024]{1,0:T(8,128)S(1)}, f32[256,1024]{1,0:T(8,128)}, u32[]{:S(2)}) copy-start(f32[256,1024]{1,0:T(8,128)} %get-tuple-element.35) | copy-start | bytes 3145732
  135.0 35.3 %collective-permute-start.11 = (bf16[256,1024]{1,0:T(8,128)(2,1)S(1)}, bf16[256,1024]{1,0:T(8,128)(2,1)S(1)}, u32[]{:S(2)}, u32[]{:S(2)}) collective-permute-start(bf16[256,1024]{1,0:T(8,128)(2,1)S(1)} %add_convert_fusion.3), channel_id=1, source_target_pairs={{0,8},{2,10},{4,12},{6,14},{8,0},{10,2},{12,4},{14,6},{1,9},{3,11}... | collective-permute-start | bytes 1572872 | tf_op jit(solution)/shard_map/ppermute | solution.py:28
  146.3 24.1 %collective-permute-start.13 = (bf16[256,1024]{1,0:T(8,128)(2,1)S(1)}, bf16[256,1024]{1,0:T(8,128)(2,1)S(1)}, u32[]{:S(2)}, u32[]{:S(2)}) collective-permute-start(bf16[256,1024]{1,0:T(8,128)(2,1)S(1)} %add_convert_fusion.2), channel_id=1, source_target_pairs={{0,4},{2,6},{4,8},{6,10},{8,12},{10,14},{12,0},{14,2},{1,5},{3,7},... | collective-permute-start | bytes 1572872 | tf_op jit(solution)/shard_map/ppermute | solution.py:28
  157.3 25.1 %copy-start.1 = (bf16[512,1024]{1,0:T(8,128)(2,1)S(1)}, bf16[512,1024]{1,0:T(8,128)(2,1)}, u32[]{:S(2)}) copy-start(bf16[512,1024]{1,0:T(8,128)(2,1)} %param.10) | copy-start | bytes 3145732
  157.5 23.6 %collective-permute-start.15 = (bf16[256,1024]{1,0:T(8,128)(2,1)S(1)}, bf16[256,1024]{1,0:T(8,128)(2,1)S(1)}, u32[]{:S(2)}, u32[]{:S(2)}) collective-permute-start(bf16[256,1024]{1,0:T(8,128)(2,1)S(1)} %add_convert_fusion.1), channel_id=1, source_target_pairs={{0,12},{2,14},{4,0},{6,2},{8,4},{10,6},{12,8},{14,10},{1,13},{3,15... | collective-permute-start | bytes 1572872 | tf_op jit(solution)/shard_map/ppermute | solution.py:28

commit v13 on v7

--- a/solution.py
+++ b/solution.py
@@ -319,10 +319,6 @@
     tiny = lax.all_to_all(
         jnp.broadcast_to(tiny[None], (owners, *tiny.shape)), "tensor", 0, 0, tiled=True
     )
-    gain_rows = channels // LANES
-    gains = tiny[:, :gain_rows].reshape(owners, channels)
-    inv_rms = lax.rsqrt(jnp.sum(tiny[:, gain_rows:], axis=0).reshape(tokens) / D + EPSILON)
-    inv_rms = jnp.broadcast_to(inv_rms[:, None], (tokens, LANES))
     own_taps = filters.T
     lag_taps = spread(own_taps)
     streams = spread(after(stream.astype(jnp.bfloat16), own_taps))
@@ -344,13 +340,20 @@
     place = place.astype(jnp.bfloat16)
 
     cache = cache_rows.transpose(1, 0, 2)
+    first_terms = history_terms(cache, *lag_taps[0][1:], row_lengths, spot_at(0), steps, None)
     near_taps = filters[:, : 2 * steps].T.astype(jnp.float32)
-    terms = sums = None
+    tiny = after(tiny, (first_terms, place, near_taps))
+    gain_rows = channels // LANES
+    gains = tiny[:, :gain_rows].reshape(owners, channels)
+    inv_rms = lax.rsqrt(jnp.sum(tiny[:, gain_rows:], axis=0).reshape(tokens) / D + EPSILON)
+    inv_rms = jnp.broadcast_to(inv_rms[:, None], (tokens, LANES))
+
+    terms, sums = first_terms, None
     parts = len(streams)
     for index, (back, near, far) in enumerate(lag_taps):
         if index:
             near = after(near, sums)
-        terms = history_terms(cache, near, far, row_lengths, spot_at(-back), steps, terms)
+            terms = history_terms(cache, near, far, row_lengths, spot_at(-back), steps, terms)
         if 2 * index < parts:
             at, *pair = streams[index]
             pair[0] = after(pair[0], terms)
@@ -369,15 +372,17 @@
     order = sorted(range(outer_size), key=lambda ahead: (ahead == 0, -min(ahead, outer_size - ahead)))
     targets = [(owner_at(ahead, 1), jnp.bfloat16) for ahead in order]
     targets += [(owner_at(ahead, 0), jnp.float32) for ahead in order]
-    shares = list(output_shares(targets[:2], gated, w_out, owners))
+    shares = []
+    for start in range(0, outer_size, 2):
+        shares += output_shares(targets[start : start + 2], gated, w_out, owners)
     across = [moved(share, 0, 1) for share in shares]
-    for start in range(2, len(targets), 6):
-        shares += output_shares(targets[start : start + 6], gated, w_out, owners)
-    across += [moved(share, 0, 1) for share in shares[2:outer_size]]
+    shares += output_shares(targets[outer_size:], gated, w_out, owners)
     out = stream
     for ahead, own_share, arrived_share in zip(order, shares[outer_size:], across):
         share = own_share + arrived_share.astype(jnp.float32)
-        out = out + (moved(share.astype(jnp.bfloat16), ahead, 0) if ahead else share)
+        if ahead:
+            share = share.astype(jnp.bfloat16)
+        out = out + (moved(share, ahead, 0) if ahead else share).astype(jnp.float32)
     return out.astype(jnp.bfloat16).reshape(steps, seqs, channels)
 
 

time: 174 us -> 159 us (0.914); the launches traced: 171 us -> 159 us
  waiting for transfers between devices: 60.3 us -> 48.1 us
  starting transfers between devices: 38.9 us -> 36.2 us
    ppermute x21, waiting for transfers between devices: 48.2 us -> 32.5 us  [moved(): return lax.ppermute(array, 'tensor', pairs)]
    all_to_all x1, waiting for transfers between devices: 12.1 us -> 15.6 us  [per_device(): lax.all_to_all(jnp.broadcast_to(tiny[None], (owners, *tiny.shape)), 'tens...]
    ppermute x21, starting transfers between devices: 26.7 us -> 23.4 us  [moved(): return lax.ppermute(array, 'tensor', pairs)]
    pallas_call x10 -> x11, Pallas kernels: 60.8 us -> 62.5 us  [kernel_call(): pl.pallas_call(kernel, in_specs=[IN_SMEM, *specs], out_specs=list(out_spe...]
    unnamed x27 -> x25, local copies, waits for them, and re-layouts: 3.84 us -> 3.58 us
  transfers between devices with their start and end apart: 23 -> 23, of which waited for: 9 -> 9; matrix products, arithmetic and copies ran while one was open for 3% -> 4% of each run, Pallas kernels for 29% -> 32%
where the time goes in v13:
time: 159 us
  Pallas kernels  62.5 us (39%)
  waiting for transfers between devices  48.1 us (30%)
  starting transfers between devices  36.2 us (23%)
  local copies, waits for them, and re-layouts  7.1 us (4%)
  other arithmetic  2.77 us (2%)
  matrix products  1.62 us (1%)
    pallas_call x11, Pallas kernels, kernel_call(): pl.pallas_call(kernel, in_specs=[IN_SMEM, *specs], out_specs=list(out_spe...  62.5 us
    ppermute x21, waiting for transfers between devices, moved(): return lax.ppermute(array, 'tensor', pairs)  32.5 us
    ppermute x21, starting transfers between devices, moved(): return lax.ppermute(array, 'tensor', pairs)  23.4 us
    all_to_all x1, waiting for transfers between devices, per_device(): lax.all_to_all(jnp.broadcast_to(tiny[None], (owners, *tiny.shape)), 'tens...  15.6 us
    all_to_all x1, starting transfers between devices, per_device(): terms = lax.all_to_all(terms, 'tensor', 0, 0, tiled=True)  7.34 us
    all_to_all x1, starting transfers between devices, per_device(): lax.all_to_all(jnp.broadcast_to(tiny[None], (owners, *tiny.shape)), 'tens...  5.41 us
    unnamed x25, local copies, waits for them, and re-layouts  3.58 us
  transfers between devices with their start and end apart: 23, of which 9 were waited for; matrix products, arithmetic and copies ran while one was open for 4% of the time, Pallas kernels for 32%

profile of v13, /device:TPU:18, one launch (start us, length us, event | category | flops | bytes accessed | tf_op | source)
XLA Modules:
  0.0 158.6 jit_solution(5702331831986891528)
XLA Ops:
  0.0 1.2 copy.24
  1.2 1.6 collective-permute-start.3
  2.8 1.6 collective-permute-start.6
  4.4 0.8 eq.92
  5.1 1.6 %multiply_reduce_fusion = (f32[256]{0:T(256)S(1)}, bf16[256,1024]{1,0:T(8,128)(2,1)}, f32[256,1024]{1,0:T(8,128)}) fusion(bf16[512,1024]{1,0:T(8,128)(2,1)S(1)} %copy-done, s32[256]{0:T(256)S(1)} %eq.92), kind=kOutput, calls=%fused_computation.4 | convolution fusion | flops 269352704 | bytes 2623488 | tf_op jit(solution)/shard_map/dot_general | solution.py:316
  6.7 0.5 collective-permute-start.7
  7.3 0.2 collective-permute-start
  7.5 1.8 %collective-permute-start.12 = (bf16[128,1024]{1,0:T(8,128)(2,1)S(1)}, bf16[128,1024]{1,0:T(8,128)(2,1)}, u32[]{:S(2)}, u32[]{:S(2)}) collective-permute-start(bf16[128,1024]{1,0:T(8,128)(2,1)S(1)} %bitcast.40), channel_id=1, source_target_pairs={{0,12},{2,14},{4,0},{6,2},{8,4},{10,6},{12,8},{14,10},{1,13},{3,15... | collective-permute-start | bytes 786440 | tf_op jit(solution)/shard_map/ppermute | solution.py:28
  9.3 0.6 broadcast_in_dim.21
  9.9 5.4 %all-to-all-start = ((f32[8,10,128]{2,1,0:T(8,128)}), f32[8,10,128]{2,1,0:T(8,128)S(1)}, u32[]{:S(2)}, u32[]{:S(2)}) async-start(f32[8,10,128]{2,1,0:T(8,128)} %broadcast_in_dim.21), calls=%async_computation | async-start | bytes 131072 | tf_op jit(solution)/shard_map/all_to_all | solution.py:319
  15.3 0.1 reshape.68
  15.5 0.1 iota_compare_fusion.2
  15.8 0.2 select_reduce_fusion
  16.0 0.2 and_convert_fusion
  16.2 0.1 pad_add_fusion.1.spot
  16.2 0.9 reshape.72
  17.1 0.6 collective-permute-start.4
  17.8 4.9 %history_terms.4.refs_0_ = bf16[8,4,8,1024]{3,2,1,0:T(8,128)(2,1)S(1)} custom-call(s32[2]{0:T(128)S(1)} %pad_add_fusion.2.spot, s32[8,128]{1,0:T(8,128)S(1)} %broadcast_in_dim.24.lengths_ref, bf16[128,1024]{1,0:T(8,128)(2,1)S(1)} %bitcast.41, bf16[128,1024]{1,0:T(8,128)(2,1)S(1)} %collective-permute-done.3.far_ref, bf16[127,8,8192]{2,1,0:T(8,128)(2,1)} %bitcast.43), custom_call_target="tpu_custom_call" | custom-call | flops 4993843200 | bytes 4161536 | tf_op jit(solution)/shard_map/history_terms/pallas_call | solution.py:51
  22.8 0.8 copy-done.2
  23.5 15.6 %all-to-all-done = f32[8,10,128]{2,1,0:T(8,128)S(1)} async-done(((f32[8,10,128]{2,1,0:T(8,128)}), f32[8,10,128]{2,1,0:T(8,128)S(1)}, u32[]{:S(2)}, u32[]{:S(2)}) %all-to-all-start) | async-done | bytes 40992 | tf_op jit(solution)/shard_map/all_to_all | solution.py:319
  39.1 1.0 collective-permute-start.8
  40.1 2.2 %collective-permute-start.10 = (bf16[128,1024]{1,0:T(8,128)(2,1)}, bf16[128,1024]{1,0:T(8,128)(2,1)S(1)}, u32[]{:S(2)}, u32[]{:S(2)}) collective-permute-start(bf16[128,1024]{1,0:T(8,128)(2,1)} %collective-permute-done.6.near_ref), channel_id=1, source_target_pairs={{0,4},{2,6},{4,8},{6,10},{8,12},{10,14},{12,0},{14,2},{1,5},{3,7},... | collective-permute-start | bytes 786440 | tf_op jit(solution)/shard_map/ppermute | solution.py:28
  42.3 0.9 collective-permute-start.13
  43.2 1.1 collective-permute-start.9
  44.3 0.1 broadcast_in_dim.25.inv_ref
  44.4 6.9 %projected_part.3.refs_0_ = f32[256,3072]{1,0:T(8,128)S(1)} custom-call(s32[2]{0:T(128)S(1)} %pad_add_fusion.2.spot, bf16[256,1024]{1,0:T(8,128)(2,1)} %get-tuple-element.23.near, bf16[256,1024]{1,0:T(8,128)(2,1)} %copy-done.6, f32[8,1024]{1,0:T(8,128)S(1)} %bitcast.34, f32[256,128]{1,0:T(8,128)S(1)} %broadcast_in_dim.25.inv_ref, bf16[8192,3072]{1,0:T(8,128)(2,1)} %w_hbm.10), custom_call_target="tpu_custom_call" | custom-call | flops 6442450944 | bytes 25165824 | tf_op jit(solution)/shard_map/projected_part/pallas_call | solution.py:51
  51.4 5.4 %history_terms.5.refs_0_ = bf16[8,4,8,1024]{3,2,1,0:T(8,128)(2,1)S(1)} custom-call(s32[2]{0:T(128)S(1)} %pad_add_fusion.4.spot, s32[8,128]{1,0:T(8,128)S(1)} %broadcast_in_dim.24.lengths_ref, bf16[128,1024]{1,0:T(8,128)(2,1)} %collective-permute-done.6.near_ref, ...), custom_call_target="tpu_custom_call", output_to_operand_aliasing={{}: (5, {})} | custom-call | flops 4993843200 | bytes 4161536 | tf_op jit(solution)/shard_map/history_terms/pallas_call | solution.py:51
  56.8 0.1 collective-permute-start.1
  56.9 0.9 collective-permute-start.11
  57.8 1.1 collective-permute-start.5
  58.9 1.0 collective-permute-done.9.far
  60.0 0.8 copy-done.7
  60.7 6.9 %projected_part.4.refs_0_ = f32[256,3072]{1,0:T(8,128)S(1)} custom-call(s32[2]{0:T(128)S(1)} %pad_add_fusion.4.spot, bf16[256,1024]{1,0:T(8,128)(2,1)} %collective-permute-done.near, bf16[256,1024]{1,0:T(8,128)(2,1)} %copy-done.7, f32[8,1024]{1,0:T(8,128)S(1)} %bitcast.35, f32[256,128]{1,0:T(8,128)S(1)} %broadcast_in_dim.25.inv_ref, ...), custom_call_target="tpu_custom_call", output_to_operand_aliasing={{}: (6, {})} | custom-call | flops 6442450944 | bytes 25165824 | tf_op jit(solution)/shard_map/projected_part/pallas_call | solution.py:51
  67.7 5.4 %history_terms.6.refs_0_ = bf16[8,4,8,1024]{3,2,1,0:T(8,128)(2,1)S(1)} custom-call(s32[2]{0:T(128)S(1)} %pad_add_fusion.3.spot, s32[8,128]{1,0:T(8,128)S(1)} %broadcast_in_dim.24.lengths_ref, bf16[128,1024]{1,0:T(8,128)(2,1)} %collective-permute-done.12.near_ref, ...), custom_call_target="tpu_custom_call", output_to_operand_aliasing={{}: (5, {})} | custom-call | flops 4993843200 | bytes 4161536 | tf_op jit(solution)/shard_map/history_terms/pallas_call | solution.py:51
  73.1 5.0 %history_terms.7 = bf16[8,4,8,1024]{3,2,1,0:T(8,128)(2,1)S(1)} custom-call(s32[2]{0:T(128)S(1)} %pad_add_fusion.1.spot, s32[8,128]{1,0:T(8,128)S(1)} %broadcast_in_dim.24.lengths_ref, bf16[128,1024]{1,0:T(8,128)(2,1)S(1)} %collective-permute-done.10.near_ref, bf16[128,1024]{1,0:T(8,128)(2,1)S(1)} %collective-permute-done.11.far_ref, ...), custom_call_target="tpu_custom_call", output_to_operand_aliasing={{}: (5, {})} | custom-call | flops 4993843200 | bytes 4161536 | tf_op jit(solution)/shard_map/history_terms/pallas_call | solution.py:51
  78.1 0.8 copy-done.4
  78.8 7.3 %all-to-all-start.1 = ((bf16[8,4,8,1024]{3,2,1,0:T(8,128)(2,1)}), bf16[8,4,8,1024]{3,2,1,0:T(8,128)(2,1)}, u32[]{:S(2)}, u32[]{:S(2)}) async-start(bf16[8,4,8,1024]{3,2,1,0:T(8,128)(2,1)} %copy-done.4), calls=%async_computation.1 | async-start | bytes 1048576 | tf_op jit(solution)/shard_map/all_to_all | solution.py:361
  86.2 1.0 copy.26.refs_2_
  87.3 0.1 pad_add_fusion.5.spot
  87.3 1.5 collective-permute-start.2
  88.8 6.9 %projected_part.5.refs_0_ = f32[256,3072]{1,0:T(8,128)S(1)} custom-call(s32[2]{0:T(128)S(1)} %pad_add_fusion.3.spot, bf16[256,1024]{1,0:T(8,128)(2,1)} %collective-permute-done.4.near, bf16[256,1024]{1,0:T(8,128)(2,1)} %collective-permute-done.5.far, f32[8,1024]{1,0:T(8,128)S(1)} %bitcast.36, ...), custom_call_target="tpu_custom_call", output_to_operand_aliasing={{}: (6, {})} | custom-call | flops 6442450944 | bytes 25165824 | tf_op jit(solution)/shard_map/projected_part/pallas_call | solution.py:51
  95.8 2.5 %collective-permute-done.2.far = bf16[256,1024]{1,0:T(8,128)(2,1)} collective-permute-done((bf16[256,1024]{1,0:T(8,128)(2,1)}, bf16[256,1024]{1,0:T(8,128)(2,1)}, u32[]{:S(2)}, u32[]{:S(2)}) %collective-permute-start.2) | collective-permute-done | bytes 524320 | tf_op jit(solution)/shard_map/ppermute | solution.py:28
  98.3 7.8 %gated_rows.1 = (f32[256,3072]{1,0:T(8,128)S(1)}, bf16[256,1024]{1,0:T(8,128)(2,1)S(1)}) custom-call(s32[2]{0:T(128)S(1)} %pad_add_fusion.1.spot, bf16[256,1024]{1,0:T(8,128)(2,1)} %collective-permute-done.1.near, bf16[256,1024]{1,0:T(8,128)(2,1)} %collective-permute-done.2.far, f32[8,1024]{1,0:T(8,128)S(1)} %bitcast.37, ...), custom_call_target="tpu_custom_call", output_to_operand_aliasing={{0}: (6, {})} | custom-call | flops 6442450944 | bytes 25165824 | tf_op jit(solution)/shard_map/gated_rows/pallas_call | solution.py:51
  106.0 3.8 %output_shares.4 = (bf16[256,1024]{1,0:T(8,128)(2,1)S(1)}, bf16[256,1024]{1,0:T(8,128)(2,1)S(1)}) custom-call(s32[2]{0:T(128)S(1)} %pad_add_fusion.5.spot, bf16[256,1024]{1,0:T(8,128)(2,1)S(1)} %get-tuple-element.28.x_ref, bf16[1024,8192]{1,0:T(8,128)(2,1)} %w_hbm.13), custom_call_target="tpu_custom_call" | custom-call | flops 1073741824 | bytes 4194304 | tf_op jit(solution)/shard_map/output_shares/pallas_call | solution.py:51
  109.8 0.5 collective-permute-start.14
  110.4 0.1 pad_add_fusion.spot
  110.5 1.6 collective-permute-start.16
  112.1 3.8 %output_shares.5 = (bf16[256,1024]{1,0:T(8,128)(2,1)S(1)}, bf16[256,1024]{1,0:T(8,128)(2,1)S(1)}) custom-call(s32[2]{0:T(128)S(1)} %pad_add_fusion.6.spot, bf16[256,1024]{1,0:T(8,128)(2,1)S(1)} %get-tuple-element.28.x_ref, bf16[1024,8192]{1,0:T(8,128)(2,1)} %w_hbm.13), custom_call_target="tpu_custom_call" | custom-call | flops 1073741824 | bytes 4194304 | tf_op jit(solution)/shard_map/output_shares/pallas_call | solution.py:51
  115.8 0.5 collective-permute-start.18
  116.4 1.6 collective-permute-start.20
  117.9 5.8 %output_shares.3 = (f32[256,1024]{1,0:T(8,128)S(1)}, f32[256,1024]{1,0:T(8,128)S(1)}, f32[256,1024]{1,0:T(8,128)S(1)}, f32[256,1024]{1,0:T(8,128)S(1)}) custom-call(s32[4]{0:T(128)S(1)} %pad_add_fusion.spot, bf16[256,1024]{1,0:T(8,128)(2,1)S(1)} %get-tuple-element.28.x_ref, bf16[1024,8192]{1,0:T(8,128)(2,1)} %w_hbm.13), custom_call_target="tpu_custom_call" | custom-call | flops 2147483648 | bytes 8388608 | tf_op jit(solution)/shard_map/output_shares/pallas_call | solution.py:51
  123.7 1.0 collective-permute-done.14
  124.7 0.1 add_convert_fusion.3
  124.9 0.8 collective-permute-start.15
  125.7 6.5 %collective-permute-done.16 = bf16[256,1024]{1,0:T(8,128)(2,1)S(1)} collective-permute-done((bf16[256,1024]{1,0:T(8,128)(2,1)S(1)}, bf16[256,1024]{1,0:T(8,128)(2,1)S(1)}, u32[]{:S(2)}, u32[]{:S(2)}) %collective-permute-start.16) | collective-permute-done | bytes 524320 | tf_op jit(solution)/shard_map/ppermute | solution.py:28
  132.2 0.1 add_convert_fusion.2
  132.3 2.1 %collective-permute-start.17 = (bf16[256,1024]{1,0:T(8,128)(2,1)S(1)}, bf16[256,1024]{1,0:T(8,128)(2,1)S(1)}, u32[]{:S(2)}, u32[]{:S(2)}) collective-permute-start(bf16[256,1024]{1,0:T(8,128)(2,1)S(1)} %add_convert_fusion.2), channel_id=1, source_target_pairs={{0,4},{2,6},{4,8},{6,10},{8,12},{10,14},{12,0},{14,2},{1,5},{3,7},... | collective-permute-start | bytes 1572872 | tf_op jit(solution)/shard_map/ppermute | solution.py:28
  134.4 3.4 %collective-permute-done.18 = bf16[256,1024]{1,0:T(8,128)(2,1)S(1)} collective-permute-done((bf16[256,1024]{1,0:T(8,128)(2,1)S(1)}, bf16[256,1024]{1,0:T(8,128)(2,1)S(1)}, u32[]{:S(2)}, u32[]{:S(2)}) %collective-permute-start.18) | collective-permute-done | bytes 524320 | tf_op jit(solution)/shard_map/ppermute | solution.py:28
  137.8 0.1 add_convert_fusion.1
  138.0 1.3 collective-permute-start.19
  139.3 4.2 %collective-permute-done.20 = bf16[256,1024]{1,0:T(8,128)(2,1)S(1)} collective-permute-done((bf16[256,1024]{1,0:T(8,128)(2,1)S(1)}, bf16[256,1024]{1,0:T(8,128)(2,1)S(1)}, u32[]{:S(2)}, u32[]{:S(2)}) %collective-permute-start.20) | collective-permute-done | bytes 524320 | tf_op jit(solution)/shard_map/ppermute | solution.py:28
  143.4 5.9 %collective-permute-done.15 = bf16[256,1024]{1,0:T(8,128)(2,1)S(1)} collective-permute-done((bf16[256,1024]{1,0:T(8,128)(2,1)S(1)}, bf16[256,1024]{1,0:T(8,128)(2,1)S(1)}, u32[]{:S(2)}, u32[]{:S(2)}) %collective-permute-start.15) | collective-permute-done | bytes 524320 | tf_op jit(solution)/shard_map/ppermute | solution.py:28
  149.3 8.0 %collective-permute-done.17 = bf16[256,1024]{1,0:T(8,128)(2,1)S(1)} collective-permute-done((bf16[256,1024]{1,0:T(8,128)(2,1)S(1)}, bf16[256,1024]{1,0:T(8,128)(2,1)S(1)}, u32[]{:S(2)}, u32[]{:S(2)}) %collective-permute-start.17) | collective-permute-done | bytes 524320 | tf_op jit(solution)/shard_map/ppermute | solution.py:28
  157.3 1.3 add_convert_fusion
  (48 shorter events, 0.5 us)
Async XLA Ops:
  0.0 5.1 %copy-start = (bf16[512,1024]{1,0:T(8,128)(2,1)S(1)}, bf16[512,1024]{1,0:T(8,128)(2,1)}, u32[]{:S(2)}) copy-start(bf16[512,1024]{1,0:T(8,128)(2,1)} %param.10) | copy-start | bytes 3145732
  0.0 9.3 %copy-start.8 = (bf16[1024]{0:T(1024)(128)(2,1)S(1)}, bf16[1024]{0:T(1024)(128)(2,1)}, u32[]{:S(2)}) copy-start(bf16[1024]{0:T(1024)(128)(2,1)} %param.11) | copy-start | bytes 6148
  0.0 15.3 %copy-start.9 = (s32[128]{0:T(128)S(1)}, s32[128]{0:T(128)}, u32[]{:S(2)}) copy-start(s32[128]{0:T(128)} %param.16) | copy-start | bytes 1540
  0.0 15.8 %copy-start.10 = (s32[64]{0:T(128)S(1)}, s32[64]{0:T(128)}, u32[]{:S(2)}) copy-start(s32[64]{0:T(128)} %param.17) | copy-start | bytes 772
  1.2 15.9 %collective-permute-start.3 = (bf16[128,1024]{1,0:T(8,128)(2,1)S(1)}, bf16[128,1024]{1,0:T(8,128)(2,1)S(1)}, u32[]{:S(2)}, u32[]{:S(2)}) collective-permute-start(bf16[128,1024]{1,0:T(8,128)(2,1)S(1)} %bitcast.38), channel_id=1, source_target_pairs={{0,2},{2,0},{4,6},{6,4},{8,10},{10,8},{12,14},{14,12},{1,3},{3,1},... | collective-permute-start | bytes 786440 | tf_op jit(solution)/shard_map/ppermute | solution.py:28
  2.8 36.3 %collective-permute-start.6 = (bf16[128,1024]{1,0:T(8,128)(2,1)S(1)}, bf16[128,1024]{1,0:T(8,128)(2,1)}, u32[]{:S(2)}, u32[]{:S(2)}) collective-permute-start(bf16[128,1024]{1,0:T(8,128)(2,1)S(1)} %bitcast.39), channel_id=1, source_target_pairs={{0,4},{2,6},{4,8},{6,10},{8,12},{10,14},{12,0},{14,2},{1,5},{3,7},... | collective-permute-start | bytes 786440 | tf_op jit(solution)/shard_map/ppermute | solution.py:28
  6.7 35.5 %collective-permute-start.7 = (bf16[256,1024]{1,0:T(8,128)(2,1)}, bf16[256,1024]{1,0:T(8,128)(2,1)S(1)}, u32[]{:S(2)}, u32[]{:S(2)}) collective-permute-start(bf16[256,1024]{1,0:T(8,128)(2,1)} %get-tuple-element.23.near), channel_id=1, source_target_pairs={{0,2},{2,0},{4,6},{6,4},{8,10},{10,8},{12,14},{14,12},{1,3},{3,1},... | collective-permute-start | bytes 1572872 | tf_op jit(solution)/shard_map/ppermute | solution.py:28
  7.3 36.0 %collective-permute-start = (bf16[256,1024]{1,0:T(8,128)(2,1)}, bf16[256,1024]{1,0:T(8,128)(2,1)}, u32[]{:S(2)}, u32[]{:S(2)}) collective-permute-start(bf16[256,1024]{1,0:T(8,128)(2,1)} %get-tuple-element.23.near), channel_id=1, source_target_pairs={{0,4},{2,6},{4,8},{6,10},{8,12},{10,14},{12,0},{14,2},{1,5},{3,7},... | collective-permute-start | bytes 1572872 | tf_op jit(solution)/shard_map/ppermute | solution.py:28
  7.5 32.6 %collective-permute-start.12 = (bf16[128,1024]{1,0:T(8,128)(2,1)S(1)}, bf16[128,1024]{1,0:T(8,128)(2,1)}, u32[]{:S(2)}, u32[]{:S(2)}) collective-permute-start(bf16[128,1024]{1,0:T(8,128)(2,1)S(1)} %bitcast.40), channel_id=1, source_target_pairs={{0,12},{2,14},{4,0},{6,2},{8,4},{10,6},{12,8},{14,10},{1,13},{3,15... | collective-permute-start | bytes 786440 | tf_op jit(solution)/shard_map/ppermute | solution.py:28
  9.9 29.2 %all-to-all-start = ((f32[8,10,128]{2,1,0:T(8,128)}), f32[8,10,128]{2,1,0:T(8,128)S(1)}, u32[]{:S(2)}, u32[]{:S(2)}) async-start(f32[8,10,128]{2,1,0:T(8,128)} %broadcast_in_dim.21), calls=%async_computation | async-start | bytes 131072 | tf_op jit(solution)/shard_map/all_to_all | solution.py:319
  17.1 40.7 %collective-permute-start.4 = (bf16[256,1024]{1,0:T(8,128)(2,1)}, bf16[256,1024]{1,0:T(8,128)(2,1)}, u32[]{:S(2)}, u32[]{:S(2)}) collective-permute-start(bf16[256,1024]{1,0:T(8,128)(2,1)} %get-tuple-element.23.near), channel_id=1, source_target_pairs={{0,12},{2,14},{4,0},{6,2},{8,4},{10,6},{12,8},{14,10},{1,13},{3,15... | collective-permute-start | bytes 1572872 | tf_op jit(solution)/shard_map/ppermute | solution.py:28
  22.7 0.8 copy-start.2
  39.1 12.2 %collective-permute-start.8 = (bf16[128,1024]{1,0:T(8,128)(2,1)}, bf16[128,1024]{1,0:T(8,128)(2,1)S(1)}, u32[]{:S(2)}, u32[]{:S(2)}) collective-permute-start(bf16[128,1024]{1,0:T(8,128)(2,1)} %collective-permute-done.6.near_ref), channel_id=1, source_target_pairs={{0,2},{2,0},{4,6},{6,4},{8,10},{10,8},{12,14},{14,12},{1,3},{3,1},... | collective-permute-start | bytes 786440 | tf_op jit(solution)/shard_map/ppermute | solution.py:28
  40.1 16.8 %collective-permute-start.10 = (bf16[128,1024]{1,0:T(8,128)(2,1)}, bf16[128,1024]{1,0:T(8,128)(2,1)S(1)}, u32[]{:S(2)}, u32[]{:S(2)}) collective-permute-start(bf16[128,1024]{1,0:T(8,128)(2,1)} %collective-permute-done.6.near_ref), channel_id=1, source_target_pairs={{0,4},{2,6},{4,8},{6,10},{8,12},{10,14},{12,0},{14,2},{1,5},{3,7},... | collective-permute-start | bytes 786440 | tf_op jit(solution)/shard_map/ppermute | solution.py:28
  42.3 2.1 %copy-start.6 = (bf16[256,1024]{1,0:T(8,128)(2,1)}, bf16[256,1024]{1,0:T(8,128)(2,1)S(1)}, u32[]{:S(2)}) copy-start(bf16[256,1024]{1,0:T(8,128)(2,1)S(1)} %collective-permute-done.7.far) | copy-start | bytes 1572868
  42.3 25.4 %collective-permute-start.13 = (bf16[128,1024]{1,0:T(8,128)(2,1)}, bf16[128,1024]{1,0:T(8,128)(2,1)S(1)}, u32[]{:S(2)}, u32[]{:S(2)}) collective-permute-start(bf16[128,1024]{1,0:T(8,128)(2,1)} %collective-permute-done.12.near_ref), channel_id=1, source_target_pairs={{0,2},{2,0},{4,6},{6,4},{8,10},{10,8},{12,14},{14,12},{1,3},{3,1},... | collective-permute-start | bytes 786440 | tf_op jit(solution)/shard_map/ppermute | solution.py:28
  43.2 16.7 %collective-permute-start.9 = (bf16[256,1024]{1,0:T(8,128)(2,1)}, bf16[256,1024]{1,0:T(8,128)(2,1)S(1)}, u32[]{:S(2)}, u32[]{:S(2)}) collective-permute-start(bf16[256,1024]{1,0:T(8,128)(2,1)} %collective-permute-done.near), channel_id=1, source_target_pairs={{0,2},{2,0},{4,6},{6,4},{8,10},{10,8},{12,14},{14,12},{1,3},{3,1},... | collective-permute-start | bytes 1572872 | tf_op jit(solution)/shard_map/ppermute | solution.py:28
  44.4 7.0 %copy-start.3 = (bf16[8,4,8,1024]{3,2,1,0:T(8,128)(2,1)S(1)}, bf16[8,4,8,1024]{3,2,1,0:T(8,128)(2,1)}, u32[]{:S(2)}) copy-start(bf16[8,4,8,1024]{3,2,1,0:T(8,128)(2,1)} %copy-done.2) | copy-start | bytes 1572868
  56.8 30.6 %collective-permute-start.1 = (bf16[256,1024]{1,0:T(8,128)(2,1)}, bf16[256,1024]{1,0:T(8,128)(2,1)}, u32[]{:S(2)}, u32[]{:S(2)}) collective-permute-start(bf16[256,1024]{1,0:T(8,128)(2,1)} %collective-permute-done.near), channel_id=1, source_target_pairs={{0,4},{2,6},{4,8},{6,10},{8,12},{10,14},{12,0},{14,2},{1,5},{3,7},... | collective-permute-start | bytes 1572872 | tf_op jit(solution)/shard_map/ppermute | solution.py:28
  56.9 16.2 %collective-permute-start.11 = (bf16[128,1024]{1,0:T(8,128)(2,1)S(1)}, bf16[128,1024]{1,0:T(8,128)(2,1)S(1)}, u32[]{:S(2)}, u32[]{:S(2)}) collective-permute-start(bf16[128,1024]{1,0:T(8,128)(2,1)S(1)} %collective-permute-done.10.near_ref), channel_id=1, source_target_pairs={{0,2},{2,0},{4,6},{6,4},{8,10},{10,8},{12,14},{14,12},{1,3},{3,1},... | collective-permute-start | bytes 786440 | tf_op jit(solution)/shard_map/ppermute | solution.py:28
  57.8 31.0 %collective-permute-start.5 = (bf16[256,1024]{1,0:T(8,128)(2,1)}, bf16[256,1024]{1,0:T(8,128)(2,1)}, u32[]{:S(2)}, u32[]{:S(2)}) collective-permute-start(bf16[256,1024]{1,0:T(8,128)(2,1)} %collective-permute-done.4.near), channel_id=1, source_target_pairs={{0,2},{2,0},{4,6},{6,4},{8,10},{10,8},{12,14},{14,12},{1,3},{3,1},... | collective-permute-start | bytes 1572872 | tf_op jit(solution)/shard_map/ppermute | solution.py:28
  60.0 0.8 copy-start.7
  78.0 0.8 copy-start.4
  78.8 19.4 %all-to-all-start.1 = ((bf16[8,4,8,1024]{3,2,1,0:T(8,128)(2,1)}), bf16[8,4,8,1024]{3,2,1,0:T(8,128)(2,1)}, u32[]{:S(2)}, u32[]{:S(2)}) async-start(bf16[8,4,8,1024]{3,2,1,0:T(8,128)(2,1)} %copy-done.4), calls=%async_computation.1 | async-start | bytes 1048576 | tf_op jit(solution)/shard_map/all_to_all | solution.py:361
  87.3 10.9 %collective-permute-start.2 = (bf16[256,1024]{1,0:T(8,128)(2,1)}, bf16[256,1024]{1,0:T(8,128)(2,1)}, u32[]{:S(2)}, u32[]{:S(2)}) collective-permute-start(bf16[256,1024]{1,0:T(8,128)(2,1)} %collective-permute-done.1.near), channel_id=1, source_target_pairs={{0,2},{2,0},{4,6},{6,4},{8,10},{10,8},{12,14},{14,12},{1,3},{3,1},... | collective-permute-start | bytes 1572872 | tf_op jit(solution)/shard_map/ppermute | solution.py:28
  109.8 14.9 %collective-permute-start.14 = (bf16[256,1024]{1,0:T(8,128)(2,1)S(1)}, bf16[256,1024]{1,0:T(8,128)(2,1)S(1)}, u32[]{:S(2)}, u32[]{:S(2)}) collective-permute-start(bf16[256,1024]{1,0:T(8,128)(2,1)S(1)} %get-tuple-element.30), channel_id=1, source_target_pairs={{0,2},{2,0},{4,6},{6,4},{8,10},{10,8},{12,14},{14,12},{1,3},{3,1},... | collective-permute-start | bytes 1572872 | tf_op jit(solution)/shard_map/ppermute | solution.py:28
  110.5 21.7 %collective-permute-start.16 = (bf16[256,1024]{1,0:T(8,128)(2,1)S(1)}, bf16[256,1024]{1,0:T(8,128)(2,1)S(1)}, u32[]{:S(2)}, u32[]{:S(2)}) collective-permute-start(bf16[256,1024]{1,0:T(8,128)(2,1)S(1)} %get-tuple-element.32), channel_id=1, source_target_pairs={{0,2},{2,0},{4,6},{6,4},{8,10},{10,8},{12,14},{14,12},{1,3},{3,1},... | collective-permute-start | bytes 1572872 | tf_op jit(solution)/shard_map/ppermute | solution.py:28
  115.8 22.0 %collective-permute-start.18 = (bf16[256,1024]{1,0:T(8,128)(2,1)S(1)}, bf16[256,1024]{1,0:T(8,128)(2,1)S(1)}, u32[]{:S(2)}, u32[]{:S(2)}) collective-permute-start(bf16[256,1024]{1,0:T(8,128)(2,1)S(1)} %get-tuple-element.34), channel_id=1, source_target_pairs={{0,2},{2,0},{4,6},{6,4},{8,10},{10,8},{12,14},{14,12},{1,3},{3,1},... | collective-permute-start | bytes 1572872 | tf_op jit(solution)/shard_map/ppermute | solution.py:28
  116.4 27.0 %collective-permute-start.20 = (bf16[256,1024]{1,0:T(8,128)(2,1)S(1)}, bf16[256,1024]{1,0:T(8,128)(2,1)S(1)}, u32[]{:S(2)}, u32[]{:S(2)}) collective-permute-start(bf16[256,1024]{1,0:T(8,128)(2,1)S(1)} %get-tuple-element.36), channel_id=1, source_target_pairs={{0,2},{2,0},{4,6},{6,4},{8,10},{10,8},{12,14},{14,12},{1,3},{3,1},... | collective-permute-start | bytes 1572872 | tf_op jit(solution)/shard_map/ppermute | solution.py:28
  124.7 32.6 %copy-start.5 = (f32[256,1024]{1,0:T(8,128)S(1)}, f32[256,1024]{1,0:T(8,128)}, u32[]{:S(2)}) copy-start(f32[256,1024]{1,0:T(8,128)} %get-tuple-element.39) | copy-start | bytes 3145732
  124.9 24.4 %collective-permute-start.15 = (bf16[256,1024]{1,0:T(8,128)(2,1)S(1)}, bf16[256,1024]{1,0:T(8,128)(2,1)S(1)}, u32[]{:S(2)}, u32[]{:S(2)}) collective-permute-start(bf16[256,1024]{1,0:T(8,128)(2,1)S(1)} %add_convert_fusion.3), channel_id=1, source_target_pairs={{0,8},{2,10},{4,12},{6,14},{8,0},{10,2},{12,4},{14,6},{1,9},{3,11}... | collective-permute-start | bytes 1572872 | tf_op jit(solution)/shard_map/ppermute | solution.py:28
  132.3 25.0 %collective-permute-start.17 = (bf16[256,1024]{1,0:T(8,128)(2,1)S(1)}, bf16[256,1024]{1,0:T(8,128)(2,1)S(1)}, u32[]{:S(2)}, u32[]{:S(2)}) collective-permute-start(bf16[256,1024]{1,0:T(8,128)(2,1)S(1)} %add_convert_fusion.2), channel_id=1, source_target_pairs={{0,4},{2,6},{4,8},{6,10},{8,12},{10,14},{12,0},{14,2},{1,5},{3,7},... | collective-permute-start | bytes 1572872 | tf_op jit(solution)/shard_map/ppermute | solution.py:28
  137.8 20.8 %copy-start.1 = (bf16[512,1024]{1,0:T(8,128)(2,1)S(1)}, bf16[512,1024]{1,0:T(8,128)(2,1)}, u32[]{:S(2)}) copy-start(bf16[512,1024]{1,0:T(8,128)(2,1)} %param.10) | copy-start | bytes 3145732
  138.0 19.4 %collective-permute-start.19 = (bf16[256,1024]{1,0:T(8,128)(2,1)S(1)}, bf16[256,1024]{1,0:T(8,128)(2,1)S(1)}, u32[]{:S(2)}, u32[]{:S(2)}) collective-permute-start(bf16[256,1024]{1,0:T(8,128)(2,1)S(1)} %add_convert_fusion.1), channel_id=1, source_target_pairs={{0,12},{2,14},{4,0},{6,2},{8,4},{10,6},{12,8},{14,10},{1,13},{3,15... | collective-permute-start | bytes 1572872 | tf_op jit(solution)/shard_map/ppermute | solution.py:28

commit v14 on v8

--- a/solution.py
+++ b/solution.py
@@ -13,7 +13,6 @@
 INNER = 2
 DEPTH = 3
 VMEM_LIMIT = 16 * 1024 * 1024
-LARGE_LIMIT = 30 * 1024 * 1024
 IN_SMEM = pl.BlockSpec(memory_space=pltpu.SMEM)
 IN_VMEM = pl.BlockSpec(memory_space=pltpu.VMEM)
 IN_HBM = pl.BlockSpec(memory_space=pltpu.HBM)
@@ -42,7 +41,7 @@
     return blocks
 
 
-def kernel_call(kernel, name, spot, operands, outputs, aliases, scratch, flops, moved_bytes, limit=VMEM_LIMIT):
+def kernel_call(kernel, name, spot, operands, outputs, aliases, scratch, flops, moved_bytes):
     specs, args = zip(*operands)
     args = [
         pltpu.with_memory_space_constraint(arg, pltpu.HBM) if spec is IN_HBM else arg
@@ -56,7 +55,7 @@
         out_shape=list(out_shape),
         input_output_aliases=aliases,
         scratch_shapes=scratch,
-        compiler_params=pltpu.CompilerParams(vmem_limit_bytes=limit),
+        compiler_params=pltpu.CompilerParams(vmem_limit_bytes=VMEM_LIMIT),
         cost_estimate=pl.CostEstimate(flops=flops, bytes_accessed=moved_bytes, transcendentals=0),
         name=name,
     )(spot, *args)
@@ -288,7 +287,6 @@
         scratch,
         4 * rows * INNER * channels * 3 * channels,
         4 * INNER * channels * 3 * channels,
-        LARGE_LIMIT if last else VMEM_LIMIT,
     )
     return out[1:] if last else out[0]
 
@@ -323,9 +321,9 @@
     return kernel_call(
         share_kernel,
         "output_shares",
-        jnp.stack(targets).astype(jnp.int32),
+        jnp.stack([which for which, _ in targets]).astype(jnp.int32),
         [(IN_VMEM, gated), (IN_HBM, w_out)],
-        [(IN_VMEM, jax.ShapeDtypeStruct((rows, wide), jnp.float32)) for _ in targets],
+        [(IN_VMEM, jax.ShapeDtypeStruct((rows, wide), kind)) for _, kind in targets],
         {},
         [pltpu.VMEM((DEPTH, channels, block), jnp.bfloat16), pltpu.SemaphoreType.DMA((DEPTH,))],
         2 * rows * channels * wide * len(targets),
@@ -376,18 +374,20 @@
     place = place.astype(jnp.bfloat16)
 
     cache = cache_rows.transpose(1, 0, 2)
+    first_terms = history_terms(cache, *lag_taps[0][1:], row_lengths, spot_at(0), steps, None)
     near_taps = filters[:, : 2 * steps].T.astype(jnp.float32)
-    def owner_at(ahead, flip):
-        return (outer + ahead) % outer_size * INNER + (inner + flip) % INNER
-
-    order = sorted(range(outer_size), key=lambda ahead: (ahead == 0, -min(ahead, outer_size - ahead)))
-    first_terms = history_terms(cache, *lag_taps[0][1:], row_lengths, spot_at(0), steps, None)
-    tiny = after(tiny, first_terms)
+    tiny = after(tiny, (first_terms, place, near_taps))
     gain_rows = channels // LANES
     gains = tiny[:, :gain_rows].reshape(owners, channels)
     inv_rms = lax.rsqrt(jnp.sum(tiny[:, gain_rows:], axis=0).reshape(tokens) / D + EPSILON)
     inv_rms = jnp.broadcast_to(inv_rms[:, None], (tokens, LANES))
 
+    def owner_at(ahead, flip):
+        return (outer + ahead) % outer_size * INNER + (inner + flip) % INNER
+
+    order = sorted(range(outer_size), key=lambda ahead: (ahead == 0, -min(ahead, outer_size - ahead)))
+    targets = [(owner_at(ahead, 1), jnp.bfloat16) for ahead in order]
+    targets += [(owner_at(ahead, 0), jnp.float32) for ahead in order]
     terms, sums = first_terms, None
     parts = len(streams)
     for index, (back, near, far) in enumerate(lag_taps):
@@ -404,17 +404,20 @@
         at, *pair = streams[index]
         ends = None
         if index == parts - 1:
-            targets = [owner_at(ahead, 1) for ahead in order]
-            ends = (steps, near_taps, place, terms, w_out, targets)
+            ends = (steps, near_taps, place, terms, w_out, [which for which, _ in targets[:2]])
         sums = projected(spot_at(-at), pair, gains, inv_rms, w_in, sums, ends)
-    gated, *across = sums
-
-    across = [moved(share, 0, 1) for share in across]
-    own_shares = output_shares([owner_at(ahead, 0) for ahead in order], gated, w_out, owners)
+    gated, *shares = sums
+
+    for start in range(2, outer_size, 2):
+        shares += output_shares(targets[start : start + 2], gated, w_out, owners)
+    across = [moved(share, 0, 1) for share in shares]
+    shares += output_shares(targets[outer_size:], gated, w_out, owners)
     out = stream
-    for ahead, own_share, arrived_share in zip(order, own_shares, across):
+    for ahead, own_share, arrived_share in zip(order, shares[outer_size:], across):
         share = own_share + arrived_share.astype(jnp.float32)
-        out = out + (moved(share.astype(jnp.bfloat16), ahead, 0) if ahead else share)
+        if ahead:
+            share = share.astype(jnp.bfloat16)
+        out = out + (moved(share, ahead, 0) if ahead else share).astype(jnp.float32)
     return out.astype(jnp.bfloat16).reshape(steps, seqs, channels)
 
 

time: 189 us -> 158 us (0.84)
  the two profiles are of different devices: /device:TPU:0 before, /device:TPU:18 now
where the time goes in v14:
time: 158 us; the launch traced here: 157 us
  Pallas kernels  61.2 us (39%)
  waiting for transfers between devices  48.9 us (31%)
  starting transfers between devices  35.4 us (22%)
  local copies, waits for them, and re-layouts  7.08 us (4%)
  other arithmetic  2.8 us (2%)
  matrix products  1.62 us (1%)
    pallas_call x10, Pallas kernels, kernel_call(): pl.pallas_call(kernel, in_specs=[IN_SMEM, *specs], out_specs=list(out_spe...  61.2 us
    ppermute x21, waiting for transfers between devices, moved(): return lax.ppermute(array, 'tensor', pairs)  33.3 us
    ppermute x21, starting transfers between devices, moved(): return lax.ppermute(array, 'tensor', pairs)  22.7 us
    all_to_all x1, waiting for transfers between devices, per_device(): lax.all_to_all(jnp.broadcast_to(tiny[None], (owners, *tiny.shape)), 'tens...  15.6 us
    all_to_all x1, starting transfers between devices, per_device(): terms = lax.all_to_all(terms, 'tensor', 0, 0, tiled=True)  7.34 us
    all_to_all x1, starting transfers between devices, per_device(): lax.all_to_all(jnp.broadcast_to(tiny[None], (owners, *tiny.shape)), 'tens...  5.41 us
    unnamed x25, local copies, waits for them, and re-layouts  3.58 us
  transfers between devices with their start and end apart: 23, of which 9 were waited for; matrix products, arithmetic and copies ran while one was open for 4% of the time, Pallas kernels for 32%

profile of v14, /device:TPU:18, one launch (start us, length us, event | category | flops | bytes accessed | tf_op | source)
XLA Modules:
  0.0 157.4 jit_solution(9356531352378006364)
XLA Ops:
  0.0 1.2 copy.24
  1.2 1.6 %collective-permute-start.3 = (bf16[128,1024]{1,0:T(8,128)(2,1)S(1)}, bf16[128,1024]{1,0:T(8,128)(2,1)S(1)}, u32[]{:S(2)}, u32[]{:S(2)}) collective-permute-start(bf16[128,1024]{1,0:T(8,128)(2,1)S(1)} %bitcast.38), channel_id=1, source_target_pairs={{0,2},{2,0},{4,6},{6,4},{8,10},{10,8},{12,14},{14,12},{1,3},{3,1},... | collective-permute-start | bytes 786440 | tf_op jit(solution)/shard_map/ppermute | solution.py:28
  2.8 1.6 %collective-permute-start.6 = (bf16[128,1024]{1,0:T(8,128)(2,1)S(1)}, bf16[128,1024]{1,0:T(8,128)(2,1)}, u32[]{:S(2)}, u32[]{:S(2)}) collective-permute-start(bf16[128,1024]{1,0:T(8,128)(2,1)S(1)} %bitcast.39), channel_id=1, source_target_pairs={{0,4},{2,6},{4,8},{6,10},{8,12},{10,14},{12,0},{14,2},{1,5},{3,7},... | collective-permute-start | bytes 786440 | tf_op jit(solution)/shard_map/ppermute | solution.py:28
  4.4 0.8 eq.92
  5.1 1.6 %multiply_reduce_fusion = (f32[256]{0:T(256)S(1)}, bf16[256,1024]{1,0:T(8,128)(2,1)}, f32[256,1024]{1,0:T(8,128)}) fusion(bf16[512,1024]{1,0:T(8,128)(2,1)S(1)} %copy-done, s32[256]{0:T(256)S(1)} %eq.92), kind=kOutput, calls=%fused_computation.4 | convolution fusion | flops 269352704 | bytes 2623488 | tf_op jit(solution)/shard_map/dot_general | solution.py:350
  6.7 0.5 collective-permute-start.7
  7.3 0.2 collective-permute-start
  7.5 1.8 %collective-permute-start.12 = (bf16[128,1024]{1,0:T(8,128)(2,1)S(1)}, bf16[128,1024]{1,0:T(8,128)(2,1)}, u32[]{:S(2)}, u32[]{:S(2)}) collective-permute-start(bf16[128,1024]{1,0:T(8,128)(2,1)S(1)} %bitcast.40), channel_id=1, source_target_pairs={{0,12},{2,14},{4,0},{6,2},{8,4},{10,6},{12,8},{14,10},{1,13},{3,15... | collective-permute-start | bytes 786440 | tf_op jit(solution)/shard_map/ppermute | solution.py:28
  9.3 0.6 broadcast_in_dim.21
  9.9 5.4 %all-to-all-start = ((f32[8,10,128]{2,1,0:T(8,128)}), f32[8,10,128]{2,1,0:T(8,128)S(1)}, u32[]{:S(2)}, u32[]{:S(2)}) async-start(f32[8,10,128]{2,1,0:T(8,128)} %broadcast_in_dim.21), calls=%async_computation | async-start | bytes 131072 | tf_op jit(solution)/shard_map/all_to_all | solution.py:353
  15.3 0.1 reshape.68
  15.5 0.1 iota_compare_fusion.2
  15.5 0.1 pad_add_fusion.2.spot
  15.8 0.2 select_reduce_fusion
  16.0 0.2 and_convert_fusion
  16.2 0.1 pad_add_fusion.5.spot
  16.2 0.9 reshape.72
  17.1 0.6 collective-permute-start.4
  17.8 4.9 %history_terms.4.refs_0_ = bf16[8,4,8,1024]{3,2,1,0:T(8,128)(2,1)S(1)} custom-call(s32[2]{0:T(128)S(1)} %pad_add_fusion.2.spot, s32[8,128]{1,0:T(8,128)S(1)} %broadcast_in_dim.24.lengths_ref, bf16[128,1024]{1,0:T(8,128)(2,1)S(1)} %bitcast.41, bf16[128,1024]{1,0:T(8,128)(2,1)S(1)} %collective-permute-done.3.far_ref, bf16[127,8,8192]{2,1,0:T(8,128)(2,1)} %bitcast.43), custom_call_target="tpu_custom_call" | custom-call | flops 4993843200 | bytes 4161536 | tf_op jit(solution)/shard_map/history_terms/pallas_call | solution.py:51
  22.7 0.8 copy-done.2
  23.5 15.6 %all-to-all-done = f32[8,10,128]{2,1,0:T(8,128)S(1)} async-done(((f32[8,10,128]{2,1,0:T(8,128)}), f32[8,10,128]{2,1,0:T(8,128)S(1)}, u32[]{:S(2)}, u32[]{:S(2)}) %all-to-all-start) | async-done | bytes 40992 | tf_op jit(solution)/shard_map/all_to_all | solution.py:353
  39.1 1.0 collective-permute-start.8
  40.1 2.2 %collective-permute-start.10 = (bf16[128,1024]{1,0:T(8,128)(2,1)}, bf16[128,1024]{1,0:T(8,128)(2,1)S(1)}, u32[]{:S(2)}, u32[]{:S(2)}) collective-permute-start(bf16[128,1024]{1,0:T(8,128)(2,1)} %collective-permute-done.6.near_ref), channel_id=1, source_target_pairs={{0,4},{2,6},{4,8},{6,10},{8,12},{10,14},{12,0},{14,2},{1,5},{3,7},... | collective-permute-start | bytes 786440 | tf_op jit(solution)/shard_map/ppermute | solution.py:28
  42.3 0.9 collective-permute-start.13
  43.2 1.1 collective-permute-start.9
  44.3 0.1 broadcast_in_dim.25.inv_ref
  44.4 6.9 %projected_part.3.refs_0_ = f32[256,3072]{1,0:T(8,128)S(1)} custom-call(s32[2]{0:T(128)S(1)} %pad_add_fusion.2.spot, bf16[256,1024]{1,0:T(8,128)(2,1)} %get-tuple-element.23.near, bf16[256,1024]{1,0:T(8,128)(2,1)} %copy-done.6, f32[8,1024]{1,0:T(8,128)S(1)} %bitcast.34, f32[256,128]{1,0:T(8,128)S(1)} %broadcast_in_dim.25.inv_ref, bf16[8192,3072]{1,0:T(8,128)(2,1)} %w_hbm.9), custom_call_target="tpu_custom_call" | custom-call | flops 6442450944 | bytes 25165824 | tf_op jit(solution)/shard_map/projected_part/pallas_call | solution.py:51
  51.4 5.4 %history_terms.5.refs_0_ = bf16[8,4,8,1024]{3,2,1,0:T(8,128)(2,1)S(1)} custom-call(s32[2]{0:T(128)S(1)} %pad_add_fusion.4.spot, s32[8,128]{1,0:T(8,128)S(1)} %broadcast_in_dim.24.lengths_ref, bf16[128,1024]{1,0:T(8,128)(2,1)} %collective-permute-done.6.near_ref, ...), custom_call_target="tpu_custom_call", output_to_operand_aliasing={{}: (5, {})} | custom-call | flops 4993843200 | bytes 4161536 | tf_op jit(solution)/shard_map/history_terms/pallas_call | solution.py:51
  56.8 0.1 collective-permute-start.1
  56.9 0.9 collective-permute-start.11
  57.8 1.1 collective-permute-start.5
  58.9 1.0 collective-permute-done.9.far
  60.0 0.8 copy-done.7
  60.8 6.9 %projected_part.4.refs_0_ = f32[256,3072]{1,0:T(8,128)S(1)} custom-call(s32[2]{0:T(128)S(1)} %pad_add_fusion.4.spot, bf16[256,1024]{1,0:T(8,128)(2,1)} %collective-permute-done.near, bf16[256,1024]{1,0:T(8,128)(2,1)} %copy-done.7, f32[8,1024]{1,0:T(8,128)S(1)} %bitcast.35, f32[256,128]{1,0:T(8,128)S(1)} %broadcast_in_dim.25.inv_ref, ...), custom_call_target="tpu_custom_call", output_to_operand_aliasing={{}: (6, {})} | custom-call | flops 6442450944 | bytes 25165824 | tf_op jit(solution)/shard_map/projected_part/pallas_call | solution.py:51
  67.7 5.4 %history_terms.6.refs_0_ = bf16[8,4,8,1024]{3,2,1,0:T(8,128)(2,1)S(1)} custom-call(s32[2]{0:T(128)S(1)} %pad_add_fusion.3.spot, s32[8,128]{1,0:T(8,128)S(1)} %broadcast_in_dim.24.lengths_ref, bf16[128,1024]{1,0:T(8,128)(2,1)} %collective-permute-done.12.near_ref, ...), custom_call_target="tpu_custom_call", output_to_operand_aliasing={{}: (5, {})} | custom-call | flops 4993843200 | bytes 4161536 | tf_op jit(solution)/shard_map/history_terms/pallas_call | solution.py:51
  73.1 5.0 %history_terms.7 = bf16[8,4,8,1024]{3,2,1,0:T(8,128)(2,1)S(1)} custom-call(s32[2]{0:T(128)S(1)} %pad_add_fusion.5.spot, s32[8,128]{1,0:T(8,128)S(1)} %broadcast_in_dim.24.lengths_ref, bf16[128,1024]{1,0:T(8,128)(2,1)S(1)} %collective-permute-done.10.near_ref, bf16[128,1024]{1,0:T(8,128)(2,1)S(1)} %collective-permute-done.11.far_ref, ...), custom_call_target="tpu_custom_call", output_to_operand_aliasing={{}: (5, {})} | custom-call | flops 4993843200 | bytes 4161536 | tf_op jit(solution)/shard_map/history_terms/pallas_call | solution.py:51
  78.1 0.8 copy-done.4
  78.8 7.3 %all-to-all-start.1 = ((bf16[8,4,8,1024]{3,2,1,0:T(8,128)(2,1)}), bf16[8,4,8,1024]{3,2,1,0:T(8,128)(2,1)}, u32[]{:S(2)}, u32[]{:S(2)}) async-start(bf16[8,4,8,1024]{3,2,1,0:T(8,128)(2,1)} %copy-done.4), calls=%async_computation.1 | async-start | bytes 1048576 | tf_op jit(solution)/shard_map/all_to_all | solution.py:401
  86.2 1.0 copy.26.refs_2_
  87.3 0.1 pad_add_fusion.1.spot
  87.3 1.5 collective-permute-start.2
  88.8 6.9 %projected_part.5.refs_0_ = f32[256,3072]{1,0:T(8,128)S(1)} custom-call(s32[2]{0:T(128)S(1)} %pad_add_fusion.3.spot, bf16[256,1024]{1,0:T(8,128)(2,1)} %collective-permute-done.4.near, bf16[256,1024]{1,0:T(8,128)(2,1)} %collective-permute-done.5.far, f32[8,1024]{1,0:T(8,128)S(1)} %bitcast.36, ...), custom_call_target="tpu_custom_call", output_to_operand_aliasing={{}: (6, {})} | custom-call | flops 6442450944 | bytes 25165824 | tf_op jit(solution)/shard_map/projected_part/pallas_call | solution.py:51
  95.7 3.4 %collective-permute-done.2.far = bf16[256,1024]{1,0:T(8,128)(2,1)} collective-permute-done((bf16[256,1024]{1,0:T(8,128)(2,1)}, bf16[256,1024]{1,0:T(8,128)(2,1)}, u32[]{:S(2)}, u32[]{:S(2)}) %collective-permute-start.2) | collective-permute-done | bytes 524320 | tf_op jit(solution)/shard_map/ppermute | solution.py:28
  99.2 10.2 %gated_rows.1 = (f32[256,3072]{1,0:T(8,128)S(1)}, bf16[256,1024]{1,0:T(8,128)(2,1)S(1)}, bf16[256,1024]{1,0:T(8,128)(2,1)S(1)}, bf16[256,1024]{1,0:T(8,128)(2,1)S(1)}) custom-call(s32[4]{0:T(128)S(1)} %pad_add_fusion.1.spot, bf16[256,1024]{1,0:T(8,128)(2,1)} %collective-permute-done.1.near, ...), custom_call_target="tpu_custom_call", output_to_operand_aliasing={{0}: (6, {})} | custom-call | flops 6442450944 | bytes 25165824 | tf_op jit(solution)/shard_map/gated_rows/pallas_call | solution.py:51
  109.4 0.2 collective-permute-start.14
  109.8 0.1 pad_add_fusion.spot
  109.8 1.8 %collective-permute-start.16 = (bf16[256,1024]{1,0:T(8,128)(2,1)S(1)}, bf16[256,1024]{1,0:T(8,128)(2,1)S(1)}, u32[]{:S(2)}, u32[]{:S(2)}) collective-permute-start(bf16[256,1024]{1,0:T(8,128)(2,1)S(1)} %get-tuple-element.32), channel_id=1, source_target_pairs={{0,2},{2,0},{4,6},{6,4},{8,10},{10,8},{12,14},{14,12},{1,3},{3,1},... | collective-permute-start | bytes 1572872 | tf_op jit(solution)/shard_map/ppermute | solution.py:28
  111.7 3.8 %output_shares.3 = (bf16[256,1024]{1,0:T(8,128)(2,1)S(1)}, bf16[256,1024]{1,0:T(8,128)(2,1)S(1)}) custom-call(s32[2]{0:T(128)S(1)} %pad_add_fusion.6.spot, bf16[256,1024]{1,0:T(8,128)(2,1)S(1)} %get-tuple-element.28.x_ref, bf16[1024,8192]{1,0:T(8,128)(2,1)} %w_hbm.11), custom_call_target="tpu_custom_call" | custom-call | flops 1073741824 | bytes 4194304 | tf_op jit(solution)/shard_map/output_shares/pallas_call | solution.py:51
  115.5 0.2 collective-permute-start.18
  115.7 1.8 %collective-permute-start.20 = (bf16[256,1024]{1,0:T(8,128)(2,1)S(1)}, bf16[256,1024]{1,0:T(8,128)(2,1)S(1)}, u32[]{:S(2)}, u32[]{:S(2)}) collective-permute-start(bf16[256,1024]{1,0:T(8,128)(2,1)S(1)} %get-tuple-element.36), channel_id=1, source_target_pairs={{0,2},{2,0},{4,6},{6,4},{8,10},{10,8},{12,14},{14,12},{1,3},{3,1},... | collective-permute-start | bytes 1572872 | tf_op jit(solution)/shard_map/ppermute | solution.py:28
  117.5 5.8 %output_shares.2 = (f32[256,1024]{1,0:T(8,128)S(1)}, f32[256,1024]{1,0:T(8,128)S(1)}, f32[256,1024]{1,0:T(8,128)S(1)}, f32[256,1024]{1,0:T(8,128)S(1)}) custom-call(s32[4]{0:T(128)S(1)} %pad_add_fusion.spot, bf16[256,1024]{1,0:T(8,128)(2,1)S(1)} %get-tuple-element.28.x_ref, bf16[1024,8192]{1,0:T(8,128)(2,1)} %w_hbm.11), custom_call_target="tpu_custom_call" | custom-call | flops 2147483648 | bytes 8388608 | tf_op jit(solution)/shard_map/output_shares/pallas_call | solution.py:51
  123.3 1.0 collective-permute-done.14
  124.4 0.1 add_convert_fusion.3
  124.5 0.2 collective-permute-start.15
  124.7 7.2 %collective-permute-done.16 = bf16[256,1024]{1,0:T(8,128)(2,1)S(1)} collective-permute-done((bf16[256,1024]{1,0:T(8,128)(2,1)S(1)}, bf16[256,1024]{1,0:T(8,128)(2,1)S(1)}, u32[]{:S(2)}, u32[]{:S(2)}) %collective-permute-start.16) | collective-permute-done | bytes 524320 | tf_op jit(solution)/shard_map/ppermute | solution.py:28
  131.9 0.1 add_convert_fusion.2
  132.0 1.9 %collective-permute-start.17 = (bf16[256,1024]{1,0:T(8,128)(2,1)S(1)}, bf16[256,1024]{1,0:T(8,128)(2,1)S(1)}, u32[]{:S(2)}, u32[]{:S(2)}) collective-permute-start(bf16[256,1024]{1,0:T(8,128)(2,1)S(1)} %add_convert_fusion.2), channel_id=1, source_target_pairs={{0,4},{2,6},{4,8},{6,10},{8,12},{10,14},{12,0},{14,2},{1,5},{3,7},... | collective-permute-start | bytes 1572872 | tf_op jit(solution)/shard_map/ppermute | solution.py:28
  133.9 3.6 %collective-permute-done.18 = bf16[256,1024]{1,0:T(8,128)(2,1)S(1)} collective-permute-done((bf16[256,1024]{1,0:T(8,128)(2,1)S(1)}, bf16[256,1024]{1,0:T(8,128)(2,1)S(1)}, u32[]{:S(2)}, u32[]{:S(2)}) %collective-permute-start.18) | collective-permute-done | bytes 524320 | tf_op jit(solution)/shard_map/ppermute | solution.py:28
  137.5 0.1 add_convert_fusion.1
  137.6 1.3 collective-permute-start.19
  138.9 4.1 %collective-permute-done.20 = bf16[256,1024]{1,0:T(8,128)(2,1)S(1)} collective-permute-done((bf16[256,1024]{1,0:T(8,128)(2,1)S(1)}, bf16[256,1024]{1,0:T(8,128)(2,1)S(1)}, u32[]{:S(2)}, u32[]{:S(2)}) %collective-permute-start.20) | collective-permute-done | bytes 524320 | tf_op jit(solution)/shard_map/ppermute | solution.py:28
  143.1 5.3 %collective-permute-done.15 = bf16[256,1024]{1,0:T(8,128)(2,1)S(1)} collective-permute-done((bf16[256,1024]{1,0:T(8,128)(2,1)S(1)}, bf16[256,1024]{1,0:T(8,128)(2,1)S(1)}, u32[]{:S(2)}, u32[]{:S(2)}) %collective-permute-start.15) | collective-permute-done | bytes 524320 | tf_op jit(solution)/shard_map/ppermute | solution.py:28
  148.4 7.7 %collective-permute-done.17 = bf16[256,1024]{1,0:T(8,128)(2,1)S(1)} collective-permute-done((bf16[256,1024]{1,0:T(8,128)(2,1)S(1)}, bf16[256,1024]{1,0:T(8,128)(2,1)S(1)}, u32[]{:S(2)}, u32[]{:S(2)}) %collective-permute-start.17) | collective-permute-done | bytes 524320 | tf_op jit(solution)/shard_map/ppermute | solution.py:28
  156.0 1.3 add_convert_fusion
  (47 shorter events, 0.4 us)
Async XLA Ops:
  0.0 5.1 %copy-start = (bf16[512,1024]{1,0:T(8,128)(2,1)S(1)}, bf16[512,1024]{1,0:T(8,128)(2,1)}, u32[]{:S(2)}) copy-start(bf16[512,1024]{1,0:T(8,128)(2,1)} %param.10) | copy-start | bytes 3145732
  0.0 9.3 %copy-start.8 = (bf16[1024]{0:T(1024)(128)(2,1)S(1)}, bf16[1024]{0:T(1024)(128)(2,1)}, u32[]{:S(2)}) copy-start(bf16[1024]{0:T(1024)(128)(2,1)} %param.11) | copy-start | bytes 6148
  0.0 15.3 %copy-start.9 = (s32[128]{0:T(128)S(1)}, s32[128]{0:T(128)}, u32[]{:S(2)}) copy-start(s32[128]{0:T(128)} %param.16) | copy-start | bytes 1540
  0.0 15.8 %copy-start.10 = (s32[64]{0:T(128)S(1)}, s32[64]{0:T(128)}, u32[]{:S(2)}) copy-start(s32[64]{0:T(128)} %param.17) | copy-start | bytes 772
  1.2 15.9 %collective-permute-start.3 = (bf16[128,1024]{1,0:T(8,128)(2,1)S(1)}, bf16[128,1024]{1,0:T(8,128)(2,1)S(1)}, u32[]{:S(2)}, u32[]{:S(2)}) collective-permute-start(bf16[128,1024]{1,0:T(8,128)(2,1)S(1)} %bitcast.38), channel_id=1, source_target_pairs={{0,2},{2,0},{4,6},{6,4},{8,10},{10,8},{12,14},{14,12},{1,3},{3,1},... | collective-permute-start | bytes 786440 | tf_op jit(solution)/shard_map/ppermute | solution.py:28
  2.8 36.3 %collective-permute-start.6 = (bf16[128,1024]{1,0:T(8,128)(2,1)S(1)}, bf16[128,1024]{1,0:T(8,128)(2,1)}, u32[]{:S(2)}, u32[]{:S(2)}) collective-permute-start(bf16[128,1024]{1,0:T(8,128)(2,1)S(1)} %bitcast.39), channel_id=1, source_target_pairs={{0,4},{2,6},{4,8},{6,10},{8,12},{10,14},{12,0},{14,2},{1,5},{3,7},... | collective-permute-start | bytes 786440 | tf_op jit(solution)/shard_map/ppermute | solution.py:28
  6.7 35.5 %collective-permute-start.7 = (bf16[256,1024]{1,0:T(8,128)(2,1)}, bf16[256,1024]{1,0:T(8,128)(2,1)S(1)}, u32[]{:S(2)}, u32[]{:S(2)}) collective-permute-start(bf16[256,1024]{1,0:T(8,128)(2,1)} %get-tuple-element.23.near), channel_id=1, source_target_pairs={{0,2},{2,0},{4,6},{6,4},{8,10},{10,8},{12,14},{14,12},{1,3},{3,1},... | collective-permute-start | bytes 1572872 | tf_op jit(solution)/shard_map/ppermute | solution.py:28
  7.3 36.0 %collective-permute-start = (bf16[256,1024]{1,0:T(8,128)(2,1)}, bf16[256,1024]{1,0:T(8,128)(2,1)}, u32[]{:S(2)}, u32[]{:S(2)}) collective-permute-start(bf16[256,1024]{1,0:T(8,128)(2,1)} %get-tuple-element.23.near), channel_id=1, source_target_pairs={{0,4},{2,6},{4,8},{6,10},{8,12},{10,14},{12,0},{14,2},{1,5},{3,7},... | collective-permute-start | bytes 1572872 | tf_op jit(solution)/shard_map/ppermute | solution.py:28
  7.5 32.6 %collective-permute-start.12 = (bf16[128,1024]{1,0:T(8,128)(2,1)S(1)}, bf16[128,1024]{1,0:T(8,128)(2,1)}, u32[]{:S(2)}, u32[]{:S(2)}) collective-permute-start(bf16[128,1024]{1,0:T(8,128)(2,1)S(1)} %bitcast.40), channel_id=1, source_target_pairs={{0,12},{2,14},{4,0},{6,2},{8,4},{10,6},{12,8},{14,10},{1,13},{3,15... | collective-permute-start | bytes 786440 | tf_op jit(solution)/shard_map/ppermute | solution.py:28
  9.9 29.2 %all-to-all-start = ((f32[8,10,128]{2,1,0:T(8,128)}), f32[8,10,128]{2,1,0:T(8,128)S(1)}, u32[]{:S(2)}, u32[]{:S(2)}) async-start(f32[8,10,128]{2,1,0:T(8,128)} %broadcast_in_dim.21), calls=%async_computation | async-start | bytes 131072 | tf_op jit(solution)/shard_map/all_to_all | solution.py:353
  17.1 40.7 %collective-permute-start.4 = (bf16[256,1024]{1,0:T(8,128)(2,1)}, bf16[256,1024]{1,0:T(8,128)(2,1)}, u32[]{:S(2)}, u32[]{:S(2)}) collective-permute-start(bf16[256,1024]{1,0:T(8,128)(2,1)} %get-tuple-element.23.near), channel_id=1, source_target_pairs={{0,12},{2,14},{4,0},{6,2},{8,4},{10,6},{12,8},{14,10},{1,13},{3,15... | collective-permute-start | bytes 1572872 | tf_op jit(solution)/shard_map/ppermute | solution.py:28
  22.7 0.8 copy-start.2
  39.1 12.2 %collective-permute-start.8 = (bf16[128,1024]{1,0:T(8,128)(2,1)}, bf16[128,1024]{1,0:T(8,128)(2,1)S(1)}, u32[]{:S(2)}, u32[]{:S(2)}) collective-permute-start(bf16[128,1024]{1,0:T(8,128)(2,1)} %collective-permute-done.6.near_ref), channel_id=1, source_target_pairs={{0,2},{2,0},{4,6},{6,4},{8,10},{10,8},{12,14},{14,12},{1,3},{3,1},... | collective-permute-start | bytes 786440 | tf_op jit(solution)/shard_map/ppermute | solution.py:28
  40.1 16.8 %collective-permute-start.10 = (bf16[128,1024]{1,0:T(8,128)(2,1)}, bf16[128,1024]{1,0:T(8,128)(2,1)S(1)}, u32[]{:S(2)}, u32[]{:S(2)}) collective-permute-start(bf16[128,1024]{1,0:T(8,128)(2,1)} %collective-permute-done.6.near_ref), channel_id=1, source_target_pairs={{0,4},{2,6},{4,8},{6,10},{8,12},{10,14},{12,0},{14,2},{1,5},{3,7},... | collective-permute-start | bytes 786440 | tf_op jit(solution)/shard_map/ppermute | solution.py:28
  42.3 2.1 %copy-start.6 = (bf16[256,1024]{1,0:T(8,128)(2,1)}, bf16[256,1024]{1,0:T(8,128)(2,1)S(1)}, u32[]{:S(2)}) copy-start(bf16[256,1024]{1,0:T(8,128)(2,1)S(1)} %collective-permute-done.7.far) | copy-start | bytes 1572868
  42.3 25.4 %collective-permute-start.13 = (bf16[128,1024]{1,0:T(8,128)(2,1)}, bf16[128,1024]{1,0:T(8,128)(2,1)S(1)}, u32[]{:S(2)}, u32[]{:S(2)}) collective-permute-start(bf16[128,1024]{1,0:T(8,128)(2,1)} %collective-permute-done.12.near_ref), channel_id=1, source_target_pairs={{0,2},{2,0},{4,6},{6,4},{8,10},{10,8},{12,14},{14,12},{1,3},{3,1},... | collective-permute-start | bytes 786440 | tf_op jit(solution)/shard_map/ppermute | solution.py:28
  43.2 16.7 %collective-permute-start.9 = (bf16[256,1024]{1,0:T(8,128)(2,1)}, bf16[256,1024]{1,0:T(8,128)(2,1)S(1)}, u32[]{:S(2)}, u32[]{:S(2)}) collective-permute-start(bf16[256,1024]{1,0:T(8,128)(2,1)} %collective-permute-done.near), channel_id=1, source_target_pairs={{0,2},{2,0},{4,6},{6,4},{8,10},{10,8},{12,14},{14,12},{1,3},{3,1},... | collective-permute-start | bytes 1572872 | tf_op jit(solution)/shard_map/ppermute | solution.py:28
  44.4 6.9 %copy-start.3 = (bf16[8,4,8,1024]{3,2,1,0:T(8,128)(2,1)S(1)}, bf16[8,4,8,1024]{3,2,1,0:T(8,128)(2,1)}, u32[]{:S(2)}) copy-start(bf16[8,4,8,1024]{3,2,1,0:T(8,128)(2,1)} %copy-done.2) | copy-start | bytes 1572868
  56.8 30.6 %collective-permute-start.1 = (bf16[256,1024]{1,0:T(8,128)(2,1)}, bf16[256,1024]{1,0:T(8,128)(2,1)}, u32[]{:S(2)}, u32[]{:S(2)}) collective-permute-start(bf16[256,1024]{1,0:T(8,128)(2,1)} %collective-permute-done.near), channel_id=1, source_target_pairs={{0,4},{2,6},{4,8},{6,10},{8,12},{10,14},{12,0},{14,2},{1,5},{3,7},... | collective-permute-start | bytes 1572872 | tf_op jit(solution)/shard_map/ppermute | solution.py:28
  56.9 16.2 %collective-permute-start.11 = (bf16[128,1024]{1,0:T(8,128)(2,1)S(1)}, bf16[128,1024]{1,0:T(8,128)(2,1)S(1)}, u32[]{:S(2)}, u32[]{:S(2)}) collective-permute-start(bf16[128,1024]{1,0:T(8,128)(2,1)S(1)} %collective-permute-done.10.near_ref), channel_id=1, source_target_pairs={{0,2},{2,0},{4,6},{6,4},{8,10},{10,8},{12,14},{14,12},{1,3},{3,1},... | collective-permute-start | bytes 786440 | tf_op jit(solution)/shard_map/ppermute | solution.py:28
  57.8 31.0 %collective-permute-start.5 = (bf16[256,1024]{1,0:T(8,128)(2,1)}, bf16[256,1024]{1,0:T(8,128)(2,1)}, u32[]{:S(2)}, u32[]{:S(2)}) collective-permute-start(bf16[256,1024]{1,0:T(8,128)(2,1)} %collective-permute-done.4.near), channel_id=1, source_target_pairs={{0,2},{2,0},{4,6},{6,4},{8,10},{10,8},{12,14},{14,12},{1,3},{3,1},... | collective-permute-start | bytes 1572872 | tf_op jit(solution)/shard_map/ppermute | solution.py:28
  60.0 0.8 copy-start.7
  78.0 0.8 copy-start.4
  78.8 20.3 %all-to-all-start.1 = ((bf16[8,4,8,1024]{3,2,1,0:T(8,128)(2,1)}), bf16[8,4,8,1024]{3,2,1,0:T(8,128)(2,1)}, u32[]{:S(2)}, u32[]{:S(2)}) async-start(bf16[8,4,8,1024]{3,2,1,0:T(8,128)(2,1)} %copy-done.4), calls=%async_computation.1 | async-start | bytes 1048576 | tf_op jit(solution)/shard_map/all_to_all | solution.py:401
  87.3 11.8 %collective-permute-start.2 = (bf16[256,1024]{1,0:T(8,128)(2,1)}, bf16[256,1024]{1,0:T(8,128)(2,1)}, u32[]{:S(2)}, u32[]{:S(2)}) collective-permute-start(bf16[256,1024]{1,0:T(8,128)(2,1)} %collective-permute-done.1.near), channel_id=1, source_target_pairs={{0,2},{2,0},{4,6},{6,4},{8,10},{10,8},{12,14},{14,12},{1,3},{3,1},... | collective-permute-start | bytes 1572872 | tf_op jit(solution)/shard_map/ppermute | solution.py:28
  109.4 14.9 %collective-permute-start.14 = (bf16[256,1024]{1,0:T(8,128)(2,1)S(1)}, bf16[256,1024]{1,0:T(8,128)(2,1)S(1)}, u32[]{:S(2)}, u32[]{:S(2)}) collective-permute-start(bf16[256,1024]{1,0:T(8,128)(2,1)S(1)} %get-tuple-element.30), channel_id=1, source_target_pairs={{0,2},{2,0},{4,6},{6,4},{8,10},{10,8},{12,14},{14,12},{1,3},{3,1},... | collective-permute-start | bytes 1572872 | tf_op jit(solution)/shard_map/ppermute | solution.py:28
  109.8 22.0 %collective-permute-start.16 = (bf16[256,1024]{1,0:T(8,128)(2,1)S(1)}, bf16[256,1024]{1,0:T(8,128)(2,1)S(1)}, u32[]{:S(2)}, u32[]{:S(2)}) collective-permute-start(bf16[256,1024]{1,0:T(8,128)(2,1)S(1)} %get-tuple-element.32), channel_id=1, source_target_pairs={{0,2},{2,0},{4,6},{6,4},{8,10},{10,8},{12,14},{14,12},{1,3},{3,1},... | collective-permute-start | bytes 1572872 | tf_op jit(solution)/shard_map/ppermute | solution.py:28
  115.5 22.0 %collective-permute-start.18 = (bf16[256,1024]{1,0:T(8,128)(2,1)S(1)}, bf16[256,1024]{1,0:T(8,128)(2,1)S(1)}, u32[]{:S(2)}, u32[]{:S(2)}) collective-permute-start(bf16[256,1024]{1,0:T(8,128)(2,1)S(1)} %get-tuple-element.34), channel_id=1, source_target_pairs={{0,2},{2,0},{4,6},{6,4},{8,10},{10,8},{12,14},{14,12},{1,3},{3,1},... | collective-permute-start | bytes 1572872 | tf_op jit(solution)/shard_map/ppermute | solution.py:28
  115.7 27.4 %collective-permute-start.20 = (bf16[256,1024]{1,0:T(8,128)(2,1)S(1)}, bf16[256,1024]{1,0:T(8,128)(2,1)S(1)}, u32[]{:S(2)}, u32[]{:S(2)}) collective-permute-start(bf16[256,1024]{1,0:T(8,128)(2,1)S(1)} %get-tuple-element.36), channel_id=1, source_target_pairs={{0,2},{2,0},{4,6},{6,4},{8,10},{10,8},{12,14},{14,12},{1,3},{3,1},... | collective-permute-start | bytes 1572872 | tf_op jit(solution)/shard_map/ppermute | solution.py:28
  124.4 31.7 %copy-start.5 = (f32[256,1024]{1,0:T(8,128)S(1)}, f32[256,1024]{1,0:T(8,128)}, u32[]{:S(2)}) copy-start(f32[256,1024]{1,0:T(8,128)} %get-tuple-element.39) | copy-start | bytes 3145732
  124.5 23.8 %collective-permute-start.15 = (bf16[256,1024]{1,0:T(8,128)(2,1)S(1)}, bf16[256,1024]{1,0:T(8,128)(2,1)S(1)}, u32[]{:S(2)}, u32[]{:S(2)}) collective-permute-start(bf16[256,1024]{1,0:T(8,128)(2,1)S(1)} %add_convert_fusion.3), channel_id=1, source_target_pairs={{0,8},{2,10},{4,12},{6,14},{8,0},{10,2},{12,4},{14,6},{1,9},{3,11}... | collective-permute-start | bytes 1572872 | tf_op jit(solution)/shard_map/ppermute | solution.py:28
  132.0 24.0 %collective-permute-start.17 = (bf16[256,1024]{1,0:T(8,128)(2,1)S(1)}, bf16[256,1024]{1,0:T(8,128)(2,1)S(1)}, u32[]{:S(2)}, u32[]{:S(2)}) collective-permute-start(bf16[256,1024]{1,0:T(8,128)(2,1)S(1)} %add_convert_fusion.2), channel_id=1, source_target_pairs={{0,4},{2,6},{4,8},{6,10},{8,12},{10,14},{12,0},{14,2},{1,5},{3,7},... | collective-permute-start | bytes 1572872 | tf_op jit(solution)/shard_map/ppermute | solution.py:28
  137.5 19.9 %copy-start.1 = (bf16[512,1024]{1,0:T(8,128)(2,1)S(1)}, bf16[512,1024]{1,0:T(8,128)(2,1)}, u32[]{:S(2)}) copy-start(bf16[512,1024]{1,0:T(8,128)(2,1)} %param.10) | copy-start | bytes 3145732
  137.6 18.4 %collective-permute-start.19 = (bf16[256,1024]{1,0:T(8,128)(2,1)S(1)}, bf16[256,1024]{1,0:T(8,128)(2,1)S(1)}, u32[]{:S(2)}, u32[]{:S(2)}) collective-permute-start(bf16[256,1024]{1,0:T(8,128)(2,1)S(1)} %add_convert_fusion.1), channel_id=1, source_target_pairs={{0,12},{2,14},{4,0},{6,2},{8,4},{10,6},{12,8},{14,10},{1,13},{3,15... | collective-permute-start | bytes 1572872 | tf_op jit(solution)/shard_map/ppermute | solution.py:28

commit v15 on v14

--- a/solution.py
+++ b/solution.py
@@ -392,7 +392,7 @@
     parts = len(streams)
     for index, (back, near, far) in enumerate(lag_taps):
         if index:
-            near = after(near, sums)
+            near = after(near, (sums, streams[-1][1]) if index == parts - 1 else sums)
             terms = history_terms(cache, near, far, row_lengths, spot_at(-back), steps, terms)
         if 2 * index < parts:
             at, *pair = streams[index]

time: 158 us -> 158 us (level)
  no operation moved by 1% of the time
where the time goes in v15:
time: 158 us; the launch traced here: 157 us
  Pallas kernels  61.2 us (39%)
  waiting for transfers between devices  48.9 us (31%)
  starting transfers between devices  35.4 us (22%)
  local copies, waits for them, and re-layouts  7.08 us (4%)
  other arithmetic  2.8 us (2%)
  matrix products  1.62 us (1%)
    pallas_call x10, Pallas kernels, kernel_call(): pl.pallas_call(kernel, in_specs=[IN_SMEM, *specs], out_specs=list(out_spe...  61.2 us
    ppermute x21, waiting for transfers between devices, moved(): return lax.ppermute(array, 'tensor', pairs)  33.3 us
    ppermute x21, starting transfers between devices, moved(): return lax.ppermute(array, 'tensor', pairs)  22.7 us
    all_to_all x1, waiting for transfers between devices, per_device(): lax.all_to_all(jnp.broadcast_to(tiny[None], (owners, *tiny.shape)), 'tens...  15.6 us
    all_to_all x1, starting transfers between devices, per_device(): terms = lax.all_to_all(terms, 'tensor', 0, 0, tiled=True)  7.34 us
    all_to_all x1, starting transfers between devices, per_device(): lax.all_to_all(jnp.broadcast_to(tiny[None], (owners, *tiny.shape)), 'tens...  5.41 us
    unnamed x25, local copies, waits for them, and re-layouts  3.58 us
  transfers between devices with their start and end apart: 23, of which 9 were waited for; matrix products, arithmetic and copies ran while one was open for 4% of the time, Pallas kernels for 32%

profile of v15, /device:TPU:18, one launch (start us, length us, event | category | flops | bytes accessed | tf_op | source)
XLA Modules:
  0.0 157.4 jit_solution(17424582225309944707)
XLA Ops:
  0.0 1.2 copy.24
  1.2 1.6 %collective-permute-start.3 = (bf16[128,1024]{1,0:T(8,128)(2,1)S(1)}, bf16[128,1024]{1,0:T(8,128)(2,1)S(1)}, u32[]{:S(2)}, u32[]{:S(2)}) collective-permute-start(bf16[128,1024]{1,0:T(8,128)(2,1)S(1)} %bitcast.38), channel_id=1, source_target_pairs={{0,2},{2,0},{4,6},{6,4},{8,10},{10,8},{12,14},{14,12},{1,3},{3,1},... | collective-permute-start | bytes 786440 | tf_op jit(solution)/shard_map/ppermute | solution.py:28
  2.8 1.6 %collective-permute-start.6 = (bf16[128,1024]{1,0:T(8,128)(2,1)S(1)}, bf16[128,1024]{1,0:T(8,128)(2,1)}, u32[]{:S(2)}, u32[]{:S(2)}) collective-permute-start(bf16[128,1024]{1,0:T(8,128)(2,1)S(1)} %bitcast.39), channel_id=1, source_target_pairs={{0,4},{2,6},{4,8},{6,10},{8,12},{10,14},{12,0},{14,2},{1,5},{3,7},... | collective-permute-start | bytes 786440 | tf_op jit(solution)/shard_map/ppermute | solution.py:28
  4.4 0.8 eq.92
  5.1 1.6 %multiply_reduce_fusion = (f32[256]{0:T(256)S(1)}, bf16[256,1024]{1,0:T(8,128)(2,1)}, f32[256,1024]{1,0:T(8,128)}) fusion(bf16[512,1024]{1,0:T(8,128)(2,1)S(1)} %copy-done, s32[256]{0:T(256)S(1)} %eq.92), kind=kOutput, calls=%fused_computation.4 | convolution fusion | flops 269352704 | bytes 2623488 | tf_op jit(solution)/shard_map/dot_general | solution.py:350
  6.7 0.5 collective-permute-start.7
  7.3 0.2 collective-permute-start
  7.5 1.8 %collective-permute-start.12 = (bf16[128,1024]{1,0:T(8,128)(2,1)S(1)}, bf16[128,1024]{1,0:T(8,128)(2,1)}, u32[]{:S(2)}, u32[]{:S(2)}) collective-permute-start(bf16[128,1024]{1,0:T(8,128)(2,1)S(1)} %bitcast.40), channel_id=1, source_target_pairs={{0,12},{2,14},{4,0},{6,2},{8,4},{10,6},{12,8},{14,10},{1,13},{3,15... | collective-permute-start | bytes 786440 | tf_op jit(solution)/shard_map/ppermute | solution.py:28
  9.3 0.6 broadcast_in_dim.21
  9.9 5.4 %all-to-all-start = ((f32[8,10,128]{2,1,0:T(8,128)}), f32[8,10,128]{2,1,0:T(8,128)S(1)}, u32[]{:S(2)}, u32[]{:S(2)}) async-start(f32[8,10,128]{2,1,0:T(8,128)} %broadcast_in_dim.21), calls=%async_computation | async-start | bytes 131072 | tf_op jit(solution)/shard_map/all_to_all | solution.py:353
  15.3 0.1 reshape.68
  15.5 0.1 iota_compare_fusion.2
  15.6 0.1 pad_add_fusion.4.spot
  15.8 0.2 select_reduce_fusion
  16.0 0.2 and_convert_fusion
  16.2 0.1 pad_add_fusion.5.spot
  16.2 0.9 reshape.72
  17.1 0.6 collective-permute-start.4
  17.8 4.9 %history_terms.4.refs_0_ = bf16[8,4,8,1024]{3,2,1,0:T(8,128)(2,1)S(1)} custom-call(s32[2]{0:T(128)S(1)} %pad_add_fusion.2.spot, s32[8,128]{1,0:T(8,128)S(1)} %broadcast_in_dim.24.lengths_ref, bf16[128,1024]{1,0:T(8,128)(2,1)S(1)} %bitcast.41, bf16[128,1024]{1,0:T(8,128)(2,1)S(1)} %collective-permute-done.3.far_ref, bf16[127,8,8192]{2,1,0:T(8,128)(2,1)} %bitcast.43), custom_call_target="tpu_custom_call" | custom-call | flops 4993843200 | bytes 4161536 | tf_op jit(solution)/shard_map/history_terms/pallas_call | solution.py:51
  22.7 0.8 copy-done.2
  23.5 15.6 %all-to-all-done = f32[8,10,128]{2,1,0:T(8,128)S(1)} async-done(((f32[8,10,128]{2,1,0:T(8,128)}), f32[8,10,128]{2,1,0:T(8,128)S(1)}, u32[]{:S(2)}, u32[]{:S(2)}) %all-to-all-start) | async-done | bytes 40992 | tf_op jit(solution)/shard_map/all_to_all | solution.py:353
  39.1 1.0 collective-permute-start.8
  40.1 2.2 %collective-permute-start.10 = (bf16[128,1024]{1,0:T(8,128)(2,1)}, bf16[128,1024]{1,0:T(8,128)(2,1)S(1)}, u32[]{:S(2)}, u32[]{:S(2)}) collective-permute-start(bf16[128,1024]{1,0:T(8,128)(2,1)} %collective-permute-done.6.near_ref), channel_id=1, source_target_pairs={{0,4},{2,6},{4,8},{6,10},{8,12},{10,14},{12,0},{14,2},{1,5},{3,7},... | collective-permute-start | bytes 786440 | tf_op jit(solution)/shard_map/ppermute | solution.py:28
  42.3 0.9 collective-permute-start.13
  43.2 1.1 collective-permute-start.9
  44.3 0.1 broadcast_in_dim.25.inv_ref
  44.4 6.9 %projected_part.3.refs_0_ = f32[256,3072]{1,0:T(8,128)S(1)} custom-call(s32[2]{0:T(128)S(1)} %pad_add_fusion.2.spot, bf16[256,1024]{1,0:T(8,128)(2,1)} %get-tuple-element.23.near, bf16[256,1024]{1,0:T(8,128)(2,1)} %copy-done.6, f32[8,1024]{1,0:T(8,128)S(1)} %bitcast.34, f32[256,128]{1,0:T(8,128)S(1)} %broadcast_in_dim.25.inv_ref, bf16[8192,3072]{1,0:T(8,128)(2,1)} %w_hbm.9), custom_call_target="tpu_custom_call" | custom-call | flops 6442450944 | bytes 25165824 | tf_op jit(solution)/shard_map/projected_part/pallas_call | solution.py:51
  51.4 5.4 %history_terms.5.refs_0_ = bf16[8,4,8,1024]{3,2,1,0:T(8,128)(2,1)S(1)} custom-call(s32[2]{0:T(128)S(1)} %pad_add_fusion.4.spot, s32[8,128]{1,0:T(8,128)S(1)} %broadcast_in_dim.24.lengths_ref, bf16[128,1024]{1,0:T(8,128)(2,1)} %collective-permute-done.6.near_ref, ...), custom_call_target="tpu_custom_call", output_to_operand_aliasing={{}: (5, {})} | custom-call | flops 4993843200 | bytes 4161536 | tf_op jit(solution)/shard_map/history_terms/pallas_call | solution.py:51
  56.8 0.1 collective-permute-start.1
  56.9 0.9 collective-permute-start.11
  57.8 1.1 collective-permute-start.5
  58.9 1.0 collective-permute-done.9.far
  60.0 0.8 copy-done.7
  60.8 6.9 %projected_part.4.refs_0_ = f32[256,3072]{1,0:T(8,128)S(1)} custom-call(s32[2]{0:T(128)S(1)} %pad_add_fusion.4.spot, bf16[256,1024]{1,0:T(8,128)(2,1)} %collective-permute-done.near, bf16[256,1024]{1,0:T(8,128)(2,1)} %copy-done.7, f32[8,1024]{1,0:T(8,128)S(1)} %bitcast.35, f32[256,128]{1,0:T(8,128)S(1)} %broadcast_in_dim.25.inv_ref, ...), custom_call_target="tpu_custom_call", output_to_operand_aliasing={{}: (6, {})} | custom-call | flops 6442450944 | bytes 25165824 | tf_op jit(solution)/shard_map/projected_part/pallas_call | solution.py:51
  67.7 5.4 %history_terms.6.refs_0_ = bf16[8,4,8,1024]{3,2,1,0:T(8,128)(2,1)S(1)} custom-call(s32[2]{0:T(128)S(1)} %pad_add_fusion.3.spot, s32[8,128]{1,0:T(8,128)S(1)} %broadcast_in_dim.24.lengths_ref, bf16[128,1024]{1,0:T(8,128)(2,1)} %collective-permute-done.12.near_ref, ...), custom_call_target="tpu_custom_call", output_to_operand_aliasing={{}: (5, {})} | custom-call | flops 4993843200 | bytes 4161536 | tf_op jit(solution)/shard_map/history_terms/pallas_call | solution.py:51
  73.1 5.0 %history_terms.7 = bf16[8,4,8,1024]{3,2,1,0:T(8,128)(2,1)S(1)} custom-call(s32[2]{0:T(128)S(1)} %pad_add_fusion.5.spot, s32[8,128]{1,0:T(8,128)S(1)} %broadcast_in_dim.24.lengths_ref, bf16[128,1024]{1,0:T(8,128)(2,1)S(1)} %collective-permute-done.10.near_ref, bf16[128,1024]{1,0:T(8,128)(2,1)S(1)} %collective-permute-done.11.far_ref, ...), custom_call_target="tpu_custom_call", output_to_operand_aliasing={{}: (5, {})} | custom-call | flops 4993843200 | bytes 4161536 | tf_op jit(solution)/shard_map/history_terms/pallas_call | solution.py:51
  78.1 0.8 copy-done.4
  78.9 7.3 %all-to-all-start.1 = ((bf16[8,4,8,1024]{3,2,1,0:T(8,128)(2,1)}), bf16[8,4,8,1024]{3,2,1,0:T(8,128)(2,1)}, u32[]{:S(2)}, u32[]{:S(2)}) async-start(bf16[8,4,8,1024]{3,2,1,0:T(8,128)(2,1)} %copy-done.4), calls=%async_computation.1 | async-start | bytes 1048576 | tf_op jit(solution)/shard_map/all_to_all | solution.py:401
  86.2 1.0 copy.26.refs_2_
  87.3 0.1 pad_add_fusion.1.spot
  87.3 1.5 collective-permute-start.2
  88.8 6.9 %projected_part.5.refs_0_ = f32[256,3072]{1,0:T(8,128)S(1)} custom-call(s32[2]{0:T(128)S(1)} %pad_add_fusion.3.spot, bf16[256,1024]{1,0:T(8,128)(2,1)} %collective-permute-done.4.near, bf16[256,1024]{1,0:T(8,128)(2,1)} %collective-permute-done.5.far, f32[8,1024]{1,0:T(8,128)S(1)} %bitcast.36, ...), custom_call_target="tpu_custom_call", output_to_operand_aliasing={{}: (6, {})} | custom-call | flops 6442450944 | bytes 25165824 | tf_op jit(solution)/shard_map/projected_part/pallas_call | solution.py:51
  95.7 3.4 %collective-permute-done.2.far = bf16[256,1024]{1,0:T(8,128)(2,1)} collective-permute-done((bf16[256,1024]{1,0:T(8,128)(2,1)}, bf16[256,1024]{1,0:T(8,128)(2,1)}, u32[]{:S(2)}, u32[]{:S(2)}) %collective-permute-start.2) | collective-permute-done | bytes 524320 | tf_op jit(solution)/shard_map/ppermute | solution.py:28
  99.2 10.2 %gated_rows.1 = (f32[256,3072]{1,0:T(8,128)S(1)}, bf16[256,1024]{1,0:T(8,128)(2,1)S(1)}, bf16[256,1024]{1,0:T(8,128)(2,1)S(1)}, bf16[256,1024]{1,0:T(8,128)(2,1)S(1)}) custom-call(s32[4]{0:T(128)S(1)} %pad_add_fusion.1.spot, bf16[256,1024]{1,0:T(8,128)(2,1)} %collective-permute-done.1.near, ...), custom_call_target="tpu_custom_call", output_to_operand_aliasing={{0}: (6, {})} | custom-call | flops 6442450944 | bytes 25165824 | tf_op jit(solution)/shard_map/gated_rows/pallas_call | solution.py:51
  109.4 0.3 collective-permute-start.14
  109.8 0.1 pad_add_fusion.spot
  109.8 1.8 %collective-permute-start.16 = (bf16[256,1024]{1,0:T(8,128)(2,1)S(1)}, bf16[256,1024]{1,0:T(8,128)(2,1)S(1)}, u32[]{:S(2)}, u32[]{:S(2)}) collective-permute-start(bf16[256,1024]{1,0:T(8,128)(2,1)S(1)} %get-tuple-element.32), channel_id=1, source_target_pairs={{0,2},{2,0},{4,6},{6,4},{8,10},{10,8},{12,14},{14,12},{1,3},{3,1},... | collective-permute-start | bytes 1572872 | tf_op jit(solution)/shard_map/ppermute | solution.py:28
  111.7 3.8 %output_shares.3 = (bf16[256,1024]{1,0:T(8,128)(2,1)S(1)}, bf16[256,1024]{1,0:T(8,128)(2,1)S(1)}) custom-call(s32[2]{0:T(128)S(1)} %pad_add_fusion.6.spot, bf16[256,1024]{1,0:T(8,128)(2,1)S(1)} %get-tuple-element.28.x_ref, bf16[1024,8192]{1,0:T(8,128)(2,1)} %w_hbm.11), custom_call_target="tpu_custom_call" | custom-call | flops 1073741824 | bytes 4194304 | tf_op jit(solution)/shard_map/output_shares/pallas_call | solution.py:51
  115.5 0.3 collective-permute-start.18
  115.7 1.8 %collective-permute-start.20 = (bf16[256,1024]{1,0:T(8,128)(2,1)S(1)}, bf16[256,1024]{1,0:T(8,128)(2,1)S(1)}, u32[]{:S(2)}, u32[]{:S(2)}) collective-permute-start(bf16[256,1024]{1,0:T(8,128)(2,1)S(1)} %get-tuple-element.36), channel_id=1, source_target_pairs={{0,2},{2,0},{4,6},{6,4},{8,10},{10,8},{12,14},{14,12},{1,3},{3,1},... | collective-permute-start | bytes 1572872 | tf_op jit(solution)/shard_map/ppermute | solution.py:28
  117.5 5.8 %output_shares.2 = (f32[256,1024]{1,0:T(8,128)S(1)}, f32[256,1024]{1,0:T(8,128)S(1)}, f32[256,1024]{1,0:T(8,128)S(1)}, f32[256,1024]{1,0:T(8,128)S(1)}) custom-call(s32[4]{0:T(128)S(1)} %pad_add_fusion.spot, bf16[256,1024]{1,0:T(8,128)(2,1)S(1)} %get-tuple-element.28.x_ref, bf16[1024,8192]{1,0:T(8,128)(2,1)} %w_hbm.11), custom_call_target="tpu_custom_call" | custom-call | flops 2147483648 | bytes 8388608 | tf_op jit(solution)/shard_map/output_shares/pallas_call | solution.py:51
  123.3 1.0 collective-permute-done.14
  124.4 0.1 add_convert_fusion.3
  124.5 0.2 collective-permute-start.15
  124.7 7.2 %collective-permute-done.16 = bf16[256,1024]{1,0:T(8,128)(2,1)S(1)} collective-permute-done((bf16[256,1024]{1,0:T(8,128)(2,1)S(1)}, bf16[256,1024]{1,0:T(8,128)(2,1)S(1)}, u32[]{:S(2)}, u32[]{:S(2)}) %collective-permute-start.16) | collective-permute-done | bytes 524320 | tf_op jit(solution)/shard_map/ppermute | solution.py:28
  131.9 0.1 add_convert_fusion.2
  132.0 1.9 %collective-permute-start.17 = (bf16[256,1024]{1,0:T(8,128)(2,1)S(1)}, bf16[256,1024]{1,0:T(8,128)(2,1)S(1)}, u32[]{:S(2)}, u32[]{:S(2)}) collective-permute-start(bf16[256,1024]{1,0:T(8,128)(2,1)S(1)} %add_convert_fusion.2), channel_id=1, source_target_pairs={{0,4},{2,6},{4,8},{6,10},{8,12},{10,14},{12,0},{14,2},{1,5},{3,7},... | collective-permute-start | bytes 1572872 | tf_op jit(solution)/shard_map/ppermute | solution.py:28
  133.9 3.6 %collective-permute-done.18 = bf16[256,1024]{1,0:T(8,128)(2,1)S(1)} collective-permute-done((bf16[256,1024]{1,0:T(8,128)(2,1)S(1)}, bf16[256,1024]{1,0:T(8,128)(2,1)S(1)}, u32[]{:S(2)}, u32[]{:S(2)}) %collective-permute-start.18) | collective-permute-done | bytes 524320 | tf_op jit(solution)/shard_map/ppermute | solution.py:28
  137.5 0.1 add_convert_fusion.1
  137.6 1.3 collective-permute-start.19
  138.9 4.1 %collective-permute-done.20 = bf16[256,1024]{1,0:T(8,128)(2,1)S(1)} collective-permute-done((bf16[256,1024]{1,0:T(8,128)(2,1)S(1)}, bf16[256,1024]{1,0:T(8,128)(2,1)S(1)}, u32[]{:S(2)}, u32[]{:S(2)}) %collective-permute-start.20) | collective-permute-done | bytes 524320 | tf_op jit(solution)/shard_map/ppermute | solution.py:28
  143.1 5.3 %collective-permute-done.15 = bf16[256,1024]{1,0:T(8,128)(2,1)S(1)} collective-permute-done((bf16[256,1024]{1,0:T(8,128)(2,1)S(1)}, bf16[256,1024]{1,0:T(8,128)(2,1)S(1)}, u32[]{:S(2)}, u32[]{:S(2)}) %collective-permute-start.15) | collective-permute-done | bytes 524320 | tf_op jit(solution)/shard_map/ppermute | solution.py:28
  148.4 7.7 %collective-permute-done.17 = bf16[256,1024]{1,0:T(8,128)(2,1)S(1)} collective-permute-done((bf16[256,1024]{1,0:T(8,128)(2,1)S(1)}, bf16[256,1024]{1,0:T(8,128)(2,1)S(1)}, u32[]{:S(2)}, u32[]{:S(2)}) %collective-permute-start.17) | collective-permute-done | bytes 524320 | tf_op jit(solution)/shard_map/ppermute | solution.py:28
  156.0 1.3 add_convert_fusion
  (47 shorter events, 0.4 us)
Async XLA Ops:
  0.0 5.1 %copy-start = (bf16[512,1024]{1,0:T(8,128)(2,1)S(1)}, bf16[512,1024]{1,0:T(8,128)(2,1)}, u32[]{:S(2)}) copy-start(bf16[512,1024]{1,0:T(8,128)(2,1)} %param.10) | copy-start | bytes 3145732
  0.0 9.3 %copy-start.8 = (bf16[1024]{0:T(1024)(128)(2,1)S(1)}, bf16[1024]{0:T(1024)(128)(2,1)}, u32[]{:S(2)}) copy-start(bf16[1024]{0:T(1024)(128)(2,1)} %param.11) | copy-start | bytes 6148
  0.0 15.3 %copy-start.9 = (s32[128]{0:T(128)S(1)}, s32[128]{0:T(128)}, u32[]{:S(2)}) copy-start(s32[128]{0:T(128)} %param.16) | copy-start | bytes 1540
  0.0 15.8 %copy-start.10 = (s32[64]{0:T(128)S(1)}, s32[64]{0:T(128)}, u32[]{:S(2)}) copy-start(s32[64]{0:T(128)} %param.17) | copy-start | bytes 772
  1.2 15.9 %collective-permute-start.3 = (bf16[128,1024]{1,0:T(8,128)(2,1)S(1)}, bf16[128,1024]{1,0:T(8,128)(2,1)S(1)}, u32[]{:S(2)}, u32[]{:S(2)}) collective-permute-start(bf16[128,1024]{1,0:T(8,128)(2,1)S(1)} %bitcast.38), channel_id=1, source_target_pairs={{0,2},{2,0},{4,6},{6,4},{8,10},{10,8},{12,14},{14,12},{1,3},{3,1},... | collective-permute-start | bytes 786440 | tf_op jit(solution)/shard_map/ppermute | solution.py:28
  2.8 36.3 %collective-permute-start.6 = (bf16[128,1024]{1,0:T(8,128)(2,1)S(1)}, bf16[128,1024]{1,0:T(8,128)(2,1)}, u32[]{:S(2)}, u32[]{:S(2)}) collective-permute-start(bf16[128,1024]{1,0:T(8,128)(2,1)S(1)} %bitcast.39), channel_id=1, source_target_pairs={{0,4},{2,6},{4,8},{6,10},{8,12},{10,14},{12,0},{14,2},{1,5},{3,7},... | collective-permute-start | bytes 786440 | tf_op jit(solution)/shard_map/ppermute | solution.py:28
  6.7 35.5 %collective-permute-start.7 = (bf16[256,1024]{1,0:T(8,128)(2,1)}, bf16[256,1024]{1,0:T(8,128)(2,1)S(1)}, u32[]{:S(2)}, u32[]{:S(2)}) collective-permute-start(bf16[256,1024]{1,0:T(8,128)(2,1)} %get-tuple-element.23.near), channel_id=1, source_target_pairs={{0,2},{2,0},{4,6},{6,4},{8,10},{10,8},{12,14},{14,12},{1,3},{3,1},... | collective-permute-start | bytes 1572872 | tf_op jit(solution)/shard_map/ppermute | solution.py:28
  7.3 36.0 %collective-permute-start = (bf16[256,1024]{1,0:T(8,128)(2,1)}, bf16[256,1024]{1,0:T(8,128)(2,1)}, u32[]{:S(2)}, u32[]{:S(2)}) collective-permute-start(bf16[256,1024]{1,0:T(8,128)(2,1)} %get-tuple-element.23.near), channel_id=1, source_target_pairs={{0,4},{2,6},{4,8},{6,10},{8,12},{10,14},{12,0},{14,2},{1,5},{3,7},... | collective-permute-start | bytes 1572872 | tf_op jit(solution)/shard_map/ppermute | solution.py:28
  7.5 32.6 %collective-permute-start.12 = (bf16[128,1024]{1,0:T(8,128)(2,1)S(1)}, bf16[128,1024]{1,0:T(8,128)(2,1)}, u32[]{:S(2)}, u32[]{:S(2)}) collective-permute-start(bf16[128,1024]{1,0:T(8,128)(2,1)S(1)} %bitcast.40), channel_id=1, source_target_pairs={{0,12},{2,14},{4,0},{6,2},{8,4},{10,6},{12,8},{14,10},{1,13},{3,15... | collective-permute-start | bytes 786440 | tf_op jit(solution)/shard_map/ppermute | solution.py:28
  9.9 29.2 %all-to-all-start = ((f32[8,10,128]{2,1,0:T(8,128)}), f32[8,10,128]{2,1,0:T(8,128)S(1)}, u32[]{:S(2)}, u32[]{:S(2)}) async-start(f32[8,10,128]{2,1,0:T(8,128)} %broadcast_in_dim.21), calls=%async_computation | async-start | bytes 131072 | tf_op jit(solution)/shard_map/all_to_all | solution.py:353
  17.1 40.7 %collective-permute-start.4 = (bf16[256,1024]{1,0:T(8,128)(2,1)}, bf16[256,1024]{1,0:T(8,128)(2,1)}, u32[]{:S(2)}, u32[]{:S(2)}) collective-permute-start(bf16[256,1024]{1,0:T(8,128)(2,1)} %get-tuple-element.23.near), channel_id=1, source_target_pairs={{0,12},{2,14},{4,0},{6,2},{8,4},{10,6},{12,8},{14,10},{1,13},{3,15... | collective-permute-start | bytes 1572872 | tf_op jit(solution)/shard_map/ppermute | solution.py:28
  22.7 0.8 copy-start.2
  39.1 12.2 %collective-permute-start.8 = (bf16[128,1024]{1,0:T(8,128)(2,1)}, bf16[128,1024]{1,0:T(8,128)(2,1)S(1)}, u32[]{:S(2)}, u32[]{:S(2)}) collective-permute-start(bf16[128,1024]{1,0:T(8,128)(2,1)} %collective-permute-done.6.near_ref), channel_id=1, source_target_pairs={{0,2},{2,0},{4,6},{6,4},{8,10},{10,8},{12,14},{14,12},{1,3},{3,1},... | collective-permute-start | bytes 786440 | tf_op jit(solution)/shard_map/ppermute | solution.py:28
  40.1 16.8 %collective-permute-start.10 = (bf16[128,1024]{1,0:T(8,128)(2,1)}, bf16[128,1024]{1,0:T(8,128)(2,1)S(1)}, u32[]{:S(2)}, u32[]{:S(2)}) collective-permute-start(bf16[128,1024]{1,0:T(8,128)(2,1)} %collective-permute-done.6.near_ref), channel_id=1, source_target_pairs={{0,4},{2,6},{4,8},{6,10},{8,12},{10,14},{12,0},{14,2},{1,5},{3,7},... | collective-permute-start | bytes 786440 | tf_op jit(solution)/shard_map/ppermute | solution.py:28
  42.3 2.1 %copy-start.6 = (bf16[256,1024]{1,0:T(8,128)(2,1)}, bf16[256,1024]{1,0:T(8,128)(2,1)S(1)}, u32[]{:S(2)}) copy-start(bf16[256,1024]{1,0:T(8,128)(2,1)S(1)} %collective-permute-done.7.far) | copy-start | bytes 1572868
  42.3 25.4 %collective-permute-start.13 = (bf16[128,1024]{1,0:T(8,128)(2,1)}, bf16[128,1024]{1,0:T(8,128)(2,1)S(1)}, u32[]{:S(2)}, u32[]{:S(2)}) collective-permute-start(bf16[128,1024]{1,0:T(8,128)(2,1)} %collective-permute-done.12.near_ref), channel_id=1, source_target_pairs={{0,2},{2,0},{4,6},{6,4},{8,10},{10,8},{12,14},{14,12},{1,3},{3,1},... | collective-permute-start | bytes 786440 | tf_op jit(solution)/shard_map/ppermute | solution.py:28
  43.2 16.7 %collective-permute-start.9 = (bf16[256,1024]{1,0:T(8,128)(2,1)}, bf16[256,1024]{1,0:T(8,128)(2,1)S(1)}, u32[]{:S(2)}, u32[]{:S(2)}) collective-permute-start(bf16[256,1024]{1,0:T(8,128)(2,1)} %collective-permute-done.near), channel_id=1, source_target_pairs={{0,2},{2,0},{4,6},{6,4},{8,10},{10,8},{12,14},{14,12},{1,3},{3,1},... | collective-permute-start | bytes 1572872 | tf_op jit(solution)/shard_map/ppermute | solution.py:28
  44.4 6.9 %copy-start.3 = (bf16[8,4,8,1024]{3,2,1,0:T(8,128)(2,1)S(1)}, bf16[8,4,8,1024]{3,2,1,0:T(8,128)(2,1)}, u32[]{:S(2)}) copy-start(bf16[8,4,8,1024]{3,2,1,0:T(8,128)(2,1)} %copy-done.2) | copy-start | bytes 1572868
  56.8 10.9 %collective-permute-start.1 = (bf16[256,1024]{1,0:T(8,128)(2,1)}, bf16[256,1024]{1,0:T(8,128)(2,1)}, u32[]{:S(2)}, u32[]{:S(2)}) collective-permute-start(bf16[256,1024]{1,0:T(8,128)(2,1)} %collective-permute-done.near), channel_id=1, source_target_pairs={{0,4},{2,6},{4,8},{6,10},{8,12},{10,14},{12,0},{14,2},{1,5},{3,7},... | collective-permute-start | bytes 1572872 | tf_op jit(solution)/shard_map/ppermute | solution.py:28
  56.9 16.2 %collective-permute-start.11 = (bf16[128,1024]{1,0:T(8,128)(2,1)S(1)}, bf16[128,1024]{1,0:T(8,128)(2,1)S(1)}, u32[]{:S(2)}, u32[]{:S(2)}) collective-permute-start(bf16[128,1024]{1,0:T(8,128)(2,1)S(1)} %collective-permute-done.10.near_ref), channel_id=1, source_target_pairs={{0,2},{2,0},{4,6},{6,4},{8,10},{10,8},{12,14},{14,12},{1,3},{3,1},... | collective-permute-start | bytes 786440 | tf_op jit(solution)/shard_map/ppermute | solution.py:28
  57.8 31.0 %collective-permute-start.5 = (bf16[256,1024]{1,0:T(8,128)(2,1)}, bf16[256,1024]{1,0:T(8,128)(2,1)}, u32[]{:S(2)}, u32[]{:S(2)}) collective-permute-start(bf16[256,1024]{1,0:T(8,128)(2,1)} %collective-permute-done.4.near), channel_id=1, source_target_pairs={{0,2},{2,0},{4,6},{6,4},{8,10},{10,8},{12,14},{14,12},{1,3},{3,1},... | collective-permute-start | bytes 1572872 | tf_op jit(solution)/shard_map/ppermute | solution.py:28
  60.0 0.8 copy-start.7
  78.1 0.8 copy-start.4
  78.9 20.3 %all-to-all-start.1 = ((bf16[8,4,8,1024]{3,2,1,0:T(8,128)(2,1)}), bf16[8,4,8,1024]{3,2,1,0:T(8,128)(2,1)}, u32[]{:S(2)}, u32[]{:S(2)}) async-start(bf16[8,4,8,1024]{3,2,1,0:T(8,128)(2,1)} %copy-done.4), calls=%async_computation.1 | async-start | bytes 1048576 | tf_op jit(solution)/shard_map/all_to_all | solution.py:401
  87.3 11.8 %collective-permute-start.2 = (bf16[256,1024]{1,0:T(8,128)(2,1)}, bf16[256,1024]{1,0:T(8,128)(2,1)}, u32[]{:S(2)}, u32[]{:S(2)}) collective-permute-start(bf16[256,1024]{1,0:T(8,128)(2,1)} %collective-permute-done.1.near), channel_id=1, source_target_pairs={{0,2},{2,0},{4,6},{6,4},{8,10},{10,8},{12,14},{14,12},{1,3},{3,1},... | collective-permute-start | bytes 1572872 | tf_op jit(solution)/shard_map/ppermute | solution.py:28
  109.4 14.9 %collective-permute-start.14 = (bf16[256,1024]{1,0:T(8,128)(2,1)S(1)}, bf16[256,1024]{1,0:T(8,128)(2,1)S(1)}, u32[]{:S(2)}, u32[]{:S(2)}) collective-permute-start(bf16[256,1024]{1,0:T(8,128)(2,1)S(1)} %get-tuple-element.30), channel_id=1, source_target_pairs={{0,2},{2,0},{4,6},{6,4},{8,10},{10,8},{12,14},{14,12},{1,3},{3,1},... | collective-permute-start | bytes 1572872 | tf_op jit(solution)/shard_map/ppermute | solution.py:28
  109.8 22.0 %collective-permute-start.16 = (bf16[256,1024]{1,0:T(8,128)(2,1)S(1)}, bf16[256,1024]{1,0:T(8,128)(2,1)S(1)}, u32[]{:S(2)}, u32[]{:S(2)}) collective-permute-start(bf16[256,1024]{1,0:T(8,128)(2,1)S(1)} %get-tuple-element.32), channel_id=1, source_target_pairs={{0,2},{2,0},{4,6},{6,4},{8,10},{10,8},{12,14},{14,12},{1,3},{3,1},... | collective-permute-start | bytes 1572872 | tf_op jit(solution)/shard_map/ppermute | solution.py:28
  115.5 22.0 %collective-permute-start.18 = (bf16[256,1024]{1,0:T(8,128)(2,1)S(1)}, bf16[256,1024]{1,0:T(8,128)(2,1)S(1)}, u32[]{:S(2)}, u32[]{:S(2)}) collective-permute-start(bf16[256,1024]{1,0:T(8,128)(2,1)S(1)} %get-tuple-element.34), channel_id=1, source_target_pairs={{0,2},{2,0},{4,6},{6,4},{8,10},{10,8},{12,14},{14,12},{1,3},{3,1},... | collective-permute-start | bytes 1572872 | tf_op jit(solution)/shard_map/ppermute | solution.py:28
  115.7 27.4 %collective-permute-start.20 = (bf16[256,1024]{1,0:T(8,128)(2,1)S(1)}, bf16[256,1024]{1,0:T(8,128)(2,1)S(1)}, u32[]{:S(2)}, u32[]{:S(2)}) collective-permute-start(bf16[256,1024]{1,0:T(8,128)(2,1)S(1)} %get-tuple-element.36), channel_id=1, source_target_pairs={{0,2},{2,0},{4,6},{6,4},{8,10},{10,8},{12,14},{14,12},{1,3},{3,1},... | collective-permute-start | bytes 1572872 | tf_op jit(solution)/shard_map/ppermute | solution.py:28
  124.4 31.7 %copy-start.5 = (f32[256,1024]{1,0:T(8,128)S(1)}, f32[256,1024]{1,0:T(8,128)}, u32[]{:S(2)}) copy-start(f32[256,1024]{1,0:T(8,128)} %get-tuple-element.39) | copy-start | bytes 3145732
  124.5 23.8 %collective-permute-start.15 = (bf16[256,1024]{1,0:T(8,128)(2,1)S(1)}, bf16[256,1024]{1,0:T(8,128)(2,1)S(1)}, u32[]{:S(2)}, u32[]{:S(2)}) collective-permute-start(bf16[256,1024]{1,0:T(8,128)(2,1)S(1)} %add_convert_fusion.3), channel_id=1, source_target_pairs={{0,8},{2,10},{4,12},{6,14},{8,0},{10,2},{12,4},{14,6},{1,9},{3,11}... | collective-permute-start | bytes 1572872 | tf_op jit(solution)/shard_map/ppermute | solution.py:28
  132.0 24.0 %collective-permute-start.17 = (bf16[256,1024]{1,0:T(8,128)(2,1)S(1)}, bf16[256,1024]{1,0:T(8,128)(2,1)S(1)}, u32[]{:S(2)}, u32[]{:S(2)}) collective-permute-start(bf16[256,1024]{1,0:T(8,128)(2,1)S(1)} %add_convert_fusion.2), channel_id=1, source_target_pairs={{0,4},{2,6},{4,8},{6,10},{8,12},{10,14},{12,0},{14,2},{1,5},{3,7},... | collective-permute-start | bytes 1572872 | tf_op jit(solution)/shard_map/ppermute | solution.py:28
  137.5 19.9 %copy-start.1 = (bf16[512,1024]{1,0:T(8,128)(2,1)S(1)}, bf16[512,1024]{1,0:T(8,128)(2,1)}, u32[]{:S(2)}) copy-start(bf16[512,1024]{1,0:T(8,128)(2,1)} %param.10) | copy-start | bytes 3145732
  137.6 18.4 %collective-permute-start.19 = (bf16[256,1024]{1,0:T(8,128)(2,1)S(1)}, bf16[256,1024]{1,0:T(8,128)(2,1)S(1)}, u32[]{:S(2)}, u32[]{:S(2)}) collective-permute-start(bf16[256,1024]{1,0:T(8,128)(2,1)S(1)} %add_convert_fusion.1), channel_id=1, source_target_pairs={{0,12},{2,14},{4,0},{6,2},{8,4},{10,6},{12,8},{14,10},{1,13},{3,15... | collective-permute-start | bytes 1572872 | tf_op jit(solution)/shard_map/ppermute | solution.py:28
